TPU v7x, 32 devices: a whole 2x2x4 slice. The times are simulated.
32 devices in a mesh: groups: 2 (over x), expert: 16 (over z, y, core).
Axes of the slice: x: 2, y: 2, z: 4, core: 2. Of those that a mesh axis runs over, the one named last changes fastest.
Arguments:
- features: bfloat16 [4096, 256], P(('groups', 'expert')), parts along dimension 0, may hold values from -6 to 6
- scenario_id: int32 [4096], P(('groups', 'expert')), parts along dimension 0, may hold values from 0 to 7, as said below
- scenario_pads: int32 [16], P('groups'), parts along dimension 0, may hold values from 2 to 32, as said below
- device_slot: int32 [16], replicated, may hold values from 0 to 15, as said below
- mentor_raw_predictions: float32 [4096, 128], P(('groups', 'expert')), parts along dimension 0, may hold values from -500 to 500
- gate_weight: bfloat16 [8, 256, 20], replicated, may hold values from -0.375 to 0.375
- common_experts_first_matrix: bfloat16 [16, 256, 1024], P(None, 'expert'), may hold values from -0.375 to 0.375
- shared_reduce: bfloat16 [16, 1024, 256], P(None, 'expert'), may hold values from -0.1875 to 0.1875
- scenario_widen: bfloat16 [16, 256, 2048], P('expert'), may hold values from -0.375 to 0.375
- scenario_narrow: bfloat16 [16, 2048, 256], P('expert'), may hold values from -0.1875 to 0.1875
- head_weight: bfloat16 [256, 128], replicated, may hold values from -0.375 to 0.375
Outputs:
- feature_grad: bfloat16 [4096, 256], P(('groups', 'expert')), parts along dimension 0
- expand_grad: float32 [32, 256, 1024], P('groups', 'expert'), parts along dimension 0
- reduce_grad: float32 [32, 1024, 256], P('groups', 'expert'), parts along dimension 0
- widen_grad: float32 [32, 256, 2048], P(('groups', 'expert')), parts along dimension 0
- narrow_grad: float32 [32, 2048, 256], P(('groups', 'expert')), parts along dimension 0
- gate_grad: float32 [16, 256, 20], P('groups'), parts along dimension 0
- head_grad: float32 [512, 128], P('groups'), parts along dimension 0
There are 2 independent parts, one for each index of `groups`. A program takes and returns all parts, laid end to end along the dimension named above; an argument that names none is the same for every part. Nothing has to cross between parts.
Inputs may be any that keep to these rules, and one draw needn't show every extreme that they name: `scenario_id`: every device holds at least 32 rows of one scenario whose entry of scenario_pads is 32. `scenario_pads`: some entry equals 32. `device_slot`: A permutation; devices 1 i to 1 i + 1 - 1 hold slots 1 m to 1 m + 1 - 1 in this order, for some m.
All inputs are finite; a program needn't handle non-finite values.
Results may differ from a plain program's by a relative error of at most 0.013.
Values may be sent and summed in bfloat16 or wider, within the bound.
No kernel may reach another device: no remote copies, remote signals or barrier semaphores. Data moves between devices by JAX's collectives and lax.ppermute only.
A program may use at most 128 MiB of HBM per device.

v0:
```python
import jax
import jax.numpy as jnp
from jax import lax
from jax.sharding import PartitionSpec as P

distillation_warmth = 2.0
highest = lax.Precision.HIGHEST


def silu_slope(affine_response):
    sigmoid = jax.nn.sigmoid(affine_response)
    return sigmoid * (1.0 + affine_response * (1.0 - sigmoid))


def contract(left, right, contraction_axis_index, right_dim):
    return lax.dot_general(
        left,
        right,
        (((contraction_axis_index,), (right_dim,)), ((), ())),
        preferred_element_type=jnp.float32,
    )


def expert_forward(inputs, weight_in, weight_out):
    affine_response = jnp.dot(inputs, weight_in, preferred_element_type=jnp.float32)
    active = jax.nn.silu(affine_response).astype(jnp.bfloat16)
    output = jnp.dot(active, weight_out, preferred_element_type=jnp.float32)
    return (output, affine_response, active)


def expert_backward(cotangent, inputs, affine_response, active, weight_in, weight_out):
    hidden_grad = contract(cotangent, weight_out, 1, 1)
    linear_grad = (hidden_grad * silu_slope(affine_response)).astype(jnp.bfloat16)
    second_grad = contract(active, cotangent, 0, 0)
    first_grad = contract(inputs, linear_grad, 0, 0)
    return (contract(linear_grad, weight_in, 1, 1), first_grad, second_grad)


def body(
    features,
    scenario_id,
    scenario_pads,
    device_slot,
    mentor_raw_predictions,
    gate_weight,
    common_experts_first_matrix,
    shared_reduce,
    scenario_widen,
    scenario_narrow,
    head_weight,
):
    row_count, model_width = features.shape
    devices = lax.axis_size("expert")
    own_index = lax.axis_index("expert")
    shared_count = common_experts_first_matrix.shape[0]
    hidden_width = common_experts_first_matrix.shape[2]
    copies = devices // shared_count
    piece_rows = row_count // copies
    scenario_count = gate_weight.shape[0]
    gate_count = gate_weight.shape[2]
    scenario_experts = gate_count - shared_count
    capacity = row_count // 4
    group_size = devices // scenario_count
    labels = jnp.arange(scenario_count, dtype=jnp.int32)
    onehot = scenario_id[:, None] == labels[None, :]
    flattened_gate = jnp.transpose(gate_weight, (1, 0, 2)).reshape(
        model_width, scenario_count * gate_count
    )
    every_logit = jnp.dot(features, flattened_gate, preferred_element_type=jnp.float32).reshape(
        row_count, scenario_count, gate_count
    )
    gate_probs = jax.nn.softmax(
        jnp.sum(jnp.where(onehot[:, :, None], every_logit, 0.0), axis=1), axis=-1
    )
    gate_round = gate_probs.astype(jnp.bfloat16)
    own_slot = lax.dynamic_slice_in_dim(device_slot, own_index, 1)[0]
    local_widen = scenario_widen[0]
    narrow_rows = scenario_narrow[0]
    split_count = 1
    share_rows = capacity // split_count
    expert_width = local_widen.shape[1]
    slice_experts = max(1, expert_width // hidden_width)
    expert_span = expert_width // slice_experts
    first_expert = own_slot % group_size // split_count * expert_width // hidden_width
    pick_matrix = (
        jnp.arange(scenario_experts)[:, None] == first_expert + jnp.arange(slice_experts)[None, :]
    ).astype(jnp.bfloat16)
    local_narrow = narrow_rows.reshape(slice_experts, expert_span, model_width)
    member = onehot.astype(jnp.int32)
    slot_rank = jnp.sum((jnp.cumsum(member, axis=0) - 1) * member, axis=1)
    kept_rows = slot_rank < jnp.sum(member * scenario_pads[None, :], axis=1)
    dispatch_mask = (
        onehot.T[:, None, :]
        & (slot_rank[None, None, :] == jnp.arange(capacity)[None, :, None])
        & kept_rows[None, None, :]
    )
    dispatch_half = dispatch_mask.astype(jnp.bfloat16)
    dispatch_wide = dispatch_mask.astype(jnp.float32)
    route_key = device_slot // group_size * split_count + device_slot % split_count
    route_mask = route_key[:, None] == jnp.arange(scenario_count * split_count)[None, :]
    route_half = route_mask.astype(jnp.bfloat16)
    route_wide = route_mask.astype(jnp.float32)

    def to_owners(values):
        per_scenario = jnp.einsum(
            "sct,tj->scj", dispatch_half, values, preferred_element_type=jnp.float32
        ).astype(jnp.bfloat16)
        return jnp.einsum(
            "es,scj->ecj", route_half, per_scenario, preferred_element_type=jnp.float32
        ).astype(jnp.bfloat16)

    def from_owners(values):
        per_scenario = jnp.einsum("es,ecj->scj", route_wide, values, precision=highest)
        return jnp.einsum("sct,scj->tj", dispatch_wide, per_scenario, precision=highest)

    rows_out = to_owners(features)
    gates_out = to_owners(gate_round[:, shared_count:])
    expand_copies = jnp.repeat(common_experts_first_matrix, copies, axis=0)
    reduce_copies = jnp.repeat(shared_reduce, copies, axis=0)
    row_tiles = jnp.tile(features.reshape(copies, piece_rows, model_width), (shared_count, 1, 1))
    expand_got, reduce_got, scenario_got, gate_got, tiles_got = (
        lax.all_to_all(expand_copies, "expert", split_axis=0, concat_axis=0, tiled=True),
        lax.all_to_all(reduce_copies, "expert", split_axis=0, concat_axis=0, tiled=True),
        lax.all_to_all(rows_out, "expert", split_axis=0, concat_axis=0, tiled=True),
        lax.all_to_all(gates_out, "expert", split_axis=0, concat_axis=0, tiled=True),
        lax.all_to_all(row_tiles, "expert", split_axis=0, concat_axis=0, tiled=True),
    )
    own_expand = expand_got.reshape(model_width, hidden_width)
    own_reduce = reduce_got.reshape(hidden_width, model_width)
    inputs = scenario_got.reshape(-1, model_width)
    scenario_chosen = jnp.dot(
        gate_got.reshape(-1, scenario_experts), pick_matrix, preferred_element_type=jnp.float32
    )
    affine_response = jnp.dot(inputs, local_widen, preferred_element_type=jnp.float32)
    active = jax.nn.silu(affine_response).astype(jnp.bfloat16)
    outputs = jnp.einsum(
        "mek,ekd->med",
        active.reshape(-1, slice_experts, expert_span),
        local_narrow,
        preferred_element_type=jnp.float32,
    )
    mixed_rows = jnp.sum(scenario_chosen[:, :, None] * outputs, axis=1)
    mixed_rows, owner_rows, chosen, owner_linear, owner_active, holder_results_matrix = (
        mixed_rows.reshape(devices, share_rows, model_width),
        inputs,
        scenario_chosen,
        affine_response,
        active,
        outputs,
    )
    shared_inputs = tiles_got.reshape(-1, model_width)
    shared_out, shared_linear, shared_active = expert_forward(shared_inputs, own_expand, own_reduce)
    mixed_returns, output_returns = (
        lax.all_to_all(mixed_rows, "expert", split_axis=0, concat_axis=0, tiled=True),
        lax.all_to_all(
            shared_out.reshape(devices, piece_rows, model_width),
            "expert",
            split_axis=0,
            concat_axis=0,
            tiled=True,
        ),
    )
    expert_outputs = output_returns.reshape(shared_count, row_count, model_width)
    shared_probs = gate_round[:, :shared_count].astype(jnp.float32)
    shared_mix = jnp.einsum("tk,ktd->td", shared_probs, expert_outputs, precision=highest)
    layer_output = shared_mix + from_owners(mixed_returns)
    layer_round = layer_output.astype(jnp.bfloat16)
    learner_raw_predictions = jnp.dot(layer_round, head_weight, preferred_element_type=jnp.float32)
    prediction_derivative = (
        distillation_warmth
        * (
            jax.nn.softmax(learner_raw_predictions / distillation_warmth, axis=-1)
            - jax.nn.softmax(mentor_raw_predictions / distillation_warmth, axis=-1)
        )
    ).astype(jnp.bfloat16)
    head_grad = contract(layer_round, prediction_derivative, 0, 0)
    output_grad = contract(prediction_derivative, head_weight, 1, 1)
    output_round = output_grad.astype(jnp.bfloat16)
    output_wide = output_round.astype(jnp.float32)
    shared_dots = jnp.einsum("td,ktd->tk", output_wide, expert_outputs, precision=highest)
    shared_cotangent = (shared_probs.T[:, :, None] * output_wide[None, :, :]).astype(jnp.bfloat16)
    cotangent_out = to_owners(output_round)
    cotangent_got, shared_arriving = (
        lax.all_to_all(cotangent_out, "expert", split_axis=0, concat_axis=0, tiled=True),
        lax.all_to_all(
            shared_cotangent.reshape(devices, piece_rows, model_width),
            "expert",
            split_axis=0,
            concat_axis=0,
            tiled=True,
        ),
    )
    input_part, expand_part, reduce_part = expert_backward(
        shared_arriving.reshape(-1, model_width),
        shared_inputs,
        shared_linear,
        shared_active,
        own_expand,
        own_reduce,
    )
    cotangent = cotangent_got.reshape(-1, model_width)
    cotangent_wide = cotangent.astype(jnp.float32)
    part_grad = jnp.einsum("md,med->me", cotangent_wide, holder_results_matrix, precision=highest)
    hidden_grad = jnp.einsum(
        "md,ekd->mek", cotangent, local_narrow, preferred_element_type=jnp.float32
    )
    linear_grad = (
        (chosen[:, :, None] * hidden_grad).reshape(-1, expert_width) * silu_slope(owner_linear)
    ).astype(jnp.bfloat16)
    gated_active = (
        chosen[:, :, None] * owner_active.reshape(-1, slice_experts, expert_span)
    ).astype(jnp.bfloat16)
    block_widen = contract(owner_rows, linear_grad, 0, 0)
    block_narrow = jnp.einsum(
        "mek,md->ekd", gated_active, cotangent, preferred_element_type=jnp.float32
    ).reshape(expert_width, model_width)
    input_grad = contract(linear_grad, local_widen, 1, 1)
    gate_columns = contract(part_grad, pick_matrix.astype(jnp.float32), 1, 1)
    owner_input = input_grad.reshape(devices, share_rows, model_width)
    owner_gate = gate_columns.reshape(devices, share_rows, scenario_experts)
    returned_rows, returned_gates, expand_pieces, reduce_pieces, shared_returns = (
        lax.all_to_all(
            owner_input.astype(jnp.bfloat16), "expert", split_axis=0, concat_axis=0, tiled=True
        ).astype(owner_input.dtype),
        lax.all_to_all(
            owner_gate.astype(jnp.bfloat16), "expert", split_axis=0, concat_axis=0, tiled=True
        ).astype(owner_gate.dtype),
        lax.all_to_all(
            expand_part.reshape(devices, -1, hidden_width).astype(jnp.bfloat16),
            "expert",
            split_axis=0,
            concat_axis=0,
            tiled=True,
        ).astype(jnp.float32),
        lax.all_to_all(
            reduce_part.reshape(devices, -1, model_width).astype(jnp.bfloat16),
            "expert",
            split_axis=0,
            concat_axis=0,
            tiled=True,
        ).astype(jnp.float32),
        lax.all_to_all(
            input_part.reshape(devices, piece_rows, model_width).astype(jnp.bfloat16),
            "expert",
            split_axis=0,
            concat_axis=0,
            tiled=True,
        ).astype(jnp.float32),
    )
    common_grad = jnp.sum(shared_returns.reshape(shared_count, row_count, model_width), axis=0)
    expand_grad = jnp.sum(
        expand_pieces.reshape(shared_count, copies, model_width // devices, hidden_width), axis=1
    )
    reduce_grad = jnp.sum(
        reduce_pieces.reshape(shared_count, copies, hidden_width // devices, model_width), axis=1
    )
    routed_grad = from_owners(returned_rows)
    routed_dots = from_owners(returned_gates)
    mix_grad = jnp.concatenate([shared_dots, routed_dots], axis=1)
    score_gradient = gate_probs * (mix_grad - jnp.sum(gate_probs * mix_grad, axis=1, keepdims=True))
    score_round = score_gradient.astype(jnp.bfloat16)
    score_wide = jnp.where(
        onehot[:, :, None], score_round[:, None, :], jnp.zeros((), jnp.bfloat16)
    ).reshape(row_count, scenario_count * gate_count)
    gate_part = jnp.transpose(
        contract(features, score_wide, 0, 0).reshape(model_width, scenario_count, gate_count),
        (1, 0, 2),
    )
    gate_input = contract(score_wide, flattened_gate, 1, 1)
    gate_total, head_total = lax.psum((gate_part, head_grad), "expert")
    feature_grad = (common_grad + routed_grad + gate_input).astype(jnp.bfloat16)
    return (
        feature_grad,
        expand_grad,
        reduce_grad,
        block_widen[None],
        block_narrow[None],
        gate_total,
        head_total,
    )


def solution(mesh):
    placed = (
        P(("groups", "expert"), None),
        P(("groups", "expert")),
        P("groups"),
        P(),
        P(("groups", "expert"), None),
        P(),
        P(None, "expert", None),
        P(None, "expert", None),
        P("expert", None, None),
        P("expert", None, None),
        P(),
    )
    return jax.shard_map(
        body,
        mesh=mesh,
        in_specs=placed,
        out_specs=(
            P(("groups", "expert"), None),
            P("groups", "expert", None),
            P("groups", "expert", None),
            P(("groups", "expert"), None, None),
            P(("groups", "expert"), None, None),
            P("groups", None, None),
            P("groups", None),
        ),
        check_vma=False,
    )
```

profile of v0, /device:TPU:0, one launch (start us, length us, event | category | flops | bytes accessed | tf_op | source)
XLA Modules:
  0.0 429.1 jit_solution(13225101821550244005)
XLA Ops:
  10.5 0.9 copy.85
  11.5 1.0 fusion.20
  13.6 7.4 %all-to-all-start.4 = ((bf16[16,32,4]{1,2,0:T(4,128)(2,1)}), bf16[16,32,4]{1,2,0:T(4,128)(2,1)S(1)}, u32[]{:S(2)}, u32[]{:S(2)}) async-start(bf16[16,32,4]{1,2,0:T(4,128)(2,1)} %copy.87), calls=%async_computation.4 | async-start | bytes 32768 | tf_op jit(solution)/shard_map/all_to_all | solution.py:125
  21.7 1.2 convolution_convert_fusion.5
  23.0 4.5 %all-to-all-done.4 = bf16[16,32,4]{1,2,0:T(4,128)(2,1)S(1)} async-done(((bf16[16,32,4]{1,2,0:T(4,128)(2,1)}), bf16[16,32,4]{1,2,0:T(4,128)(2,1)S(1)}, u32[]{:S(2)}, u32[]{:S(2)}) %all-to-all-start.4) | async-done | bytes 4128 | tf_op jit(solution)/shard_map/all_to_all | solution.py:125
  27.5 12.6 %all_to_all.70 = bf16[16,32,256]{2,1,0:T(8,128)(2,1)S(1)} all-to-all(bf16[16,32,256]{2,1,0:T(8,128)(2,1)S(1)} %copy.90), channel_id=1, replica_groups=mesh['groups'=2,'expert'=16] {'expert'}, dimensions={0} | all-to-all | bytes 524288 | tf_op jit(solution)/shard_map/all_to_all | solution.py:124
  40.2 18.0 %all_to_all.71 = bf16[16,16,1024]{2,1,0:T(8,128)(2,1)S(1)} all-to-all(bf16[16,16,1024]{2,1,0:T(8,128)(2,1)} %param.17), channel_id=1, replica_groups=mesh['groups'=2,'expert'=16] {'expert'}, dimensions={0} | all-to-all | bytes 1048576 | tf_op jit(solution)/shard_map/all_to_all | solution.py:122
  58.1 18.7 %all_to_all.72 = bf16[16,64,256]{2,1,0:T(8,128)(2,1)} all-to-all(bf16[16,64,256]{2,1,0:T(8,128)(2,1)} %param.18), channel_id=1, replica_groups=mesh['groups'=2,'expert'=16] {'expert'}, dimensions={0} | all-to-all | bytes 1048576 | tf_op jit(solution)/shard_map/all_to_all | solution.py:123
  76.8 1.1 tile.2
  77.9 4.0 all-to-all-start
  84.8 3.3 multiply_convert_fusion.4
  88.1 1.3 copy-done.5
  89.4 2.5 multiply_reduce_fusion
  91.9 12.9 %all-to-all-done = bf16[16,128,256]{2,1,0:T(8,128)(2,1)S(1)} async-done(((bf16[16,128,256]{2,1,0:T(8,128)(2,1)}), bf16[16,128,256]{2,1,0:T(8,128)(2,1)S(1)}, u32[]{:S(2)}, u32[]{:S(2)}) %all-to-all-start) | async-done | bytes 1048608 | tf_op jit(solution)/shard_map/all_to_all | solution.py:126
  104.9 6.9 %all-to-all-start.6 = ((f32[16,32,256]{2,1,0:T(8,128)}), f32[16,32,256]{2,1,0:T(8,128)S(1)}, u32[]{:S(2)}, u32[]{:S(2)}) async-start(f32[16,32,256]{2,1,0:T(8,128)} %bitcast.184), calls=%async_computation.6 | async-start | bytes 1048576 | tf_op jit(solution)/shard_map/all_to_all | solution.py:154
  111.8 4.6 %multiply_convert_fusion.1 = (bf16[2048,1024]{1,0:T(8,128)(2,1)S(1)}, f32[2048,1024]{1,0:T(8,128)}) fusion(bf16[2048,256]{1,0:T(8,128)(2,1)S(1)} %bitcast.173, bf16[256,1024]{1,0:T(8,128)(2,1)S(1)} %bitcast.179), kind=kOutput, calls=%fused_computation.6 | convolution fusion | flops 1084227584 | bytes 14155776 | tf_op jit(solution)/shard_map/dot_general | solution.py:25
  116.4 2.6 fusion.73
  119.0 7.2 %all-to-all-done.6 = f32[16,32,256]{2,1,0:T(8,128)S(1)} async-done(((f32[16,32,256]{2,1,0:T(8,128)}), f32[16,32,256]{2,1,0:T(8,128)S(1)}, u32[]{:S(2)}, u32[]{:S(2)}) %all-to-all-start.6) | async-done | bytes 524320 | tf_op jit(solution)/shard_map/all_to_all | solution.py:154
  127.0 4.1 all-to-all-start.3
  132.0 1.6 fusion.26
  133.6 38.6 %all-to-all-done.3 = f32[16,128,256]{2,1,0:T(8,128)S(1)} async-done(((f32[16,128,256]{2,1,0:T(8,128)}), f32[16,128,256]{2,1,0:T(8,128)S(1)}, u32[]{:S(2)}, u32[]{:S(2)}) %all-to-all-start.3) | async-done | bytes 2097184 | tf_op jit(solution)/shard_map/all_to_all | solution.py:155
  172.2 2.0 fusion.9
  174.3 1.0 fusion.18
  175.3 1.1 fusion.71
  176.5 1.7 fusion.72
  178.2 1.1 convolution_convert_fusion.4
  179.4 21.1 %all_to_all.73 = bf16[16,32,256]{2,1,0:T(8,128)(2,1)S(1)} all-to-all(bf16[16,32,256]{2,1,0:T(8,128)(2,1)S(1)} %copy.96), channel_id=1, replica_groups=mesh['groups'=2,'expert'=16] {'expert'}, dimensions={0} | all-to-all | bytes 524288 | tf_op jit(solution)/shard_map/all_to_all | solution.py:184
  200.4 3.8 fusion.24
  205.0 1.4 convert_element_type.134
  206.4 1.3 copy.100
  207.7 4.1 all-to-all-start.11
  211.8 2.2 multiply_convert_fusion.5
  214.1 4.3 all-to-all-done.11
  218.3 4.3 %all-to-all-start.7 = ((bf16[16,128,256]{2,1,0:T(8,128)(2,1)}), bf16[16,128,256]{2,1,0:T(8,128)(2,1)}, u32[]{:S(2)}, u32[]{:S(2)}) async-start(bf16[16,128,256]{2,1,0:T(8,128)(2,1)} %multiply_convert_fusion.5), calls=%async_computation.7 | async-start | bytes 2097152 | tf_op jit(solution)/shard_map/all_to_all | solution.py:185
  222.7 2.0 multiply_bitcast_fusion
  225.0 1.9 copy-done.4
  226.9 1.6 multiply_convert_fusion.3
  228.4 1.3 copy-done.3
  229.8 1.5 convolution_convert_fusion.3
  231.2 14.4 %all-to-all-done.7 = bf16[16,128,256]{2,1,0:T(8,128)(2,1)} async-done(((bf16[16,128,256]{2,1,0:T(8,128)(2,1)}), bf16[16,128,256]{2,1,0:T(8,128)(2,1)}, u32[]{:S(2)}, u32[]{:S(2)}) %all-to-all-start.7) | async-done | bytes 1048608 | tf_op jit(solution)/shard_map/all_to_all | solution.py:185
  245.6 6.8 %all-to-all-start.10 = ((bf16[16,32,256]{2,1,0:T(8,128)(2,1)}), bf16[16,32,256]{2,1,0:T(8,128)(2,1)S(1)}, u32[]{:S(2)}, u32[]{:S(2)}) async-start(bf16[16,32,256]{2,1,0:T(8,128)(2,1)} %convolution_convert_fusion.3), calls=%async_computation.10 | async-start | bytes 524288 | tf_op jit(solution)/shard_map/all_to_all | solution.py:222
  252.4 6.0 %fusion.3 = bf16[1024,2048]{0,1:T(8,128)(2,1)} fusion(f32[2048,1024]{1,0:T(8,128)} %get-tuple-element.48), kind=kLoop, calls=%fused_computation.8 | loop fusion | flops 10485760 | bytes 12582912 | tf_op jit(solution)/shard_map/convert_element_type | solution.py:26
  258.4 6.6 %copy.104 = bf16[1024,2048]{1,0:T(8,128)(2,1)} copy(bf16[1024,2048]{0,1:T(8,128)(2,1)} %fusion.3) | data formatting | bytes 8388608 | tf_op jit(solution)/shard_map/convert_element_type | solution.py:26
  265.0 4.6 %convolution_convert_fusion.1 = bf16[16,64,256]{2,1,0:T(8,128)(2,1)} fusion(bf16[16,64,2048]{2,1,0:T(8,128)(2,1)} %bitcast.165, bf16[2048,256,1]{1,0,2:T(8,128)(2,1)} %bitcast.39), kind=kOutput, calls=%fused_computation.28 | convolution fusion | flops 1074003968 | bytes 5767168 | tf_op jit(solution)/shard_map/dot_general | solution.py:16
  270.3 6.0 %all-to-all-start.13 = ((bf16[16,64,256]{2,1,0:T(8,128)(2,1)}), bf16[16,64,256]{2,1,0:T(8,128)(2,1)S(1)}, u32[]{:S(2)}, u32[]{:S(2)}) async-start(bf16[16,64,256]{2,1,0:T(8,128)(2,1)} %convolution_convert_fusion.1), calls=%async_computation.13 | async-start | bytes 1048576 | tf_op jit(solution)/shard_map/all_to_all | solution.py:235
  276.4 6.1 %multiply_convert_fusion = bf16[2048,1024]{1,0:T(8,128)(2,1)S(1)} fusion(f32[2048,1024]{1,0:T(8,128)} %get-tuple-element.48, bf16[2048,256]{1,0:T(8,128)(2,1)} %bitcast.20, bf16[1024,256]{1,0:T(8,128)(2,1)S(1)} %bitcast.182), kind=kOutput, calls=%fused_computation.5 | convolution fusion | flops 1092616192 | bytes 14155776 | tf_op jit(solution)/shard_map/dot_general | solution.py:16
  282.5 2.0 copy-done.48
  284.5 2.1 convolution_convert_fusion.2
  286.6 4.2 all-to-all-done.13
  290.8 4.1 all-to-all-start.12
  294.9 3.3 fusion.4
  298.2 3.9 copy.106
  302.2 2.2 fusion.7
  304.4 4.8 %convolution_convert_fusion = bf16[16,128,256]{2,1,0:T(8,128)(2,1)} fusion(bf16[16,128,1024]{2,1,0:T(8,128)(2,1)} %bitcast.191, bf16[256,1024,1]{1,0,2:T(8,128)(2,1)} %bitcast.180), kind=kOutput, calls=%fused_computation.26 | convolution fusion | flops 1074266112 | bytes 5767168 | tf_op jit(solution)/shard_map/dot_general | solution.py:16
  309.4 6.0 %all-to-all-start.8 = ((bf16[16,128,256]{2,1,0:T(8,128)(2,1)}), bf16[16,128,256]{2,1,0:T(8,128)(2,1)}, u32[]{:S(2)}, u32[]{:S(2)}) async-start(bf16[16,128,256]{2,1,0:T(8,128)(2,1)} %convolution_convert_fusion), calls=%async_computation.8 | async-start | bytes 2097152 | tf_op jit(solution)/shard_map/all_to_all | solution.py:242
  315.4 0.9 fusion.74
  316.3 2.0 convolution_bitcast_fusion
  318.4 0.9 fusion.45
  320.5 3.8 convolution_bitcast_fusion.1
  324.4 90.6 %all-reduce.3.cloned.1.call-done = (f32[8,256,20]{1,2,0:T(8,128)}, f32[256,128]{1,0:T(8,128)}) async-done(((f32[8,256,20]{1,2,0:T(8,128)}, f32[256,128]{1,0:T(8,128)}), (f32[8,256,20]{1,2,0:T(8,128)}, f32[256,128]{1,0:T(8,128)})) %all-reduce.3.cloned.1.call-update) | async-done | bytes 294928 | tf_op jit(solution)/shard_map/psum | solution.py:270
  414.9 1.7 copy.107
  416.9 1.1 convert_element_type.140
  418.0 1.1 convert_element_type.143
  419.0 1.4 convert_reduce_fusion
  (143 shorter events, 13.2 us)
Async XLA Ops:
  7.2 77.7 %copy-start = (bf16[1,256,2048]{2,1,0:T(8,128)(2,1)S(1)}, bf16[1,256,2048]{2,1,0:T(8,128)(2,1)}, u32[]{:S(2)}) copy-start(bf16[1,256,2048]{2,1,0:T(8,128)(2,1)} %param.19) | copy-start | bytes 3145732
  7.2 74.8 %copy-start.47 = (s32[16]{0:T(128)S(1)}, s32[16]{0:T(128)}, u32[]{:S(2)}) copy-start(s32[16]{0:T(128)} %param.14) | copy-start | bytes 196
  7.2 69.6 %copy-start.17 = (bf16[128,256]{1,0:T(8,128)(2,1)S(1)}, bf16[128,256]{1,0:T(8,128)(2,1)}, u32[]{:S(2)}) copy-start(bf16[128,256]{1,0:T(8,128)(2,1)} %param.11) | copy-start | bytes 196612
  8.0 13.1 %copy-start.37 = (pred[8,128]{1,0:T(8,128)(4,1)}, pred[8,128]{1,0:T(8,128)(4,1)S(1)}, u32[]{:S(2)}) copy-start(pred[8,128]{1,0:T(8,128)(4,1)S(1)} %iota_compare_fusion.3) | copy-start | bytes 3076
  9.4 11.7 %copy-start.28 = (s32[16]{0:T(128)}, s32[16]{0:T(128)S(1)}, u32[]{:S(2)}) copy-start(s32[16]{0:T(128)S(1)} %and_select_fusion) | copy-start | bytes 196
  9.5 11.6 %copy-start.34 = (pred[128,8]{0,1:T(8,128)(4,1)}, pred[128,8]{0,1:T(8,128)(4,1)S(1)}, u32[]{:S(2)}) copy-start(pred[128,8]{0,1:T(8,128)(4,1)S(1)} %copy.84) | copy-start | bytes 3076
  10.5 10.5 %copy-start.42 = (pred[128]{0:T(512)(128)(4,1)}, pred[128]{0:T(512)(128)(4,1)S(1)}, u32[]{:S(2)}) copy-start(pred[128]{0:T(512)(128)(4,1)S(1)} %lt.20) | copy-start | bytes 388
  12.6 8.6 %copy-start.32 = (f32[128]{0:T(128)}, f32[128]{0:T(128)S(1)}, u32[]{:S(2)}) copy-start(f32[128]{0:T(128)S(1)} %reduce_max.27) | copy-start | bytes 1540
  12.6 8.5 %copy-start.40 = (f32[128]{0:T(128)}, f32[128]{0:T(128)S(1)}, u32[]{:S(2)}) copy-start(f32[128]{0:T(128)S(1)} %fusion.48) | copy-start | bytes 1540
  13.6 13.9 %all-to-all-start.4 = ((bf16[16,32,4]{1,2,0:T(4,128)(2,1)}), bf16[16,32,4]{1,2,0:T(4,128)(2,1)S(1)}, u32[]{:S(2)}, u32[]{:S(2)}) async-start(bf16[16,32,4]{1,2,0:T(4,128)(2,1)} %copy.87), calls=%async_computation.4 | async-start | bytes 32768 | tf_op jit(solution)/shard_map/all_to_all | solution.py:125
  21.1 0.6 copy-start.25
  40.2 48.0 %copy-start.11 = (bf16[16,32,256]{2,1,0:T(8,128)(2,1)}, bf16[16,32,256]{2,1,0:T(8,128)(2,1)S(1)}, u32[]{:S(2)}) copy-start(bf16[16,32,256]{2,1,0:T(8,128)(2,1)S(1)} %all_to_all.70) | copy-start | bytes 786436
  58.1 53.6 %copy-start.19 = (bf16[16,16,1024]{2,1,0:T(8,128)(2,1)}, bf16[16,16,1024]{2,1,0:T(8,128)(2,1)S(1)}, u32[]{:S(2)}) copy-start(bf16[16,16,1024]{2,1,0:T(8,128)(2,1)S(1)} %all_to_all.71) | copy-start | bytes 1572868
  77.9 27.0 %all-to-all-start = ((bf16[16,128,256]{2,1,0:T(8,128)(2,1)}), bf16[16,128,256]{2,1,0:T(8,128)(2,1)S(1)}, u32[]{:S(2)}, u32[]{:S(2)}) async-start(bf16[16,128,256]{2,1,0:T(8,128)(2,1)} %tile.2), calls=%async_computation | async-start | bytes 2097152 | tf_op jit(solution)/shard_map/all_to_all | solution.py:126
  84.5 3.6 copy-start.45
  84.8 3.3 copy-start.31
  84.8 4.6 %copy-start.16 = (bf16[1,2048,256]{2,1,0:T(8,128)(2,1)S(1)}, bf16[1,2048,256]{2,1,0:T(8,128)(2,1)}, u32[]{:S(2)}) copy-start(bf16[1,2048,256]{2,1,0:T(8,128)(2,1)} %param.20) | copy-start | bytes 3145732
  88.1 1.3 copy-start.5
  104.9 11.5 %copy-start.14 = (bf16[16,128,256]{2,1,0:T(8,128)(2,1)}, bf16[16,128,256]{2,1,0:T(8,128)(2,1)S(1)}, u32[]{:S(2)}) copy-start(bf16[16,128,256]{2,1,0:T(8,128)(2,1)S(1)} %all-to-all-done) | copy-start | bytes 3145732
  104.9 21.3 %all-to-all-start.6 = ((f32[16,32,256]{2,1,0:T(8,128)}), f32[16,32,256]{2,1,0:T(8,128)S(1)}, u32[]{:S(2)}, u32[]{:S(2)}) async-start(f32[16,32,256]{2,1,0:T(8,128)} %bitcast.184), calls=%async_computation.6 | async-start | bytes 1048576 | tf_op jit(solution)/shard_map/all_to_all | solution.py:154
  111.8 4.7 %copy-start.20 = (bf16[16,64,256]{2,1,0:T(8,128)(2,1)S(1)}, bf16[16,64,256]{2,1,0:T(8,128)(2,1)}, u32[]{:S(2)}) copy-start(bf16[16,64,256]{2,1,0:T(8,128)(2,1)} %all_to_all.72) | copy-start | bytes 1572868
  116.4 14.7 %copy-start.27 = (f32[128,128]{1,0:T(8,128)S(1)}, f32[128,128]{1,0:T(8,128)}, u32[]{:S(2)}) copy-start(f32[128,128]{1,0:T(8,128)} %param.15) | copy-start | bytes 196612
  126.2 0.8 copy-start.10
  127.0 45.2 %all-to-all-start.3 = ((f32[16,128,256]{2,1,0:T(8,128)}), f32[16,128,256]{2,1,0:T(8,128)S(1)}, u32[]{:S(2)}, u32[]{:S(2)}) async-start(f32[16,128,256]{2,1,0:T(8,128)} %fusion.73), calls=%async_computation.3 | async-start | bytes 4194304 | tf_op jit(solution)/shard_map/all_to_all | solution.py:155
  176.5 1.7 copy-start.23
  179.3 25.0 %copy-start.46 = (s32[2]{0:T(128)S(1)}, s32[2]{0:T(128)}, u32[]{:S(2)}) copy-start(s32[2]{0:T(128)} %copy-done.45) | copy-start | bytes 28
  207.7 10.6 %all-to-all-start.11 = ((bf16[16,32,4]{1,2,0:T(4,128)(2,1)}), bf16[16,32,4]{1,2,0:T(4,128)(2,1)}, u32[]{:S(2)}, u32[]{:S(2)}) async-start(bf16[16,32,4]{1,2,0:T(4,128)(2,1)} %copy.100), calls=%async_computation.11 | async-start | bytes 32768 | tf_op jit(solution)/shard_map/all_to_all | solution.py:225
  218.3 27.3 %all-to-all-start.7 = ((bf16[16,128,256]{2,1,0:T(8,128)(2,1)}), bf16[16,128,256]{2,1,0:T(8,128)(2,1)}, u32[]{:S(2)}, u32[]{:S(2)}) async-start(bf16[16,128,256]{2,1,0:T(8,128)(2,1)} %multiply_convert_fusion.5), calls=%async_computation.7 | async-start | bytes 2097152 | tf_op jit(solution)/shard_map/all_to_all | solution.py:185
  224.7 2.2 copy-start.4
  228.4 1.4 copy-start.3
  245.6 24.0 %all-to-all-start.10 = ((bf16[16,32,256]{2,1,0:T(8,128)(2,1)}), bf16[16,32,256]{2,1,0:T(8,128)(2,1)S(1)}, u32[]{:S(2)}, u32[]{:S(2)}) async-start(bf16[16,32,256]{2,1,0:T(8,128)(2,1)} %convolution_convert_fusion.3), calls=%async_computation.10 | async-start | bytes 524288 | tf_op jit(solution)/shard_map/all_to_all | solution.py:222
  265.0 11.3 %copy-start.21 = (bf16[16,64,256]{2,1,0:T(8,128)(2,1)S(1)}, bf16[16,64,256]{2,1,0:T(8,128)(2,1)}, u32[]{:S(2)}) copy-start(bf16[16,64,256]{2,1,0:T(8,128)(2,1)} %all_to_all.72) | copy-start | bytes 1572868
  269.6 0.7 copy-start.12
  270.3 20.5 %all-to-all-start.13 = ((bf16[16,64,256]{2,1,0:T(8,128)(2,1)}), bf16[16,64,256]{2,1,0:T(8,128)(2,1)S(1)}, u32[]{:S(2)}, u32[]{:S(2)}) async-start(bf16[16,64,256]{2,1,0:T(8,128)(2,1)} %convolution_convert_fusion.1), calls=%async_computation.13 | async-start | bytes 1048576 | tf_op jit(solution)/shard_map/all_to_all | solution.py:235
  276.3 8.1 %copy-start.15 = (bf16[16,128,256]{2,1,0:T(8,128)(2,1)S(1)}, bf16[16,128,256]{2,1,0:T(8,128)(2,1)}, u32[]{:S(2)}) copy-start(bf16[16,128,256]{2,1,0:T(8,128)(2,1)} %copy-done.14) | copy-start | bytes 3145732
  282.5 2.0 copy-start.48
  290.8 11.4 %copy-start.6 = (bf16[16,64,256]{2,1,0:T(8,128)(2,1)}, bf16[16,64,256]{2,1,0:T(8,128)(2,1)S(1)}, u32[]{:S(2)}) copy-start(bf16[16,64,256]{2,1,0:T(8,128)(2,1)S(1)} %all-to-all-done.13) | copy-start | bytes 1572868
  290.8 18.6 %all-to-all-start.12 = ((bf16[16,16,1024]{2,1,0:T(8,128)(2,1)}), bf16[16,16,1024]{2,1,0:T(8,128)(2,1)S(1)}, u32[]{:S(2)}, u32[]{:S(2)}) async-start(bf16[16,16,1024]{2,1,0:T(8,128)(2,1)} %bitcast.183), calls=%async_computation.12 | async-start | bytes 1048576 | tf_op jit(solution)/shard_map/all_to_all | solution.py:228
  304.4 11.0 %copy-start.24 = (bf16[128,128]{0,1:T(8,128)(2,1)S(1)}, bf16[128,128]{0,1:T(8,128)(2,1)}, u32[]{:S(2)}) copy-start(bf16[128,128]{0,1:T(8,128)(2,1)} %copy-done.23) | copy-start | bytes 98308
  304.4 11.9 %copy-start.2 = (bf16[2,1024,512]{2,1,0:T(8,128)(2,1)S(1)}, bf16[2,1024,512]{2,1,0:T(8,128)(2,1)}, u32[]{:S(2)}) copy-start(bf16[2,1024,512]{2,1,0:T(8,128)(2,1)} %copy.106) | copy-start | bytes 6291460
  309.2 9.2 %copy-start.29 = (s32[16]{0:T(128)S(1)}, s32[16]{0:T(128)}, u32[]{:S(2)}) copy-start(s32[16]{0:T(128)} %copy-done.28) | copy-start | bytes 196
  309.2 10.1 %copy-start.38 = (pred[8,128]{1,0:T(8,128)(4,1)S(1)}, pred[8,128]{1,0:T(8,128)(4,1)}, u32[]{:S(2)}) copy-start(pred[8,128]{1,0:T(8,128)(4,1)} %copy-done.37) | copy-start | bytes 3076
  309.2 10.1 %copy-start.43 = (pred[128]{0:T(512)(128)(4,1)S(1)}, pred[128]{0:T(512)(128)(4,1)}, u32[]{:S(2)}) copy-start(pred[128]{0:T(512)(128)(4,1)} %copy-done.42) | copy-start | bytes 388
  309.2 10.3 %copy-start.33 = (f32[128]{0:T(128)S(1)}, f32[128]{0:T(128)}, u32[]{:S(2)}) copy-start(f32[128]{0:T(128)} %copy-done.32) | copy-start | bytes 1540
  309.2 10.3 %copy-start.41 = (f32[128]{0:T(128)S(1)}, f32[128]{0:T(128)}, u32[]{:S(2)}) copy-start(f32[128]{0:T(128)} %copy-done.40) | copy-start | bytes 1540
  309.2 10.3 %copy-start.35 = (pred[128,8]{0,1:T(8,128)(4,1)S(1)}, pred[128,8]{0,1:T(8,128)(4,1)}, u32[]{:S(2)}) copy-start(pred[128,8]{0,1:T(8,128)(4,1)} %copy-done.34) | copy-start | bytes 3076
  309.2 10.4 %copy-start.18 = (bf16[128,256]{1,0:T(8,128)(2,1)S(1)}, bf16[128,256]{1,0:T(8,128)(2,1)}, u32[]{:S(2)}) copy-start(bf16[128,256]{1,0:T(8,128)(2,1)} %param.11) | copy-start | bytes 196612
  309.4 9.0 %copy-start.8 = (bf16[16,16,1024]{2,1,0:T(8,128)(2,1)}, bf16[16,16,1024]{2,1,0:T(8,128)(2,1)S(1)}, u32[]{:S(2)}) copy-start(bf16[16,16,1024]{2,1,0:T(8,128)(2,1)S(1)} %all-to-all-done.12) | copy-start | bytes 1572868
  309.4 109.7 %all-to-all-start.8 = ((bf16[16,128,256]{2,1,0:T(8,128)(2,1)}), bf16[16,128,256]{2,1,0:T(8,128)(2,1)}, u32[]{:S(2)}, u32[]{:S(2)}) async-start(bf16[16,128,256]{2,1,0:T(8,128)(2,1)} %convolution_convert_fusion), calls=%async_computation.8 | async-start | bytes 2097152 | tf_op jit(solution)/shard_map/all_to_all | solution.py:242
  315.3 99.6 %all-reduce.3.cloned.1.call-start = ((), (), s32[]{:S(2)}) async-start(), calls=%async_computation.14 | async-start | bytes 655360 | tf_op jit(solution)/shard_map/psum | solution.py:270
  318.4 98.3 %copy-start.13 = (bf16[16,32,256]{2,1,0:T(8,128)(2,1)S(1)}, bf16[16,32,256]{2,1,0:T(8,128)(2,1)}, u32[]{:S(2)}) copy-start(bf16[16,32,256]{2,1,0:T(8,128)(2,1)} %copy-done.12) | copy-start | bytes 786436
  318.4 98.3 %copy-start.30 = (s32[16]{0:T(128)S(1)}, s32[16]{0:T(128)}, u32[]{:S(2)}) copy-start(s32[16]{0:T(128)} %copy-done.28) | copy-start | bytes 196
  318.4 99.6 %copy-start.7 = (bf16[16,64,256]{2,1,0:T(8,128)(2,1)S(1)}, bf16[16,64,256]{2,1,0:T(8,128)(2,1)}, u32[]{:S(2)}) copy-start(bf16[16,64,256]{2,1,0:T(8,128)(2,1)} %copy-done.6) | copy-start | bytes 1572868
  319.3 97.6 %copy-start.9 = (bf16[16,16,1024]{2,1,0:T(8,128)(2,1)S(1)}, bf16[16,16,1024]{2,1,0:T(8,128)(2,1)}, u32[]{:S(2)}) copy-start(bf16[16,16,1024]{2,1,0:T(8,128)(2,1)} %copy-done.8) | copy-start | bytes 1572868
  320.5 99.9 %copy-start.39 = (pred[8,128]{1,0:T(8,128)(4,1)S(1)}, pred[8,128]{1,0:T(8,128)(4,1)}, u32[]{:S(2)}) copy-start(pred[8,128]{1,0:T(8,128)(4,1)} %copy-done.37) | copy-start | bytes 3076
  320.5 99.9 %copy-start.44 = (pred[128]{0:T(512)(128)(4,1)S(1)}, pred[128]{0:T(512)(128)(4,1)}, u32[]{:S(2)}) copy-start(pred[128]{0:T(512)(128)(4,1)} %copy-done.42) | copy-start | bytes 388
  320.5 100.2 %copy-start.22 = (bf16[8,256,20]{1,0,2:T(8,128)(2,1)S(1)}, bf16[8,256,20]{1,0,2:T(8,128)(2,1)}, u32[]{:S(2)}) copy-start(bf16[8,256,20]{1,0,2:T(8,128)(2,1)} %param.16) | copy-start | bytes 245764
  320.5 100.2 %copy-start.36 = (pred[128,8]{0,1:T(8,128)(4,1)S(1)}, pred[128,8]{0,1:T(8,128)(4,1)}, u32[]{:S(2)}) copy-start(pred[128,8]{0,1:T(8,128)(4,1)} %copy-done.34) | copy-start | bytes 3076
  320.5 101.7 %copy-start.1 = (bf16[1,256,2048]{2,1,0:T(8,128)(2,1)S(1)}, bf16[1,256,2048]{2,1,0:T(8,128)(2,1)}, u32[]{:S(2)}) copy-start(bf16[1,256,2048]{2,1,0:T(8,128)(2,1)} %param.19) | copy-start | bytes 3145732
  414.9 6.7 %copy-start.26 = (f32[256,128]{1,0:T(8,128)S(1)}, f32[256,128]{1,0:T(8,128)}, u32[]{:S(2)}) copy-start(f32[256,128]{1,0:T(8,128)} %get-tuple-element.61) | copy-start | bytes 393220
Sparse Core Ops, SparseCore 0:
  320.6 94.2 all-reduce.2
where the time goes:
time: 432 us; the launch traced here: 429 us
  waiting for transfers between devices  177 us (41%)
  blocking collectives  70.4 us (16%)
  matrix products  61.5 us (14%)
  starting transfers between devices  53.8 us (12%)
  local copies, waits for them, and re-layouts  29.2 us (7%)
  other arithmetic  20.7 us (5%)
  between operations  16.7 us (4%)
    psum x1, waiting for transfers between devices, body(): gate_total, head_total = lax.psum((gate_part, head_grad), 'expert')  90.6 us
    all_to_all x1, waiting for transfers between devices, body(): lax.all_to_all(shared_out.reshape(devices, piece_rows, model_width), 'exp...  38.6 us
    dot_general x11, matrix products, contract(): lax.dot_general(left, right, (((contraction_axis_index,), (right_dim,)),...  27.1 us
    all_to_all x1, blocking collectives, body(): lax.all_to_all(cotangent_out, 'expert', split_axis=0, concat_axis=0, tile...  21.1 us
    all_to_all x1, blocking collectives, body(): lax.all_to_all(reduce_copies, 'expert', split_axis=0, concat_axis=0, tile...  18.7 us
    all_to_all x1, blocking collectives, body(): lax.all_to_all(expand_copies, 'expert', split_axis=0, concat_axis=0, tile...  18 us
    all_to_all x1, waiting for transfers between devices, body(): lax.all_to_all(shared_cotangent.reshape(devices, piece_rows, model_width)...  14.4 us
    all_to_all x1, waiting for transfers between devices, body(): lax.all_to_all(row_tiles, 'expert', split_axis=0, concat_axis=0, tiled=True)  12.9 us
  transfers between devices with their start and end apart: 11, of which 9 were waited for; matrix products, arithmetic and copies ran while one was open for 18% of the time, Pallas kernels for 0%

commit v1 on v0

v1 whole, which is shorter than its diff:
```python
import functools

import jax
import jax.numpy as jnp
from jax import lax
from jax.experimental import pallas as pl
from jax.experimental.pallas import tpu as pltpu
from jax.sharding import PartitionSpec as P

AXIS = "expert"
TILE = 256
AUX = 32
bf16 = jnp.bfloat16
f32 = jnp.float32


def mm(left, right, left_dim=1, right_dim=0):
    return lax.dot_general(
        left, right, (((left_dim,), (right_dim,)), ((), ())), preferred_element_type=f32
    )


def call(kernel, out_shapes, operands, in_specs=None, scratch=(), flops=0, nbytes=0, limit=48):
    specs = in_specs or [None] * len(operands)
    specs = [pl.BlockSpec(memory_space=pltpu.VMEM) if s is None else s for s in specs]
    return pl.pallas_call(
        kernel,
        out_shape=out_shapes,
        in_specs=specs,
        out_specs=[pl.BlockSpec(memory_space=pltpu.VMEM) for _ in out_shapes],
        scratch_shapes=list(scratch),
        compiler_params=pltpu.CompilerParams(vmem_limit_bytes=limit * 1024 * 1024),
        cost_estimate=pl.CostEstimate(flops=flops, bytes_accessed=nbytes, transcendentals=0),
    )(*operands)


SCALARS = pl.BlockSpec(memory_space=pltpu.SMEM)


def struct(shape, kind):
    return jax.ShapeDtypeStruct(shape, kind)


def sigmoid(v):
    return 0.5 * (1.0 + jnp.tanh(0.5 * v))


def eye(size):
    rows = lax.broadcasted_iota(jnp.int32, (size, size), 0)
    cols = lax.broadcasted_iota(jnp.int32, (size, size), 1)
    return (rows == cols).astype(f32).astype(bf16)


def spread(tile, expert_lanes):
    rows = lax.broadcasted_iota(jnp.int32, (AUX, TILE), 0)
    lanes = lax.broadcasted_iota(jnp.int32, (AUX, TILE), 1) + tile * TILE
    first = rows * expert_lanes
    return ((lanes >= first) & (lanes < first + expert_lanes)).astype(f32).astype(bf16)


def side_of(piece):
    half = piece.shape[1] // 2
    return jnp.concatenate([piece[:, :half], piece[:, half:]], axis=0)


def selector(side, gate_count, scenario, capacity):
    wide = side.astype(f32)
    which = wide[gate_count : gate_count + 1, :]
    slot = wide[gate_count + 1 : gate_count + 2, :]
    ranks = lax.broadcasted_iota(jnp.int32, (capacity, side.shape[1]), 0).astype(f32)
    hit = (ranks == slot) & (which == scenario.astype(f32))
    return hit.astype(f32).astype(bf16)


def prep_kernel(gate_count, capacity, pads, feats, sid, gate_rows, pack, probs, scr):
    rows = feats.shape[0]
    scenarios = gate_rows.shape[0] // AUX
    x = feats[...]
    logits = mm(gate_rows[...], x, 1, 1)
    own = jnp.zeros((AUX, rows), f32)
    ids = sid[...]
    pad = jnp.zeros((1, rows), f32)
    for s in range(scenarios):
        hit = ids == s
        own = own + jnp.where(hit, logits[s * AUX : (s + 1) * AUX], 0.0)
        pad = pad + jnp.where(hit, pads[s].astype(f32), 0.0)
    live = lax.broadcasted_iota(jnp.int32, (AUX, rows), 0) < gate_count
    own = jnp.where(live, own, -jnp.inf)
    top = jnp.max(own, axis=0, keepdims=True)
    raised = jnp.exp(own - top)
    share = raised / jnp.sum(raised, axis=0, keepdims=True)
    probs[...] = share
    labels = lax.broadcasted_iota(jnp.int32, (AUX, rows), 0)
    member = (ids == labels).astype(f32)
    earlier = (
        lax.broadcasted_iota(jnp.int32, (rows, rows), 0)
        < lax.broadcasted_iota(jnp.int32, (rows, rows), 1)
    ).astype(f32).astype(bf16)
    rank = jnp.sum(mm(member.astype(bf16), earlier) * member, axis=0, keepdims=True)
    slot = jnp.where(rank < pad, rank, -1.0)
    scr[...] = share
    scr[gate_count : gate_count + 1, :] = ids.astype(f32)
    scr[gate_count + 1 : gate_count + 2, :] = slot
    side = scr[...].astype(bf16)
    pack[:rows, :] = x
    pack[rows:, :rows] = side[: AUX // 2]
    pack[rows:, rows:] = side[AUX // 2 :]


def compact_kernel(n, gate_count, capacity, with_gates, scal, *refs):
    sides, values, outs = refs[:n], refs[n : 2 * n], refs[2 * n :]
    m = values[0].shape[0]
    rows = sides[0].shape[1] - AUX // 2
    for k in range(n):
        for b in range(m):
            side = side_of(sides[k][b, sides[k].shape[1] - AUX // 2 :, :])
            at = (k * m + b) * capacity
            value = values[k][b, :rows, :]
            for which, out in enumerate(outs):
                sel = selector(side, gate_count, scal[which], capacity)
                width = value.shape[1]
                out[at : at + capacity, :width] = mm(sel, value).astype(bf16)
                if with_gates:
                    out[at : at + capacity, width : width + AUX] = mm(sel, side, 1, 1).astype(bf16)
                    out[at : at + capacity, width + AUX :] = jnp.zeros(
                        (capacity, out.shape[1] - width - AUX), bf16
                    )


def chosen_gate(x, width, column):
    gates = x[:, width:].astype(f32)
    lanes = lax.broadcasted_iota(jnp.int32, gates.shape, 1)
    return jnp.sum(jnp.where(lanes == column, gates, 0.0), axis=1, keepdims=True)


def scenario_forward_kernel(shared, span, scal, own, other, widen, narrow, out_own, out_other, xs, gated):
    half, width = out_own.shape
    total = widen.shape[1]
    xs[:half, :] = own[...]
    xs[half:, :] = other[...]
    chunk = min(2 * half, 512)

    def tile(j, _):
        lanes = pl.ds(pl.multiple_of(j * TILE, TILE), TILE)
        column = shared + scal[2] + (j * TILE) // span
        for at in range(0, 2 * half, chunk):
            x = xs[at : at + chunk, :]
            linear = mm(x[:, :width], widen[:, lanes])
            active = (linear * sigmoid(linear)).astype(bf16).astype(f32)
            gated[at : at + chunk, lanes] = (chosen_gate(x, width, column) * active).astype(bf16)
        return 0

    lax.fori_loop(0, total // TILE, tile, 0)
    out_own[...] = mm(gated[:half, :], narrow[...]).astype(bf16)
    out_other[...] = mm(gated[half:, :], narrow[...]).astype(bf16)


def unpack(pieces, rows, fs, gs):
    n, m = len(pieces), pieces[0].shape[0]
    for k in range(n):
        for b in range(m):
            at = (k * m + b) * rows
            fs[at : at + rows, :] = pieces[k][b, :rows, :]
            gs[at : at + rows, :] = mm(side_of(pieces[k][b, rows:, :]), eye(AUX), 0, 0).astype(bf16)


def shared_forward_kernel(n, gate_count, capacity, expert_lanes, scal, *refs):
    pieces = refs[:n]
    w1, w2, from_own, from_other = refs[n : n + 4]
    outs = refs[n + 4 : 2 * n + 4]
    fs, gs, gated = refs[2 * n + 4 :]
    m, rows, _ = outs[0].shape
    unpack(pieces, rows, fs, gs)
    total = n * m * rows
    chunk = min(total, 1024)

    def tile(j, _):
        lanes = pl.ds(pl.multiple_of(j * TILE, TILE), TILE)
        for at in range(0, total, chunk):
            linear = mm(fs[at : at + chunk, :], w1[:, lanes])
            active = linear * sigmoid(linear)
            gate = mm(gs[at : at + chunk, :], spread(j, expert_lanes))
            gated[at : at + chunk, lanes] = (gate * active).astype(bf16)
        return 0

    lax.fori_loop(0, w1.shape[1] // TILE, tile, 0)
    for at in range(0, total, chunk):
        mixed = mm(gated[at : at + chunk, :], w2[...])
        for piece in range(at // rows, (at + chunk) // rows):
            k, b = piece // m, piece % m
            side = side_of(pieces[k][b, rows:, :])
            slots = slice(piece * capacity, (piece + 1) * capacity)
            extra = mm(selector(side, gate_count, scal[0], capacity), from_own[slots, :], 0, 0)
            extra += mm(selector(side, gate_count, scal[1], capacity), from_other[slots, :], 0, 0)
            outs[k][b] = (mixed[piece * rows - at : (piece + 1) * rows - at] + extra).astype(bf16)


def softmax(v):
    raised = jnp.exp(v - jnp.max(v, axis=1, keepdims=True))
    return raised / jnp.sum(raised, axis=1, keepdims=True)


def head_kernel(count, *refs):
    parts = refs[:count]
    head, mentor, grad, head_part = refs[count:]
    layer = parts[0][...].astype(f32)
    for part in parts[1:]:
        layer = layer + part[...].astype(f32)
    rounded = layer.astype(bf16)
    student = mm(rounded, head[...])
    value = (2.0 * (softmax(student * 0.5) - softmax(mentor[...] * 0.5))).astype(bf16)
    grad[...] = value
    head_part[...] = mm(rounded, value, 0, 0)


def shared_backward_kernel(n, expert_lanes, *refs):
    pieces, logits = refs[:n], refs[n : 2 * n]
    head, w1, w2, dx, mix, dw1, dw2, fs, gs, os, linear_grad = refs[2 * n :]
    m, rows, _ = logits[0].shape
    unpack(pieces, rows, fs, gs)
    for k in range(n):
        for b in range(m):
            at = (k * m + b) * rows
            os[at : at + rows, :] = mm(logits[k][b], head[...], 1, 1).astype(bf16)
    total = n * m * rows
    chunk = min(total, 1024)
    mix[...] = jnp.zeros_like(mix)

    def tile(j, _):
        lanes = pl.ds(pl.multiple_of(j * TILE, TILE), TILE)
        picks = spread(j, expert_lanes)
        for at in range(0, total, chunk):
            x = fs[at : at + chunk, :]
            cotangent = os[at : at + chunk, :]
            linear = mm(x, w1[:, lanes])
            sig = sigmoid(linear)
            active = linear * sig
            gate = mm(gs[at : at + chunk, :], picks)
            hidden = mm(cotangent, w2[lanes, :], 1, 1)
            mix[at : at + chunk, :] += mm((active * hidden).astype(bf16), picks, 1, 1)
            slope = sig + active * (1.0 - sig)
            grad = (gate * hidden * slope).astype(bf16)
            linear_grad[at : at + chunk, lanes] = grad
            first = mm(x, grad, 0, 0)
            second = mm((gate * active).astype(bf16), cotangent, 0, 0)
            if at == 0:
                dw1[:, lanes] = first
                dw2[lanes, :] = second
            else:
                dw1[:, lanes] += first
                dw2[lanes, :] += second
        return 0

    lax.fori_loop(0, w1.shape[1] // TILE, tile, 0)
    for at in range(0, total, chunk):
        dx[at : at + chunk, :] = mm(linear_grad[at : at + chunk, :], w1[...], 1, 1)


def scenario_backward_kernel(
    shared, span, scal, own, other, logit_own, logit_other, head, widen, narrow,
    out_own, out_other, dwiden, dnarrow, xs, os, linear_grad, mix,
):
    half = out_own.shape[0]
    width = narrow.shape[1]
    total = widen.shape[1]
    xs[:half, :] = own[...]
    xs[half:, :] = other[...]
    os[:half, :] = mm(logit_own[...], head[...], 1, 1).astype(bf16)
    os[half:, :] = mm(logit_other[...], head[...], 1, 1).astype(bf16)
    mix[...] = jnp.zeros_like(mix)
    chunk = min(2 * half, 512)

    def tile(j, _):
        lanes = pl.ds(pl.multiple_of(j * TILE, TILE), TILE)
        column = shared + scal[2] + (j * TILE) // span
        picks = (
            lax.broadcasted_iota(jnp.int32, (TILE, mix.shape[1]), 1) == column
        ).astype(f32).astype(bf16)
        for at in range(0, 2 * half, chunk):
            x = xs[at : at + chunk, :]
            gate = chosen_gate(x, width, column)
            x = x[:, :width]
            cotangent = os[at : at + chunk, :]
            linear = mm(x, widen[:, lanes])
            sig = sigmoid(linear)
            active = (linear * sig)
            hidden = mm(cotangent, narrow[lanes, :], 1, 1)
            mix[at : at + chunk, :] += mm((active * hidden).astype(bf16), picks)
            slope = sig + active * (1.0 - sig)
            grad = (gate * hidden * slope).astype(bf16)
            linear_grad[at : at + chunk, lanes] = grad
            first = mm(x, grad, 0, 0)
            second = mm((gate * active).astype(bf16), cotangent, 0, 0)
            if at == 0:
                dwiden[:, lanes] = first
                dnarrow[lanes, :] = second
            else:
                dwiden[:, lanes] += first
                dnarrow[lanes, :] += second
        return 0

    lax.fori_loop(0, total // TILE, tile, 0)
    for at, out in ((0, out_own), (half, out_other)):
        out[:, :width] = mm(linear_grad[at : at + half, :], widen[...], 1, 1).astype(bf16)
        out[:, width:] = mix[at : at + half, :].astype(bf16)


def scatter_kernel(n, gate_count, capacity, scal, *refs):
    sides = refs[:n]
    dx, mix, from_own, from_other = refs[n : n + 4]
    outs = refs[n + 4 :]
    m, width = outs[0].shape[0], outs[0].shape[2]
    rows = dx.shape[0] // (n * m)
    for k in range(n):
        for b in range(m):
            piece = k * m + b
            side = side_of(sides[k][b, sides[k].shape[1] - AUX // 2 :, :])
            slots = slice(piece * capacity, (piece + 1) * capacity)
            extra = mm(selector(side, gate_count, scal[0], capacity), from_own[slots, :], 0, 0)
            extra += mm(selector(side, gate_count, scal[1], capacity), from_other[slots, :], 0, 0)
            span = slice(piece * rows, (piece + 1) * rows)
            outs[k][b, :rows, :] = (dx[span, :] + extra[:, :width]).astype(bf16)
            dots = (mix[span, :] + extra[:, width : width + AUX]).astype(bf16)
            turned = mm(eye(AUX), dots, 1, 1).astype(bf16)
            outs[k][b, rows:, :rows] = turned[: AUX // 2]
            outs[k][b, rows:, rows:] = turned[AUX // 2 :]


def final_kernel(count, gate_count, *refs):
    parts = refs[:count]
    feats, sid, probs, gate_rows, out, gate_part, wide = refs[count:]
    rows = feats.shape[0]
    total = parts[0][...].astype(f32)
    for part in parts[1:]:
        total = total + part[...].astype(f32)
    tail = total[rows:]
    half = tail.shape[1] // 2
    dots = jnp.concatenate([tail[:, :half], tail[:, half:]], axis=0)
    share = probs[...]
    live = lax.broadcasted_iota(jnp.int32, (AUX, rows), 0) < gate_count
    dots = jnp.where(live, dots, 0.0)
    score = share * (dots - jnp.sum(share * dots, axis=0, keepdims=True))
    score = score.astype(bf16).astype(f32)
    ids = sid[...]
    for s in range(gate_rows.shape[0] // AUX):
        wide[s * AUX : (s + 1) * AUX, :] = jnp.where(ids == s, score, 0.0).astype(bf16)
    gate_part[...] = mm(wide[...], feats[...])
    out[...] = (total[:rows] + mm(wide[...], gate_rows[...], 0, 0)).astype(bf16)


def body(
    features,
    scenario_id,
    scenario_pads,
    device_slot,
    mentor,
    gate_weight,
    expand,
    reduce,
    scenario_widen,
    scenario_narrow,
    head,
):
    rows, width = features.shape
    devices = lax.axis_size(AXIS)
    index = lax.axis_index(AXIS)
    core = index % 2
    chips = devices // 2
    near = 2 ** ((chips.bit_length() - 1) // 2)
    far = chips // near
    flat = chips <= 8
    n, m = (chips, 1) if flat else (near, far)
    shared, depth, hidden = expand.shape
    lanes = hidden // chips
    scenarios, _, gates = gate_weight.shape
    capacity = rows // 4
    group = devices // scenarios
    slot_width = scenario_widen.shape[2]
    span = min(hidden, slot_width)
    classes = head.shape[1]
    all_rows = chips * rows
    slots = chips * capacity
    hidden_chip = shared * lanes
    groups = [[2 * r + c for r in range(chips)] for c in range(2)]

    def send(value, mask):
        return lax.ppermute(value, AXIS, [(i, i ^ mask) for i in range(devices)])

    def gather(value):
        column = [value] + [send(value, 2 * near * b) for b in range(1, far)]
        if flat:
            out = []
            for b in range(far):
                out += [column[b][None]] + [send(column[b], 2 * a)[None] for a in range(1, near)]
            return out
        stacked = jnp.stack(column)
        return [stacked] + [send(stacked, 2 * a) for a in range(1, near)]

    def scatter(parts):
        if flat:
            column = []
            for b in range(far):
                total = parts[b * near][0].astype(f32)
                for a in range(1, near):
                    total = total + send(parts[b * near + a][0], 2 * a).astype(f32)
                column.append(total if b == 0 else total.astype(bf16))
        else:
            total = parts[0].astype(f32)
            for a in range(1, near):
                total = total + send(parts[a], 2 * a).astype(f32)
            column = [total[0]] + [total[b].astype(bf16) for b in range(1, far)]
        return [column[0]] + [send(column[b], 2 * near * b) for b in range(1, far)]

    def total_of(value):
        mask = 1
        while mask < devices:
            value = value + send(value, mask)
            mask *= 2
        return value

    def ordered(mine, theirs):
        return jnp.where(core == 0, mine, theirs), jnp.where(core == 0, theirs, mine)

    own_slot = lax.dynamic_index_in_dim(device_slot, index, keepdims=False)
    other_slot = lax.dynamic_index_in_dim(device_slot, index ^ 1, keepdims=False)
    first_expert = own_slot % group * slot_width // hidden
    scal = jnp.stack([own_slot // group, other_slot // group, first_expert]).astype(jnp.int32)
    sid = scenario_id.reshape(1, rows)
    gate_rows = jnp.pad(
        jnp.transpose(gate_weight, (0, 2, 1)), ((0, 0), (0, AUX - gates), (0, 0))
    ).reshape(scenarios * AUX, width)
    widen, narrow = scenario_widen[0], scenario_narrow[0]

    pieces = expand.reshape(shared, depth, chips, lanes).transpose(2, 0, 1, 3)
    pieces = lax.all_to_all(
        pieces, AXIS, split_axis=0, concat_axis=0, tiled=True, axis_index_groups=groups
    )
    low, high = ordered(pieces, send(pieces, 1))
    w1 = jnp.stack([low, high]).transpose(1, 0, 3, 2, 4).reshape(width, hidden_chip)
    low, high = ordered(reduce, send(reduce, 1))
    w2 = jnp.stack([low, high], axis=1).reshape(hidden_chip, width)

    pack_rows = rows + AUX // 2
    pack, probs = call(
        functools.partial(prep_kernel, gates, capacity),
        [struct((pack_rows, width), bf16), struct((AUX, rows), f32)],
        [scenario_pads, features, sid, gate_rows],
        [SCALARS, None, None, None],
        [pltpu.VMEM((AUX, rows), f32)],
    )
    got = gather(pack)

    def compact(values, value_width, with_gates):
        out_width = value_width + 128 * with_gates
        return call(
            functools.partial(compact_kernel, n, gates, capacity, with_gates),
            [struct((slots, out_width), bf16)] * 2,
            [scal, *got, *values],
            [SCALARS] + [None] * (2 * n),
        )

    x_own, x_send = compact(got, width, True)
    x_other = send(x_send, 1)
    scen_flops = 4 * slots * width * slot_width
    out_own, out_send = call(
        functools.partial(scenario_forward_kernel, shared, span),
        [struct((slots, width), bf16)] * 2,
        [scal, x_own, x_other, widen, narrow],
        [SCALARS] + [None] * 4,
        [pltpu.VMEM((2 * slots, width + 128), bf16), pltpu.VMEM((2 * slots, slot_width), bf16)],
        flops=2 * scen_flops,
    )
    out_other = send(out_send, 1)
    shared_flops = 2 * all_rows * width * hidden_chip
    row_scratch = [pltpu.VMEM((all_rows, width), bf16), pltpu.VMEM((all_rows, AUX), bf16)]
    parts = call(
        functools.partial(shared_forward_kernel, n, gates, capacity, lanes),
        [struct((m, rows, width), bf16)] * n,
        [scal, *got, w1, w2, out_own, out_other],
        [SCALARS] + [None] * (n + 4),
        row_scratch + [pltpu.VMEM((all_rows, hidden_chip), bf16)],
        flops=2 * shared_flops,
    )
    layer_parts = scatter(parts)
    logit_grad, head_part = call(
        functools.partial(head_kernel, len(layer_parts)),
        [struct((rows, classes), bf16), struct((width, classes), f32)],
        [*layer_parts, head, mentor],
    )
    logits = gather(logit_grad)
    head_total = total_of(head_part)

    l_own, l_send = compact(logits, classes, False)
    l_other = send(l_send, 1)
    dx, mix, dw1, dw2 = call(
        functools.partial(shared_backward_kernel, n, lanes),
        [
            struct((all_rows, width), f32),
            struct((all_rows, AUX), f32),
            struct((width, hidden_chip), f32),
            struct((hidden_chip, width), f32),
        ],
        [*got, *logits, head, w1, w2],
        None,
        row_scratch
        + [pltpu.VMEM((all_rows, width), bf16), pltpu.VMEM((all_rows, hidden_chip), bf16)],
        flops=5 * shared_flops,
    )
    dw1 = dw1.reshape(chips, 2, depth, shared, lanes)
    kept = lax.dynamic_index_in_dim(dw1, core, 1, False)
    sent = lax.dynamic_index_in_dim(dw1, 1 - core, 1, False).astype(bf16)
    dw1 = (kept + send(sent, 1).astype(f32)).astype(bf16)
    dw1 = lax.all_to_all(
        dw1, AXIS, split_axis=0, concat_axis=0, tiled=True, axis_index_groups=groups
    )
    expand_grad = dw1.transpose(2, 1, 0, 3).reshape(shared, depth, hidden).astype(f32)
    dw2 = dw2.reshape(shared, 2, lanes // 2, width)
    kept = lax.dynamic_index_in_dim(dw2, core, 1, False)
    sent = lax.dynamic_index_in_dim(dw2, 1 - core, 1, False).astype(bf16)
    reduce_grad = kept + send(sent, 1).astype(f32)

    dx_own, dx_send, widen_grad, narrow_grad = call(
        functools.partial(scenario_backward_kernel, shared, span),
        [struct((slots, width + 128), bf16)] * 2
        + [struct((width, slot_width), f32), struct((slot_width, width), f32)],
        [scal, x_own, x_other, l_own, l_other, head, widen, narrow],
        [SCALARS] + [None] * 7,
        [
            pltpu.VMEM((2 * slots, width + 128), bf16),
            pltpu.VMEM((2 * slots, width), bf16),
            pltpu.VMEM((2 * slots, slot_width), bf16),
            pltpu.VMEM((2 * slots, 128), f32),
        ],
        flops=5 * scen_flops,
    )
    dx_other = send(dx_send, 1)
    grad_parts = call(
        functools.partial(scatter_kernel, n, gates, capacity),
        [struct((m, pack_rows, width), bf16)] * n,
        [scal, *got, dx, mix, dx_own, dx_other],
        [SCALARS] + [None] * (n + 4),
    )
    grad_parts = scatter(grad_parts)
    feature_grad, gate_part = call(
        functools.partial(final_kernel, len(grad_parts), gates),
        [struct((rows, width), bf16), struct((scenarios * AUX, width), f32)],
        [*grad_parts, features, sid, probs, gate_rows],
        None,
        [pltpu.VMEM((scenarios * AUX, rows), bf16)],
    )
    gate_part = gate_part.reshape(scenarios, AUX, width)[:, :gates]
    gate_total = jnp.transpose(total_of(gate_part), (0, 2, 1))
    return (
        feature_grad,
        expand_grad,
        reduce_grad,
        widen_grad[None],
        narrow_grad[None],
        gate_total,
        head_total,
    )


def solution(mesh):
    placed = (
        P(("groups", "expert"), None),
        P(("groups", "expert")),
        P("groups"),
        P(),
        P(("groups", "expert"), None),
        P(),
        P(None, "expert", None),
        P(None, "expert", None),
        P("expert", None, None),
        P("expert", None, None),
        P(),
    )
    return jax.shard_map(
        body,
        mesh=mesh,
        in_specs=placed,
        out_specs=(
            P(("groups", "expert"), None),
            P("groups", "expert", None),
            P("groups", "expert", None),
            P(("groups", "expert"), None, None),
            P(("groups", "expert"), None, None),
            P("groups", None, None),
            P("groups", None),
        ),
        check_vma=False,
    )
```

time: 432 us -> 173 us (0.40)
  waiting for transfers between devices: 177 us -> 51 us
  blocking collectives: 70.4 us -> 0 us
  matrix products: 61.5 us -> 0 us
  Pallas kernels: 0 us -> 37.2 us
  local copies, waits for them, and re-layouts: 29.2 us -> 13.6 us
  other arithmetic: 20.7 us -> 7.67 us
  between operations: 16.7 us -> 6.3 us
    psum x1 -> x0, waiting for transfers between devices: 90.6 us -> none  [body(): gate_total, head_total = lax.psum((gate_part, head_grad), 'expert')]
    all_to_all x10 -> x2, waiting for transfers between devices: 86.3 us -> 0.01 us  [the longest x1 0.01 us: body(): lax.all_to_all(pieces, AXIS, split_axis=0, concat_axis=0, tiled=True, axi...]
    all_to_all x4 -> x0, blocking collectives: 70.4 us -> none  [the longest x1 21.1 us: body(): lax.all_to_all(cotangent_out, 'expert', split_axis=0, concat_axis=0, tile...]
    dot_general x33 -> x0, matrix products: 61.5 us -> none  [the longest x11 27.1 us: contract(): lax.dot_general(left, right, (((contraction_axis_index,), (right_dim,)),...]
    ppermute x0 -> x44, waiting for transfers between devices: none -> 51 us  [send(): return lax.ppermute(value, AXIS, [(i, i ^ mask) for i in range(devices)])]
    ppermute x0 -> x44, starting transfers between devices: none -> 45.2 us  [send(): return lax.ppermute(value, AXIS, [(i, i ^ mask) for i in range(devices)])]
    all_to_all x10 -> x2, starting transfers between devices: 53.7 us -> 11.3 us  [the longest x1 7.28 us: body(): lax.all_to_all(pieces, AXIS, split_axis=0, concat_axis=0, tiled=True, axi...]
    pallas_call x0 -> x10, Pallas kernels: none -> 37.2 us  [call(): pl.pallas_call(kernel, out_shape=out_shapes, in_specs=specs, out_specs=[p...]
  transfers between devices with their start and end apart: 11 -> 46, of which waited for: 9 -> 21; matrix products, arithmetic and copies ran while one was open for 18% -> 7% of each run, Pallas kernels for 0% -> 17%
where the time goes in v1:
time: 173 us; the launch traced here: 172 us
  starting transfers between devices  56.5 us (33%)
  waiting for transfers between devices  51 us (29%)
  Pallas kernels  37.2 us (22%)
  local copies, waits for them, and re-layouts  13.6 us (8%)
  other arithmetic  7.67 us (4%)
  between operations  6.3 us (4%)
    ppermute x44, waiting for transfers between devices, send(): return lax.ppermute(value, AXIS, [(i, i ^ mask) for i in range(devices)])  51 us
    ppermute x44, starting transfers between devices, send(): return lax.ppermute(value, AXIS, [(i, i ^ mask) for i in range(devices)])  45.2 us
    pallas_call x10, Pallas kernels, call(): pl.pallas_call(kernel, out_shape=out_shapes, in_specs=specs, out_specs=[p...  37.2 us
    unnamed x37, local copies, waits for them, and re-layouts  7.88 us
    all_to_all x1, starting transfers between devices, body(): lax.all_to_all(pieces, AXIS, split_axis=0, concat_axis=0, tiled=True, axi...  7.28 us
    all_to_all x1, starting transfers between devices, body(): lax.all_to_all(dw1, AXIS, split_axis=0, concat_axis=0, tiled=True, axis_i...  4.03 us
  transfers between devices with their start and end apart: 46, of which 21 were waited for; matrix products, arithmetic and copies ran while one was open for 7% of the time, Pallas kernels for 17%

profile of v1, /device:TPU:0, one launch (start us, length us, event | category | flops | bytes accessed | tf_op | source)
XLA Modules:
  0.0 172.4 jit_solution(4734224891469299516)
XLA Ops:
  0.7 1.2 copy.28
  1.9 1.1 copy.35
  3.1 7.3 %all-to-all-start = ((bf16[8,16,16,128]{3,1,2,0:T(8,128)(2,1)}), bf16[8,16,16,128]{3,1,2,0:T(8,128)(2,1)}, u32[]{:S(2)}, u32[]{:S(2)}) async-start(bf16[8,16,16,128]{3,1,2,0:T(8,128)(2,1)} %bitcast.108), calls=%async_computation | async-start | bytes 1048576 | tf_op jit(solution)/shard_map/all_to_all | solution.py:435
  11.2 3.9 %collective-permute-start.5 = (bf16[144,256]{1,0:T(8,128)(2,1)S(1)}, bf16[144,256]{1,0:T(8,128)(2,1)S(1)}, u32[]{:S(2)}, u32[]{:S(2)}) collective-permute-start(bf16[144,256]{1,0:T(8,128)(2,1)S(1)} %get-tuple-element.43), channel_id=1, source_target_pairs={{0,12},{1,13},{2,14},{3,15},{4,8},{5,9},{6,10},{7,11},{8,4},{9,5},... | collective-permute-start | bytes 221192 | tf_op jit(solution)/shard_map/ppermute | solution.py:387
  15.7 1.9 %collective-permute-start = (bf16[144,256]{1,0:T(8,128)(2,1)S(1)}, bf16[144,256]{1,0:T(8,128)(2,1)S(1)}, u32[]{:S(2)}, u32[]{:S(2)}) collective-permute-start(bf16[144,256]{1,0:T(8,128)(2,1)S(1)} %get-tuple-element.43), channel_id=1, source_target_pairs={{0,2},{1,3},{2,0},{3,1},{4,6},{5,7},{6,4},{7,5},{8,10},{9,11},{10,... | collective-permute-start | bytes 221192 | tf_op jit(solution)/shard_map/ppermute | solution.py:387
  23.5 2.5 %collective-permute-done.5 = bf16[144,256]{1,0:T(8,128)(2,1)S(1)} collective-permute-done((bf16[144,256]{1,0:T(8,128)(2,1)S(1)}, bf16[144,256]{1,0:T(8,128)(2,1)S(1)}, u32[]{:S(2)}, u32[]{:S(2)}) %collective-permute-start.5) | collective-permute-done | bytes 73760 | tf_op jit(solution)/shard_map/ppermute | solution.py:387
  26.0 1.5 collective-permute-start.6
  27.5 3.6 %collective-permute-done.3 = bf16[144,256]{1,0:T(8,128)(2,1)S(1)} collective-permute-done((bf16[144,256]{1,0:T(8,128)(2,1)S(1)}, bf16[144,256]{1,0:T(8,128)(2,1)S(1)}, u32[]{:S(2)}, u32[]{:S(2)}) %collective-permute-start.3) | collective-permute-done | bytes 73760 | tf_op jit(solution)/shard_map/ppermute | solution.py:387
  31.1 1.5 collective-permute-start.4
  33.3 2.2 %collective-permute-done.4 = bf16[144,256]{1,0:T(8,128)(2,1)S(1)} collective-permute-done((bf16[144,256]{1,0:T(8,128)(2,1)S(1)}, bf16[144,256]{1,0:T(8,128)(2,1)S(1)}, u32[]{:S(2)}, u32[]{:S(2)}) %collective-permute-start.4) | collective-permute-done | bytes 73760 | tf_op jit(solution)/shard_map/ppermute | solution.py:387
  35.5 1.5 collective-permute-done.2
  37.0 1.6 shard_map.163
  39.0 1.1 collective-permute-done.9.other
  40.2 3.8 %shard_map.164 = (bf16[256,256]{1,0:T(8,128)(2,1)S(1)}, bf16[256,256]{1,0:T(8,128)(2,1)S(1)}) custom-call(s32[3]{0:T(128)S(1)} %pad_add_fusion.scal, bf16[256,384]{1,0:T(8,128)(2,1)S(1)} %get-tuple-element.44.own, bf16[256,384]{1,0:T(8,128)(2,1)S(1)} %collective-permute-done.9.other, bf16[256,2048]{1,0:T(8,128)(2,1)S(1)} %bitcast.182, ...), custom_call_target="tpu_custom_call" | custom-call | flops 1073741824 | tf_op jit(solution)/shard_map/pallas_call | solution.py:26
  44.2 1.3 select_bitcast_fusion.1
  45.7 1.3 select_bitcast_fusion.3
  47.4 5.9 %shard_map.165 = (bf16[1,128,256]{2,1,0:T(8,128)(2,1)S(1)}, bf16[1,128,256]{2,1,0:T(8,128)(2,1)S(1)}, bf16[1,128,256]{2,1,0:T(8,128)(2,1)S(1)}, bf16[1,128,256]{...) custom-call(s32[3]{0:T(128)S(1)} %pad_add_fusion.scal, ...), custom_call_target="tpu_custom_call" | custom-call | flops 2147483648 | tf_op jit(solution)/shard_map/pallas_call | solution.py:26
  53.3 0.9 collective-permute-start.12
  54.2 1.2 collective-permute-start.11
  56.2 1.2 collective-permute-start.16
  57.5 0.9 collective-permute-done.12
  58.9 2.3 %collective-permute-done.14 = bf16[128,256]{1,0:T(8,128)(2,1)S(1)} collective-permute-done((bf16[128,256]{1,0:T(8,128)(2,1)S(1)}, bf16[128,256]{1,0:T(8,128)(2,1)S(1)}, u32[]{:S(2)}, u32[]{:S(2)}) %collective-permute-start.14) | collective-permute-done | bytes 65568 | tf_op jit(solution)/shard_map/ppermute | solution.py:387
  61.1 1.0 collective-permute-start.15
  62.2 2.0 %collective-permute-start.17 = (bf16[128,256]{1,0:T(8,128)(2,1)S(1)}, bf16[128,256]{1,0:T(8,128)(2,1)S(1)}, u32[]{:S(2)}, u32[]{:S(2)}) collective-permute-start(bf16[128,256]{1,0:T(8,128)(2,1)S(1)} %fusion.6), channel_id=1, source_target_pairs={{0,12},{1,13},{2,14},{3,15},{4,8},{5,9},{6,10},{7,11},{8,4},{9,5},... | collective-permute-start | bytes 196616 | tf_op jit(solution)/shard_map/ppermute | solution.py:387
  64.2 4.5 %collective-permute-done.15.refs_2_ = bf16[128,256]{1,0:T(8,128)(2,1)S(1)} collective-permute-done((bf16[128,256]{1,0:T(8,128)(2,1)S(1)}, bf16[128,256]{1,0:T(8,128)(2,1)S(1)}, u32[]{:S(2)}, u32[]{:S(2)}) %collective-permute-start.15) | collective-permute-done | bytes 65568 | tf_op jit(solution)/shard_map/ppermute | solution.py:387
  69.1 1.7 collective-permute-start.23
  70.9 1.1 collective-permute-start.21
  71.9 1.7 collective-permute-start.19
  73.6 0.9 collective-permute-start.18
  74.9 0.9 collective-permute-start.24
  75.8 1.3 collective-permute-start.22
  77.9 1.0 collective-permute-done.24
  78.8 0.9 collective-permute-done.22
  79.7 1.3 collective-permute-done.20
  81.0 1.4 shard_map.168
  83.0 1.0 collective-permute-done.25.logit_other
  84.0 1.2 copy-done.6
  85.2 1.2 copy-done.8
  86.4 0.9 copy-done.10
  87.4 0.9 copy-done.12
  88.3 8.7 %shard_map.169 = (bf16[256,384]{1,0:T(8,128)(2,1)S(1)}, bf16[256,384]{1,0:T(8,128)(2,1)S(1)}, f32[256,2048]{1,0:T(8,128)}, f32[2048,256]{1,0:T(8,128)}) custom-call(s32[3]{0:T(128)S(1)} %pad_add_fusion.scal, bf16[256,384]{1,0:T(8,128)(2,1)S(1)} %copy-done.10, bf16[256,384]{1,0:T(8,128)(2,1)S(1)} %copy-done.12, ...), custom_call_target="tpu_custom_call" | custom-call | flops 2684354560 | tf_op jit(solution)/shard_map/pallas_call | solution.py:26
  97.1 12.0 %shard_map.167 = (f32[1024,256]{1,0:T(8,128)S(1)}, f32[1024,32]{1,0:T(8,128)S(1)}, f32[256,2048]{1,0:T(8,128)}, f32[2048,256]{1,0:T(8,128)}) custom-call(bf16[1,144,256]{2,1,0:T(8,128)(2,1)S(1)} %bitcast.113, bf16[1,144,256]{2,1,0:T(8,128)(2,1)S(1)} %bitcast.137, bf16[1,144,256]{2,1,0:T(8,128)(2,1)S(1)} %bitcast.131, bf16[1,144,256]{2,1,0:T(8,128)(2,1)S(1)} %bitcast.155, ...), custom_call_target="tpu_custom_call" | custom-call | flops 5368709120 | tf_op jit(solution)/shard_map/pallas_call | solution.py:26
  109.1 2.1 %fusion.2 = bf16[16,64,256]{2,1,0:T(8,128)(2,1)} fusion(f32[16,2,64,256]{3,2,1,0:T(8,128)} %bitcast.199, s32[]{:T(128)S(6)} %select_n.76), kind=kLoop, calls=%fused_computation.10 | loop fusion | bytes 1048580 | tf_op jit(solution)/shard_map/convert_element_type | solution.py:519
  111.6 2.0 %copy.30 = f32[32,8,16,128]{3,2,1,0:T(8,128)S(1)} copy(f32[32,8,16,128]{3,1,2,0:T(8,128)} %bitcast.197) | data formatting | bytes 4194304
  113.6 1.7 shard_map.170
  116.3 1.3 collective-permute-start.27
  118.4 1.7 collective-permute-done.28
  120.5 2.7 %collective-permute-done.30 = bf16[144,256]{1,0:T(8,128)(2,1)S(1)} collective-permute-done((bf16[144,256]{1,0:T(8,128)(2,1)S(1)}, bf16[144,256]{1,0:T(8,128)(2,1)S(1)}, u32[]{:S(2)}, u32[]{:S(2)}) %collective-permute-start.30) | collective-permute-done | bytes 73760 | tf_op jit(solution)/shard_map/ppermute | solution.py:387
  123.6 0.9 collective-permute-done.32
  124.5 1.4 collective-permute-start.31
  125.9 1.9 %collective-permute-start.33 = (bf16[144,256]{1,0:T(8,128)(2,1)S(1)}, bf16[144,256]{1,0:T(8,128)(2,1)S(1)}, u32[]{:S(2)}, u32[]{:S(2)}) collective-permute-start(bf16[144,256]{1,0:T(8,128)(2,1)S(1)} %fusion.3), channel_id=1, source_target_pairs={{0,12},{1,13},{2,14},{3,15},{4,8},{5,9},{6,10},{7,11},{8,4},{9,5},... | collective-permute-start | bytes 221192 | tf_op jit(solution)/shard_map/ppermute | solution.py:387
  129.0 3.7 %collective-permute-done.31.refs_2_ = bf16[144,256]{1,0:T(8,128)(2,1)S(1)} collective-permute-done((bf16[144,256]{1,0:T(8,128)(2,1)S(1)}, bf16[144,256]{1,0:T(8,128)(2,1)S(1)}, u32[]{:S(2)}, u32[]{:S(2)}) %collective-permute-start.31) | collective-permute-done | bytes 73760 | tf_op jit(solution)/shard_map/ppermute | solution.py:387
  132.6 0.9 shard_map.171
  133.7 0.9 fusion
  134.6 4.0 %all-to-all-start.1 = ((bf16[8,16,16,128]{3,2,1,0:T(8,128)(2,1)}), bf16[8,16,16,128]{3,2,1,0:T(8,128)(2,1)S(1)}, u32[]{:S(2)}, u32[]{:S(2)}) async-start(bf16[8,16,16,128]{3,2,1,0:T(8,128)(2,1)} %fusion), calls=%async_computation.1 | async-start | bytes 1048576 | tf_op jit(solution)/shard_map/all_to_all | solution.py:513
  138.7 2.1 %collective-permute-start.37 = (f32[8,20,256]{2,0,1:T(8,128)S(1)}, f32[8,20,256]{2,0,1:T(8,128)S(1)}, u32[]{:S(2)}, u32[]{:S(2)}) collective-permute-start(f32[8,20,256]{2,0,1:T(8,128)S(1)} %copy_add_fusion), channel_id=1, source_target_pairs={{0,2},{1,3},{2,0},{3,1},{4,6},{5,7},{6,4},{7,5},{8,10},{9,11},{10,... | collective-permute-start | bytes 491528 | tf_op jit(solution)/shard_map/ppermute | solution.py:387
  140.8 1.5 collective-permute-start.42
  142.3 7.1 %collective-permute-done.37 = f32[8,20,256]{2,0,1:T(8,128)S(1)} collective-permute-done((f32[8,20,256]{2,0,1:T(8,128)S(1)}, f32[8,20,256]{2,0,1:T(8,128)S(1)}, u32[]{:S(2)}, u32[]{:S(2)}) %collective-permute-start.37) | collective-permute-done | bytes 163872 | tf_op jit(solution)/shard_map/ppermute | solution.py:387
  149.4 2.3 %collective-permute-start.38 = (f32[8,20,256]{2,0,1:T(8,128)S(1)}, f32[8,20,256]{2,0,1:T(8,128)S(1)}, u32[]{:S(2)}, u32[]{:S(2)}) collective-permute-start(f32[8,20,256]{2,0,1:T(8,128)S(1)} %add.101), channel_id=1, source_target_pairs={{0,4},{1,5},{2,6},{3,7},{4,0},{5,1},{6,2},{7,3},{8,12},{9,13},{10,... | collective-permute-start | bytes 491528 | tf_op jit(solution)/shard_map/ppermute | solution.py:387
  151.7 3.8 %collective-permute-start.43 = (f32[256,128]{1,0:T(8,128)S(1)}, f32[256,128]{1,0:T(8,128)S(1)}, u32[]{:S(2)}, u32[]{:S(2)}) collective-permute-start(f32[256,128]{1,0:T(8,128)S(1)} %add.106), channel_id=1, source_target_pairs={{0,8},{1,9},{2,10},{3,11},{4,12},{5,13},{6,14},{7,15},{8,0},{9,1},... | collective-permute-start | bytes 393224 | tf_op jit(solution)/shard_map/ppermute | solution.py:387
  155.5 5.8 %collective-permute-done.43 = f32[256,128]{1,0:T(8,128)S(1)} collective-permute-done((f32[256,128]{1,0:T(8,128)S(1)}, f32[256,128]{1,0:T(8,128)S(1)}, u32[]{:S(2)}, u32[]{:S(2)}) %collective-permute-start.43) | collective-permute-done | bytes 131104 | tf_op jit(solution)/shard_map/ppermute | solution.py:387
  162.1 2.1 %bitcast_add_fusion = f32[16,64,256]{2,1,0:T(8,128)} fusion(bf16[16,64,256]{2,1,0:T(8,128)(2,1)} %collective-permute-done.35, f32[16,2,64,256]{3,2,1,0:T(8,128)S(1)} %bitcast.200, s32[]{:T(128)S(6)} %select_n.75), kind=kLoop, calls=%fused_computation.4 | loop fusion | flops 524288 | bytes 2621444 | tf_op jit(solution)/shard_map/add | solution.py:520
  164.3 5.5 %collective-permute-done.39 = f32[8,20,256]{2,0,1:T(8,128)S(1)} collective-permute-done((f32[8,20,256]{2,0,1:T(8,128)S(1)}, f32[8,20,256]{2,0,1:T(8,128)S(1)}, u32[]{:S(2)}, u32[]{:S(2)}) %collective-permute-start.39) | collective-permute-done | bytes 163872 | tf_op jit(solution)/shard_map/ppermute | solution.py:387
  171.2 1.1 reshape.75
  (108 shorter events, 14.4 us)
Async XLA Ops:
  0.6 9.7 %copy-start.14 = (bf16[8,256,20]{1,0,2:T(8,128)(2,1)S(1)}, bf16[8,256,20]{1,0,2:T(8,128)(2,1)}, u32[]{:S(2)}) copy-start(bf16[8,256,20]{1,0,2:T(8,128)(2,1)} %param.16) | copy-start | bytes 245764
  0.6 9.8 %copy-start = (bf16[128,256]{1,0:T(8,128)(2,1)S(1)}, bf16[128,256]{1,0:T(8,128)(2,1)}, u32[]{:S(2)}) copy-start(bf16[128,256]{1,0:T(8,128)(2,1)} %refs_4_.3) | copy-start | bytes 196612
  0.7 9.8 %copy-start.4 = (s32[8]{0:T(128)S(1)}, s32[8]{0:T(128)}, u32[]{:S(2)}) copy-start(s32[8]{0:T(128)} %pads.1) | copy-start | bytes 100
  0.7 9.8 %copy-start.3 = (s32[128]{0:T(128)S(1)}, s32[128]{0:T(128)}, u32[]{:S(2)}) copy-start(s32[128]{0:T(128)} %param.12) | copy-start | bytes 1540
  0.7 17.0 %copy-start.15 = (s32[16]{0:T(128)S(1)}, s32[16]{0:T(128)}, u32[]{:S(2)}) copy-start(s32[16]{0:T(128)} %param.14) | copy-start | bytes 196
  1.9 38.3 %copy-start.5 = (bf16[1,256,2048]{2,1,0:T(8,128)(2,1)S(1)}, bf16[1,256,2048]{2,1,0:T(8,128)(2,1)}, u32[]{:S(2)}) copy-start(bf16[1,256,2048]{2,1,0:T(8,128)(2,1)} %param.19) | copy-start | bytes 3145732
  1.9 38.3 %copy-start.7 = (bf16[1,2048,256]{2,1,0:T(8,128)(2,1)S(1)}, bf16[1,2048,256]{2,1,0:T(8,128)(2,1)}, u32[]{:S(2)}) copy-start(bf16[1,2048,256]{2,1,0:T(8,128)(2,1)} %param.20) | copy-start | bytes 3145732
  3.1 35.5 %all-to-all-start = ((bf16[8,16,16,128]{3,1,2,0:T(8,128)(2,1)}), bf16[8,16,16,128]{3,1,2,0:T(8,128)(2,1)}, u32[]{:S(2)}, u32[]{:S(2)}) async-start(bf16[8,16,16,128]{3,1,2,0:T(8,128)(2,1)} %bitcast.108), calls=%async_computation | async-start | bytes 1048576 | tf_op jit(solution)/shard_map/all_to_all | solution.py:435
  10.3 33.9 %collective-permute-start.8 = (bf16[16,64,256]{2,1,0:T(8,128)(2,1)}, bf16[16,64,256]{2,1,0:T(8,128)(2,1)}, u32[]{:S(2)}, u32[]{:S(2)}) collective-permute-start(bf16[16,64,256]{2,1,0:T(8,128)(2,1)} %param.18), channel_id=1, source_target_pairs={{0,1},{1,0},{2,3},{3,2},{4,5},{5,4},{6,7},{7,6},{8,9},{9,8},{10,11... | collective-permute-start | bytes 1572872 | tf_op jit(solution)/shard_map/ppermute | solution.py:387
  11.2 14.8 %collective-permute-start.5 = (bf16[144,256]{1,0:T(8,128)(2,1)S(1)}, bf16[144,256]{1,0:T(8,128)(2,1)S(1)}, u32[]{:S(2)}, u32[]{:S(2)}) collective-permute-start(bf16[144,256]{1,0:T(8,128)(2,1)S(1)} %get-tuple-element.43), channel_id=1, source_target_pairs={{0,12},{1,13},{2,14},{3,15},{4,8},{5,9},{6,10},{7,11},{8,4},{9,5},... | collective-permute-start | bytes 221192 | tf_op jit(solution)/shard_map/ppermute | solution.py:387
  15.1 16.1 %collective-permute-start.3 = (bf16[144,256]{1,0:T(8,128)(2,1)S(1)}, bf16[144,256]{1,0:T(8,128)(2,1)S(1)}, u32[]{:S(2)}, u32[]{:S(2)}) collective-permute-start(bf16[144,256]{1,0:T(8,128)(2,1)S(1)} %get-tuple-element.43), channel_id=1, source_target_pairs={{0,8},{1,9},{2,10},{3,11},{4,12},{5,13},{6,14},{7,15},{8,0},{9,1},... | collective-permute-start | bytes 221192 | tf_op jit(solution)/shard_map/ppermute | solution.py:387
  15.1 17.5 %collective-permute-start.1 = (bf16[144,256]{1,0:T(8,128)(2,1)S(1)}, bf16[144,256]{1,0:T(8,128)(2,1)S(1)}, u32[]{:S(2)}, u32[]{:S(2)}) collective-permute-start(bf16[144,256]{1,0:T(8,128)(2,1)S(1)} %get-tuple-element.43), channel_id=1, source_target_pairs={{0,4},{1,5},{2,6},{3,7},{4,0},{5,1},{6,2},{7,3},{8,12},{9,13},{10,... | collective-permute-start | bytes 221192 | tf_op jit(solution)/shard_map/ppermute | solution.py:387
  15.7 17.5 %collective-permute-start = (bf16[144,256]{1,0:T(8,128)(2,1)S(1)}, bf16[144,256]{1,0:T(8,128)(2,1)S(1)}, u32[]{:S(2)}, u32[]{:S(2)}) collective-permute-start(bf16[144,256]{1,0:T(8,128)(2,1)S(1)} %get-tuple-element.43), channel_id=1, source_target_pairs={{0,2},{1,3},{2,0},{3,1},{4,6},{5,7},{6,4},{7,5},{8,10},{9,11},{10,... | collective-permute-start | bytes 221192 | tf_op jit(solution)/shard_map/ppermute | solution.py:387
  26.0 7.2 %collective-permute-start.6 = (bf16[144,256]{1,0:T(8,128)(2,1)S(1)}, bf16[144,256]{1,0:T(8,128)(2,1)S(1)}, u32[]{:S(2)}, u32[]{:S(2)}) collective-permute-start(bf16[144,256]{1,0:T(8,128)(2,1)S(1)} %collective-permute-done.5), channel_id=1, source_target_pairs={{0,2},{1,3},{2,0},{3,1},{4,6},{5,7},{6,4},{7,5},{8,10},{9,11},{10,... | collective-permute-start | bytes 221192 | tf_op jit(solution)/shard_map/ppermute | solution.py:387
  31.1 4.4 %collective-permute-start.4 = (bf16[144,256]{1,0:T(8,128)(2,1)S(1)}, bf16[144,256]{1,0:T(8,128)(2,1)S(1)}, u32[]{:S(2)}, u32[]{:S(2)}) collective-permute-start(bf16[144,256]{1,0:T(8,128)(2,1)S(1)} %collective-permute-done.3), channel_id=1, source_target_pairs={{0,2},{1,3},{2,0},{3,1},{4,6},{5,7},{6,4},{7,5},{8,10},{9,11},{10,... | collective-permute-start | bytes 221192 | tf_op jit(solution)/shard_map/ppermute | solution.py:387
  32.6 4.4 %collective-permute-start.2 = (bf16[144,256]{1,0:T(8,128)(2,1)S(1)}, bf16[144,256]{1,0:T(8,128)(2,1)S(1)}, u32[]{:S(2)}, u32[]{:S(2)}) collective-permute-start(bf16[144,256]{1,0:T(8,128)(2,1)S(1)} %collective-permute-done.1), channel_id=1, source_target_pairs={{0,2},{1,3},{2,0},{3,1},{4,6},{5,7},{6,4},{7,5},{8,10},{9,11},{10,... | collective-permute-start | bytes 221192 | tf_op jit(solution)/shard_map/ppermute | solution.py:387
  38.5 7.0 %copy-start.9 = (bf16[256,384]{1,0:T(8,128)(2,1)}, bf16[256,384]{1,0:T(8,128)(2,1)S(1)}, u32[]{:S(2)}) copy-start(bf16[256,384]{1,0:T(8,128)(2,1)S(1)} %get-tuple-element.44.own) | copy-start | bytes 589828
  38.5 1.7 collective-permute-start.9
  38.5 7.2 %collective-permute-start.7 = (bf16[8,16,16,128]{3,1,2,0:T(8,128)(2,1)}, bf16[8,16,16,128]{3,1,2,0:T(8,128)(2,1)}, u32[]{:S(2)}, u32[]{:S(2)}) collective-permute-start(bf16[8,16,16,128]{3,1,2,0:T(8,128)(2,1)} %all-to-all-done), channel_id=1, source_target_pairs={{0,1},{1,0},{2,3},{3,2},{4,5},{5,4},{6,7},{7,6},{8,9},{9,8},{10,11... | collective-permute-start | bytes 1572872 | tf_op jit(solution)/shard_map/ppermute | solution.py:387
  40.2 5.3 %copy-start.11 = (bf16[256,384]{1,0:T(8,128)(2,1)}, bf16[256,384]{1,0:T(8,128)(2,1)S(1)}, u32[]{:S(2)}) copy-start(bf16[256,384]{1,0:T(8,128)(2,1)S(1)} %collective-permute-done.9.other) | copy-start | bytes 589828
  44.0 3.4 %collective-permute-start.10 = (bf16[256,256]{1,0:T(8,128)(2,1)S(1)}, bf16[256,256]{1,0:T(8,128)(2,1)S(1)}, u32[]{:S(2)}, u32[]{:S(2)}) collective-permute-start(bf16[256,256]{1,0:T(8,128)(2,1)S(1)} %get-tuple-element.47), channel_id=1, source_target_pairs={{0,1},{1,0},{2,3},{3,2},{4,5},{5,4},{6,7},{7,6},{8,9},{9,8},{10,11... | collective-permute-start | bytes 393224 | tf_op jit(solution)/shard_map/ppermute | solution.py:387
  47.4 21.2 %copy-start.1 = (f32[128,128]{1,0:T(8,128)S(1)}, f32[128,128]{1,0:T(8,128)}, u32[]{:S(2)}) copy-start(f32[128,128]{1,0:T(8,128)} %refs_5_.1) | copy-start | bytes 196612
  47.4 21.2 %copy-start.2 = (bf16[256,128]{1,0:T(8,128)(2,1)S(1)}, bf16[256,128]{1,0:T(8,128)(2,1)}, u32[]{:S(2)}) copy-start(bf16[256,128]{1,0:T(8,128)(2,1)} %head.1) | copy-start | bytes 196612
  53.3 5.0 %collective-permute-start.12 = (bf16[128,256]{1,0:T(8,128)(2,1)S(1)}, bf16[128,256]{1,0:T(8,128)(2,1)S(1)}, u32[]{:S(2)}, u32[]{:S(2)}) collective-permute-start(bf16[128,256]{1,0:T(8,128)(2,1)S(1)} %bitcast.193), channel_id=1, source_target_pairs={{0,2},{1,3},{2,0},{3,1},{4,6},{5,7},{6,4},{7,5},{8,10},{9,11},{10,... | collective-permute-start | bytes 196616 | tf_op jit(solution)/shard_map/ppermute | solution.py:387
  54.2 9.9 %collective-permute-start.11 = (bf16[128,256]{1,0:T(8,128)(2,1)S(1)}, bf16[128,256]{1,0:T(8,128)(2,1)S(1)}, u32[]{:S(2)}, u32[]{:S(2)}) collective-permute-start(bf16[128,256]{1,0:T(8,128)(2,1)S(1)} %bitcast.190), channel_id=1, source_target_pairs={{0,2},{1,3},{2,0},{3,1},{4,6},{5,7},{6,4},{7,5},{8,10},{9,11},{10,... | collective-permute-start | bytes 196616 | tf_op jit(solution)/shard_map/ppermute | solution.py:387
  55.4 5.7 %collective-permute-start.14 = (bf16[128,256]{1,0:T(8,128)(2,1)S(1)}, bf16[128,256]{1,0:T(8,128)(2,1)S(1)}, u32[]{:S(2)}, u32[]{:S(2)}) collective-permute-start(bf16[128,256]{1,0:T(8,128)(2,1)S(1)} %bitcast.192), channel_id=1, source_target_pairs={{0,2},{1,3},{2,0},{3,1},{4,6},{5,7},{6,4},{7,5},{8,10},{9,11},{10,... | collective-permute-start | bytes 196616 | tf_op jit(solution)/shard_map/ppermute | solution.py:387
  56.2 5.9 %collective-permute-start.16 = (bf16[128,256]{1,0:T(8,128)(2,1)S(1)}, bf16[128,256]{1,0:T(8,128)(2,1)S(1)}, u32[]{:S(2)}, u32[]{:S(2)}) collective-permute-start(bf16[128,256]{1,0:T(8,128)(2,1)S(1)} %bitcast.191), channel_id=1, source_target_pairs={{0,2},{1,3},{2,0},{3,1},{4,6},{5,7},{6,4},{7,5},{8,10},{9,11},{10,... | collective-permute-start | bytes 196616 | tf_op jit(solution)/shard_map/ppermute | solution.py:387
  58.3 5.8 %collective-permute-start.13 = (bf16[128,256]{1,0:T(8,128)(2,1)S(1)}, bf16[128,256]{1,0:T(8,128)(2,1)S(1)}, u32[]{:S(2)}, u32[]{:S(2)}) collective-permute-start(bf16[128,256]{1,0:T(8,128)(2,1)S(1)} %fusion.8), channel_id=1, source_target_pairs={{0,4},{1,5},{2,6},{3,7},{4,0},{5,1},{6,2},{7,3},{8,12},{9,13},{10,... | collective-permute-start | bytes 196616 | tf_op jit(solution)/shard_map/ppermute | solution.py:387
  61.1 7.5 %collective-permute-start.15 = (bf16[128,256]{1,0:T(8,128)(2,1)S(1)}, bf16[128,256]{1,0:T(8,128)(2,1)S(1)}, u32[]{:S(2)}, u32[]{:S(2)}) collective-permute-start(bf16[128,256]{1,0:T(8,128)(2,1)S(1)} %fusion.7), channel_id=1, source_target_pairs={{0,8},{1,9},{2,10},{3,11},{4,12},{5,13},{6,14},{7,15},{8,0},{9,1},... | collective-permute-start | bytes 196616 | tf_op jit(solution)/shard_map/ppermute | solution.py:387
  62.2 6.5 %collective-permute-start.17 = (bf16[128,256]{1,0:T(8,128)(2,1)S(1)}, bf16[128,256]{1,0:T(8,128)(2,1)S(1)}, u32[]{:S(2)}, u32[]{:S(2)}) collective-permute-start(bf16[128,256]{1,0:T(8,128)(2,1)S(1)} %fusion.6), channel_id=1, source_target_pairs={{0,12},{1,13},{2,14},{3,15},{4,8},{5,9},{6,10},{7,11},{8,4},{9,5},... | collective-permute-start | bytes 196616 | tf_op jit(solution)/shard_map/ppermute | solution.py:387
  69.1 5.8 %collective-permute-start.23 = (bf16[128,128]{1,0:T(8,128)(2,1)S(1)}, bf16[128,128]{1,0:T(8,128)(2,1)S(1)}, u32[]{:S(2)}, u32[]{:S(2)}) collective-permute-start(bf16[128,128]{1,0:T(8,128)(2,1)S(1)} %get-tuple-element.56), channel_id=1, source_target_pairs={{0,12},{1,13},{2,14},{3,15},{4,8},{5,9},{6,10},{7,11},{8,4},{9,5},... | collective-permute-start | bytes 98312 | tf_op jit(solution)/shard_map/ppermute | solution.py:387
  70.9 5.0 %collective-permute-start.21 = (bf16[128,128]{1,0:T(8,128)(2,1)S(1)}, bf16[128,128]{1,0:T(8,128)(2,1)S(1)}, u32[]{:S(2)}, u32[]{:S(2)}) collective-permute-start(bf16[128,128]{1,0:T(8,128)(2,1)S(1)} %get-tuple-element.56), channel_id=1, source_target_pairs={{0,8},{1,9},{2,10},{3,11},{4,12},{5,13},{6,14},{7,15},{8,0},{9,1},... | collective-permute-start | bytes 98312 | tf_op jit(solution)/shard_map/ppermute | solution.py:387
  71.9 5.2 %collective-permute-start.19 = (bf16[128,128]{1,0:T(8,128)(2,1)S(1)}, bf16[128,128]{1,0:T(8,128)(2,1)S(1)}, u32[]{:S(2)}, u32[]{:S(2)}) collective-permute-start(bf16[128,128]{1,0:T(8,128)(2,1)S(1)} %get-tuple-element.56), channel_id=1, source_target_pairs={{0,4},{1,5},{2,6},{3,7},{4,0},{5,1},{6,2},{7,3},{8,12},{9,13},{10,... | collective-permute-start | bytes 98312 | tf_op jit(solution)/shard_map/ppermute | solution.py:387
  73.6 4.3 %collective-permute-start.18 = (bf16[128,128]{1,0:T(8,128)(2,1)S(1)}, bf16[128,128]{1,0:T(8,128)(2,1)S(1)}, u32[]{:S(2)}, u32[]{:S(2)}) collective-permute-start(bf16[128,128]{1,0:T(8,128)(2,1)S(1)} %get-tuple-element.56), channel_id=1, source_target_pairs={{0,2},{1,3},{2,0},{3,1},{4,6},{5,7},{6,4},{7,5},{8,10},{9,11},{10,... | collective-permute-start | bytes 98312 | tf_op jit(solution)/shard_map/ppermute | solution.py:387
  74.9 3.9 %collective-permute-start.24 = (bf16[128,128]{1,0:T(8,128)(2,1)S(1)}, bf16[128,128]{1,0:T(8,128)(2,1)S(1)}, u32[]{:S(2)}, u32[]{:S(2)}) collective-permute-start(bf16[128,128]{1,0:T(8,128)(2,1)S(1)} %collective-permute-done.23), channel_id=1, source_target_pairs={{0,2},{1,3},{2,0},{3,1},{4,6},{5,7},{6,4},{7,5},{8,10},{9,11},{10,... | collective-permute-start | bytes 98312 | tf_op jit(solution)/shard_map/ppermute | solution.py:387
  75.8 3.9 %collective-permute-start.22 = (bf16[128,128]{1,0:T(8,128)(2,1)S(1)}, bf16[128,128]{1,0:T(8,128)(2,1)S(1)}, u32[]{:S(2)}, u32[]{:S(2)}) collective-permute-start(bf16[128,128]{1,0:T(8,128)(2,1)S(1)} %collective-permute-done.21), channel_id=1, source_target_pairs={{0,2},{1,3},{2,0},{3,1},{4,6},{5,7},{6,4},{7,5},{8,10},{9,11},{10,... | collective-permute-start | bytes 98312 | tf_op jit(solution)/shard_map/ppermute | solution.py:387
  77.1 3.9 %collective-permute-start.20 = (bf16[128,128]{1,0:T(8,128)(2,1)S(1)}, bf16[128,128]{1,0:T(8,128)(2,1)S(1)}, u32[]{:S(2)}, u32[]{:S(2)}) collective-permute-start(bf16[128,128]{1,0:T(8,128)(2,1)S(1)} %collective-permute-done.19), channel_id=1, source_target_pairs={{0,2},{1,3},{2,0},{3,1},{4,6},{5,7},{6,4},{7,5},{8,10},{9,11},{10,... | collective-permute-start | bytes 98312 | tf_op jit(solution)/shard_map/ppermute | solution.py:387
  82.4 1.5 collective-permute-start.25
  82.5 33.8 %collective-permute-start.40 = (f32[256,128]{1,0:T(8,128)S(1)}, f32[256,128]{1,0:T(8,128)S(1)}, u32[]{:S(2)}, u32[]{:S(2)}) collective-permute-start(f32[256,128]{1,0:T(8,128)S(1)} %get-tuple-element.78), channel_id=1, source_target_pairs={{0,1},{1,0},{2,3},{3,2},{4,5},{5,4},{6,7},{7,6},{8,9},{9,8},{10,11... | collective-permute-start | bytes 393224 | tf_op jit(solution)/shard_map/ppermute | solution.py:387
  84.0 1.2 copy-start.6
  85.2 1.2 copy-start.8
  86.4 0.9 copy-start.10
  87.4 0.9 copy-start.12
  97.0 16.6 %collective-permute-start.26 = (bf16[256,384]{1,0:T(8,128)(2,1)S(1)}, bf16[256,384]{1,0:T(8,128)(2,1)S(1)}, u32[]{:S(2)}, u32[]{:S(2)}) collective-permute-start(bf16[256,384]{1,0:T(8,128)(2,1)S(1)} %get-tuple-element.62), channel_id=1, source_target_pairs={{0,1},{1,0},{2,3},{3,2},{4,5},{5,4},{6,7},{7,6},{8,9},{9,8},{10,11... | collective-permute-start | bytes 589832 | tf_op jit(solution)/shard_map/ppermute | solution.py:387
  111.2 50.9 %collective-permute-start.35 = (bf16[16,64,256]{2,1,0:T(8,128)(2,1)}, bf16[16,64,256]{2,1,0:T(8,128)(2,1)}, u32[]{:S(2)}, u32[]{:S(2)}) collective-permute-start(bf16[16,64,256]{2,1,0:T(8,128)(2,1)} %fusion.2), channel_id=1, source_target_pairs={{0,1},{1,0},{2,3},{3,2},{4,5},{5,4},{6,7},{7,6},{8,9},{9,8},{10,11... | collective-permute-start | bytes 1572872 | tf_op jit(solution)/shard_map/ppermute | solution.py:387
  115.3 4.8 %collective-permute-start.28 = (bf16[144,256]{1,0:T(8,128)(2,1)S(1)}, bf16[144,256]{1,0:T(8,128)(2,1)S(1)}, u32[]{:S(2)}, u32[]{:S(2)}) collective-permute-start(bf16[144,256]{1,0:T(8,128)(2,1)S(1)} %bitcast.189), channel_id=1, source_target_pairs={{0,2},{1,3},{2,0},{3,1},{4,6},{5,7},{6,4},{7,5},{8,10},{9,11},{10,... | collective-permute-start | bytes 221192 | tf_op jit(solution)/shard_map/ppermute | solution.py:387
  116.2 17.5 %collective-permute-start.34 = (bf16[8,16,16,128]{3,2,1,0:T(8,128)(2,1)S(1)}, bf16[8,16,16,128]{3,2,1,0:T(8,128)(2,1)S(1)}, u32[]{:S(2)}, u32[]{:S(2)}) collective-permute-start(bf16[8,16,16,128]{3,2,1,0:T(8,128)(2,1)S(1)} %fusion.1), channel_id=1, source_target_pairs={{0,1},{1,0},{2,3},{3,2},{4,5},{5,4},{6,7},{7,6},{8,9},{9,8},{10,11... | collective-permute-start | bytes 1572872 | tf_op jit(solution)/shard_map/ppermute | solution.py:387
  116.3 9.6 %collective-permute-start.27 = (bf16[144,256]{1,0:T(8,128)(2,1)S(1)}, bf16[144,256]{1,0:T(8,128)(2,1)S(1)}, u32[]{:S(2)}, u32[]{:S(2)}) collective-permute-start(bf16[144,256]{1,0:T(8,128)(2,1)S(1)} %bitcast.186), channel_id=1, source_target_pairs={{0,2},{1,3},{2,0},{3,1},{4,6},{5,7},{6,4},{7,5},{8,10},{9,11},{10,... | collective-permute-start | bytes 221192 | tf_op jit(solution)/shard_map/ppermute | solution.py:387
  117.6 5.6 %collective-permute-start.30 = (bf16[144,256]{1,0:T(8,128)(2,1)S(1)}, bf16[144,256]{1,0:T(8,128)(2,1)S(1)}, u32[]{:S(2)}, u32[]{:S(2)}) collective-permute-start(bf16[144,256]{1,0:T(8,128)(2,1)S(1)} %bitcast.188), channel_id=1, source_target_pairs={{0,2},{1,3},{2,0},{3,1},{4,6},{5,7},{6,4},{7,5},{8,10},{9,11},{10,... | collective-permute-start | bytes 221192 | tf_op jit(solution)/shard_map/ppermute | solution.py:387
  120.1 4.4 %collective-permute-start.32 = (bf16[144,256]{1,0:T(8,128)(2,1)S(1)}, bf16[144,256]{1,0:T(8,128)(2,1)S(1)}, u32[]{:S(2)}, u32[]{:S(2)}) collective-permute-start(bf16[144,256]{1,0:T(8,128)(2,1)S(1)} %bitcast.187), channel_id=1, source_target_pairs={{0,2},{1,3},{2,0},{3,1},{4,6},{5,7},{6,4},{7,5},{8,10},{9,11},{10,... | collective-permute-start | bytes 221192 | tf_op jit(solution)/shard_map/ppermute | solution.py:387
  123.2 5.1 %collective-permute-start.29 = (bf16[144,256]{1,0:T(8,128)(2,1)S(1)}, bf16[144,256]{1,0:T(8,128)(2,1)S(1)}, u32[]{:S(2)}, u32[]{:S(2)}) collective-permute-start(bf16[144,256]{1,0:T(8,128)(2,1)S(1)} %fusion.5), channel_id=1, source_target_pairs={{0,4},{1,5},{2,6},{3,7},{4,0},{5,1},{6,2},{7,3},{8,12},{9,13},{10,... | collective-permute-start | bytes 221192 | tf_op jit(solution)/shard_map/ppermute | solution.py:387
  124.5 8.2 %collective-permute-start.31 = (bf16[144,256]{1,0:T(8,128)(2,1)S(1)}, bf16[144,256]{1,0:T(8,128)(2,1)S(1)}, u32[]{:S(2)}, u32[]{:S(2)}) collective-permute-start(bf16[144,256]{1,0:T(8,128)(2,1)S(1)} %fusion.4), channel_id=1, source_target_pairs={{0,8},{1,9},{2,10},{3,11},{4,12},{5,13},{6,14},{7,15},{8,0},{9,1},... | collective-permute-start | bytes 221192 | tf_op jit(solution)/shard_map/ppermute | solution.py:387
  125.9 6.8 %collective-permute-start.33 = (bf16[144,256]{1,0:T(8,128)(2,1)S(1)}, bf16[144,256]{1,0:T(8,128)(2,1)S(1)}, u32[]{:S(2)}, u32[]{:S(2)}) collective-permute-start(bf16[144,256]{1,0:T(8,128)(2,1)S(1)} %fusion.3), channel_id=1, source_target_pairs={{0,12},{1,13},{2,14},{3,15},{4,8},{5,9},{6,10},{7,11},{8,4},{9,5},... | collective-permute-start | bytes 221192 | tf_op jit(solution)/shard_map/ppermute | solution.py:387
  128.4 12.4 %collective-permute-start.41 = (f32[256,128]{1,0:T(8,128)S(1)}, f32[256,128]{1,0:T(8,128)S(1)}, u32[]{:S(2)}, u32[]{:S(2)}) collective-permute-start(f32[256,128]{1,0:T(8,128)S(1)} %add.104), channel_id=1, source_target_pairs={{0,2},{1,3},{2,0},{3,1},{4,6},{5,7},{6,4},{7,5},{8,10},{9,11},{10,... | collective-permute-start | bytes 393224 | tf_op jit(solution)/shard_map/ppermute | solution.py:387
  133.6 5.1 %collective-permute-start.36 = (f32[8,20,256]{2,0,1:T(8,128)S(1)}, f32[8,20,256]{2,0,1:T(8,128)S(1)}, u32[]{:S(2)}, u32[]{:S(2)}) collective-permute-start(f32[8,20,256]{2,0,1:T(8,128)S(1)} %copy.26), channel_id=1, source_target_pairs={{0,1},{1,0},{2,3},{3,2},{4,5},{5,4},{6,7},{7,6},{8,9},{9,8},{10,11... | collective-permute-start | bytes 491528 | tf_op jit(solution)/shard_map/ppermute | solution.py:387
  134.6 27.5 %copy-start.13 = (f32[2048,256]{1,0:T(8,128)S(1)}, f32[2048,256]{1,0:T(8,128)}, u32[]{:S(2)}) copy-start(f32[2048,256]{1,0:T(8,128)} %get-tuple-element.74) | copy-start | bytes 6291460
  134.6 35.9 %all-to-all-start.1 = ((bf16[8,16,16,128]{3,2,1,0:T(8,128)(2,1)}), bf16[8,16,16,128]{3,2,1,0:T(8,128)(2,1)S(1)}, u32[]{:S(2)}, u32[]{:S(2)}) async-start(bf16[8,16,16,128]{3,2,1,0:T(8,128)(2,1)} %fusion), calls=%async_computation.1 | async-start | bytes 1048576 | tf_op jit(solution)/shard_map/all_to_all | solution.py:513
  138.7 10.7 %collective-permute-start.37 = (f32[8,20,256]{2,0,1:T(8,128)S(1)}, f32[8,20,256]{2,0,1:T(8,128)S(1)}, u32[]{:S(2)}, u32[]{:S(2)}) collective-permute-start(f32[8,20,256]{2,0,1:T(8,128)S(1)} %copy_add_fusion), channel_id=1, source_target_pairs={{0,2},{1,3},{2,0},{3,1},{4,6},{5,7},{6,4},{7,5},{8,10},{9,11},{10,... | collective-permute-start | bytes 491528 | tf_op jit(solution)/shard_map/ppermute | solution.py:387
  140.8 10.9 %collective-permute-start.42 = (f32[256,128]{1,0:T(8,128)S(1)}, f32[256,128]{1,0:T(8,128)S(1)}, u32[]{:S(2)}, u32[]{:S(2)}) collective-permute-start(f32[256,128]{1,0:T(8,128)S(1)} %add.105), channel_id=1, source_target_pairs={{0,4},{1,5},{2,6},{3,7},{4,0},{5,1},{6,2},{7,3},{8,12},{9,13},{10,... | collective-permute-start | bytes 393224 | tf_op jit(solution)/shard_map/ppermute | solution.py:387
  149.4 12.5 %collective-permute-start.38 = (f32[8,20,256]{2,0,1:T(8,128)S(1)}, f32[8,20,256]{2,0,1:T(8,128)S(1)}, u32[]{:S(2)}, u32[]{:S(2)}) collective-permute-start(f32[8,20,256]{2,0,1:T(8,128)S(1)} %add.101), channel_id=1, source_target_pairs={{0,4},{1,5},{2,6},{3,7},{4,0},{5,1},{6,2},{7,3},{8,12},{9,13},{10,... | collective-permute-start | bytes 491528 | tf_op jit(solution)/shard_map/ppermute | solution.py:387
  151.7 9.5 %collective-permute-start.43 = (f32[256,128]{1,0:T(8,128)S(1)}, f32[256,128]{1,0:T(8,128)S(1)}, u32[]{:S(2)}, u32[]{:S(2)}) collective-permute-start(f32[256,128]{1,0:T(8,128)S(1)} %add.106), channel_id=1, source_target_pairs={{0,8},{1,9},{2,10},{3,11},{4,12},{5,13},{6,14},{7,15},{8,0},{9,1},... | collective-permute-start | bytes 393224 | tf_op jit(solution)/shard_map/ppermute | solution.py:387
  162.0 7.9 %collective-permute-start.39 = (f32[8,20,256]{2,0,1:T(8,128)S(1)}, f32[8,20,256]{2,0,1:T(8,128)S(1)}, u32[]{:S(2)}, u32[]{:S(2)}) collective-permute-start(f32[8,20,256]{2,0,1:T(8,128)S(1)} %add.102), channel_id=1, source_target_pairs={{0,8},{1,9},{2,10},{3,11},{4,12},{5,13},{6,14},{7,15},{8,0},{9,1},... | collective-permute-start | bytes 491528 | tf_op jit(solution)/shard_map/ppermute | solution.py:387

commit v2 on v1

v2 whole, which is shorter than its diff:
```python
import functools

import jax
import jax.numpy as jnp
from jax import lax
from jax.experimental import pallas as pl
from jax.experimental.pallas import tpu as pltpu
from jax.sharding import PartitionSpec as P

AXIS = "expert"
TILE = 256
AUX = 32
bf16 = jnp.bfloat16
f32 = jnp.float32
CHUNK = 256
SMALL, BIG = 24, 32


def mm(left, right, left_dim=1, right_dim=0):
    return lax.dot_general(
        left, right, (((left_dim,), (right_dim,)), ((), ())), preferred_element_type=f32
    )


def call(kernel, out_shapes, operands, in_specs=None, scratch=(), flops=0, nbytes=0, limit=48):
    specs = in_specs or [None] * len(operands)
    specs = [pl.BlockSpec(memory_space=pltpu.VMEM) if s is None else s for s in specs]
    return pl.pallas_call(
        kernel,
        out_shape=out_shapes,
        in_specs=specs,
        out_specs=[pl.BlockSpec(memory_space=pltpu.VMEM) for _ in out_shapes],
        scratch_shapes=list(scratch),
        compiler_params=pltpu.CompilerParams(vmem_limit_bytes=limit * 1024 * 1024),
        cost_estimate=pl.CostEstimate(flops=flops, bytes_accessed=nbytes, transcendentals=0),
    )(*operands)


SCALARS = pl.BlockSpec(memory_space=pltpu.SMEM)


def struct(shape, kind):
    return jax.ShapeDtypeStruct(shape, kind)


def sigmoid(v):
    return 0.5 * (1.0 + jnp.tanh(0.5 * v))


def eye(size):
    rows = lax.broadcasted_iota(jnp.int32, (size, size), 0)
    cols = lax.broadcasted_iota(jnp.int32, (size, size), 1)
    return (rows == cols).astype(f32).astype(bf16)


def spread(tile, expert_lanes):
    rows = lax.broadcasted_iota(jnp.int32, (AUX, TILE), 0)
    lanes = lax.broadcasted_iota(jnp.int32, (AUX, TILE), 1) + tile * TILE
    first = rows * expert_lanes
    return ((lanes >= first) & (lanes < first + expert_lanes)).astype(f32).astype(bf16)


def turn_matrix(size, depth, core):
    place = lax.broadcasted_iota(jnp.int32, (size, size), 0)
    column = lax.broadcasted_iota(jnp.int32, (size, size), 1)
    half = size // 2
    other = place // half
    place = place - other * half
    chip = place // depth
    which = jnp.where(core == 0, other, 1 - other)
    return (column == (chip * 2 + which) * depth + (place - chip * depth)).astype(f32).astype(bf16)


def side_of(piece):
    half = piece.shape[1] // 2
    return jnp.concatenate([piece[:, :half], piece[:, half:]], axis=0)


def selector(side, gate_count, scenario, capacity):
    wide = side.astype(f32)
    which = wide[gate_count : gate_count + 1, :]
    slot = wide[gate_count + 1 : gate_count + 2, :]
    ranks = lax.broadcasted_iota(jnp.int32, (capacity, side.shape[1]), 0).astype(f32)
    hit = (ranks == slot) & (which == scenario.astype(f32))
    return hit.astype(f32).astype(bf16)


def prep_kernel(gate_count, tiled, pads, feats, sid, gate_rows, expand, pack, probs, pieces, scr):
    rows = feats.shape[0]
    scenarios = gate_rows.shape[0] // AUX
    x = feats[...]
    logits = mm(gate_rows[...], x, 1, 1)
    own = jnp.zeros((AUX, rows), f32)
    ids = sid[...]
    pad = jnp.zeros((1, rows), f32)
    for s in range(scenarios):
        hit = ids == s
        own = own + jnp.where(hit, logits[s * AUX : (s + 1) * AUX], 0.0)
        pad = pad + jnp.where(hit, pads[s].astype(f32), 0.0)
    labels = lax.broadcasted_iota(jnp.int32, (AUX, rows), 0)
    own = jnp.where(labels < gate_count, own, -jnp.inf)
    top = jnp.max(own, axis=0, keepdims=True)
    raised = jnp.exp(own - top)
    share = raised / jnp.sum(raised, axis=0, keepdims=True)
    probs[...] = share
    member = (ids == labels).astype(f32)
    earlier = (
        lax.broadcasted_iota(jnp.int32, (rows, rows), 0)
        < lax.broadcasted_iota(jnp.int32, (rows, rows), 1)
    ).astype(f32).astype(bf16)
    rank = jnp.sum(mm(member.astype(bf16), earlier) * member, axis=0, keepdims=True)
    slot = jnp.where(rank < pad, rank, -1.0)
    scr[...] = share
    scr[gate_count : gate_count + 1, :] = ids.astype(f32)
    scr[gate_count + 1 : gate_count + 2, :] = slot
    side = scr[...].astype(bf16)
    pack[:rows, :] = x
    pack[rows:, :rows] = side[: AUX // 2]
    pack[rows:, rows:] = side[AUX // 2 :]
    if tiled:
        chips, _, total = pieces.shape
        count = expand.shape[0]
        lanes = total // count
        for k in range(count):
            for chip in range(chips):
                pieces[chip, :, k * lanes : (k + 1) * lanes] = expand[
                    k, :, chip * lanes : (chip + 1) * lanes
                ]
    else:
        pieces[...] = expand[...]


def unpack_kernel(n, gate_count, capacity, depth, scal, *refs):
    pieces = refs[:n]
    xp, xpt, gates, sel_own, sel_other, x_own, x_other = refs[n:]
    m = pieces[0].shape[0]
    rows = pieces[0].shape[1] - AUX // 2
    width = xp.shape[1]
    turn = turn_matrix(width, depth, scal[3])
    tail = jnp.zeros((capacity, x_own.shape[1] - width - AUX), bf16)
    for k in range(n):
        for b in range(m):
            at = (k * m + b) * rows
            x = pieces[k][b, :rows, :]
            side = side_of(pieces[k][b, rows:, :])
            xp[at : at + rows, :] = mm(x, turn, 1, 1).astype(bf16)
            xpt[:, at : at + rows] = mm(turn, x, 1, 1).astype(bf16)
            gates[at : at + rows, :] = mm(side, eye(AUX), 0, 0).astype(bf16)
            spot = slice((k * m + b) * capacity, (k * m + b + 1) * capacity)
            for which, sel_out, out in ((0, sel_own, x_own), (1, sel_other, x_other)):
                sel = selector(side, gate_count, scal[which], capacity)
                sel_out[spot, :] = sel
                out[spot, :width] = mm(sel, x).astype(bf16)
                out[spot, width : width + AUX] = mm(sel, side, 1, 1).astype(bf16)
                out[spot, width + AUX :] = tail


def compact_kernel(n, sel_own, sel_other, *refs):
    values, outs = refs[:n], refs[n:]
    m = values[0].shape[0]
    capacity = outs[0].shape[0] // (n * m)
    for k in range(n):
        for b in range(m):
            spot = slice((k * m + b) * capacity, (k * m + b + 1) * capacity)
            for sel, out in zip((sel_own, sel_other), outs):
                out[spot, :] = mm(sel[spot, :], values[k][b]).astype(bf16)


def chosen_gate(x, width, column):
    gates = x[:, width:].astype(f32)
    lanes = lax.broadcasted_iota(jnp.int32, gates.shape, 1)
    return jnp.sum(jnp.where(lanes == column, gates, 0.0), axis=1, keepdims=True)


def hidden_lanes(j):
    return pl.ds(pl.multiple_of(j * TILE, TILE), TILE)


def scenario_forward_kernel(shared, span, scal, own, other, widen, narrow, out_own, out_other, gated):
    half, width = out_own.shape
    chunk = min(half, CHUNK)

    def tile(j, _):
        lanes = hidden_lanes(j)
        column = shared + scal[2] + (j * TILE) // span
        for base, source in ((0, own), (half, other)):
            for at in range(0, half, chunk):
                x = source[at : at + chunk, :]
                linear = mm(x[:, :width], widen[:, lanes])
                active = linear * sigmoid(linear)
                gate = chosen_gate(x, width, column)
                gated[base + at : base + at + chunk, lanes] = (gate * active).astype(bf16)
        return 0

    lax.fori_loop(0, widen.shape[1] // TILE, tile, 0)
    out_own[...] = mm(gated[:half, :], narrow[...]).astype(bf16)
    out_other[...] = mm(gated[half:, :], narrow[...]).astype(bf16)


def scenario_slope_kernel(
    shared, span, scal, own, other, widen, active_out, gated_turned, slope_out, turned
):
    half = own.shape[0]
    width = widen.shape[0]
    chunk = min(half, CHUNK)
    for base, source in ((0, own), (half, other)):
        for at in range(0, half, chunk):
            turned[:, base + at : base + at + chunk] = mm(
                eye(width), source[at : at + chunk, :width], 1, 1
            ).astype(bf16)

    def tile(j, _):
        lanes = hidden_lanes(j)
        column = shared + scal[2] + (j * TILE) // span
        for base, source in ((0, own), (half, other)):
            for at in range(0, half, chunk):
                x = source[at : at + chunk, :]
                gate = chosen_gate(x, width, column)
                linear = mm(x[:, :width], widen[:, lanes])
                sig = sigmoid(linear)
                active = linear * sig
                spot = slice(base + at, base + at + chunk)
                active_out[spot, lanes] = active.astype(bf16)
                slope_out[spot, lanes] = (gate * (sig + active * (1.0 - sig))).astype(bf16)
                gated_turned[lanes, spot] = jnp.transpose(gate * active).astype(bf16)
        return 0

    lax.fori_loop(0, widen.shape[1] // TILE, tile, 0)


def shared_forward_kernel(first, gate_rows, build, core, xp, gates, w1a, w1b, w2a, w2b, *refs):
    sel_own, sel_other, from_own, from_other = refs[:4]
    outs = refs[4:]
    gated = outs[-1]
    outs = outs[:-1]
    if build:
        w1, w2 = outs[-2:]
        outs = outs[:-2]
        half = w1a.shape[0]
        w1[:half, :] = w1a[...]
        w1[half:, :] = w1b[...]
        experts, part, _ = w2a.shape
        for k in range(experts):
            mine, theirs = w2a[k], w2b[k]
            low = jnp.where(core[3] == 0, mine, theirs)
            high = jnp.where(core[3] == 0, theirs, mine)
            w2[2 * k * part : (2 * k + 1) * part, :] = low
            w2[(2 * k + 1) * part : 2 * (k + 1) * part, :] = high
    else:
        w1, w2 = w1a, w2a
    m, rows, _ = outs[0].shape
    capacity = sel_own.shape[0] * rows // xp.shape[0]
    total = len(outs) * m * rows
    chunk = min(total, CHUNK)

    def tile(j, _):
        lanes = hidden_lanes(j)
        picks = spread(j, gate_rows)
        for at in range(0, total, chunk):
            spot = slice(first + at, first + at + chunk)
            linear = mm(xp[spot, :], w1[:, lanes])
            active = linear * sigmoid(linear)
            gated[at : at + chunk, lanes] = (mm(gates[spot, :], picks) * active).astype(bf16)
        return 0

    lax.fori_loop(0, w1.shape[1] // TILE, tile, 0)
    chunk = min(total, 512)
    for at in range(0, total, chunk):
        mixed = mm(gated[at : at + chunk, :], w2[...])
        for piece in range(at // rows, (at + chunk) // rows):
            start = (first // rows + piece) * capacity
            spot = slice(start, start + capacity)
            extra = mm(sel_own[spot, :], from_own[spot, :], 0, 0)
            extra += mm(sel_other[spot, :], from_other[spot, :], 0, 0)
            value = mixed[piece * rows - at : (piece + 1) * rows - at] + extra
            outs[piece // m][piece % m] = value.astype(bf16)


def shared_slope_kernel(gate_rows, xp, gates, w1, active_out, gated_turned, slope_out):
    total = xp.shape[0]
    chunk = min(total, CHUNK)

    def tile(j, _):
        lanes = hidden_lanes(j)
        picks = spread(j, gate_rows)
        for at in range(0, total, chunk):
            spot = slice(at, at + chunk)
            linear = mm(xp[spot, :], w1[:, lanes])
            sig = sigmoid(linear)
            active = linear * sig
            gate = mm(gates[spot, :], picks)
            active_out[spot, lanes] = active.astype(bf16)
            slope_out[spot, lanes] = (gate * (sig + active * (1.0 - sig))).astype(bf16)
            gated_turned[lanes, spot] = jnp.transpose(gate * active).astype(bf16)
        return 0

    lax.fori_loop(0, w1.shape[1] // TILE, tile, 0)


def softmax(v):
    raised = jnp.exp(v - jnp.max(v, axis=1, keepdims=True))
    return raised / jnp.sum(raised, axis=1, keepdims=True)


def head_kernel(count, *refs):
    parts = refs[:count]
    head, mentor, grad, head_part = refs[count:]
    layer = parts[0][...].astype(f32)
    for part in parts[1:]:
        layer = layer + part[...].astype(f32)
    rounded = layer.astype(bf16)
    student = mm(rounded, head[...])
    value = (2.0 * (softmax(student * 0.5) - softmax(mentor[...] * 0.5))).astype(bf16)
    grad[...] = value
    head_part[...] = mm(rounded, value, 0, 0)


def shared_backward_kernel(n, gate_rows, depth, scal, *refs):
    logits = refs[:n]
    head, xpt, active, slope, w1, w2 = refs[n : n + 6]
    dx, mix, keep, sent, os, linear_grad = refs[n + 6 :]
    m, rows, _ = logits[0].shape
    for k in range(n):
        for b in range(m):
            at = (k * m + b) * rows
            os[at : at + rows, :] = mm(logits[k][b], head[...], 1, 1).astype(bf16)
    total = n * m * rows
    chunk = min(total, 2 * CHUNK)
    half = keep.shape[0]
    mix[...] = jnp.zeros_like(mix)

    def tile(j, _):
        lanes = hidden_lanes(j)
        picks = spread(j, gate_rows)
        for at in range(0, total, chunk):
            spot = slice(at, at + chunk)
            hidden = mm(os[spot, :], w2[lanes, :], 1, 1)
            linear_grad[spot, lanes] = (hidden * slope[spot, lanes].astype(f32)).astype(bf16)
            product = (hidden * active[spot, lanes].astype(f32)).astype(bf16)
            mix[spot, :] += mm(product, picks, 1, 1)
        first = mm(xpt[...], linear_grad[:, lanes])
        keep[:, lanes] = first[:half]
        sent[:, lanes] = first[half:].astype(bf16)
        return 0

    lax.fori_loop(0, w1.shape[1] // TILE, tile, 0)
    turn = turn_matrix(w1.shape[0], depth, scal[3])
    chunk = min(total, 1024)
    for at in range(0, total, chunk):
        spot = slice(at, at + chunk)
        value = mm(linear_grad[spot, :], w1[...], 1, 1).astype(bf16)
        dx[spot, :] = mm(value, turn).astype(bf16)


def reduce_grad_kernel(gate_rows, scal, gated_turned, os, keep, sent):
    part = keep.shape[1]

    def tile(j, _):
        value = mm(gated_turned[hidden_lanes(j), :], os[...])
        for e in range(TILE // gate_rows):
            low = value[e * gate_rows : e * gate_rows + part]
            high = value[e * gate_rows + part : (e + 1) * gate_rows]
            k = j * (TILE // gate_rows) + e
            keep[k] = jnp.where(scal[3] == 0, low, high)
            sent[k] = jnp.where(scal[3] == 0, high, low).astype(bf16)
        return 0

    lax.fori_loop(0, gated_turned.shape[0] // TILE, tile, 0)


def scenario_backward_kernel(
    shared, span, scal, logit_own, logit_other, head, widen, narrow, active, slope,
    out_own, out_other, os, linear_grad, mix,
):
    half = out_own.shape[0]
    width = narrow.shape[1]
    os[:half, :] = mm(logit_own[...], head[...], 1, 1).astype(bf16)
    os[half:, :] = mm(logit_other[...], head[...], 1, 1).astype(bf16)
    mix[...] = jnp.zeros_like(mix)
    chunk = min(2 * half, 2 * CHUNK)

    def tile(j, _):
        lanes = hidden_lanes(j)
        column = shared + scal[2] + (j * TILE) // span
        picks = (
            lax.broadcasted_iota(jnp.int32, (TILE, mix.shape[1]), 1) == column
        ).astype(f32).astype(bf16)
        for at in range(0, 2 * half, chunk):
            spot = slice(at, at + chunk)
            hidden = mm(os[spot, :], narrow[lanes, :], 1, 1)
            linear_grad[spot, lanes] = (hidden * slope[spot, lanes].astype(f32)).astype(bf16)
            product = (hidden * active[spot, lanes].astype(f32)).astype(bf16)
            mix[spot, :] += mm(product, picks)
        return 0

    lax.fori_loop(0, widen.shape[1] // TILE, tile, 0)
    for at, out in ((0, out_own), (half, out_other)):
        out[:, :width] = mm(linear_grad[at : at + half, :], widen[...], 1, 1).astype(bf16)
        out[:, width:] = mix[at : at + half, :].astype(bf16)


def scenario_weight_kernel(turned, linear_grad, gated_turned, os, dwiden, dnarrow):
    def tile(j, _):
        lanes = hidden_lanes(j)
        dwiden[:, lanes] = mm(turned[...], linear_grad[:, lanes])
        dnarrow[lanes, :] = mm(gated_turned[lanes, :], os[...])
        return 0

    lax.fori_loop(0, dwiden.shape[1] // TILE, tile, 0)


def scatter_kernel(n, gate_count, *refs):
    pieces = refs[:n]
    sel_own, sel_other, gates, dx, mix, from_own, from_other = refs[n : n + 7]
    outs, gate_part, wide = refs[n + 7 : -2], refs[-2], refs[-1]
    m, packed, width = outs[0].shape
    rows = packed - AUX // 2
    capacity = sel_own.shape[0] // (n * m)
    live = lax.broadcasted_iota(jnp.int32, (rows, AUX), 1) < gate_count
    total = jnp.zeros(gate_part.shape, f32)
    for k in range(n):
        for b in range(m):
            piece = k * m + b
            slots = slice(piece * capacity, (piece + 1) * capacity)
            extra = mm(sel_own[slots, :], from_own[slots, :], 0, 0)
            extra += mm(sel_other[slots, :], from_other[slots, :], 0, 0)
            spot = slice(piece * rows, (piece + 1) * rows)
            outs[k][b, :rows, :] = (dx[spot, :].astype(f32) + extra[:, :width]).astype(bf16)
            dots = mix[spot, :] + extra[:, width : width + AUX]
            turned = mm(eye(AUX), dots.astype(bf16), 1, 1).astype(bf16)
            outs[k][b, rows:, :rows] = turned[: AUX // 2]
            outs[k][b, rows:, rows:] = turned[AUX // 2 :]
            share = jnp.where(live, gates[spot, :].astype(f32), 0.0)
            share = share / jnp.sum(share, axis=1, keepdims=True)
            score = share * (dots - jnp.sum(share * dots, axis=1, keepdims=True))
            score = mm(eye(AUX), score.astype(bf16), 1, 1)
            ids = side_of(pieces[k][b, rows:, :])[gate_count : gate_count + 1, :].astype(f32)
            for s in range(gate_part.shape[0] // AUX):
                wide[s * AUX : (s + 1) * AUX, :] = jnp.where(ids == s, score, 0.0).astype(bf16)
            total = total + mm(wide[...], pieces[k][b, :rows, :])
    gate_part[...] = total


def final_kernel(count, gate_count, *refs):
    parts = refs[:count]
    feats, sid, probs, gate_rows, out, wide = refs[count:]
    rows = feats.shape[0]
    total = parts[0][...].astype(f32)
    for part in parts[1:]:
        total = total + part[...].astype(f32)
    tail = total[rows:]
    half = tail.shape[1] // 2
    dots = jnp.concatenate([tail[:, :half], tail[:, half:]], axis=0)
    share = probs[...]
    live = lax.broadcasted_iota(jnp.int32, (AUX, rows), 0) < gate_count
    dots = jnp.where(live, dots, 0.0)
    score = share * (dots - jnp.sum(share * dots, axis=0, keepdims=True))
    score = score.astype(bf16).astype(f32)
    ids = sid[...]
    for s in range(gate_rows.shape[0] // AUX):
        wide[s * AUX : (s + 1) * AUX, :] = jnp.where(ids == s, score, 0.0).astype(bf16)
    out[...] = (total[:rows] + mm(wide[...], gate_rows[...], 0, 0)).astype(bf16)


def expand_grad_kernel(pieces, out):
    count, _, hidden = out.shape
    chips = pieces.shape[0]
    lanes = hidden // chips
    for k in range(count):
        for chip in range(chips):
            out[k, :, chip * lanes : (chip + 1) * lanes] = pieces[
                chip, :, k * lanes : (k + 1) * lanes
            ].astype(f32)


def body(
    features,
    scenario_id,
    scenario_pads,
    device_slot,
    mentor,
    gate_weight,
    expand,
    reduce,
    scenario_widen,
    scenario_narrow,
    head,
):
    rows, width = features.shape
    devices = lax.axis_size(AXIS)
    index = lax.axis_index(AXIS)
    core = index % 2
    chips = devices // 2
    near = 2 ** ((chips.bit_length() - 1) // 2)
    far = chips // near
    flat = chips <= 8
    n, m = (chips, 1) if flat else (near, far)
    shared, depth, hidden = expand.shape
    lanes = hidden // chips
    scenarios, _, gates = gate_weight.shape
    capacity = rows // 4
    group = devices // scenarios
    slot_width = scenario_widen.shape[2]
    span = min(hidden, slot_width)
    classes = head.shape[1]
    all_rows = chips * rows
    slots = chips * capacity
    hidden_chip = shared * lanes
    groups = [[2 * r + c for r in range(chips)] for c in range(2)]

    def send(value, mask):
        return lax.ppermute(value, AXIS, [(i, i ^ mask) for i in range(devices)])

    def gather(value):
        column = [value] + [send(value, 2 * near * b) for b in range(1, far)]
        if flat:
            out = [v[None] for v in column]
            for a in range(1, near):
                out += [send(v, 2 * a)[None] for v in column]
            return out
        stacked = jnp.stack(column)
        return [stacked] + [send(stacked, 2 * a) for a in range(1, near)]

    def scatter(home, away):
        if flat:
            column = []
            for b in range(far):
                total = home[b][0].astype(f32)
                for a in range(1, near):
                    total = total + send(away[(a - 1) * far + b][0], 2 * a).astype(f32)
                column.append(total if b == 0 else total.astype(bf16))
        else:
            total = home[0].astype(f32)
            for a in range(1, near):
                total = total + send(away[a - 1], 2 * a).astype(f32)
            column = [total[0]] + [total[b].astype(bf16) for b in range(1, far)]
        return [column[0]] + [send(column[b], 2 * near * b) for b in range(1, far)]

    def total_of(value):
        value = value + send(value, 1)
        mask = 2
        while mask < devices:
            half = value.astype(bf16)
            value = half.astype(f32) + send(half, mask).astype(f32)
            mask *= 2
        return value

    own_slot = lax.dynamic_index_in_dim(device_slot, index, keepdims=False)
    other_slot = lax.dynamic_index_in_dim(device_slot, index ^ 1, keepdims=False)
    first_expert = own_slot % group * slot_width // hidden
    scal = jnp.stack([own_slot // group, other_slot // group, first_expert, core]).astype(jnp.int32)
    sid = scenario_id.reshape(1, rows)
    gate_rows = jnp.pad(
        jnp.transpose(gate_weight, (0, 2, 1)), ((0, 0), (0, AUX - gates), (0, 0))
    ).reshape(scenarios * AUX, width)
    widen, narrow = scenario_widen[0], scenario_narrow[0]
    tiled = lanes % 128 == 0 and depth % 16 == 0
    if not tiled:
        expand = expand.reshape(shared, depth, chips, lanes).transpose(2, 1, 0, 3)
        expand = expand.reshape(chips, depth, hidden_chip)

    pack_rows = rows + AUX // 2
    pack, probs, pieces = call(
        functools.partial(prep_kernel, gates, tiled),
        [
            struct((pack_rows, width), bf16),
            struct((AUX, rows), f32),
            struct((chips, depth, hidden_chip), bf16),
        ],
        [scenario_pads, features, sid, gate_rows, expand],
        [SCALARS] + [None] * 4,
        [pltpu.VMEM((AUX, rows), f32)],
        flops=10**9,
        limit=16,
    )
    w2a = reduce
    w2b = send(reduce, 1)
    w1a = lax.all_to_all(
        pieces, AXIS, split_axis=0, concat_axis=0, tiled=True, axis_index_groups=groups
    ).reshape(width // 2, hidden_chip)
    w1b = send(w1a, 1)

    got = gather(pack)
    xp, xpt, gate_columns, sel_own, sel_other, x_own, x_send = call(
        functools.partial(unpack_kernel, n, gates, capacity, depth),
        [
            struct((all_rows, width), bf16),
            struct((width, all_rows), bf16),
            struct((all_rows, AUX), bf16),
            struct((slots, rows), bf16),
            struct((slots, rows), bf16),
            struct((slots, width + 128), bf16),
            struct((slots, width + 128), bf16),
        ],
        [scal, *got],
        [SCALARS] + [None] * n,
        flops=2 * 10**9,
        limit=SMALL,
    )
    x_other = send(x_send, 1)
    out_own, out_send = call(
        functools.partial(scenario_forward_kernel, shared, span),
        [struct((slots, width), bf16)] * 2,
        [scal, x_own, x_other, widen, narrow],
        [SCALARS] + [None] * 4,
        [pltpu.VMEM((2 * slots, slot_width), bf16)],
        flops=3 * 10**9,
        limit=SMALL,
    )
    out_other = send(out_send, 1)
    mixing = [sel_own, sel_other, out_own, out_other]
    home_rows = far * rows
    *away, w1, w2 = call(
        functools.partial(shared_forward_kernel, home_rows, lanes, True),
        [struct((m, rows, width), bf16)] * (n - n // near)
        + [struct((width, hidden_chip), bf16), struct((hidden_chip, width), bf16)],
        [scal, xp, gate_columns, w1a, w1b, w2a, w2b, *mixing],
        [SCALARS] + [None] * 10,
        [pltpu.VMEM((all_rows - home_rows, hidden_chip), bf16)],
        flops=3 * 10**9,
        limit=SMALL,
    )
    home = call(
        functools.partial(shared_forward_kernel, 0, lanes, False),
        [struct((m, rows, width), bf16)] * (n // near),
        [scal, xp, gate_columns, w1, w1, w2, w2, *mixing],
        [SCALARS] + [None] * 10,
        [pltpu.VMEM((home_rows, hidden_chip), bf16)],
        flops=3 * 10**9,
        limit=SMALL,
    )
    layer_parts = scatter(home, away)
    active, gated_turned, slope = call(
        functools.partial(shared_slope_kernel, lanes),
        [
            struct((all_rows, hidden_chip), bf16),
            struct((hidden_chip, all_rows), bf16),
            struct((all_rows, hidden_chip), bf16),
        ],
        [xp, gate_columns, w1],
        flops=6 * 10**9,
        limit=BIG,
    )
    scen_active, scen_gated, scen_slope, x_turned = call(
        functools.partial(scenario_slope_kernel, shared, span),
        [
            struct((2 * slots, slot_width), bf16),
            struct((slot_width, 2 * slots), bf16),
            struct((2 * slots, slot_width), bf16),
            struct((width, 2 * slots), bf16),
        ],
        [scal, x_own, x_other, widen],
        [SCALARS] + [None] * 3,
        flops=4 * 10**9,
        limit=BIG,
    )
    logit_grad, head_part = call(
        functools.partial(head_kernel, len(layer_parts)),
        [struct((rows, classes), bf16), struct((width, classes), f32)],
        [*layer_parts, head, mentor],
        flops=10**9,
        limit=8,
    )
    logits = gather(logit_grad)
    head_total = total_of(head_part)

    l_own, l_send = call(
        functools.partial(compact_kernel, n),
        [struct((slots, classes), bf16)] * 2,
        [sel_own, sel_other, *logits],
        flops=10**9,
        limit=SMALL,
    )
    l_other = send(l_send, 1)
    dx, mix, dw1_keep, dw1_send, os, _ = call(
        functools.partial(shared_backward_kernel, n, lanes, depth),
        [
            struct((all_rows, width), bf16),
            struct((all_rows, AUX), f32),
            struct((width // 2, hidden_chip), f32),
            struct((width // 2, hidden_chip), bf16),
            struct((all_rows, width), bf16),
            struct((all_rows, hidden_chip), bf16),
        ],
        [scal, *logits, head, xpt, active, slope, w1, w2],
        [SCALARS] + [None] * (n + 6),
        flops=5 * 10**9,
        limit=BIG,
    )
    dw1 = (dw1_keep + send(dw1_send, 1).astype(f32)).astype(bf16)
    dw1 = lax.all_to_all(
        dw1.reshape(chips, depth, hidden_chip),
        AXIS, split_axis=0, concat_axis=0, tiled=True, axis_index_groups=groups,
    )
    if tiled:
        (expand_grad,) = call(
            expand_grad_kernel, [struct((shared, depth, hidden), f32)], [dw1], limit=8
        )
    else:
        expand_grad = dw1.reshape(chips, depth, shared, lanes).transpose(2, 1, 0, 3)
        expand_grad = expand_grad.reshape(shared, depth, hidden).astype(f32)

    dx_own, dx_send, scen_os, scen_grad = call(
        functools.partial(scenario_backward_kernel, shared, span),
        [struct((slots, width + 128), bf16)] * 2
        + [struct((2 * slots, width), bf16), struct((2 * slots, slot_width), bf16)],
        [scal, l_own, l_other, head, widen, narrow, scen_active, scen_slope],
        [SCALARS] + [None] * 7,
        [pltpu.VMEM((2 * slots, 128), f32)],
        flops=2 * 10**9,
        limit=BIG,
    )
    dx_other = send(dx_send, 1)
    *grad_parts, gate_part = call(
        functools.partial(scatter_kernel, n, gates),
        [struct((m, pack_rows, width), bf16)] * n + [struct((scenarios * AUX, width), f32)],
        [*got, sel_own, sel_other, gate_columns, dx, mix, dx_own, dx_other],
        None,
        [pltpu.VMEM((scenarios * AUX, rows), bf16)],
        flops=2 * 10**9,
        limit=SMALL,
    )
    grad_parts = scatter(grad_parts[: n // near], grad_parts[n // near :])
    gate_part = gate_part.reshape(scenarios, AUX, width)[:, :gates]
    gate_total = jnp.transpose(total_of(gate_part), (0, 2, 1))
    dw2_keep, dw2_send = call(
        functools.partial(reduce_grad_kernel, lanes),
        [struct((shared, lanes // 2, width), f32), struct((shared, lanes // 2, width), bf16)],
        [scal, gated_turned, os],
        [SCALARS] + [None] * 2,
        flops=2 * 10**9,
        limit=BIG,
    )
    reduce_grad = dw2_keep + send(dw2_send, 1).astype(f32)
    widen_grad, narrow_grad = call(
        scenario_weight_kernel,
        [struct((width, slot_width), f32), struct((slot_width, width), f32)],
        [x_turned, scen_grad, scen_gated, scen_os],
        flops=3 * 10**9,
        limit=BIG,
    )
    (feature_grad,) = call(
        functools.partial(final_kernel, len(grad_parts), gates),
        [struct((rows, width), bf16)],
        [*grad_parts, features, sid, probs, gate_rows],
        None,
        [pltpu.VMEM((scenarios * AUX, rows), bf16)],
        flops=10**9,
        limit=8,
    )
    return (
        feature_grad,
        expand_grad,
        reduce_grad,
        widen_grad[None],
        narrow_grad[None],
        gate_total,
        head_total,
    )


def solution(mesh):
    placed = (
        P(("groups", "expert"), None),
        P(("groups", "expert")),
        P("groups"),
        P(),
        P(("groups", "expert"), None),
        P(),
        P(None, "expert", None),
        P(None, "expert", None),
        P("expert", None, None),
        P("expert", None, None),
        P(),
    )
    return jax.shard_map(
        body,
        mesh=mesh,
        in_specs=placed,
        out_specs=(
            P(("groups", "expert"), None),
            P("groups", "expert", None),
            P("groups", "expert", None),
            P(("groups", "expert"), None, None),
            P(("groups", "expert"), None, None),
            P("groups", None, None),
            P("groups", None),
        ),
        check_vma=False,
    )
```

time: 173 us -> 166 us (0.960)
  waiting for transfers between devices: 51 us -> 25.4 us
  Pallas kernels: 37.2 us -> 52.8 us
  starting transfers between devices: 56.5 us -> 60.8 us
  other arithmetic: 7.67 us -> 4.8 us
    ppermute x44, waiting for transfers between devices: 51 us -> 25.4 us  [send(): return lax.ppermute(value, AXIS, [(i, i ^ mask) for i in range(devices)])]
    pallas_call x10 -> x16, Pallas kernels: 37.2 us -> 52.8 us  [call(): pl.pallas_call(kernel, out_shape=out_shapes, in_specs=specs, out_specs=[p...]
    unnamed x37 -> x96, local copies, waits for them, and re-layouts: 7.88 us -> 14.7 us
    ppermute x44, starting transfers between devices: 45.2 us -> 50 us  [send(): return lax.ppermute(value, AXIS, [(i, i ^ mask) for i in range(devices)])]
    convert_element_type x4 -> x0, local copies, waits for them, and re-layouts: 3.9 us -> none  [the longest x1 2.09 us: body(): sent = lax.dynamic_index_in_dim(dw2, 1 - core, 1, False).astype(bf16)]
    another operation x5 -> x1, other arithmetic: 2.82 us -> 0.08 us  [body(): jnp.stack([own_slot // group, other_slot // group, first_expert, core])]
  transfers between devices with their start and end apart: 46 -> 46, of which waited for: 21 -> 13; matrix products, arithmetic and copies ran while one was open for 7% -> 3% of each run, Pallas kernels for 17% -> 27%
where the time goes in v2:
time: 166 us
  starting transfers between devices  60.8 us (37%)
  Pallas kernels  52.8 us (32%)
  waiting for transfers between devices  25.4 us (15%)
  local copies, waits for them, and re-layouts  15.3 us (9%)
  between operations  6.47 us (4%)
  other arithmetic  4.8 us (3%)
    pallas_call x16, Pallas kernels, call(): pl.pallas_call(kernel, out_shape=out_shapes, in_specs=specs, out_specs=[p...  52.8 us
    ppermute x44, starting transfers between devices, send(): return lax.ppermute(value, AXIS, [(i, i ^ mask) for i in range(devices)])  50 us
    ppermute x44, waiting for transfers between devices, send(): return lax.ppermute(value, AXIS, [(i, i ^ mask) for i in range(devices)])  25.4 us
    unnamed x96, local copies, waits for them, and re-layouts  14.7 us
    all_to_all x1, starting transfers between devices, body(): lax.all_to_all(pieces, AXIS, split_axis=0, concat_axis=0, tiled=True, axi...  7.28 us
    all_to_all x1, starting transfers between devices, body(): lax.all_to_all(dw1.reshape(chips, depth, hidden_chip), AXIS, split_axis=0...  3.49 us
  transfers between devices with their start and end apart: 46, of which 13 were waited for; matrix products, arithmetic and copies ran while one was open for 3% of the time, Pallas kernels for 27%

profile of v2, /device:TPU:0, one launch (start us, length us, event | category | flops | bytes accessed | tf_op | source)
XLA Modules:
  0.0 165.5 jit_solution(7818011899926395786)
XLA Ops:
  0.6 0.9 copy.21
  1.6 1.0 copy-done.3
  2.6 0.8 copy-done.24
  4.8 1.6 shard_map.162
  6.4 7.3 %all-to-all-start = ((bf16[8,16,2048]{2,1,0:T(8,128)(2,1)}), bf16[8,16,2048]{2,1,0:T(8,128)(2,1)S(1)}, u32[]{:S(2)}, u32[]{:S(2)}) async-start(bf16[8,16,2048]{2,1,0:T(8,128)(2,1)} %get-tuple-element.67), calls=%async_computation | async-start | bytes 1048576 | tf_op jit(solution)/shard_map/all_to_all | solution.py:578
  13.6 2.0 %collective-permute-start = (bf16[144,256]{1,0:T(8,128)(2,1)S(1)}, bf16[144,256]{1,0:T(8,128)(2,1)S(1)}, u32[]{:S(2)}, u32[]{:S(2)}) collective-permute-start(bf16[144,256]{1,0:T(8,128)(2,1)S(1)} %get-tuple-element.62), channel_id=1, source_target_pairs={{0,4},{1,5},{2,6},{3,7},{4,0},{5,1},{6,2},{7,3},{8,12},{9,13},{10,... | collective-permute-start | bytes 221192 | tf_op jit(solution)/shard_map/ppermute | solution.py:512
  15.7 2.4 %collective-permute-start.1 = (bf16[144,256]{1,0:T(8,128)(2,1)S(1)}, bf16[144,256]{1,0:T(8,128)(2,1)S(1)}, u32[]{:S(2)}, u32[]{:S(2)}) collective-permute-start(bf16[144,256]{1,0:T(8,128)(2,1)S(1)} %get-tuple-element.62), channel_id=1, source_target_pairs={{0,8},{1,9},{2,10},{3,11},{4,12},{5,13},{6,14},{7,15},{8,0},{9,1},... | collective-permute-start | bytes 221192 | tf_op jit(solution)/shard_map/ppermute | solution.py:512
  18.1 2.0 %collective-permute-start.3 = (bf16[144,256]{1,0:T(8,128)(2,1)S(1)}, bf16[144,256]{1,0:T(8,128)(2,1)S(1)}, u32[]{:S(2)}, u32[]{:S(2)}) collective-permute-start(bf16[144,256]{1,0:T(8,128)(2,1)S(1)} %get-tuple-element.62), channel_id=1, source_target_pairs={{0,2},{1,3},{2,0},{3,1},{4,6},{5,7},{6,4},{7,5},{8,10},{9,11},{10,... | collective-permute-start | bytes 221192 | tf_op jit(solution)/shard_map/ppermute | solution.py:512
  25.9 1.2 collective-permute-start.4
  27.1 6.6 %collective-permute-done.1 = bf16[144,256]{1,0:T(8,128)(2,1)S(1)} collective-permute-done((bf16[144,256]{1,0:T(8,128)(2,1)S(1)}, bf16[144,256]{1,0:T(8,128)(2,1)S(1)}, u32[]{:S(2)}, u32[]{:S(2)}) %collective-permute-start.1) | collective-permute-done | bytes 73760 | tf_op jit(solution)/shard_map/ppermute | solution.py:512
  33.7 1.5 collective-permute-start.5
  38.0 2.1 %collective-permute-done.6 = bf16[144,256]{1,0:T(8,128)(2,1)S(1)} collective-permute-done((bf16[144,256]{1,0:T(8,128)(2,1)S(1)}, bf16[144,256]{1,0:T(8,128)(2,1)S(1)}, u32[]{:S(2)}, u32[]{:S(2)}) %collective-permute-start.6) | collective-permute-done | bytes 73760 | tf_op jit(solution)/shard_map/ppermute | solution.py:512
  40.1 0.9 copy-done.8
  41.0 0.9 copy-done.11
  41.9 0.9 copy-done.14
  42.8 2.4 %shard_map.163 = (bf16[1024,256]{1,0:T(8,128)(2,1)S(1)}, bf16[256,1024]{1,0:T(8,128)(2,1)S(1)}, bf16[1024,32]{1,0:T(8,128)(2,1)S(1)}, bf16[256,128]{1,0:T(8,128)...) custom-call(s32[4]{0:T(128)S(1)} %pad_add_fusion.scal.core, ...), custom_call_target="tpu_custom_call" | custom-call | flops 2000000000 | tf_op jit(solution)/shard_map/pallas_call | solution.py:28
  45.3 0.8 copy-done.33
  46.1 0.8 copy-done.35
  46.8 0.7 copy-done.37
  50.1 1.4 collective-permute-done.9.other
  51.5 0.9 copy-done.44
  52.4 4.1 %shard_map.164 = (bf16[256,256]{1,0:T(8,128)(2,1)S(1)}, bf16[256,256]{1,0:T(8,128)(2,1)S(1)}) custom-call(s32[4]{0:T(128)S(1)} %pad_add_fusion.scal.core, bf16[256,384]{1,0:T(8,128)(2,1)S(1)} %copy-done.44, bf16[256,384]{1,0:T(8,128)(2,1)} %collective-permute-done.9.other, bf16[256,2048]{1,0:T(8,128)(2,1)S(1)} %bitcast.71, bf16[2048,256]{1,0:T(8,128)(2,1)S(1)} %bitcast.74), custom_call_target="tpu_custom_call" | custom-call | flops 3000000000 | tf_op jit(solution)/shard_map/pallas_call | solution.py:28
  56.7 1.2 collective-permute-done.10.refs_3_
  57.9 4.3 %shard_map.165 = (bf16[1,128,256]{2,1,0:T(8,128)(2,1)S(1)}, bf16[1,128,256]{2,1,0:T(8,128)(2,1)S(1)}, bf16[1,128,256]{2,1,0:T(8,128)(2,1)S(1)}, bf16[1,128,256]{...) custom-call(s32[4]{0:T(128)S(1)} %pad_add_fusion.scal.core, ...), custom_call_target="tpu_custom_call" | custom-call | flops 3000000000 | tf_op jit(solution)/shard_map/pallas_call | solution.py:28
  62.9 1.5 collective-permute-start.12
  65.0 1.5 collective-permute-start.16
  66.4 3.7 %shard_map.166 = (bf16[1,128,256]{2,1,0:T(8,128)(2,1)S(1)}, bf16[1,128,256]{2,1,0:T(8,128)(2,1)S(1)}, bf16[1,128,256]{2,1,0:T(8,128)(2,1)S(1)}, bf16[1,128,256]{2,1,0:T(8,128)(2,1)S(1)}) custom-call(s32[4]{0:T(128)S(1)} %pad_add_fusion.scal.core, bf16[1024,256]{1,0:T(8,128)(2,1)S(1)} %copy-done.34, bf16[1024,32]{1,0:T(8,128)(2,1)S(1)} %copy-done.38, ...), custom_call_target="tpu_custom_call" | custom-call | flops 3000000000 | tf_op jit(solution)/shard_map/pallas_call | solution.py:28
  70.3 1.4 collective-permute-start.15
  71.7 3.1 %collective-permute-start.17 = (bf16[128,256]{1,0:T(8,128)(2,1)S(1)}, bf16[128,256]{1,0:T(8,128)(2,1)S(1)}, u32[]{:S(2)}, u32[]{:S(2)}) collective-permute-start(bf16[128,256]{1,0:T(8,128)(2,1)S(1)} %fusion.3), channel_id=1, source_target_pairs={{0,12},{1,13},{2,14},{3,15},{4,8},{5,9},{6,10},{7,11},{8,4},{9,5},... | collective-permute-start | bytes 196616 | tf_op jit(solution)/shard_map/ppermute | solution.py:512
  74.8 2.2 %collective-permute-done.15.refs_2_ = bf16[128,256]{1,0:T(8,128)(2,1)S(1)} collective-permute-done((bf16[128,256]{1,0:T(8,128)(2,1)S(1)}, bf16[128,256]{1,0:T(8,128)(2,1)S(1)}, u32[]{:S(2)}, u32[]{:S(2)}) %collective-permute-start.15) | collective-permute-done | bytes 65568 | tf_op jit(solution)/shard_map/ppermute | solution.py:512
  77.1 0.8 collective-permute-done.17.refs_3_
  78.4 1.2 collective-permute-start.18
  79.6 2.4 %collective-permute-start.19 = (bf16[128,128]{1,0:T(8,128)(2,1)S(1)}, bf16[128,128]{1,0:T(8,128)(2,1)S(1)}, u32[]{:S(2)}, u32[]{:S(2)}) collective-permute-start(bf16[128,128]{1,0:T(8,128)(2,1)S(1)} %get-tuple-element.82), channel_id=1, source_target_pairs={{0,8},{1,9},{2,10},{3,11},{4,12},{5,13},{6,14},{7,15},{8,0},{9,1},... | collective-permute-start | bytes 98312 | tf_op jit(solution)/shard_map/ppermute | solution.py:512
  82.0 0.8 collective-permute-start.20
  82.8 4.9 %shard_map.171 = (bf16[512,2048]{1,0:T(8,128)(2,1)S(1)}, bf16[2048,512]{1,0:T(8,128)(2,1)S(1)}, bf16[512,2048]{1,0:T(8,128)(2,1)S(1)}, bf16[256,512]{1,0:T(8,128)(2,1)S(1)}) custom-call(s32[4]{0:T(128)S(1)} %pad_add_fusion.scal.core, bf16[256,384]{1,0:T(8,128)(2,1)S(1)} %copy-done.45, bf16[256,384]{1,0:T(8,128)(2,1)} %collective-permute-done.9.other, ...), custom_call_target="tpu_custom_call" | custom-call | flops 4000000000 | tf_op jit(solution)/shard_map/pallas_call | solution.py:28
  87.7 1.0 collective-permute-start.21
  88.7 1.1 collective-permute-start.22
  89.8 0.9 collective-permute-start.23
  90.8 1.1 collective-permute-start.24
  91.8 5.4 %shard_map.168 = (bf16[1024,2048]{1,0:T(8,128)(2,1)S(1)}, bf16[2048,1024]{1,0:T(8,128)(2,1)S(1)}, bf16[1024,2048]{1,0:T(8,128)(2,1)S(1)}) custom-call(bf16[1024,256]{1,0:T(8,128)(2,1)S(1)} %copy-done.34, bf16[1024,32]{1,0:T(8,128)(2,1)S(1)} %copy-done.38, bf16[256,2048]{1,0:T(8,128)(2,1)S(1)} %get-tuple-element.72.w1a.w1b.w1.refs_12_), custom_call_target="tpu_custom_call" | custom-call | flops 6000000000 | tf_op jit(solution)/shard_map/pallas_call | solution.py:28
  98.9 8.8 %shard_map.169 = (bf16[1024,256]{1,0:T(8,128)(2,1)S(1)}, f32[1024,32]{1,0:T(8,128)S(1)}, f32[128,2048]{1,0:T(8,128)S(1)}, bf16[128,2048]{1,0:T(8,128)(2,1)S(1)},...) custom-call(s32[4]{0:T(128)S(1)} %pad_add_fusion.scal.core, bf16[1,128,128]{2,1,0:T(8,128)(2,1)S(1)} %bitcast.101, ...), custom_call_target="tpu_custom_call" | custom-call | flops 5000000000 | tf_op jit(solution)/shard_map/pallas_call | solution.py:28
  107.7 3.0 %shard_map.176 = (f32[16,64,256]{2,1,0:T(8,128)S(1)}, bf16[16,64,256]{2,1,0:T(8,128)(2,1)S(1)}) custom-call(s32[4]{0:T(128)S(1)} %pad_add_fusion.scal.core, bf16[2048,1024]{1,0:T(8,128)(2,1)S(1)} %get-tuple-element.105.gated_turned, bf16[1024,256]{1,0:T(8,128)(2,1)S(1)} %get-tuple-element.106.os), custom_call_target="tpu_custom_call" | custom-call | flops 2000000000 | tf_op jit(solution)/shard_map/pallas_call | solution.py:28
  111.3 1.0 collective-permute-start.41
  112.3 5.0 %shard_map.172 = (bf16[256,384]{1,0:T(8,128)(2,1)S(1)}, bf16[256,384]{1,0:T(8,128)(2,1)S(1)}, bf16[512,256]{1,0:T(8,128)(2,1)S(1)}, bf16[512,2048]{1,0:T(8,128)(2,1)S(1)}) custom-call(s32[4]{0:T(128)S(1)} %pad_add_fusion.scal.core, bf16[256,128]{1,0:T(8,128)(2,1)S(1)} %get-tuple-element.88.logit_own, ...), custom_call_target="tpu_custom_call" | custom-call | flops 2000000000 | tf_op jit(solution)/shard_map/pallas_call | solution.py:28
  117.6 4.5 %shard_map.177 = (f32[256,2048]{1,0:T(8,128)}, f32[2048,256]{1,0:T(8,128)}) custom-call(bf16[256,512]{1,0:T(8,128)(2,1)S(1)} %get-tuple-element.109.turned, bf16[512,2048]{1,0:T(8,128)(2,1)S(1)} %get-tuple-element.110.linear_grad, bf16[2048,512]{1,0:T(8,128)(2,1)S(1)} %get-tuple-element.111.gated_turned, bf16[512,256]{1,0:T(8,128)(2,1)S(1)} %get-tuple-element.112.os), custom_call_target="tpu_custom_call" | custom-call | flops 3000000000 | tf_op jit(solution)/shard_map/pallas_call | solution.py:28
  122.1 3.4 %collective-permute-start.43 = (bf16[256,128]{1,0:T(8,128)(2,1)S(1)}, bf16[256,128]{1,0:T(8,128)(2,1)S(1)}, u32[]{:S(2)}, u32[]{:S(2)}) collective-permute-start(bf16[256,128]{1,0:T(8,128)(2,1)S(1)} %add_convert_fusion.4), channel_id=1, source_target_pairs={{0,8},{1,9},{2,10},{3,11},{4,12},{5,13},{6,14},{7,15},{8,0},{9,1},... | collective-permute-start | bytes 196616 | tf_op jit(solution)/shard_map/ppermute | solution.py:512
  125.5 2.5 %shard_map.173 = (bf16[1,144,256]{2,1,0:T(8,128)(2,1)S(1)}, bf16[1,144,256]{2,1,0:T(8,128)(2,1)S(1)}, bf16[1,144,256]{2,1,0:T(8,128)(2,1)S(1)}, bf16[1,144,256]{...) custom-call(bf16[1,144,256]{2,1,0:T(8,128)(2,1)S(1)} %bitcast.77, ...), custom_call_target="tpu_custom_call" | custom-call | flops 2000000000 | tf_op jit(solution)/shard_map/pallas_call | solution.py:28
  128.1 1.4 collective-permute-start.27
  129.4 0.7 collective-permute-start.28
  130.2 1.3 collective-permute-start.30
  132.2 1.1 collective-permute-done.27
  133.3 1.3 collective-permute-start.32
  134.9 1.5 collective-permute-done.30
  136.4 1.2 collective-permute-done.32
  137.9 3.1 %collective-permute-start.33 = (bf16[144,256]{1,0:T(8,128)(2,1)S(1)}, bf16[144,256]{1,0:T(8,128)(2,1)S(1)}, u32[]{:S(2)}, u32[]{:S(2)}) collective-permute-start(bf16[144,256]{1,0:T(8,128)(2,1)S(1)} %fusion), channel_id=1, source_target_pairs={{0,12},{1,13},{2,14},{3,15},{4,8},{5,9},{6,10},{7,11},{8,4},{9,5},... | collective-permute-start | bytes 221192 | tf_op jit(solution)/shard_map/ppermute | solution.py:512
  141.1 1.1 collective-permute-start.37
  142.2 0.9 add_convert_fusion
  143.1 3.5 %all-to-all-start.1 = ((bf16[8,16,2048]{2,1,0:T(8,128)(2,1)}), bf16[8,16,2048]{2,1,0:T(8,128)(2,1)S(1)}, u32[]{:S(2)}, u32[]{:S(2)}) async-start(bf16[8,16,2048]{2,1,0:T(8,128)(2,1)} %bitcast.44), calls=%async_computation.1 | async-start | bytes 1048576 | tf_op jit(solution)/shard_map/all_to_all | solution.py:691
  146.6 2.0 %collective-permute-start.38 = (bf16[8,20,256]{2,0,1:T(8,128)(2,1)S(1)}, bf16[8,20,256]{2,0,1:T(8,128)(2,1)S(1)}, u32[]{:S(2)}, u32[]{:S(2)}) collective-permute-start(bf16[8,20,256]{2,0,1:T(8,128)(2,1)S(1)} %add_convert_fusion.2), channel_id=1, source_target_pairs={{0,4},{1,5},{2,6},{3,7},{4,0},{5,1},{6,2},{7,3},{8,12},{9,13},{10,... | collective-permute-start | bytes 245768 | tf_op jit(solution)/shard_map/ppermute | solution.py:512
  148.7 0.9 shard_map.174
  149.5 6.1 %collective-permute-done.38 = bf16[8,20,256]{2,0,1:T(8,128)(2,1)S(1)} collective-permute-done((bf16[8,20,256]{2,0,1:T(8,128)(2,1)S(1)}, bf16[8,20,256]{2,0,1:T(8,128)(2,1)S(1)}, u32[]{:S(2)}, u32[]{:S(2)}) %collective-permute-start.38) | collective-permute-done | bytes 81952 | tf_op jit(solution)/shard_map/ppermute | solution.py:512
  155.6 5.5 %collective-permute-start.39 = (bf16[8,20,256]{2,0,1:T(8,128)(2,1)S(1)}, bf16[8,20,256]{2,0,1:T(8,128)(2,1)S(1)}, u32[]{:S(2)}, u32[]{:S(2)}) collective-permute-start(bf16[8,20,256]{2,0,1:T(8,128)(2,1)S(1)} %add_convert_fusion.1), channel_id=1, source_target_pairs={{0,8},{1,9},{2,10},{3,11},{4,12},{5,13},{6,14},{7,15},{8,0},{9,1},... | collective-permute-start | bytes 245768 | tf_op jit(solution)/shard_map/ppermute | solution.py:512
  161.1 2.1 %convert_add_fusion = f32[16,64,256]{2,1,0:T(8,128)} fusion(f32[16,64,256]{2,1,0:T(8,128)S(1)} %get-tuple-element.107, bf16[16,64,256]{2,1,0:T(8,128)(2,1)} %collective-permute-done.35), kind=kLoop, calls=%fused_computation | loop fusion | flops 524288 | bytes 2621440 | tf_op jit(solution)/shard_map/add | solution.py:734
  164.5 1.0 shard_map.175
  (162 shorter events, 14.6 us)
Async XLA Ops:
  4.8 15.3 %copy-start.46 = (s32[16]{0:T(128)S(1)}, s32[16]{0:T(128)}, u32[]{:S(2)}) copy-start(s32[16]{0:T(128)} %param.14) | copy-start | bytes 196
  6.4 43.6 %all-to-all-start = ((bf16[8,16,2048]{2,1,0:T(8,128)(2,1)}), bf16[8,16,2048]{2,1,0:T(8,128)(2,1)S(1)}, u32[]{:S(2)}, u32[]{:S(2)}) async-start(bf16[8,16,2048]{2,1,0:T(8,128)(2,1)} %get-tuple-element.67), calls=%async_computation | async-start | bytes 1048576 | tf_op jit(solution)/shard_map/all_to_all | solution.py:578
  13.6 12.2 %collective-permute-start = (bf16[144,256]{1,0:T(8,128)(2,1)S(1)}, bf16[144,256]{1,0:T(8,128)(2,1)S(1)}, u32[]{:S(2)}, u32[]{:S(2)}) collective-permute-start(bf16[144,256]{1,0:T(8,128)(2,1)S(1)} %get-tuple-element.62), channel_id=1, source_target_pairs={{0,4},{1,5},{2,6},{3,7},{4,0},{5,1},{6,2},{7,3},{8,12},{9,13},{10,... | collective-permute-start | bytes 221192 | tf_op jit(solution)/shard_map/ppermute | solution.py:512
  15.7 18.0 %collective-permute-start.1 = (bf16[144,256]{1,0:T(8,128)(2,1)S(1)}, bf16[144,256]{1,0:T(8,128)(2,1)S(1)}, u32[]{:S(2)}, u32[]{:S(2)}) collective-permute-start(bf16[144,256]{1,0:T(8,128)(2,1)S(1)} %get-tuple-element.62), channel_id=1, source_target_pairs={{0,8},{1,9},{2,10},{3,11},{4,12},{5,13},{6,14},{7,15},{8,0},{9,1},... | collective-permute-start | bytes 221192 | tf_op jit(solution)/shard_map/ppermute | solution.py:512
  18.0 17.7 %collective-permute-start.2 = (bf16[144,256]{1,0:T(8,128)(2,1)S(1)}, bf16[144,256]{1,0:T(8,128)(2,1)S(1)}, u32[]{:S(2)}, u32[]{:S(2)}) collective-permute-start(bf16[144,256]{1,0:T(8,128)(2,1)S(1)} %get-tuple-element.62), channel_id=1, source_target_pairs={{0,12},{1,13},{2,14},{3,15},{4,8},{5,9},{6,10},{7,11},{8,4},{9,5},... | collective-permute-start | bytes 221192 | tf_op jit(solution)/shard_map/ppermute | solution.py:512
  18.1 19.0 %collective-permute-start.3 = (bf16[144,256]{1,0:T(8,128)(2,1)S(1)}, bf16[144,256]{1,0:T(8,128)(2,1)S(1)}, u32[]{:S(2)}, u32[]{:S(2)}) collective-permute-start(bf16[144,256]{1,0:T(8,128)(2,1)S(1)} %get-tuple-element.62), channel_id=1, source_target_pairs={{0,2},{1,3},{2,0},{3,1},{4,6},{5,7},{6,4},{7,5},{8,10},{9,11},{10,... | collective-permute-start | bytes 221192 | tf_op jit(solution)/shard_map/ppermute | solution.py:512
  25.9 19.3 %copy-start.5 = (bf16[144,256]{1,0:T(8,128)(2,1)}, bf16[144,256]{1,0:T(8,128)(2,1)S(1)}, u32[]{:S(2)}) copy-start(bf16[144,256]{1,0:T(8,128)(2,1)S(1)} %collective-permute-done) | copy-start | bytes 221188
  25.9 11.8 %collective-permute-start.4 = (bf16[144,256]{1,0:T(8,128)(2,1)S(1)}, bf16[144,256]{1,0:T(8,128)(2,1)S(1)}, u32[]{:S(2)}, u32[]{:S(2)}) collective-permute-start(bf16[144,256]{1,0:T(8,128)(2,1)S(1)} %collective-permute-done), channel_id=1, source_target_pairs={{0,2},{1,3},{2,0},{3,1},{4,6},{5,7},{6,4},{7,5},{8,10},{9,11},{10,... | collective-permute-start | bytes 221192 | tf_op jit(solution)/shard_map/ppermute | solution.py:512
  33.7 4.4 %collective-permute-start.5 = (bf16[144,256]{1,0:T(8,128)(2,1)S(1)}, bf16[144,256]{1,0:T(8,128)(2,1)S(1)}, u32[]{:S(2)}, u32[]{:S(2)}) collective-permute-start(bf16[144,256]{1,0:T(8,128)(2,1)S(1)} %collective-permute-done.1), channel_id=1, source_target_pairs={{0,2},{1,3},{2,0},{3,1},{4,6},{5,7},{6,4},{7,5},{8,10},{9,11},{10,... | collective-permute-start | bytes 221192 | tf_op jit(solution)/shard_map/ppermute | solution.py:512
  35.8 4.4 %collective-permute-start.6 = (bf16[144,256]{1,0:T(8,128)(2,1)S(1)}, bf16[144,256]{1,0:T(8,128)(2,1)S(1)}, u32[]{:S(2)}, u32[]{:S(2)}) collective-permute-start(bf16[144,256]{1,0:T(8,128)(2,1)S(1)} %collective-permute-done.2), channel_id=1, source_target_pairs={{0,2},{1,3},{2,0},{3,1},{4,6},{5,7},{6,4},{7,5},{8,10},{9,11},{10,... | collective-permute-start | bytes 221192 | tf_op jit(solution)/shard_map/ppermute | solution.py:512
  42.8 8.7 %copy-start = (bf16[1,256,2048]{2,1,0:T(8,128)(2,1)S(1)}, bf16[1,256,2048]{2,1,0:T(8,128)(2,1)}, u32[]{:S(2)}) copy-start(bf16[1,256,2048]{2,1,0:T(8,128)(2,1)} %param.19) | copy-start | bytes 3145732
  42.8 8.7 %copy-start.1 = (bf16[1,2048,256]{2,1,0:T(8,128)(2,1)S(1)}, bf16[1,2048,256]{2,1,0:T(8,128)(2,1)}, u32[]{:S(2)}) copy-start(bf16[1,2048,256]{2,1,0:T(8,128)(2,1)} %param.20) | copy-start | bytes 3145732
  49.5 2.0 %collective-permute-start.9 = (bf16[256,384]{1,0:T(8,128)(2,1)}, bf16[256,384]{1,0:T(8,128)(2,1)}, u32[]{:S(2)}, u32[]{:S(2)}) collective-permute-start(bf16[256,384]{1,0:T(8,128)(2,1)} %get-tuple-element.69), channel_id=1, source_target_pairs={{0,1},{1,0},{2,3},{3,2},{4,5},{5,4},{6,7},{7,6},{8,9},{9,8},{10,11... | collective-permute-start | bytes 589832 | tf_op jit(solution)/shard_map/ppermute | solution.py:512
  49.5 8.4 %collective-permute-start.8 = (bf16[16,64,256]{2,1,0:T(8,128)(2,1)S(1)}, bf16[16,64,256]{2,1,0:T(8,128)(2,1)}, u32[]{:S(2)}, u32[]{:S(2)}) collective-permute-start(bf16[16,64,256]{2,1,0:T(8,128)(2,1)S(1)} %copy-done.4), channel_id=1, source_target_pairs={{0,1},{1,0},{2,3},{3,2},{4,5},{5,4},{6,7},{7,6},{8,9},{9,8},{10,11... | collective-permute-start | bytes 1572872 | tf_op jit(solution)/shard_map/ppermute | solution.py:512
  50.0 7.9 %collective-permute-start.7 = (bf16[128,2048]{1,0:T(8,128)(2,1)S(1)}, bf16[128,2048]{1,0:T(8,128)(2,1)S(1)}, u32[]{:S(2)}, u32[]{:S(2)}) collective-permute-start(bf16[128,2048]{1,0:T(8,128)(2,1)S(1)} %bitcast.66), channel_id=1, source_target_pairs={{0,1},{1,0},{2,3},{3,2},{4,5},{5,4},{6,7},{7,6},{8,9},{9,8},{10,11... | collective-permute-start | bytes 1572872 | tf_op jit(solution)/shard_map/ppermute | solution.py:512
  56.5 1.4 collective-permute-start.10
  62.3 7.8 %copy-start.31 = (bf16[2048,256]{1,0:T(8,128)(2,1)}, bf16[2048,256]{1,0:T(8,128)(2,1)S(1)}, u32[]{:S(2)}) copy-start(bf16[2048,256]{1,0:T(8,128)(2,1)S(1)} %get-tuple-element.73.w2a.w2b.refs_13_) | copy-start | bytes 3145732
  62.3 29.5 %copy-start.29 = (bf16[256,2048]{1,0:T(8,128)(2,1)}, bf16[256,2048]{1,0:T(8,128)(2,1)S(1)}, u32[]{:S(2)}) copy-start(bf16[256,2048]{1,0:T(8,128)(2,1)S(1)} %get-tuple-element.72.w1a.w1b.w1.refs_12_) | copy-start | bytes 3145732
  62.3 12.5 %collective-permute-start.11 = (bf16[128,256]{1,0:T(8,128)(2,1)S(1)}, bf16[128,256]{1,0:T(8,128)(2,1)S(1)}, u32[]{:S(2)}, u32[]{:S(2)}) collective-permute-start(bf16[128,256]{1,0:T(8,128)(2,1)S(1)} %bitcast.96), channel_id=1, source_target_pairs={{0,2},{1,3},{2,0},{3,1},{4,6},{5,7},{6,4},{7,5},{8,10},{9,11},{10,... | collective-permute-start | bytes 196616 | tf_op jit(solution)/shard_map/ppermute | solution.py:512
  62.9 7.2 %collective-permute-start.12 = (bf16[128,256]{1,0:T(8,128)(2,1)S(1)}, bf16[128,256]{1,0:T(8,128)(2,1)S(1)}, u32[]{:S(2)}, u32[]{:S(2)}) collective-permute-start(bf16[128,256]{1,0:T(8,128)(2,1)S(1)} %bitcast.99), channel_id=1, source_target_pairs={{0,2},{1,3},{2,0},{3,1},{4,6},{5,7},{6,4},{7,5},{8,10},{9,11},{10,... | collective-permute-start | bytes 196616 | tf_op jit(solution)/shard_map/ppermute | solution.py:512
  64.4 5.8 %collective-permute-start.14 = (bf16[128,256]{1,0:T(8,128)(2,1)S(1)}, bf16[128,256]{1,0:T(8,128)(2,1)S(1)}, u32[]{:S(2)}, u32[]{:S(2)}) collective-permute-start(bf16[128,256]{1,0:T(8,128)(2,1)S(1)} %bitcast.98), channel_id=1, source_target_pairs={{0,2},{1,3},{2,0},{3,1},{4,6},{5,7},{6,4},{7,5},{8,10},{9,11},{10,... | collective-permute-start | bytes 196616 | tf_op jit(solution)/shard_map/ppermute | solution.py:512
  65.0 6.7 %collective-permute-start.16 = (bf16[128,256]{1,0:T(8,128)(2,1)S(1)}, bf16[128,256]{1,0:T(8,128)(2,1)S(1)}, u32[]{:S(2)}, u32[]{:S(2)}) collective-permute-start(bf16[128,256]{1,0:T(8,128)(2,1)S(1)} %bitcast.97), channel_id=1, source_target_pairs={{0,2},{1,3},{2,0},{3,1},{4,6},{5,7},{6,4},{7,5},{8,10},{9,11},{10,... | collective-permute-start | bytes 196616 | tf_op jit(solution)/shard_map/ppermute | solution.py:512
  66.4 11.5 %copy-start.22 = (f32[128,128]{1,0:T(8,128)S(1)}, f32[128,128]{1,0:T(8,128)}, u32[]{:S(2)}) copy-start(f32[128,128]{1,0:T(8,128)} %refs_5_.1) | copy-start | bytes 196612
  66.4 11.5 %copy-start.23 = (bf16[256,128]{1,0:T(8,128)(2,1)S(1)}, bf16[256,128]{1,0:T(8,128)(2,1)}, u32[]{:S(2)}) copy-start(bf16[256,128]{1,0:T(8,128)(2,1)} %head.1) | copy-start | bytes 196612
  70.2 4.7 %collective-permute-start.13 = (bf16[128,256]{1,0:T(8,128)(2,1)S(1)}, bf16[128,256]{1,0:T(8,128)(2,1)S(1)}, u32[]{:S(2)}, u32[]{:S(2)}) collective-permute-start(bf16[128,256]{1,0:T(8,128)(2,1)S(1)} %fusion.5), channel_id=1, source_target_pairs={{0,4},{1,5},{2,6},{3,7},{4,0},{5,1},{6,2},{7,3},{8,12},{9,13},{10,... | collective-permute-start | bytes 196616 | tf_op jit(solution)/shard_map/ppermute | solution.py:512
  70.3 12.6 %copy-start.45 = (bf16[256,384]{1,0:T(8,128)(2,1)S(1)}, bf16[256,384]{1,0:T(8,128)(2,1)}, u32[]{:S(2)}) copy-start(bf16[256,384]{1,0:T(8,128)(2,1)} %copy-done.43) | copy-start | bytes 589828
  70.3 6.8 %collective-permute-start.15 = (bf16[128,256]{1,0:T(8,128)(2,1)S(1)}, bf16[128,256]{1,0:T(8,128)(2,1)S(1)}, u32[]{:S(2)}, u32[]{:S(2)}) collective-permute-start(bf16[128,256]{1,0:T(8,128)(2,1)S(1)} %fusion.4), channel_id=1, source_target_pairs={{0,8},{1,9},{2,10},{3,11},{4,12},{5,13},{6,14},{7,15},{8,0},{9,1},... | collective-permute-start | bytes 196616 | tf_op jit(solution)/shard_map/ppermute | solution.py:512
  71.7 6.2 %collective-permute-start.17 = (bf16[128,256]{1,0:T(8,128)(2,1)S(1)}, bf16[128,256]{1,0:T(8,128)(2,1)S(1)}, u32[]{:S(2)}, u32[]{:S(2)}) collective-permute-start(bf16[128,256]{1,0:T(8,128)(2,1)S(1)} %fusion.3), channel_id=1, source_target_pairs={{0,12},{1,13},{2,14},{3,15},{4,8},{5,9},{6,10},{7,11},{8,4},{9,5},... | collective-permute-start | bytes 196616 | tf_op jit(solution)/shard_map/ppermute | solution.py:512
  78.4 10.3 %collective-permute-start.18 = (bf16[128,128]{1,0:T(8,128)(2,1)S(1)}, bf16[128,128]{1,0:T(8,128)(2,1)S(1)}, u32[]{:S(2)}, u32[]{:S(2)}) collective-permute-start(bf16[128,128]{1,0:T(8,128)(2,1)S(1)} %get-tuple-element.82), channel_id=1, source_target_pairs={{0,4},{1,5},{2,6},{3,7},{4,0},{5,1},{6,2},{7,3},{8,12},{9,13},{10,... | collective-permute-start | bytes 98312 | tf_op jit(solution)/shard_map/ppermute | solution.py:512
  79.6 10.2 %collective-permute-start.19 = (bf16[128,128]{1,0:T(8,128)(2,1)S(1)}, bf16[128,128]{1,0:T(8,128)(2,1)S(1)}, u32[]{:S(2)}, u32[]{:S(2)}) collective-permute-start(bf16[128,128]{1,0:T(8,128)(2,1)S(1)} %get-tuple-element.82), channel_id=1, source_target_pairs={{0,8},{1,9},{2,10},{3,11},{4,12},{5,13},{6,14},{7,15},{8,0},{9,1},... | collective-permute-start | bytes 98312 | tf_op jit(solution)/shard_map/ppermute | solution.py:512
  82.0 8.7 %collective-permute-start.20 = (bf16[128,128]{1,0:T(8,128)(2,1)S(1)}, bf16[128,128]{1,0:T(8,128)(2,1)S(1)}, u32[]{:S(2)}, u32[]{:S(2)}) collective-permute-start(bf16[128,128]{1,0:T(8,128)(2,1)S(1)} %get-tuple-element.82), channel_id=1, source_target_pairs={{0,12},{1,13},{2,14},{3,15},{4,8},{5,9},{6,10},{7,11},{8,4},{9,5},... | collective-permute-start | bytes 98312 | tf_op jit(solution)/shard_map/ppermute | solution.py:512
  87.7 9.6 %collective-permute-start.21 = (bf16[128,128]{1,0:T(8,128)(2,1)S(1)}, bf16[128,128]{1,0:T(8,128)(2,1)S(1)}, u32[]{:S(2)}, u32[]{:S(2)}) collective-permute-start(bf16[128,128]{1,0:T(8,128)(2,1)S(1)} %get-tuple-element.82), channel_id=1, source_target_pairs={{0,2},{1,3},{2,0},{3,1},{4,6},{5,7},{6,4},{7,5},{8,10},{9,11},{10,... | collective-permute-start | bytes 98312 | tf_op jit(solution)/shard_map/ppermute | solution.py:512
  88.7 8.6 %collective-permute-start.22 = (bf16[128,128]{1,0:T(8,128)(2,1)S(1)}, bf16[128,128]{1,0:T(8,128)(2,1)S(1)}, u32[]{:S(2)}, u32[]{:S(2)}) collective-permute-start(bf16[128,128]{1,0:T(8,128)(2,1)S(1)} %collective-permute-done.18), channel_id=1, source_target_pairs={{0,2},{1,3},{2,0},{3,1},{4,6},{5,7},{6,4},{7,5},{8,10},{9,11},{10,... | collective-permute-start | bytes 98312 | tf_op jit(solution)/shard_map/ppermute | solution.py:512
  89.8 7.6 %collective-permute-start.23 = (bf16[128,128]{1,0:T(8,128)(2,1)S(1)}, bf16[128,128]{1,0:T(8,128)(2,1)S(1)}, u32[]{:S(2)}, u32[]{:S(2)}) collective-permute-start(bf16[128,128]{1,0:T(8,128)(2,1)S(1)} %collective-permute-done.19), channel_id=1, source_target_pairs={{0,2},{1,3},{2,0},{3,1},{4,6},{5,7},{6,4},{7,5},{8,10},{9,11},{10,... | collective-permute-start | bytes 98312 | tf_op jit(solution)/shard_map/ppermute | solution.py:512
  90.8 6.6 %collective-permute-start.24 = (bf16[128,128]{1,0:T(8,128)(2,1)S(1)}, bf16[128,128]{1,0:T(8,128)(2,1)S(1)}, u32[]{:S(2)}, u32[]{:S(2)}) collective-permute-start(bf16[128,128]{1,0:T(8,128)(2,1)S(1)} %collective-permute-done.20), channel_id=1, source_target_pairs={{0,2},{1,3},{2,0},{3,1},{4,6},{5,7},{6,4},{7,5},{8,10},{9,11},{10,... | collective-permute-start | bytes 98312 | tf_op jit(solution)/shard_map/ppermute | solution.py:512
  97.3 14.0 %collective-permute-start.40 = (f32[256,128]{1,0:T(8,128)S(1)}, f32[256,128]{1,0:T(8,128)S(1)}, u32[]{:S(2)}, u32[]{:S(2)}) collective-permute-start(f32[256,128]{1,0:T(8,128)S(1)} %get-tuple-element.116), channel_id=1, source_target_pairs={{0,1},{1,0},{2,3},{3,2},{4,5},{5,4},{6,7},{7,6},{8,9},{9,8},{10,11... | collective-permute-start | bytes 393224 | tf_op jit(solution)/shard_map/ppermute | solution.py:512
  97.6 14.7 %collective-permute-start.25 = (bf16[256,128]{1,0:T(8,128)(2,1)S(1)}, bf16[256,128]{1,0:T(8,128)(2,1)S(1)}, u32[]{:S(2)}, u32[]{:S(2)}) collective-permute-start(bf16[256,128]{1,0:T(8,128)(2,1)S(1)} %get-tuple-element.89), channel_id=1, source_target_pairs={{0,1},{1,0},{2,3},{3,2},{4,5},{5,4},{6,7},{7,6},{8,9},{9,8},{10,11... | collective-permute-start | bytes 196616 | tf_op jit(solution)/shard_map/ppermute | solution.py:512
  107.7 33.4 %collective-permute-start.34 = (bf16[128,2048]{1,0:T(8,128)(2,1)S(1)}, bf16[128,2048]{1,0:T(8,128)(2,1)S(1)}, u32[]{:S(2)}, u32[]{:S(2)}) collective-permute-start(bf16[128,2048]{1,0:T(8,128)(2,1)S(1)} %get-tuple-element.104), channel_id=1, source_target_pairs={{0,1},{1,0},{2,3},{3,2},{4,5},{5,4},{6,7},{7,6},{8,9},{9,8},{10,11... | collective-permute-start | bytes 1572872 | tf_op jit(solution)/shard_map/ppermute | solution.py:512
  110.7 50.4 %collective-permute-start.35 = (bf16[16,64,256]{2,1,0:T(8,128)(2,1)S(1)}, bf16[16,64,256]{2,1,0:T(8,128)(2,1)}, u32[]{:S(2)}, u32[]{:S(2)}) collective-permute-start(bf16[16,64,256]{2,1,0:T(8,128)(2,1)S(1)} %get-tuple-element.108), channel_id=1, source_target_pairs={{0,1},{1,0},{2,3},{3,2},{4,5},{5,4},{6,7},{7,6},{8,9},{9,8},{10,11... | collective-permute-start | bytes 1572872 | tf_op jit(solution)/shard_map/ppermute | solution.py:512
  111.3 6.1 %collective-permute-start.41 = (bf16[256,128]{1,0:T(8,128)(2,1)S(1)}, bf16[256,128]{1,0:T(8,128)(2,1)S(1)}, u32[]{:S(2)}, u32[]{:S(2)}) collective-permute-start(bf16[256,128]{1,0:T(8,128)(2,1)S(1)} %add_convert_fusion.6), channel_id=1, source_target_pairs={{0,2},{1,3},{2,0},{3,1},{4,6},{5,7},{6,4},{7,5},{8,10},{9,11},{10,... | collective-permute-start | bytes 196616 | tf_op jit(solution)/shard_map/ppermute | solution.py:512
  117.3 8.2 %collective-permute-start.26 = (bf16[256,384]{1,0:T(8,128)(2,1)S(1)}, bf16[256,384]{1,0:T(8,128)(2,1)S(1)}, u32[]{:S(2)}, u32[]{:S(2)}) collective-permute-start(bf16[256,384]{1,0:T(8,128)(2,1)S(1)} %get-tuple-element.93), channel_id=1, source_target_pairs={{0,1},{1,0},{2,3},{3,2},{4,5},{5,4},{6,7},{7,6},{8,9},{9,8},{10,11... | collective-permute-start | bytes 589832 | tf_op jit(solution)/shard_map/ppermute | solution.py:512
  117.4 4.6 %collective-permute-start.42 = (bf16[256,128]{1,0:T(8,128)(2,1)S(1)}, bf16[256,128]{1,0:T(8,128)(2,1)S(1)}, u32[]{:S(2)}, u32[]{:S(2)}) collective-permute-start(bf16[256,128]{1,0:T(8,128)(2,1)S(1)} %add_convert_fusion.5), channel_id=1, source_target_pairs={{0,4},{1,5},{2,6},{3,7},{4,0},{5,1},{6,2},{7,3},{8,12},{9,13},{10,... | collective-permute-start | bytes 196616 | tf_op jit(solution)/shard_map/ppermute | solution.py:512
  117.5 8.0 %copy-start.6 = (bf16[144,256]{1,0:T(8,128)(2,1)S(1)}, bf16[144,256]{1,0:T(8,128)(2,1)}, u32[]{:S(2)}) copy-start(bf16[144,256]{1,0:T(8,128)(2,1)} %copy-done.5) | copy-start | bytes 221188
  117.5 8.0 %copy-start.9 = (bf16[144,256]{1,0:T(8,128)(2,1)S(1)}, bf16[144,256]{1,0:T(8,128)(2,1)}, u32[]{:S(2)}) copy-start(bf16[144,256]{1,0:T(8,128)(2,1)} %copy-done.7) | copy-start | bytes 221188
  117.5 8.0 %copy-start.12 = (bf16[144,256]{1,0:T(8,128)(2,1)S(1)}, bf16[144,256]{1,0:T(8,128)(2,1)}, u32[]{:S(2)}) copy-start(bf16[144,256]{1,0:T(8,128)(2,1)} %copy-done.10) | copy-start | bytes 221188
  117.5 8.0 %copy-start.15 = (bf16[144,256]{1,0:T(8,128)(2,1)S(1)}, bf16[144,256]{1,0:T(8,128)(2,1)}, u32[]{:S(2)}) copy-start(bf16[144,256]{1,0:T(8,128)(2,1)} %copy-done.13) | copy-start | bytes 221188
  117.6 8.0 %copy-start.17 = (bf16[144,256]{1,0:T(8,128)(2,1)S(1)}, bf16[144,256]{1,0:T(8,128)(2,1)}, u32[]{:S(2)}) copy-start(bf16[144,256]{1,0:T(8,128)(2,1)} %copy-done.16) | copy-start | bytes 221188
  117.6 8.0 %copy-start.19 = (bf16[144,256]{1,0:T(8,128)(2,1)S(1)}, bf16[144,256]{1,0:T(8,128)(2,1)}, u32[]{:S(2)}) copy-start(bf16[144,256]{1,0:T(8,128)(2,1)} %copy-done.18) | copy-start | bytes 221188
  117.6 8.0 %copy-start.21 = (bf16[144,256]{1,0:T(8,128)(2,1)S(1)}, bf16[144,256]{1,0:T(8,128)(2,1)}, u32[]{:S(2)}) copy-start(bf16[144,256]{1,0:T(8,128)(2,1)} %copy-done.20) | copy-start | bytes 221188
  122.1 8.1 %collective-permute-start.43 = (bf16[256,128]{1,0:T(8,128)(2,1)S(1)}, bf16[256,128]{1,0:T(8,128)(2,1)S(1)}, u32[]{:S(2)}, u32[]{:S(2)}) collective-permute-start(bf16[256,128]{1,0:T(8,128)(2,1)S(1)} %add_convert_fusion.4), channel_id=1, source_target_pairs={{0,8},{1,9},{2,10},{3,11},{4,12},{5,13},{6,14},{7,15},{8,0},{9,1},... | collective-permute-start | bytes 196616 | tf_op jit(solution)/shard_map/ppermute | solution.py:512
  128.1 5.2 %collective-permute-start.27 = (bf16[144,256]{1,0:T(8,128)(2,1)S(1)}, bf16[144,256]{1,0:T(8,128)(2,1)S(1)}, u32[]{:S(2)}, u32[]{:S(2)}) collective-permute-start(bf16[144,256]{1,0:T(8,128)(2,1)S(1)} %bitcast.95), channel_id=1, source_target_pairs={{0,2},{1,3},{2,0},{3,1},{4,6},{5,7},{6,4},{7,5},{8,10},{9,11},{10,... | collective-permute-start | bytes 221192 | tf_op jit(solution)/shard_map/ppermute | solution.py:512
  129.4 5.4 %collective-permute-start.28 = (bf16[144,256]{1,0:T(8,128)(2,1)S(1)}, bf16[144,256]{1,0:T(8,128)(2,1)S(1)}, u32[]{:S(2)}, u32[]{:S(2)}) collective-permute-start(bf16[144,256]{1,0:T(8,128)(2,1)S(1)} %bitcast.94), channel_id=1, source_target_pairs={{0,2},{1,3},{2,0},{3,1},{4,6},{5,7},{6,4},{7,5},{8,10},{9,11},{10,... | collective-permute-start | bytes 221192 | tf_op jit(solution)/shard_map/ppermute | solution.py:512
  130.2 6.2 %collective-permute-start.30 = (bf16[144,256]{1,0:T(8,128)(2,1)S(1)}, bf16[144,256]{1,0:T(8,128)(2,1)S(1)}, u32[]{:S(2)}, u32[]{:S(2)}) collective-permute-start(bf16[144,256]{1,0:T(8,128)(2,1)S(1)} %bitcast.93), channel_id=1, source_target_pairs={{0,2},{1,3},{2,0},{3,1},{4,6},{5,7},{6,4},{7,5},{8,10},{9,11},{10,... | collective-permute-start | bytes 221192 | tf_op jit(solution)/shard_map/ppermute | solution.py:512
  133.3 4.4 %collective-permute-start.32 = (bf16[144,256]{1,0:T(8,128)(2,1)S(1)}, bf16[144,256]{1,0:T(8,128)(2,1)S(1)}, u32[]{:S(2)}, u32[]{:S(2)}) collective-permute-start(bf16[144,256]{1,0:T(8,128)(2,1)S(1)} %bitcast.92), channel_id=1, source_target_pairs={{0,2},{1,3},{2,0},{3,1},{4,6},{5,7},{6,4},{7,5},{8,10},{9,11},{10,... | collective-permute-start | bytes 221192 | tf_op jit(solution)/shard_map/ppermute | solution.py:512
  134.9 3.0 %collective-permute-start.36 = (f32[8,20,256]{2,0,1:T(8,128)S(1)}, f32[8,20,256]{2,0,1:T(8,128)S(1)}, u32[]{:S(2)}, u32[]{:S(2)}) collective-permute-start(f32[8,20,256]{2,0,1:T(8,128)S(1)} %copy.20), channel_id=1, source_target_pairs={{0,1},{1,0},{2,3},{3,2},{4,5},{5,4},{6,7},{7,6},{8,9},{9,8},{10,11... | collective-permute-start | bytes 491528 | tf_op jit(solution)/shard_map/ppermute | solution.py:512
  136.4 12.2 %collective-permute-start.29 = (bf16[144,256]{1,0:T(8,128)(2,1)S(1)}, bf16[144,256]{1,0:T(8,128)(2,1)S(1)}, u32[]{:S(2)}, u32[]{:S(2)}) collective-permute-start(bf16[144,256]{1,0:T(8,128)(2,1)S(1)} %fusion.2), channel_id=1, source_target_pairs={{0,4},{1,5},{2,6},{3,7},{4,0},{5,1},{6,2},{7,3},{8,12},{9,13},{10,... | collective-permute-start | bytes 221192 | tf_op jit(solution)/shard_map/ppermute | solution.py:512
  136.4 12.2 %copy-start.25 = (bf16[128,256]{1,0:T(8,128)(2,1)S(1)}, bf16[128,256]{1,0:T(8,128)(2,1)}, u32[]{:S(2)}) copy-start(bf16[128,256]{1,0:T(8,128)(2,1)} %refs_4_.3) | copy-start | bytes 196612
  136.4 12.2 %copy-start.28 = (s32[128]{0:T(128)S(1)}, s32[128]{0:T(128)}, u32[]{:S(2)}) copy-start(s32[128]{0:T(128)} %param.12) | copy-start | bytes 1540
  137.6 11.0 %collective-permute-start.31 = (bf16[144,256]{1,0:T(8,128)(2,1)S(1)}, bf16[144,256]{1,0:T(8,128)(2,1)S(1)}, u32[]{:S(2)}, u32[]{:S(2)}) collective-permute-start(bf16[144,256]{1,0:T(8,128)(2,1)S(1)} %fusion.1), channel_id=1, source_target_pairs={{0,8},{1,9},{2,10},{3,11},{4,12},{5,13},{6,14},{7,15},{8,0},{9,1},... | collective-permute-start | bytes 221192 | tf_op jit(solution)/shard_map/ppermute | solution.py:512
  137.9 10.7 %collective-permute-start.33 = (bf16[144,256]{1,0:T(8,128)(2,1)S(1)}, bf16[144,256]{1,0:T(8,128)(2,1)S(1)}, u32[]{:S(2)}, u32[]{:S(2)}) collective-permute-start(bf16[144,256]{1,0:T(8,128)(2,1)S(1)} %fusion), channel_id=1, source_target_pairs={{0,12},{1,13},{2,14},{3,15},{4,8},{5,9},{6,10},{7,11},{8,4},{9,5},... | collective-permute-start | bytes 221192 | tf_op jit(solution)/shard_map/ppermute | solution.py:512
  141.1 5.5 %collective-permute-start.37 = (bf16[8,20,256]{2,0,1:T(8,128)(2,1)S(1)}, bf16[8,20,256]{2,0,1:T(8,128)(2,1)S(1)}, u32[]{:S(2)}, u32[]{:S(2)}) collective-permute-start(bf16[8,20,256]{2,0,1:T(8,128)(2,1)S(1)} %add_convert_fusion.3), channel_id=1, source_target_pairs={{0,2},{1,3},{2,0},{3,1},{4,6},{5,7},{6,4},{7,5},{8,10},{9,11},{10,... | collective-permute-start | bytes 245768 | tf_op jit(solution)/shard_map/ppermute | solution.py:512
  143.1 21.4 %all-to-all-start.1 = ((bf16[8,16,2048]{2,1,0:T(8,128)(2,1)}), bf16[8,16,2048]{2,1,0:T(8,128)(2,1)S(1)}, u32[]{:S(2)}, u32[]{:S(2)}) async-start(bf16[8,16,2048]{2,1,0:T(8,128)(2,1)} %bitcast.44), calls=%async_computation.1 | async-start | bytes 1048576 | tf_op jit(solution)/shard_map/all_to_all | solution.py:691
  146.6 9.0 %collective-permute-start.38 = (bf16[8,20,256]{2,0,1:T(8,128)(2,1)S(1)}, bf16[8,20,256]{2,0,1:T(8,128)(2,1)S(1)}, u32[]{:S(2)}, u32[]{:S(2)}) collective-permute-start(bf16[8,20,256]{2,0,1:T(8,128)(2,1)S(1)} %add_convert_fusion.2), channel_id=1, source_target_pairs={{0,4},{1,5},{2,6},{3,7},{4,0},{5,1},{6,2},{7,3},{8,12},{9,13},{10,... | collective-permute-start | bytes 245768 | tf_op jit(solution)/shard_map/ppermute | solution.py:512
  155.6 8.2 %collective-permute-start.39 = (bf16[8,20,256]{2,0,1:T(8,128)(2,1)S(1)}, bf16[8,20,256]{2,0,1:T(8,128)(2,1)S(1)}, u32[]{:S(2)}, u32[]{:S(2)}) collective-permute-start(bf16[8,20,256]{2,0,1:T(8,128)(2,1)S(1)} %add_convert_fusion.1), channel_id=1, source_target_pairs={{0,8},{1,9},{2,10},{3,11},{4,12},{5,13},{6,14},{7,15},{8,0},{9,1},... | collective-permute-start | bytes 245768 | tf_op jit(solution)/shard_map/ppermute | solution.py:512
  (29 other events, 70.6 us)

commit v3 on v1

v3 whole, which is shorter than its diff:
```python
import functools

import jax
import jax.numpy as jnp
from jax import lax
from jax.experimental import pallas as pl
from jax.experimental.pallas import tpu as pltpu
from jax.sharding import PartitionSpec as P

AXIS = "expert"
TILE = 512
AUX = 32
bf16 = jnp.bfloat16
f32 = jnp.float32
CHUNK = 512
FIRST, SMALL, BIG = 60, 16, 32
COST = 100000


def mm(left, right, left_dim=1, right_dim=0):
    return lax.dot_general(
        left, right, (((left_dim,), (right_dim,)), ((), ())), preferred_element_type=f32
    )


def call(kernel, out_shapes, operands, in_specs=None, scratch=(), limit=48):
    specs = in_specs or [None] * len(operands)
    specs = [pl.BlockSpec(memory_space=pltpu.VMEM) if s is None else s for s in specs]
    return pl.pallas_call(
        kernel,
        out_shape=out_shapes,
        in_specs=specs,
        out_specs=[pl.BlockSpec(memory_space=pltpu.VMEM) for _ in out_shapes],
        scratch_shapes=list(scratch),
        compiler_params=pltpu.CompilerParams(vmem_limit_bytes=limit * 1024 * 1024),
        cost_estimate=pl.CostEstimate(flops=COST, bytes_accessed=COST, transcendentals=0),
    )(*operands)


SCALARS = pl.BlockSpec(memory_space=pltpu.SMEM)


def own_core():
    return lax.rem(lax.axis_index(AXIS), 2)


def struct(shape, kind):
    return jax.ShapeDtypeStruct(shape, kind)


def sigmoid(v):
    return 0.5 * (1.0 + jnp.tanh(0.5 * v))


def eye(size):
    rows = lax.broadcasted_iota(jnp.int32, (size, size), 0)
    cols = lax.broadcasted_iota(jnp.int32, (size, size), 1)
    return (rows == cols).astype(f32).astype(bf16)


def spread(tile, size, expert_lanes):
    rows = lax.broadcasted_iota(jnp.int32, (AUX, size), 0)
    lanes = lax.broadcasted_iota(jnp.int32, (AUX, size), 1) + tile * size
    first = rows * expert_lanes
    return ((lanes >= first) & (lanes < first + expert_lanes)).astype(f32).astype(bf16)


def turn_matrix(size, depth, core):
    place = lax.broadcasted_iota(jnp.int32, (size, size), 0)
    column = lax.broadcasted_iota(jnp.int32, (size, size), 1)
    half = size // 2
    other = place // half
    place = place - other * half
    chip = place // depth
    which = jnp.where(core == 0, other, 1 - other)
    return (column == (chip * 2 + which) * depth + (place - chip * depth)).astype(f32).astype(bf16)


def side_of(piece):
    half = piece.shape[1] // 2
    return jnp.concatenate([piece[:, :half], piece[:, half:]], axis=0)


def selector(side, gate_count, owner, capacity):
    wide = side.astype(f32)
    which = wide[gate_count : gate_count + 1, :]
    slot = wide[gate_count + 1 : gate_count + 2, :]
    ranks = lax.broadcasted_iota(jnp.int32, (capacity, side.shape[1]), 0).astype(f32)
    hit = (ranks == slot) & (which == owner)
    return hit.astype(f32).astype(bf16)


def placement(own_side, gate_count):
    wide = own_side.astype(f32)
    rows = [wide[gate_count + 2 + i : gate_count + 3 + i, :] for i in range(4)]
    return (rows[0], rows[1]), (rows[2], rows[3])


def gate_picks(first):
    shape = (AUX, first.shape[1])
    rows = lax.broadcasted_iota(jnp.int32, shape, 0)
    lanes = lax.broadcasted_iota(jnp.int32, shape, 1)
    return ((rows - lanes).astype(f32) == first).astype(f32).astype(bf16)


def by_scenario(ids, scenarios):
    labels = lax.broadcasted_iota(jnp.int32, (scenarios, ids.shape[1]), 0)
    return (labels == ids).astype(f32)[None]


def prep_kernel(shared, hidden, slot_width, pads, slots, feats, sid, gate, pack, probs, scr):
    scenarios = pads.shape[0]
    gate_count = gate.shape[0] // scenarios
    rows = feats.shape[0]
    x = feats[...]
    ids = sid[...]
    scr[...] = jnp.zeros_like(scr)
    pad = jnp.zeros((1, rows), f32)
    for s in range(scenarios):
        pad = pad + jnp.where(ids == s, pads[s].astype(f32), 0.0)
    logits = mm(gate[...], x, 1, 1).reshape(gate_count, scenarios, rows)
    own = jnp.sum(logits * by_scenario(ids, scenarios), axis=1)
    top = jnp.max(own, axis=0, keepdims=True)
    raised = jnp.exp(own - top)
    scr[:gate_count, :] = raised / jnp.sum(raised, axis=0, keepdims=True)
    probs[...] = scr[...]
    labels = lax.broadcasted_iota(jnp.int32, (AUX, rows), 0)
    member = (ids == labels).astype(f32)
    earlier = (
        lax.broadcasted_iota(jnp.int32, (rows, rows), 0)
        < lax.broadcasted_iota(jnp.int32, (rows, rows), 1)
    ).astype(f32).astype(bf16)
    rank = jnp.sum(mm(member.astype(bf16), earlier) * member, axis=0, keepdims=True)
    slot = jnp.where(rank < pad, rank, -1.0)
    scr[gate_count : gate_count + 1, :] = ids.astype(f32)
    scr[gate_count + 1 : gate_count + 2, :] = slot
    index = lax.axis_index(AXIS)
    group = slots.shape[0] // scenarios
    for i, device in enumerate((index, index + 1 - 2 * lax.rem(index, 2))):
        owned = slots[device]
        first = shared + lax.rem(owned, group) * slot_width // hidden
        for j, value in enumerate((owned // group, first)):
            at = gate_count + 2 + 2 * i + j
            scr[at : at + 1, :] = jnp.zeros((1, rows), f32) + value.astype(f32)
    side = scr[...].astype(bf16)
    pack[:rows, :] = x
    pack[rows:, :rows] = side[: AUX // 2]
    pack[rows:, rows:] = side[AUX // 2 :]


def tile_kernel(tiled, expand, pieces):
    if tiled:
        chips, _, total = pieces.shape
        count = expand.shape[0]
        lanes = total // count
        for k in range(count):
            for chip in range(chips):
                pieces[chip, :, k * lanes : (k + 1) * lanes] = expand[
                    k, :, chip * lanes : (chip + 1) * lanes
                ]
    else:
        pieces[...] = expand[...]


def own_place(pieces, gate_count):
    return placement(side_of(pieces[0][0, pieces[0].shape[1] - AUX // 2 :, :]), gate_count)


def compact_kernel(n, gate_count, capacity, *refs):
    pieces, logits, outs = refs[:n], refs[n:-2], refs[-2:]
    m = pieces[0].shape[0]
    rows = pieces[0].shape[1] - AUX // 2
    width = pieces[0].shape[2]
    places = own_place(pieces, gate_count)
    for k in range(n):
        for b in range(m):
            x = pieces[k][b, :rows, :]
            side = side_of(pieces[k][b, rows:, :])
            spot = slice((k * m + b) * capacity, (k * m + b + 1) * capacity)
            for (owner, first), out in zip(places, outs):
                sel = selector(side, gate_count, owner, capacity)
                out[spot, :width] = mm(sel, x).astype(bf16)
                gates = mm(sel, side, 1, 1).astype(bf16)
                out[spot, width : width + rows] = mm(gates, gate_picks(first)).astype(bf16)
                if logits:
                    out[spot, width + rows :] = mm(sel, logits[k][b]).astype(bf16)


def chosen_gate(x, width, expert):
    gates = x[:, width : width + 128].astype(f32)
    lanes = lax.broadcasted_iota(jnp.int32, gates.shape, 1)
    return jnp.sum(jnp.where(lanes == expert, gates, 0.0), axis=1, keepdims=True)


def hidden_lanes(j, size):
    return pl.ds(pl.multiple_of(j * size, size), size)


def scenario_forward_kernel(hidden, own, other, widen, narrow, out_own, out_other, gated):
    half, width = out_own.shape
    total = widen.shape[1]
    size, chunk = min(TILE, total), min(half, CHUNK)

    def tile(j, _):
        lanes = hidden_lanes(j, size)
        for base, source in ((0, own), (half, other)):
            for at in range(0, half, chunk):
                x = source[at : at + chunk, :]
                gate = chosen_gate(x, width, (j * size) // hidden)
                linear = mm(x[:, :width], widen[:, lanes])
                spot = slice(base + at, base + at + chunk)
                gated[spot, lanes] = (gate * (linear * sigmoid(linear))).astype(bf16)
        return 0

    lax.fori_loop(0, total // size, tile, 0)
    out_own[...] = mm(gated[:half, :], narrow[...]).astype(bf16)
    out_other[...] = mm(gated[half:, :], narrow[...]).astype(bf16)


def unpack(pieces, turn, xs, gates, xt=None):
    m, packed, _ = pieces[0].shape
    rows = packed - AUX // 2
    for k in range(len(pieces)):
        for b in range(m):
            spot = slice((k * m + b) * rows, (k * m + b + 1) * rows)
            x = pieces[k][b, :rows, :]
            xs[spot, :] = mm(x, turn, 1, 1).astype(bf16)
            gates[spot, :] = mm(side_of(pieces[k][b, rows:, :]), eye(AUX), 0, 0).astype(bf16)
            if xt is not None:
                xt[:, spot] = mm(turn, x, 1, 1).astype(bf16)


def join_weights(w1a, w1b, w2a, w2b, w1, w2):
    half = w1a.shape[0]
    w1[:half, :] = w1a[...]
    w1[half:, :] = w1b[...]
    experts, part, _ = w2a.shape
    core = own_core()
    for k in range(experts):
        mine, theirs = w2a[k], w2b[k]
        w2[2 * k * part : (2 * k + 1) * part, :] = jnp.where(core == 0, mine, theirs)
        w2[(2 * k + 1) * part : 2 * (k + 1) * part, :] = jnp.where(core == 0, theirs, mine)


def shared_forward_kernel(n, start, gate_rows, gate_count, depth, *refs):
    own, pieces = refs[0], refs[1 : n + 1]
    w1a, w1b, w2a, w2b, from_own, from_other, out, xs, gates, w1, w2, gated = refs[n + 1 :]
    join_weights(w1a, w1b, w2a, w2b, w1, w2)
    unpack(pieces, turn_matrix(w1.shape[0], depth, own_core()), xs, gates)
    count, rows, _ = out.shape
    m = pieces[0].shape[0]
    capacity = from_own.shape[0] // (w1.shape[0] // (2 * depth))
    places = own_place([own], gate_count)
    total = count * rows
    size, chunk = min(TILE, w1.shape[1]), min(total, CHUNK)

    def tile(j, _):
        lanes = hidden_lanes(j, size)
        picks = spread(j, size, gate_rows)
        for at in range(0, total, chunk):
            spot = slice(at, at + chunk)
            linear = mm(xs[spot, :], w1[:, lanes])
            active = linear * sigmoid(linear)
            gated[spot, lanes] = (mm(gates[spot, :], picks) * active).astype(bf16)
        return 0

    lax.fori_loop(0, w1.shape[1] // size, tile, 0)
    for at in range(0, total, chunk):
        mixed = mm(gated[at : at + chunk, :], w2[...])
        for piece in range(at // rows, (at + chunk) // rows):
            side = side_of(pieces[piece // m][piece % m, rows:, :])
            spot = slice((start + piece) * capacity, (start + piece + 1) * capacity)
            value = mixed[piece * rows - at : (piece + 1) * rows - at]
            for (owner, _), source in zip(places, (from_own, from_other)):
                value += mm(selector(side, gate_count, owner, capacity), source[spot, :], 0, 0)
            out[piece] = value.astype(bf16)


def softmax(v):
    raised = jnp.exp(v - jnp.max(v, axis=1, keepdims=True))
    return raised / jnp.sum(raised, axis=1, keepdims=True)


def head_kernel(count, *refs):
    parts = refs[:count]
    head, mentor, grad, head_part = refs[count:]
    layer = parts[0][...].astype(f32)
    for part in parts[1:]:
        layer = layer + part[...].astype(f32)
    rounded = layer.astype(bf16)
    student = mm(rounded, head[...])
    value = (2.0 * (softmax(student * 0.5) - softmax(mentor[...] * 0.5))).astype(bf16)
    grad[...] = value
    head_part[...] = mm(rounded, value, 0, 0)


def shared_backward_kernel(n, gate_rows, depth, *refs):
    pieces, logits = refs[:n], refs[n : 2 * n]
    head, w1a, w1b, w2a, w2b = refs[2 * n : 2 * n + 5]
    dx, mix, keep, sent, keep2, sent2 = refs[2 * n + 5 : 2 * n + 11]
    xp, xpt, gates, w1, w2, os, linear_grad, weighed = refs[2 * n + 11 :]
    core = own_core()
    turn = turn_matrix(w1.shape[0], depth, core)
    join_weights(w1a, w1b, w2a, w2b, w1, w2)
    unpack(pieces, turn, xp, gates, xpt)
    m, rows, _ = logits[0].shape
    for k in range(n):
        for b in range(m):
            at = (k * m + b) * rows
            os[at : at + rows, :] = mm(logits[k][b], head[...], 1, 1).astype(bf16)
    total = n * m * rows
    size, chunk = min(TILE, w1.shape[1]), min(total, CHUNK)
    half, part = keep.shape[0], keep2.shape[1]
    mix[...] = jnp.zeros_like(mix)

    def tile(j, _):
        lanes = hidden_lanes(j, size)
        picks = spread(j, size, gate_rows)
        for at in range(0, total, chunk):
            spot = slice(at, at + chunk)
            linear = mm(xp[spot, :], w1[:, lanes])
            hidden = mm(os[spot, :], w2[lanes, :], 1, 1)
            gate = mm(gates[spot, :], picks)
            sig = sigmoid(linear)
            active = linear * sig
            mix[spot, :] += mm((hidden * active).astype(bf16), picks, 1, 1)
            slope = sig + active * (1.0 - sig)
            linear_grad[spot, lanes] = (gate * hidden * slope).astype(bf16)
            weighed[spot, :] = (gate * active).astype(bf16)
        first = mm(xpt[...], linear_grad[:, lanes])
        keep[:, lanes] = first[:half].astype(keep.dtype)
        sent[:, lanes] = first[half:].astype(bf16)
        second = mm(weighed[...], os[...], 0, 0)
        for e in range(size // gate_rows):
            low = second[e * gate_rows : e * gate_rows + part]
            high = second[e * gate_rows + part : (e + 1) * gate_rows]
            k = j * (size // gate_rows) + e
            keep2[k] = jnp.where(core == 0, low, high)
            sent2[k] = jnp.where(core == 0, high, low).astype(bf16)
        return 0

    lax.fori_loop(0, w1.shape[1] // size, tile, 0)
    chunk = min(total, 1024)
    for at in range(0, total, chunk):
        spot = slice(at, at + chunk)
        value = mm(linear_grad[spot, :], w1[...], 1, 1).astype(bf16)
        dx[spot, :] = mm(value, turn).astype(bf16)


def scenario_backward_kernel(
    hidden_units, own, other, head, widen, narrow,
    out_own, out_other, dwiden, dnarrow, xs, xt, os, linear_grad, weighed, mix,
):
    half = out_own.shape[0]
    width = narrow.shape[1]
    total = widen.shape[1]
    xs[:half, :] = own[...]
    xs[half:, :] = other[...]
    os[...] = mm(xs[:, width + 128 :], head[...], 1, 1).astype(bf16)
    mix[...] = jnp.zeros_like(mix)
    size, chunk = min(TILE, total), min(2 * half, CHUNK)
    for at in range(0, 2 * half, chunk):
        xt[:, at : at + chunk] = mm(eye(width), xs[at : at + chunk, :width], 1, 1).astype(bf16)

    def tile(j, _):
        lanes = hidden_lanes(j, size)
        column = (j * size) // hidden_units
        picks = (
            lax.broadcasted_iota(jnp.int32, (size, mix.shape[1]), 1) == column
        ).astype(f32).astype(bf16)
        for at in range(0, 2 * half, chunk):
            spot = slice(at, at + chunk)
            x = xs[spot, :]
            gate = chosen_gate(x, width, column)
            linear = mm(x[:, :width], widen[:, lanes])
            hidden = mm(os[spot, :], narrow[lanes, :], 1, 1)
            sig = sigmoid(linear)
            active = linear * sig
            mix[spot, :] += mm((hidden * active).astype(bf16), picks)
            slope = sig + active * (1.0 - sig)
            linear_grad[spot, lanes] = (gate * hidden * slope).astype(bf16)
            weighed[spot, :] = (gate * active).astype(bf16)
        dwiden[:, lanes] = mm(xt[...], linear_grad[:, lanes])
        dnarrow[lanes, :] = mm(weighed[...], os[...], 0, 0)
        return 0

    lax.fori_loop(0, total // size, tile, 0)
    for at, out in ((0, out_own), (half, out_other)):
        out[:, :width] = mm(linear_grad[at : at + half, :], widen[...], 1, 1).astype(bf16)
        out[:, width:] = mix[at : at + half, :].astype(bf16)


def scatter_kernel(n, gate_count, *refs):
    pieces = refs[:n]
    dx, mix, from_own, from_other, home, away, gate_part = refs[n:]
    m, packed, width = pieces[0].shape
    rows = packed - AUX // 2
    capacity = from_own.shape[0] // (n * m)
    places = own_place(pieces, gate_count)
    live = lax.broadcasted_iota(jnp.int32, (rows, AUX), 1) < gate_count
    total = jnp.zeros(gate_part.shape, f32)
    for k in range(n):
        for b in range(m):
            piece = k * m + b
            out, to = (home, piece) if piece < home.shape[0] else (away, piece - home.shape[0])
            spot = slice(piece * capacity, (piece + 1) * capacity)
            full = slice(piece * rows, (piece + 1) * rows)
            side = side_of(pieces[k][b, rows:, :])
            value, dots = dx[full, :].astype(f32), mix[full, :].astype(f32)
            for (owner, first), source in zip(places, (from_own, from_other)):
                extra = mm(selector(side, gate_count, owner, capacity), source[spot, :], 0, 0)
                value += extra[:, :width]
                dots += mm(extra[:, width:].astype(bf16), gate_picks(first), 1, 1)
            out[to, :rows, :] = value.astype(bf16)
            turned = mm(eye(AUX), dots.astype(bf16), 1, 1).astype(bf16)
            out[to, rows:, :rows] = turned[: AUX // 2]
            out[to, rows:, rows:] = turned[AUX // 2 :]
            share = mm(side, eye(AUX), 0, 0)
            share = jnp.where(live, share, 0.0)
            share = share / jnp.sum(share, axis=1, keepdims=True)
            score = share * (dots - jnp.sum(share * dots, axis=1, keepdims=True))
            score = mm(eye(AUX), score.astype(bf16), 1, 1)[:gate_count]
            ids = side[gate_count : gate_count + 1, :].astype(f32)
            wide = score[:, None, :] * by_scenario(ids.astype(jnp.int32), total.shape[0] // gate_count)
            wide = wide.reshape(total.shape[0], rows).astype(bf16)
            total = total + mm(wide, pieces[k][b, :rows, :])
    gate_part[...] = total


def final_kernel(count, gate_count, *refs):
    parts = refs[:count]
    feats, sid, probs, gate, out = refs[count:]
    rows = feats.shape[0]
    total = parts[0][...].astype(f32)
    for part in parts[1:]:
        total = total + part[...].astype(f32)
    tail = total[rows:]
    half = tail.shape[1] // 2
    dots = jnp.concatenate([tail[:, :half], tail[:, half:]], axis=0)
    share = probs[...]
    live = lax.broadcasted_iota(jnp.int32, (AUX, rows), 0) < gate_count
    dots = jnp.where(live, dots, 0.0)
    score = share * (dots - jnp.sum(share * dots, axis=0, keepdims=True))
    score = score.astype(bf16).astype(f32)[:gate_count]
    wide = score[:, None, :] * by_scenario(sid[...], gate.shape[0] // gate_count)
    wide = wide.reshape(gate.shape[0], rows).astype(bf16)
    out[...] = (total[:rows] + mm(wide, gate[...], 0, 0)).astype(bf16)


def expand_grad_kernel(pieces, out):
    count, _, hidden = out.shape
    chips = pieces.shape[0]
    lanes = hidden // chips
    for k in range(count):
        for chip in range(chips):
            out[k, :, chip * lanes : (chip + 1) * lanes] = pieces[
                chip, :, k * lanes : (k + 1) * lanes
            ].astype(f32)


def body(
    features,
    scenario_id,
    scenario_pads,
    device_slot,
    mentor,
    gate_weight,
    expand,
    reduce,
    scenario_widen,
    scenario_narrow,
    head,
):
    rows, width = features.shape
    devices = lax.axis_size(AXIS)
    chips = devices // 2
    near = 2 ** ((chips.bit_length() - 1) // 2)
    far = chips // near
    n, m = near, far
    shared, depth, hidden = expand.shape
    lanes = hidden // chips
    scenarios, _, gates = gate_weight.shape
    capacity = rows // 4
    slot_width = scenario_widen.shape[2]
    classes = head.shape[1]
    all_rows = chips * rows
    assert gates + 6 <= AUX and rows == 128
    slots = chips * capacity
    hidden_chip = shared * lanes
    groups = [[2 * r + c for r in range(chips)] for c in range(2)]

    def send(value, mask):
        return lax.ppermute(value, AXIS, [(i, i ^ mask) for i in range(devices)])

    def gather(value):
        column = [value] + [send(value, 2 * near * b) for b in range(1, far)]
        stacked = jnp.stack(column)
        return [stacked] + [send(stacked, 2 * a) for a in range(1, near)]

    def total_of(value):
        value = value + send(value, 1)
        mask = 2
        while mask < devices:
            half = value.astype(bf16)
            value = half.astype(f32) + send(half, mask).astype(f32)
            mask *= 2
        return value

    sid = scenario_id.reshape(1, rows)
    gate = jnp.transpose(gate_weight, (2, 0, 1)).reshape(gates * scenarios, width)
    widen, narrow = scenario_widen[0], scenario_narrow[0]
    tiled = lanes % 128 == 0 and depth % 16 == 0
    if not tiled:
        expand = expand.reshape(shared, depth, chips, lanes).transpose(2, 1, 0, 3)
        expand = expand.reshape(chips, depth, hidden_chip)

    pack_rows = rows + AUX // 2
    pack, probs = call(
        functools.partial(prep_kernel, shared, hidden, slot_width),
        [struct((pack_rows, width), bf16), struct((AUX, rows), f32)],
        [scenario_pads, device_slot, features, sid, gate],
        [SCALARS] * 2 + [None] * 3,
        [pltpu.VMEM((AUX, rows), f32)],
        limit=FIRST,
    )
    column = [pack] + [send(pack, 2 * near * b) for b in range(1, far)]
    stacked = jnp.stack(column)
    stacked, expand = lax.optimization_barrier((stacked, expand))
    got = [stacked] + [send(stacked, 2 * a) for a in range(1, near)]
    (pieces,) = call(
        functools.partial(tile_kernel, tiled),
        [struct((chips, depth, hidden_chip), bf16)],
        [expand],
        limit=8,
    )
    w2a = reduce
    w2b = send(reduce, 1)
    w1a = lax.all_to_all(
        pieces, AXIS, split_axis=0, concat_axis=0, tiled=True, axis_index_groups=groups
    ).reshape(width // 2, hidden_chip)
    x_own, x_send = call(
        functools.partial(compact_kernel, n, gates, capacity),
        [struct((slots, width + 128), bf16)] * 2,
        got,
        limit=SMALL,
    )
    x_other = send(x_send, 1)
    out_own, out_send = call(
        functools.partial(scenario_forward_kernel, hidden),
        [struct((slots, width), bf16)] * 2,
        [x_own, x_other, widen, narrow],
        scratch=[pltpu.VMEM((2 * slots, slot_width), bf16)],
        limit=SMALL,
    )
    w1a, out_send = lax.optimization_barrier((w1a, out_send))
    out_other = send(out_send, 1)
    w1b = send(w1a, 1)
    weights = [w1a, w1b, w2a, w2b]
    weight_scratch = [
        pltpu.VMEM((width, hidden_chip), bf16),
        pltpu.VMEM((hidden_chip, width), bf16),
    ]

    def forward(pieces, start):
        count = len(pieces) * far
        (out,) = call(
            functools.partial(shared_forward_kernel, len(pieces), start, lanes, gates, depth),
            [struct((count, rows, width), bf16)],
            [got[0], *pieces, *weights, out_own, out_other],
            scratch=[
                pltpu.VMEM((count * rows, width), bf16),
                pltpu.VMEM((count * rows, AUX), bf16),
                *weight_scratch,
                pltpu.VMEM((count * rows, hidden_chip), bf16),
            ],
            limit=BIG,
        )
        return out

    away = forward(got[1:], far)
    home = forward(got[:1], 0)
    total = home.astype(f32)
    for a in range(1, near):
        total = total + send(away[(a - 1) * far : a * far], 2 * a).astype(f32)
    total = total.astype(bf16)
    layer_parts = [total[0]] + [send(total[b], 2 * near * b) for b in range(1, far)]
    logit_grad, head_part = call(
        functools.partial(head_kernel, len(layer_parts)),
        [struct((rows, classes), bf16), struct((width, classes), f32)],
        [*layer_parts, head, mentor],
        limit=8,
    )
    logits = gather(logit_grad)
    head_total = total_of(head_part)

    x_own, x_send = call(
        functools.partial(compact_kernel, n, gates, capacity),
        [struct((slots, width + 128 + classes), bf16)] * 2,
        [*got, *logits],
        limit=SMALL,
    )
    x_other = send(x_send, 1)
    dx, mix, dw1_keep, dw1_send, dw2_keep, dw2_send = call(
        functools.partial(shared_backward_kernel, n, lanes, depth),
        [
            struct((all_rows, width), bf16),
            struct((all_rows, AUX), f32),
            struct((width // 2, hidden_chip), bf16),
            struct((width // 2, hidden_chip), bf16),
            struct((shared, lanes // 2, width), f32),
            struct((shared, lanes // 2, width), bf16),
        ],
        [*got, *logits, head, *weights],
        scratch=[
            pltpu.VMEM((all_rows, width), bf16),
            pltpu.VMEM((width, all_rows), bf16),
            pltpu.VMEM((all_rows, AUX), bf16),
            *weight_scratch,
            pltpu.VMEM((all_rows, width), bf16),
            pltpu.VMEM((all_rows, hidden_chip), bf16),
            pltpu.VMEM((all_rows, min(TILE, hidden_chip)), bf16),
        ],
        limit=BIG,
    )
    dw1 = (dw1_keep.astype(f32) + send(dw1_send, 1).astype(f32)).astype(bf16)
    dw1, x_own = lax.optimization_barrier((dw1, x_own))
    dw1 = lax.all_to_all(
        dw1.reshape(chips, depth, hidden_chip),
        AXIS, split_axis=0, concat_axis=0, tiled=True, axis_index_groups=groups,
    )
    dx_own, dx_send, widen_grad, narrow_grad = call(
        functools.partial(scenario_backward_kernel, hidden),
        [struct((slots, width + 128), bf16)] * 2
        + [struct((width, slot_width), f32), struct((slot_width, width), f32)],
        [x_own, x_other, head, widen, narrow],
        None,
        [
            pltpu.VMEM((2 * slots, width + 128 + classes), bf16),
            pltpu.VMEM((width, 2 * slots), bf16),
            pltpu.VMEM((2 * slots, width), bf16),
            pltpu.VMEM((2 * slots, slot_width), bf16),
            pltpu.VMEM((2 * slots, min(TILE, slot_width)), bf16),
            pltpu.VMEM((2 * slots, 128), f32),
        ],
        limit=BIG,
    )
    dx_other = send(dx_send, 1)
    reduce_grad = dw2_keep + send(dw2_send, 1).astype(f32)
    dw1, dx_own = lax.optimization_barrier((dw1, dx_own))
    grad_home, grad_away, gate_part = call(
        functools.partial(scatter_kernel, n, gates),
        [
            struct((far, pack_rows, width), bf16),
            struct((chips - far, pack_rows, width), bf16),
            struct((gates * scenarios, width), f32),
        ],
        [*got, dx, mix, dx_own, dx_other],
        limit=SMALL,
    )
    total = grad_home.astype(f32)
    for a in range(1, near):
        total = total + send(grad_away[(a - 1) * far : a * far], 2 * a).astype(f32)
    total = total.astype(bf16)
    grad_parts = [total[0]] + [send(total[b], 2 * near * b) for b in range(1, far)]
    gate_total = total_of(gate_part).reshape(gates, scenarios, width)
    gate_total = jnp.transpose(gate_total, (1, 2, 0))
    if tiled:
        (expand_grad,) = call(
            expand_grad_kernel, [struct((shared, depth, hidden), f32)], [dw1], limit=8
        )
    else:
        expand_grad = dw1.reshape(chips, depth, shared, lanes).transpose(2, 1, 0, 3)
        expand_grad = expand_grad.reshape(shared, depth, hidden).astype(f32)

    (feature_grad,) = call(
        functools.partial(final_kernel, len(grad_parts), gates),
        [struct((rows, width), bf16)],
        [*grad_parts, features, sid, probs, gate],
        limit=8,
    )
    return (
        feature_grad,
        expand_grad,
        reduce_grad,
        widen_grad[None],
        narrow_grad[None],
        gate_total,
        head_total,
    )


def solution(mesh):
    placed = (
        P(("groups", "expert"), None),
        P(("groups", "expert")),
        P("groups"),
        P(),
        P(("groups", "expert"), None),
        P(),
        P(None, "expert", None),
        P(None, "expert", None),
        P("expert", None, None),
        P("expert", None, None),
        P(),
    )
    return jax.shard_map(
        body,
        mesh=mesh,
        in_specs=placed,
        out_specs=(
            P(("groups", "expert"), None),
            P("groups", "expert", None),
            P("groups", "expert", None),
            P(("groups", "expert"), None, None),
            P(("groups", "expert"), None, None),
            P("groups", None, None),
            P("groups", None),
        ),
        check_vma=False,
    )
```

time: 173 us -> 148 us (0.86)
  starting transfers between devices: 56.5 us -> 41.8 us
  local copies, waits for them, and re-layouts: 13.6 us -> 6.35 us
  between operations: 6.3 us -> 0.96 us
  Pallas kernels: 37.2 us -> 42 us
  other arithmetic: 7.67 us -> 5.47 us
    ppermute x44 -> x32, starting transfers between devices: 45.2 us -> 33.2 us  [send(): return lax.ppermute(value, AXIS, [(i, i ^ mask) for i in range(devices)])]
    pallas_call x10 -> x13, Pallas kernels: 37.2 us -> 42 us  [call(): pl.pallas_call(kernel, out_shape=out_shapes, in_specs=specs, out_specs=[p...]
    convert_element_type x4 -> x0, local copies, waits for them, and re-layouts: 3.9 us -> none  [the longest x1 2.09 us: body(): sent = lax.dynamic_index_in_dim(dw2, 1 - core, 1, False).astype(bf16)]
    all_to_all x1, starting transfers between devices: 7.28 us -> 4.88 us  [body(): lax.all_to_all(pieces, AXIS, split_axis=0, concat_axis=0, tiled=True, axi...]
    another operation x5 -> x2, other arithmetic: 2.82 us -> 0.94 us  [the longest x1 0.92 us: body(): stacked = jnp.stack(column)]
    unnamed x37 -> x42, local copies, waits for them, and re-layouts: 7.88 us -> 6.31 us
    ppermute x44 -> x32, waiting for transfers between devices: 51 us -> 49.8 us  [send(): return lax.ppermute(value, AXIS, [(i, i ^ mask) for i in range(devices)])]
  transfers between devices with their start and end apart: 46 -> 34, of which waited for: 21 -> 18; matrix products, arithmetic and copies ran while one was open for 7% -> 2% of each run, Pallas kernels for 17% -> 16%
where the time goes in v3:
time: 148 us
  waiting for transfers between devices  51.1 us (35%)
  Pallas kernels  42 us (28%)
  starting transfers between devices  41.8 us (28%)
  local copies, waits for them, and re-layouts  6.35 us (4%)
  other arithmetic  5.47 us (4%)
    ppermute x32, waiting for transfers between devices, send(): return lax.ppermute(value, AXIS, [(i, i ^ mask) for i in range(devices)])  49.8 us
    pallas_call x13, Pallas kernels, call(): pl.pallas_call(kernel, out_shape=out_shapes, in_specs=specs, out_specs=[p...  42 us
    ppermute x32, starting transfers between devices, send(): return lax.ppermute(value, AXIS, [(i, i ^ mask) for i in range(devices)])  33.2 us
    unnamed x42, local copies, waits for them, and re-layouts  6.31 us
    all_to_all x1, starting transfers between devices, body(): lax.all_to_all(pieces, AXIS, split_axis=0, concat_axis=0, tiled=True, axi...  4.88 us
    all_to_all x1, starting transfers between devices, body(): lax.all_to_all(dw1.reshape(chips, depth, hidden_chip), AXIS, split_axis=0...  3.68 us
  transfers between devices with their start and end apart: 34, of which 18 were waited for; matrix products, arithmetic and copies ran while one was open for 2% of the time, Pallas kernels for 16%

profile of v3, /device:TPU:0, one launch (start us, length us, event | category | flops | bytes accessed | tf_op | source)
XLA Modules:
  0.0 147.6 jit_solution(8382158730378990831)
XLA Ops:
  0.7 1.9 %shard_map.162 = (bf16[144,256]{1,0:T(8,128)(2,1)}, f32[32,128]{1,0:T(8,128)}) custom-call(s32[8]{0:T(128)} %pads.1, s32[16]{0:T(128)} %slots.1, bf16[128,256]{1,0:T(8,128)(2,1)} %refs_4_.9, s32[1,128]{1,0:T(1,128)} %bitcast.49, bf16[160,256]{1,0:T(8,128)(2,1)} %bitcast.46), custom_call_target="tpu_custom_call" | custom-call | flops 100000 | bytes 100000 | tf_op jit(solution)/shard_map/pallas_call | solution.py:29
  2.6 5.0 %collective-permute-start.2 = (bf16[144,256]{1,0:T(8,128)(2,1)}, bf16[144,256]{1,0:T(8,128)(2,1)S(1)}, u32[]{:S(2)}, u32[]{:S(2)}) collective-permute-start(bf16[144,256]{1,0:T(8,128)(2,1)} %get-tuple-element.38), channel_id=1, source_target_pairs={{0,12},{1,13},{2,14},{3,15},{4,8},{5,9},{6,10},{7,11},{8,4},{9,5},... | collective-permute-start | bytes 221192 | tf_op jit(solution)/shard_map/ppermute | solution.py:493
  7.6 0.6 collective-permute-start
  8.2 2.4 %collective-permute-done.2 = bf16[144,256]{1,0:T(8,128)(2,1)S(1)} collective-permute-done((bf16[144,256]{1,0:T(8,128)(2,1)}, bf16[144,256]{1,0:T(8,128)(2,1)S(1)}, u32[]{:S(2)}, u32[]{:S(2)}) %collective-permute-start.2) | collective-permute-done | bytes 73760 | tf_op jit(solution)/shard_map/ppermute | solution.py:493
  10.6 3.4 %collective-permute-done.1 = bf16[144,256]{1,0:T(8,128)(2,1)S(1)} collective-permute-done((bf16[144,256]{1,0:T(8,128)(2,1)}, bf16[144,256]{1,0:T(8,128)(2,1)S(1)}, u32[]{:S(2)}, u32[]{:S(2)}) %collective-permute-start.1) | collective-permute-done | bytes 73760 | tf_op jit(solution)/shard_map/ppermute | solution.py:493
  14.1 0.9 pad_maximum_fusion.refs_0_.refs_1_
  15.0 1.0 copy-done.7
  16.0 0.9 shard_map.163
  16.9 4.9 %all-to-all-start = ((bf16[8,16,2048]{2,1,0:T(8,128)(2,1)}), bf16[8,16,2048]{2,1,0:T(8,128)(2,1)S(1)}, u32[]{:S(2)}, u32[]{:S(2)}) async-start(bf16[8,16,2048]{2,1,0:T(8,128)(2,1)} %shard_map.163), calls=%async_computation | async-start | bytes 1048576 | tf_op jit(solution)/shard_map/all_to_all | solution.py:538
  21.8 2.0 %collective-permute-start.3 = (bf16[4,144,256]{2,1,0:T(8,128)(2,1)S(1)}, bf16[4,144,256]{2,1,0:T(8,128)(2,1)S(1)}, u32[]{:S(2)}, u32[]{:S(2)}) collective-permute-start(bf16[4,144,256]{2,1,0:T(8,128)(2,1)S(1)} %pad_maximum_fusion.refs_0_.refs_1_), channel_id=1, source_target_pairs={{0,2},{1,3},{2,0},{3,1},{4,6},{5,7},{6,4},{7,5},{8,10},{9,11},{10,... | collective-permute-start | bytes 884744 | tf_op jit(solution)/shard_map/ppermute | solution.py:493
  23.8 10.7 %collective-permute-done.3.refs_1_ = bf16[4,144,256]{2,1,0:T(8,128)(2,1)S(1)} collective-permute-done((bf16[4,144,256]{2,1,0:T(8,128)(2,1)S(1)}, bf16[4,144,256]{2,1,0:T(8,128)(2,1)S(1)}, u32[]{:S(2)}, u32[]{:S(2)}) %collective-permute-start.3) | collective-permute-done | bytes 294944 | tf_op jit(solution)/shard_map/ppermute | solution.py:493
  34.6 1.3 shard_map.164
  35.9 0.5 collective-permute-start.6
  36.4 0.9 collective-permute-done.4.other
  37.4 1.2 copy-done.2
  38.6 2.3 %shard_map.165 = (bf16[256,256]{1,0:T(8,128)(2,1)S(1)}, bf16[256,256]{1,0:T(8,128)(2,1)S(1)}) custom-call(bf16[256,384]{1,0:T(8,128)(2,1)S(1)} %get-tuple-element.41.own, bf16[256,384]{1,0:T(8,128)(2,1)S(1)} %collective-permute-done.4.other, bf16[256,2048]{1,0:T(8,128)(2,1)S(1)} %bitcast.42, bf16[2048,256]{1,0:T(8,128)(2,1)S(1)} %bitcast.44), custom_call_target="tpu_custom_call" | custom-call | flops 100000 | bytes 100000 | tf_op jit(solution)/shard_map/pallas_call | solution.py:29
  41.1 0.4 collective-permute-start.7
  41.5 1.6 %collective-permute-done.7.refs_7_ = bf16[256,256]{1,0:T(8,128)(2,1)S(1)} collective-permute-done((bf16[256,256]{1,0:T(8,128)(2,1)S(1)}, bf16[256,256]{1,0:T(8,128)(2,1)S(1)}, u32[]{:S(2)}, u32[]{:S(2)}) %collective-permute-start.7) | collective-permute-done | bytes 131104 | tf_op jit(solution)/shard_map/ppermute | solution.py:493
  43.1 3.1 %shard_map.167 = bf16[4,128,256]{2,1,0:T(8,128)(2,1)S(1)} custom-call(bf16[4,144,256]{2,1,0:T(8,128)(2,1)S(1)} %pad_maximum_fusion.refs_0_.refs_1_, bf16[4,144,256]{2,1,0:T(8,128)(2,1)S(1)} %collective-permute-done.3.refs_1_, bf16[128,2048]{1,0:T(8,128)(2,1)S(1)} %bitcast.39, bf16[128,2048]{1,0:T(8,128)(2,1)S(1)} %collective-permute-done.5.refs_3_.refs_6_, ...), custom_call_target="tpu_custom_call" | custom-call | flops 100000 | bytes 100000 | tf_op jit(solution)/shard_map/pallas_call | solution.py:29
  46.4 3.1 %shard_map.166 = bf16[4,128,256]{2,1,0:T(8,128)(2,1)S(1)} custom-call(bf16[4,144,256]{2,1,0:T(8,128)(2,1)S(1)} %pad_maximum_fusion.refs_0_.refs_1_, bf16[4,144,256]{2,1,0:T(8,128)(2,1)S(1)} %pad_maximum_fusion.refs_0_.refs_1_, bf16[128,2048]{1,0:T(8,128)(2,1)S(1)} %bitcast.40, bf16[128,2048]{1,0:T(8,128)(2,1)S(1)} %collective-permute-done.5.refs_3_.refs_6_, ...), custom_call_target="tpu_custom_call" | custom-call | flops 100000 | bytes 100000 | tf_op jit(solution)/shard_map/pallas_call | solution.py:29
  49.5 5.2 %collective-permute-done.8 = bf16[4,128,256]{2,1,0:T(8,128)(2,1)S(1)} collective-permute-done((bf16[4,128,256]{2,1,0:T(8,128)(2,1)S(1)}, bf16[4,128,256]{2,1,0:T(8,128)(2,1)S(1)}, u32[]{:S(2)}, u32[]{:S(2)}) %collective-permute-start.8) | collective-permute-done | bytes 262176 | tf_op jit(solution)/shard_map/ppermute | solution.py:493
  54.8 3.3 %collective-permute-start.11 = (bf16[128,256]{1,0:T(8,128)(2,1)S(1)}, bf16[128,256]{1,0:T(8,128)(2,1)S(1)}, u32[]{:S(2)}, u32[]{:S(2)}) collective-permute-start(bf16[128,256]{1,0:T(8,128)(2,1)S(1)} %get-tuple-element.73), channel_id=1, source_target_pairs={{0,12},{1,13},{2,14},{3,15},{4,8},{5,9},{6,10},{7,11},{8,4},{9,5},... | collective-permute-start | bytes 196616 | tf_op jit(solution)/shard_map/ppermute | solution.py:493
  58.1 1.1 collective-permute-start.9
  59.2 2.0 %collective-permute-done.11.refs_3_ = bf16[128,256]{1,0:T(8,128)(2,1)S(1)} collective-permute-done((bf16[128,256]{1,0:T(8,128)(2,1)S(1)}, bf16[128,256]{1,0:T(8,128)(2,1)S(1)}, u32[]{:S(2)}, u32[]{:S(2)}) %collective-permute-start.11) | collective-permute-done | bytes 65568 | tf_op jit(solution)/shard_map/ppermute | solution.py:493
  61.2 2.3 %collective-permute-done.10.refs_2_ = bf16[128,256]{1,0:T(8,128)(2,1)S(1)} collective-permute-done((bf16[128,256]{1,0:T(8,128)(2,1)S(1)}, bf16[128,256]{1,0:T(8,128)(2,1)S(1)}, u32[]{:S(2)}, u32[]{:S(2)}) %collective-permute-start.10) | collective-permute-done | bytes 65568 | tf_op jit(solution)/shard_map/ppermute | solution.py:493
  63.5 0.5 shard_map.168
  64.0 2.6 %collective-permute-start.14 = (bf16[128,128]{1,0:T(8,128)(2,1)S(1)}, bf16[128,128]{1,0:T(8,128)(2,1)S(1)}, u32[]{:S(2)}, u32[]{:S(2)}) collective-permute-start(bf16[128,128]{1,0:T(8,128)(2,1)S(1)} %get-tuple-element.47), channel_id=1, source_target_pairs={{0,12},{1,13},{2,14},{3,15},{4,8},{5,9},{6,10},{7,11},{8,4},{9,5},... | collective-permute-start | bytes 98312 | tf_op jit(solution)/shard_map/ppermute | solution.py:493
  66.7 1.8 %collective-permute-start.12 = (bf16[128,128]{1,0:T(8,128)(2,1)S(1)}, bf16[128,128]{1,0:T(8,128)(2,1)S(1)}, u32[]{:S(2)}, u32[]{:S(2)}) collective-permute-start(bf16[128,128]{1,0:T(8,128)(2,1)S(1)} %get-tuple-element.47), channel_id=1, source_target_pairs={{0,4},{1,5},{2,6},{3,7},{4,0},{5,1},{6,2},{7,3},{8,12},{9,13},{10,... | collective-permute-start | bytes 98312 | tf_op jit(solution)/shard_map/ppermute | solution.py:493
  68.5 1.3 collective-permute-done.14
  69.8 1.7 %collective-permute-done.13 = bf16[128,128]{1,0:T(8,128)(2,1)S(1)} collective-permute-done((bf16[128,128]{1,0:T(8,128)(2,1)S(1)}, bf16[128,128]{1,0:T(8,128)(2,1)S(1)}, u32[]{:S(2)}, u32[]{:S(2)}) %collective-permute-start.13) | collective-permute-done | bytes 32800 | tf_op jit(solution)/shard_map/ppermute | solution.py:493
  71.5 0.6 collective-permute-start.15
  72.1 4.4 %collective-permute-done.15.refs_3_ = bf16[4,128,128]{2,1,0:T(8,128)(2,1)S(1)} collective-permute-done((bf16[4,128,128]{2,1,0:T(8,128)(2,1)S(1)}, bf16[4,128,128]{2,1,0:T(8,128)(2,1)S(1)}, u32[]{:S(2)}, u32[]{:S(2)}) %collective-permute-start.15) | collective-permute-done | bytes 131104 | tf_op jit(solution)/shard_map/ppermute | solution.py:493
  76.6 12.3 %shard_map.169 = (bf16[1024,256]{1,0:T(8,128)(2,1)S(1)}, f32[1024,32]{1,0:T(8,128)S(1)}, bf16[128,2048]{1,0:T(8,128)(2,1)S(1)}, bf16[128,2048]{1,0:T(8,128)(2,1)...) custom-call(bf16[4,144,256]{2,1,0:T(8,128)(2,1)S(1)} %pad_maximum_fusion.refs_0_.refs_1_, ...), custom_call_target="tpu_custom_call" | custom-call | flops 100000 | bytes 100000 | tf_op jit(solution)/shard_map/pallas_call | solution.py:29
  88.9 1.0 copy-done.4
  89.9 0.8 shard_map.170
  90.6 1.1 collective-permute-done.16
  91.8 0.9 add_convert_fusion
  92.7 3.7 %all-to-all-start.1 = ((bf16[8,16,2048]{2,1,0:T(8,128)(2,1)}), bf16[8,16,2048]{2,1,0:T(8,128)(2,1)S(1)}, u32[]{:S(2)}, u32[]{:S(2)}) async-start(bf16[8,16,2048]{2,1,0:T(8,128)(2,1)} %bitcast.51), calls=%async_computation.1 | async-start | bytes 1048576 | tf_op jit(solution)/shard_map/all_to_all | solution.py:627
  96.6 0.4 collective-permute-start.17
  96.9 1.0 collective-permute-done.28
  98.0 0.9 add_convert_fusion.8
  98.9 1.7 %collective-permute-start.29 = (bf16[256,128]{1,0:T(8,128)(2,1)S(1)}, bf16[256,128]{1,0:T(8,128)(2,1)S(1)}, u32[]{:S(2)}, u32[]{:S(2)}) collective-permute-start(bf16[256,128]{1,0:T(8,128)(2,1)S(1)} %add_convert_fusion.8), channel_id=1, source_target_pairs={{0,2},{1,3},{2,0},{3,1},{4,6},{5,7},{6,4},{7,5},{8,10},{9,11},{10,... | collective-permute-start | bytes 196616 | tf_op jit(solution)/shard_map/ppermute | solution.py:493
  100.7 7.4 %shard_map.171 = (bf16[256,384]{1,0:T(8,128)(2,1)S(1)}, bf16[256,384]{1,0:T(8,128)(2,1)}, f32[256,2048]{1,0:T(8,128)}, f32[2048,256]{1,0:T(8,128)}) custom-call(bf16[256,512]{1,0:T(8,128)(2,1)S(1)} %get-tuple-element.54.own, bf16[256,512]{1,0:T(8,128)(2,1)S(1)} %collective-permute-done.17.other, bf16[256,128]{1,0:T(8,128)(2,1)S(1)} %copy-done.6, ...), custom_call_target="tpu_custom_call" | custom-call | flops 100000 | bytes 100000 | tf_op jit(solution)/shard_map/pallas_call | solution.py:29
  108.1 1.5 %collective-permute-start.30 = (bf16[256,128]{1,0:T(8,128)(2,1)S(1)}, bf16[256,128]{1,0:T(8,128)(2,1)S(1)}, u32[]{:S(2)}, u32[]{:S(2)}) collective-permute-start(bf16[256,128]{1,0:T(8,128)(2,1)S(1)} %add_convert_fusion.7), channel_id=1, source_target_pairs={{0,4},{1,5},{2,6},{3,7},{4,0},{5,1},{6,2},{7,3},{8,12},{9,13},{10,... | collective-permute-start | bytes 196616 | tf_op jit(solution)/shard_map/ppermute | solution.py:493
  109.9 1.3 all-to-all-done.1.pieces
  111.2 1.0 copy-done.9
  112.2 1.0 copy-done.11
  113.3 0.9 copy-done.15
  114.2 6.4 %shard_map.172 = (bf16[4,144,256]{2,1,0:T(8,128)(2,1)S(1)}, bf16[4,144,256]{2,1,0:T(8,128)(2,1)S(1)}, f32[160,256]{1,0:T(8,128)S(1)}) custom-call(bf16[4,144,256]{2,1,0:T(8,128)(2,1)S(1)} %pad_maximum_fusion.refs_0_.refs_1_, bf16[4,144,256]{2,1,0:T(8,128)(2,1)S(1)} %collective-permute-done.3.refs_1_, bf16[1024,256]{1,0:T(8,128)(2,1)S(1)} %copy-done.9, ...), custom_call_target="tpu_custom_call" | custom-call | flops 100000 | bytes 100000 | tf_op jit(solution)/shard_map/pallas_call | solution.py:29
  120.8 1.4 collective-permute-start.31
  122.2 0.6 collective-permute-start.19
  122.8 1.5 %collective-permute-start.25 = (bf16[160,256]{1,0:T(8,128)(2,1)S(1)}, bf16[160,256]{1,0:T(8,128)(2,1)S(1)}, u32[]{:S(2)}, u32[]{:S(2)}) collective-permute-start(bf16[160,256]{1,0:T(8,128)(2,1)S(1)} %add_convert_fusion.5), channel_id=1, source_target_pairs={{0,2},{1,3},{2,0},{3,1},{4,6},{5,7},{6,4},{7,5},{8,10},{9,11},{10,... | collective-permute-start | bytes 245768 | tf_op jit(solution)/shard_map/ppermute | solution.py:493
  124.3 3.3 %collective-permute-done.31 = bf16[256,128]{1,0:T(8,128)(2,1)S(1)} collective-permute-done((bf16[256,128]{1,0:T(8,128)(2,1)S(1)}, bf16[256,128]{1,0:T(8,128)(2,1)S(1)}, u32[]{:S(2)}, u32[]{:S(2)}) %collective-permute-start.31) | collective-permute-done | bytes 65568 | tf_op jit(solution)/shard_map/ppermute | solution.py:493
  127.6 0.7 convert_add_fusion.1
  128.3 4.5 %collective-permute-done.25 = bf16[160,256]{1,0:T(8,128)(2,1)S(1)} collective-permute-done((bf16[160,256]{1,0:T(8,128)(2,1)S(1)}, bf16[160,256]{1,0:T(8,128)(2,1)S(1)}, u32[]{:S(2)}, u32[]{:S(2)}) %collective-permute-start.25) | collective-permute-done | bytes 81952 | tf_op jit(solution)/shard_map/ppermute | solution.py:493
  132.8 1.4 collective-permute-start.26
  134.3 2.0 %collective-permute-start.22 = (bf16[144,256]{1,0:T(8,128)(2,1)S(1)}, bf16[144,256]{1,0:T(8,128)(2,1)S(1)}, u32[]{:S(2)}, u32[]{:S(2)}) collective-permute-start(bf16[144,256]{1,0:T(8,128)(2,1)S(1)} %get-tuple-element.69), channel_id=1, source_target_pairs={{0,12},{1,13},{2,14},{3,15},{4,8},{5,9},{6,10},{7,11},{8,4},{9,5},... | collective-permute-start | bytes 221192 | tf_op jit(solution)/shard_map/ppermute | solution.py:493
  136.6 2.2 %collective-permute-start.20 = (bf16[144,256]{1,0:T(8,128)(2,1)S(1)}, bf16[144,256]{1,0:T(8,128)(2,1)S(1)}, u32[]{:S(2)}, u32[]{:S(2)}) collective-permute-start(bf16[144,256]{1,0:T(8,128)(2,1)S(1)} %get-tuple-element.71), channel_id=1, source_target_pairs={{0,4},{1,5},{2,6},{3,7},{4,0},{5,1},{6,2},{7,3},{8,12},{9,13},{10,... | collective-permute-start | bytes 221192 | tf_op jit(solution)/shard_map/ppermute | solution.py:493
  138.8 1.3 collective-permute-start.27
  140.2 1.1 convert_add_fusion
  141.2 1.0 shard_map.174
  142.3 3.4 %collective-permute-done.21.refs_2_ = bf16[144,256]{1,0:T(8,128)(2,1)S(1)} collective-permute-done((bf16[144,256]{1,0:T(8,128)(2,1)S(1)}, bf16[144,256]{1,0:T(8,128)(2,1)S(1)}, u32[]{:S(2)}, u32[]{:S(2)}) %collective-permute-start.21) | collective-permute-done | bytes 73760 | tf_op jit(solution)/shard_map/ppermute | solution.py:493
  145.7 0.9 shard_map.173
  146.9 0.7 add_bitcast_fusion
  (75 shorter events, 1.9 us)
Async XLA Ops:
  0.6 35.3 %copy-start = (bf16[16,64,256]{2,1,0:T(8,128)(2,1)S(1)}, bf16[16,64,256]{2,1,0:T(8,128)(2,1)}, u32[]{:S(2)}) copy-start(bf16[16,64,256]{2,1,0:T(8,128)(2,1)} %refs_7_.1) | copy-start | bytes 1572868
  0.6 36.7 %copy-start.1 = (bf16[1,256,2048]{2,1,0:T(8,128)(2,1)S(1)}, bf16[1,256,2048]{2,1,0:T(8,128)(2,1)}, u32[]{:S(2)}) copy-start(bf16[1,256,2048]{2,1,0:T(8,128)(2,1)} %param.19) | copy-start | bytes 3145732
  2.6 8.0 %collective-permute-start.2 = (bf16[144,256]{1,0:T(8,128)(2,1)}, bf16[144,256]{1,0:T(8,128)(2,1)S(1)}, u32[]{:S(2)}, u32[]{:S(2)}) collective-permute-start(bf16[144,256]{1,0:T(8,128)(2,1)} %get-tuple-element.38), channel_id=1, source_target_pairs={{0,12},{1,13},{2,14},{3,15},{4,8},{5,9},{6,10},{7,11},{8,4},{9,5},... | collective-permute-start | bytes 221192 | tf_op jit(solution)/shard_map/ppermute | solution.py:493
  7.6 6.4 %collective-permute-start.1 = (bf16[144,256]{1,0:T(8,128)(2,1)}, bf16[144,256]{1,0:T(8,128)(2,1)S(1)}, u32[]{:S(2)}, u32[]{:S(2)}) collective-permute-start(bf16[144,256]{1,0:T(8,128)(2,1)} %get-tuple-element.38), channel_id=1, source_target_pairs={{0,8},{1,9},{2,10},{3,11},{4,12},{5,13},{6,14},{7,15},{8,0},{9,1},... | collective-permute-start | bytes 221192 | tf_op jit(solution)/shard_map/ppermute | solution.py:493
  7.6 6.4 %collective-permute-start = (bf16[144,256]{1,0:T(8,128)(2,1)}, bf16[144,256]{1,0:T(8,128)(2,1)S(1)}, u32[]{:S(2)}, u32[]{:S(2)}) collective-permute-start(bf16[144,256]{1,0:T(8,128)(2,1)} %get-tuple-element.38), channel_id=1, source_target_pairs={{0,4},{1,5},{2,6},{3,7},{4,0},{5,1},{6,2},{7,3},{8,12},{9,13},{10,... | collective-permute-start | bytes 221192 | tf_op jit(solution)/shard_map/ppermute | solution.py:493
  15.0 1.0 copy-start.7
  16.9 24.0 %all-to-all-start = ((bf16[8,16,2048]{2,1,0:T(8,128)(2,1)}), bf16[8,16,2048]{2,1,0:T(8,128)(2,1)S(1)}, u32[]{:S(2)}, u32[]{:S(2)}) async-start(bf16[8,16,2048]{2,1,0:T(8,128)(2,1)} %shard_map.163), calls=%async_computation | async-start | bytes 1048576 | tf_op jit(solution)/shard_map/all_to_all | solution.py:538
  21.8 12.8 %collective-permute-start.3 = (bf16[4,144,256]{2,1,0:T(8,128)(2,1)S(1)}, bf16[4,144,256]{2,1,0:T(8,128)(2,1)S(1)}, u32[]{:S(2)}, u32[]{:S(2)}) collective-permute-start(bf16[4,144,256]{2,1,0:T(8,128)(2,1)S(1)} %pad_maximum_fusion.refs_0_.refs_1_), channel_id=1, source_target_pairs={{0,2},{1,3},{2,0},{3,1},{4,6},{5,7},{6,4},{7,5},{8,10},{9,11},{10,... | collective-permute-start | bytes 884744 | tf_op jit(solution)/shard_map/ppermute | solution.py:493
  35.9 1.5 %collective-permute-start.4 = (bf16[256,384]{1,0:T(8,128)(2,1)S(1)}, bf16[256,384]{1,0:T(8,128)(2,1)S(1)}, u32[]{:S(2)}, u32[]{:S(2)}) collective-permute-start(bf16[256,384]{1,0:T(8,128)(2,1)S(1)} %get-tuple-element.42), channel_id=1, source_target_pairs={{0,1},{1,0},{2,3},{3,2},{4,5},{5,4},{6,7},{7,6},{8,9},{9,8},{10,11... | collective-permute-start | bytes 589832 | tf_op jit(solution)/shard_map/ppermute | solution.py:493
  35.9 5.6 %collective-permute-start.6 = (bf16[16,64,256]{2,1,0:T(8,128)(2,1)S(1)}, bf16[16,64,256]{2,1,0:T(8,128)(2,1)S(1)}, u32[]{:S(2)}, u32[]{:S(2)}) collective-permute-start(bf16[16,64,256]{2,1,0:T(8,128)(2,1)S(1)} %copy-done), channel_id=1, source_target_pairs={{0,1},{1,0},{2,3},{3,2},{4,5},{5,4},{6,7},{7,6},{8,9},{9,8},{10,11... | collective-permute-start | bytes 1572872 | tf_op jit(solution)/shard_map/ppermute | solution.py:493
  37.4 1.2 copy-start.2
  40.9 2.2 %collective-permute-start.5 = (bf16[128,2048]{1,0:T(8,128)(2,1)S(1)}, bf16[128,2048]{1,0:T(8,128)(2,1)S(1)}, u32[]{:S(2)}, u32[]{:S(2)}) collective-permute-start(bf16[128,2048]{1,0:T(8,128)(2,1)S(1)} %bitcast.38), channel_id=1, source_target_pairs={{0,1},{1,0},{2,3},{3,2},{4,5},{5,4},{6,7},{7,6},{8,9},{9,8},{10,11... | collective-permute-start | bytes 1572872 | tf_op jit(solution)/shard_map/ppermute | solution.py:493
  41.1 2.0 %collective-permute-start.7 = (bf16[256,256]{1,0:T(8,128)(2,1)S(1)}, bf16[256,256]{1,0:T(8,128)(2,1)S(1)}, u32[]{:S(2)}, u32[]{:S(2)}) collective-permute-start(bf16[256,256]{1,0:T(8,128)(2,1)S(1)} %get-tuple-element.46), channel_id=1, source_target_pairs={{0,1},{1,0},{2,3},{3,2},{4,5},{5,4},{6,7},{7,6},{8,9},{9,8},{10,11... | collective-permute-start | bytes 393224 | tf_op jit(solution)/shard_map/ppermute | solution.py:493
  46.2 17.3 %copy-start.6 = (bf16[256,128]{1,0:T(8,128)(2,1)S(1)}, bf16[256,128]{1,0:T(8,128)(2,1)}, u32[]{:S(2)}) copy-start(bf16[256,128]{1,0:T(8,128)(2,1)} %head.1) | copy-start | bytes 196612
  46.2 17.3 %copy-start.17 = (f32[128,128]{1,0:T(8,128)S(1)}, f32[128,128]{1,0:T(8,128)}, u32[]{:S(2)}) copy-start(f32[128,128]{1,0:T(8,128)} %refs_5_.1) | copy-start | bytes 196612
  46.3 8.4 %collective-permute-start.8 = (bf16[4,128,256]{2,1,0:T(8,128)(2,1)S(1)}, bf16[4,128,256]{2,1,0:T(8,128)(2,1)S(1)}, u32[]{:S(2)}, u32[]{:S(2)}) collective-permute-start(bf16[4,128,256]{2,1,0:T(8,128)(2,1)S(1)} %shard_map.167), channel_id=1, source_target_pairs={{0,2},{1,3},{2,0},{3,1},{4,6},{5,7},{6,4},{7,5},{8,10},{9,11},{10,... | collective-permute-start | bytes 786440 | tf_op jit(solution)/shard_map/ppermute | solution.py:493
  54.8 6.5 %collective-permute-start.11 = (bf16[128,256]{1,0:T(8,128)(2,1)S(1)}, bf16[128,256]{1,0:T(8,128)(2,1)S(1)}, u32[]{:S(2)}, u32[]{:S(2)}) collective-permute-start(bf16[128,256]{1,0:T(8,128)(2,1)S(1)} %get-tuple-element.73), channel_id=1, source_target_pairs={{0,12},{1,13},{2,14},{3,15},{4,8},{5,9},{6,10},{7,11},{8,4},{9,5},... | collective-permute-start | bytes 196616 | tf_op jit(solution)/shard_map/ppermute | solution.py:493
  58.1 5.4 %collective-permute-start.10 = (bf16[128,256]{1,0:T(8,128)(2,1)S(1)}, bf16[128,256]{1,0:T(8,128)(2,1)S(1)}, u32[]{:S(2)}, u32[]{:S(2)}) collective-permute-start(bf16[128,256]{1,0:T(8,128)(2,1)S(1)} %get-tuple-element.74), channel_id=1, source_target_pairs={{0,8},{1,9},{2,10},{3,11},{4,12},{5,13},{6,14},{7,15},{8,0},{9,1},... | collective-permute-start | bytes 196616 | tf_op jit(solution)/shard_map/ppermute | solution.py:493
  58.1 5.4 %collective-permute-start.9 = (bf16[128,256]{1,0:T(8,128)(2,1)S(1)}, bf16[128,256]{1,0:T(8,128)(2,1)S(1)}, u32[]{:S(2)}, u32[]{:S(2)}) collective-permute-start(bf16[128,256]{1,0:T(8,128)(2,1)S(1)} %get-tuple-element.75), channel_id=1, source_target_pairs={{0,4},{1,5},{2,6},{3,7},{4,0},{5,1},{6,2},{7,3},{8,12},{9,13},{10,... | collective-permute-start | bytes 196616 | tf_op jit(solution)/shard_map/ppermute | solution.py:493
  64.0 7.5 %copy-start.16 = (f32[256,128]{1,0:T(8,128)}, f32[256,128]{1,0:T(8,128)S(1)}, u32[]{:S(2)}) copy-start(f32[256,128]{1,0:T(8,128)S(1)} %get-tuple-element.68) | copy-start | bytes 393220
  64.0 5.8 %collective-permute-start.14 = (bf16[128,128]{1,0:T(8,128)(2,1)S(1)}, bf16[128,128]{1,0:T(8,128)(2,1)S(1)}, u32[]{:S(2)}, u32[]{:S(2)}) collective-permute-start(bf16[128,128]{1,0:T(8,128)(2,1)S(1)} %get-tuple-element.47), channel_id=1, source_target_pairs={{0,12},{1,13},{2,14},{3,15},{4,8},{5,9},{6,10},{7,11},{8,4},{9,5},... | collective-permute-start | bytes 98312 | tf_op jit(solution)/shard_map/ppermute | solution.py:493
  66.7 4.8 %collective-permute-start.13 = (bf16[128,128]{1,0:T(8,128)(2,1)S(1)}, bf16[128,128]{1,0:T(8,128)(2,1)S(1)}, u32[]{:S(2)}, u32[]{:S(2)}) collective-permute-start(bf16[128,128]{1,0:T(8,128)(2,1)S(1)} %get-tuple-element.47), channel_id=1, source_target_pairs={{0,8},{1,9},{2,10},{3,11},{4,12},{5,13},{6,14},{7,15},{8,0},{9,1},... | collective-permute-start | bytes 98312 | tf_op jit(solution)/shard_map/ppermute | solution.py:493
  66.7 4.8 %collective-permute-start.12 = (bf16[128,128]{1,0:T(8,128)(2,1)S(1)}, bf16[128,128]{1,0:T(8,128)(2,1)S(1)}, u32[]{:S(2)}, u32[]{:S(2)}) collective-permute-start(bf16[128,128]{1,0:T(8,128)(2,1)S(1)} %get-tuple-element.47), channel_id=1, source_target_pairs={{0,4},{1,5},{2,6},{3,7},{4,0},{5,1},{6,2},{7,3},{8,12},{9,13},{10,... | collective-permute-start | bytes 98312 | tf_op jit(solution)/shard_map/ppermute | solution.py:493
  71.5 5.0 %collective-permute-start.15 = (bf16[4,128,128]{2,1,0:T(8,128)(2,1)S(1)}, bf16[4,128,128]{2,1,0:T(8,128)(2,1)S(1)}, u32[]{:S(2)}, u32[]{:S(2)}) collective-permute-start(bf16[4,128,128]{2,1,0:T(8,128)(2,1)S(1)} %pad_maximum_fusion.1.refs_2_), channel_id=1, source_target_pairs={{0,2},{1,3},{2,0},{3,1},{4,6},{5,7},{6,4},{7,5},{8,10},{9,11},{10,... | collective-permute-start | bytes 393224 | tf_op jit(solution)/shard_map/ppermute | solution.py:493
  88.9 1.0 copy-start.4
  89.8 2.8 %copy-start.8 = (bf16[1024,256]{1,0:T(8,128)(2,1)}, bf16[1024,256]{1,0:T(8,128)(2,1)S(1)}, u32[]{:S(2)}) copy-start(bf16[1024,256]{1,0:T(8,128)(2,1)S(1)} %get-tuple-element.48.refs_2_) | copy-start | bytes 1572868
  89.8 2.8 %copy-start.10 = (f32[1024,32]{1,0:T(8,128)}, f32[1024,32]{1,0:T(8,128)S(1)}, u32[]{:S(2)}) copy-start(f32[1024,32]{1,0:T(8,128)S(1)} %get-tuple-element.49.refs_3_) | copy-start | bytes 393220
  89.8 10.8 %copy-start.3 = (bf16[1,2048,256]{2,1,0:T(8,128)(2,1)S(1)}, bf16[1,2048,256]{2,1,0:T(8,128)(2,1)}, u32[]{:S(2)}) copy-start(bf16[1,2048,256]{2,1,0:T(8,128)(2,1)} %param.20) | copy-start | bytes 3145732
  89.8 1.9 %collective-permute-start.16 = (bf16[128,2048]{1,0:T(8,128)(2,1)S(1)}, bf16[128,2048]{1,0:T(8,128)(2,1)S(1)}, u32[]{:S(2)}, u32[]{:S(2)}) collective-permute-start(bf16[128,2048]{1,0:T(8,128)(2,1)S(1)} %get-tuple-element.51), channel_id=1, source_target_pairs={{0,1},{1,0},{2,3},{3,2},{4,5},{5,4},{6,7},{7,6},{8,9},{9,8},{10,11... | collective-permute-start | bytes 1572872 | tf_op jit(solution)/shard_map/ppermute | solution.py:493
  90.6 2.1 %copy-start.20 = (bf16[256,512]{1,0:T(8,128)(2,1)}, bf16[256,512]{1,0:T(8,128)(2,1)S(1)}, u32[]{:S(2)}) copy-start(bf16[256,512]{1,0:T(8,128)(2,1)S(1)} %get-tuple-element.55) | copy-start | bytes 786436
  92.7 18.5 %all-to-all-start.1 = ((bf16[8,16,2048]{2,1,0:T(8,128)(2,1)}), bf16[8,16,2048]{2,1,0:T(8,128)(2,1)S(1)}, u32[]{:S(2)}, u32[]{:S(2)}) async-start(bf16[8,16,2048]{2,1,0:T(8,128)(2,1)} %bitcast.51), calls=%async_computation.1 | async-start | bytes 1048576 | tf_op jit(solution)/shard_map/all_to_all | solution.py:627
  96.4 1.6 %collective-permute-start.28 = (f32[256,128]{1,0:T(8,128)}, f32[256,128]{1,0:T(8,128)S(1)}, u32[]{:S(2)}, u32[]{:S(2)}) collective-permute-start(f32[256,128]{1,0:T(8,128)} %copy-done.16), channel_id=1, source_target_pairs={{0,1},{1,0},{2,3},{3,2},{4,5},{5,4},{6,7},{7,6},{8,9},{9,8},{10,11... | collective-permute-start | bytes 393224 | tf_op jit(solution)/shard_map/ppermute | solution.py:493
  96.6 4.1 %collective-permute-start.17 = (bf16[256,512]{1,0:T(8,128)(2,1)}, bf16[256,512]{1,0:T(8,128)(2,1)S(1)}, u32[]{:S(2)}, u32[]{:S(2)}) collective-permute-start(bf16[256,512]{1,0:T(8,128)(2,1)} %copy-done.20), channel_id=1, source_target_pairs={{0,1},{1,0},{2,3},{3,2},{4,5},{5,4},{6,7},{7,6},{8,9},{9,8},{10,11... | collective-permute-start | bytes 786440 | tf_op jit(solution)/shard_map/ppermute | solution.py:493
  98.9 9.2 %collective-permute-start.29 = (bf16[256,128]{1,0:T(8,128)(2,1)S(1)}, bf16[256,128]{1,0:T(8,128)(2,1)S(1)}, u32[]{:S(2)}, u32[]{:S(2)}) collective-permute-start(bf16[256,128]{1,0:T(8,128)(2,1)S(1)} %add_convert_fusion.8), channel_id=1, source_target_pairs={{0,2},{1,3},{2,0},{3,1},{4,6},{5,7},{6,4},{7,5},{8,10},{9,11},{10,... | collective-permute-start | bytes 196616 | tf_op jit(solution)/shard_map/ppermute | solution.py:493
  108.1 1.6 %copy-start.14 = (bf16[256,384]{1,0:T(8,128)(2,1)}, bf16[256,384]{1,0:T(8,128)(2,1)S(1)}, u32[]{:S(2)}) copy-start(bf16[256,384]{1,0:T(8,128)(2,1)S(1)} %get-tuple-element.57.refs_4_) | copy-start | bytes 589828
  108.1 3.1 %collective-permute-start.18 = (bf16[256,384]{1,0:T(8,128)(2,1)}, bf16[256,384]{1,0:T(8,128)(2,1)S(1)}, u32[]{:S(2)}, u32[]{:S(2)}) collective-permute-start(bf16[256,384]{1,0:T(8,128)(2,1)} %get-tuple-element.58), channel_id=1, source_target_pairs={{0,1},{1,0},{2,3},{3,2},{4,5},{5,4},{6,7},{7,6},{8,9},{9,8},{10,11... | collective-permute-start | bytes 589832 | tf_op jit(solution)/shard_map/ppermute | solution.py:493
  108.1 12.6 %collective-permute-start.30 = (bf16[256,128]{1,0:T(8,128)(2,1)S(1)}, bf16[256,128]{1,0:T(8,128)(2,1)S(1)}, u32[]{:S(2)}, u32[]{:S(2)}) collective-permute-start(bf16[256,128]{1,0:T(8,128)(2,1)S(1)} %add_convert_fusion.7), channel_id=1, source_target_pairs={{0,4},{1,5},{2,6},{3,7},{4,0},{5,1},{6,2},{7,3},{8,12},{9,13},{10,... | collective-permute-start | bytes 196616 | tf_op jit(solution)/shard_map/ppermute | solution.py:493
  109.7 30.5 %collective-permute-start.23 = (bf16[16,64,256]{2,1,0:T(8,128)(2,1)}, bf16[16,64,256]{2,1,0:T(8,128)(2,1)S(1)}, u32[]{:S(2)}, u32[]{:S(2)}) collective-permute-start(bf16[16,64,256]{2,1,0:T(8,128)(2,1)} %get-tuple-element.64), channel_id=1, source_target_pairs={{0,1},{1,0},{2,3},{3,2},{4,5},{5,4},{6,7},{7,6},{8,9},{9,8},{10,11... | collective-permute-start | bytes 1572872 | tf_op jit(solution)/shard_map/ppermute | solution.py:493
  111.2 1.0 copy-start.9
  112.2 1.0 copy-start.11
  113.3 0.9 copy-start.15
  114.2 25.9 %copy-start.5 = (f32[16,64,256]{2,1,0:T(8,128)S(1)}, f32[16,64,256]{2,1,0:T(8,128)}, u32[]{:S(2)}) copy-start(f32[16,64,256]{2,1,0:T(8,128)} %copy-done.4) | copy-start | bytes 3145732
  120.6 2.1 %collective-permute-start.24 = (f32[160,256]{1,0:T(8,128)S(1)}, f32[160,256]{1,0:T(8,128)S(1)}, u32[]{:S(2)}, u32[]{:S(2)}) collective-permute-start(f32[160,256]{1,0:T(8,128)S(1)} %get-tuple-element.67), channel_id=1, source_target_pairs={{0,1},{1,0},{2,3},{3,2},{4,5},{5,4},{6,7},{7,6},{8,9},{9,8},{10,11... | collective-permute-start | bytes 491528 | tf_op jit(solution)/shard_map/ppermute | solution.py:493
  120.8 6.9 %collective-permute-start.31 = (bf16[256,128]{1,0:T(8,128)(2,1)S(1)}, bf16[256,128]{1,0:T(8,128)(2,1)S(1)}, u32[]{:S(2)}, u32[]{:S(2)}) collective-permute-start(bf16[256,128]{1,0:T(8,128)(2,1)S(1)} %add_convert_fusion.6), channel_id=1, source_target_pairs={{0,8},{1,9},{2,10},{3,11},{4,12},{5,13},{6,14},{7,15},{8,0},{9,1},... | collective-permute-start | bytes 196616 | tf_op jit(solution)/shard_map/ppermute | solution.py:493
  122.2 12.0 %collective-permute-start.19 = (bf16[4,144,256]{2,1,0:T(8,128)(2,1)S(1)}, bf16[4,144,256]{2,1,0:T(8,128)(2,1)S(1)}, u32[]{:S(2)}, u32[]{:S(2)}) collective-permute-start(bf16[4,144,256]{2,1,0:T(8,128)(2,1)S(1)} %get-tuple-element.60), channel_id=1, source_target_pairs={{0,2},{1,3},{2,0},{3,1},{4,6},{5,7},{6,4},{7,5},{8,10},{9,11},{10,... | collective-permute-start | bytes 884744 | tf_op jit(solution)/shard_map/ppermute | solution.py:493
  122.8 10.0 %collective-permute-start.25 = (bf16[160,256]{1,0:T(8,128)(2,1)S(1)}, bf16[160,256]{1,0:T(8,128)(2,1)S(1)}, u32[]{:S(2)}, u32[]{:S(2)}) collective-permute-start(bf16[160,256]{1,0:T(8,128)(2,1)S(1)} %add_convert_fusion.5), channel_id=1, source_target_pairs={{0,2},{1,3},{2,0},{3,1},{4,6},{5,7},{6,4},{7,5},{8,10},{9,11},{10,... | collective-permute-start | bytes 245768 | tf_op jit(solution)/shard_map/ppermute | solution.py:493
  132.8 5.9 %collective-permute-start.26 = (bf16[160,256]{1,0:T(8,128)(2,1)S(1)}, bf16[160,256]{1,0:T(8,128)(2,1)S(1)}, u32[]{:S(2)}, u32[]{:S(2)}) collective-permute-start(bf16[160,256]{1,0:T(8,128)(2,1)S(1)} %add_convert_fusion.4), channel_id=1, source_target_pairs={{0,4},{1,5},{2,6},{3,7},{4,0},{5,1},{6,2},{7,3},{8,12},{9,13},{10,... | collective-permute-start | bytes 245768 | tf_op jit(solution)/shard_map/ppermute | solution.py:493
  134.3 8.0 %collective-permute-start.22 = (bf16[144,256]{1,0:T(8,128)(2,1)S(1)}, bf16[144,256]{1,0:T(8,128)(2,1)S(1)}, u32[]{:S(2)}, u32[]{:S(2)}) collective-permute-start(bf16[144,256]{1,0:T(8,128)(2,1)S(1)} %get-tuple-element.69), channel_id=1, source_target_pairs={{0,12},{1,13},{2,14},{3,15},{4,8},{5,9},{6,10},{7,11},{8,4},{9,5},... | collective-permute-start | bytes 221192 | tf_op jit(solution)/shard_map/ppermute | solution.py:493
  136.4 9.3 %collective-permute-start.21 = (bf16[144,256]{1,0:T(8,128)(2,1)S(1)}, bf16[144,256]{1,0:T(8,128)(2,1)S(1)}, u32[]{:S(2)}, u32[]{:S(2)}) collective-permute-start(bf16[144,256]{1,0:T(8,128)(2,1)S(1)} %get-tuple-element.70), channel_id=1, source_target_pairs={{0,8},{1,9},{2,10},{3,11},{4,12},{5,13},{6,14},{7,15},{8,0},{9,1},... | collective-permute-start | bytes 221192 | tf_op jit(solution)/shard_map/ppermute | solution.py:493
  136.6 9.1 %collective-permute-start.20 = (bf16[144,256]{1,0:T(8,128)(2,1)S(1)}, bf16[144,256]{1,0:T(8,128)(2,1)S(1)}, u32[]{:S(2)}, u32[]{:S(2)}) collective-permute-start(bf16[144,256]{1,0:T(8,128)(2,1)S(1)} %get-tuple-element.71), channel_id=1, source_target_pairs={{0,4},{1,5},{2,6},{3,7},{4,0},{5,1},{6,2},{7,3},{8,12},{9,13},{10,... | collective-permute-start | bytes 221192 | tf_op jit(solution)/shard_map/ppermute | solution.py:493
  138.8 8.1 %collective-permute-start.27 = (bf16[160,256]{1,0:T(8,128)(2,1)S(1)}, bf16[160,256]{1,0:T(8,128)(2,1)S(1)}, u32[]{:S(2)}, u32[]{:S(2)}) collective-permute-start(bf16[160,256]{1,0:T(8,128)(2,1)S(1)} %add_convert_fusion.3), channel_id=1, source_target_pairs={{0,8},{1,9},{2,10},{3,11},{4,12},{5,13},{6,14},{7,15},{8,0},{9,1},... | collective-permute-start | bytes 245768 | tf_op jit(solution)/shard_map/ppermute | solution.py:493
  140.1 5.6 %copy-start.12 = (bf16[8,256,20]{1,0,2:T(8,128)(2,1)S(1)}, bf16[8,256,20]{1,0,2:T(8,128)(2,1)}, u32[]{:S(2)}) copy-start(bf16[8,256,20]{1,0,2:T(8,128)(2,1)} %param.16) | copy-start | bytes 245764
  140.1 5.6 %copy-start.13 = (bf16[128,256]{1,0:T(8,128)(2,1)S(1)}, bf16[128,256]{1,0:T(8,128)(2,1)}, u32[]{:S(2)}) copy-start(bf16[128,256]{1,0:T(8,128)(2,1)} %refs_4_.9) | copy-start | bytes 196612
  140.1 5.6 %copy-start.18 = (f32[32,128]{1,0:T(8,128)S(1)}, f32[32,128]{1,0:T(8,128)}, u32[]{:S(2)}) copy-start(f32[32,128]{1,0:T(8,128)} %get-tuple-element.61.refs_6_) | copy-start | bytes 49156
  140.1 5.6 %copy-start.19 = (s32[128]{0:T(128)S(1)}, s32[128]{0:T(128)}, u32[]{:S(2)}) copy-start(s32[128]{0:T(128)} %param.12) | copy-start | bytes 1540

commit v4 on v3

--- a/solution.py
+++ b/solution.py
@@ -12,7 +12,7 @@
 AUX = 32
 bf16 = jnp.bfloat16
 f32 = jnp.float32
-CHUNK = 512
+CHUNK = 256
 FIRST, SMALL, BIG = 60, 16, 32
 COST = 100000
 
@@ -199,7 +199,7 @@
 def scenario_forward_kernel(hidden, own, other, widen, narrow, out_own, out_other, gated):
     half, width = out_own.shape
     total = widen.shape[1]
-    size, chunk = min(TILE, total), min(half, CHUNK)
+    size, chunk = min(TILE, total), min(half, max(CHUNK, half // 2))
 
     def tile(j, _):
         lanes = hidden_lanes(j, size)
@@ -212,9 +212,15 @@
                 gated[spot, lanes] = (gate * (linear * sigmoid(linear))).astype(bf16)
         return 0
 
-    lax.fori_loop(0, total // size, tile, 0)
+    lax.fori_loop(0, total // size, tile, 0, unroll=True)
     out_own[...] = mm(gated[:half, :], narrow[...]).astype(bf16)
     out_other[...] = mm(gated[half:, :], narrow[...]).astype(bf16)
+
+
+def put(outs, split, k, b, value, rows=slice(None), lanes=slice(None)):
+    out, at, count = (outs[0], b, split) if b < split else (outs[1], b - split, None)
+    count = count or outs[1].shape[0] // (outs[0].shape[0] // split)
+    out[k * count + at, rows, lanes] = value
 
 
 def unpack(pieces, turn, xs, gates, xt=None):
@@ -242,17 +248,17 @@
         w2[(2 * k + 1) * part : 2 * (k + 1) * part, :] = jnp.where(core == 0, theirs, mine)
 
 
-def shared_forward_kernel(n, start, gate_rows, gate_count, depth, *refs):
+def shared_forward_kernel(n, start, split, gate_rows, gate_count, depth, *refs):
     own, pieces = refs[0], refs[1 : n + 1]
-    w1a, w1b, w2a, w2b, from_own, from_other, out, xs, gates, w1, w2, gated = refs[n + 1 :]
+    w1a, w1b, w2a, w2b, from_own, from_other, *outs, xs, gates, w1, w2, gated = refs[n + 1 :]
     join_weights(w1a, w1b, w2a, w2b, w1, w2)
     unpack(pieces, turn_matrix(w1.shape[0], depth, own_core()), xs, gates)
-    count, rows, _ = out.shape
-    m = pieces[0].shape[0]
+    m, packed, _ = pieces[0].shape
+    count, rows = n * m, packed - AUX // 2
     capacity = from_own.shape[0] // (w1.shape[0] // (2 * depth))
     places = own_place([own], gate_count)
     total = count * rows
-    size, chunk = min(TILE, w1.shape[1]), min(total, CHUNK)
+    size, chunk = min(TILE, w1.shape[1]), min(total, max(CHUNK, total // 4))
 
     def tile(j, _):
         lanes = hidden_lanes(j, size)
@@ -264,7 +270,7 @@
             gated[spot, lanes] = (mm(gates[spot, :], picks) * active).astype(bf16)
         return 0
 
-    lax.fori_loop(0, w1.shape[1] // size, tile, 0)
+    lax.fori_loop(0, w1.shape[1] // size, tile, 0, unroll=True)
     for at in range(0, total, chunk):
         mixed = mm(gated[at : at + chunk, :], w2[...])
         for piece in range(at // rows, (at + chunk) // rows):
@@ -273,7 +279,7 @@
             value = mixed[piece * rows - at : (piece + 1) * rows - at]
             for (owner, _), source in zip(places, (from_own, from_other)):
                 value += mm(selector(side, gate_count, owner, capacity), source[spot, :], 0, 0)
-            out[piece] = value.astype(bf16)
+            put(outs, split, piece // m, piece % m, value.astype(bf16))
 
 
 def softmax(v):
@@ -309,7 +315,7 @@
             at = (k * m + b) * rows
             os[at : at + rows, :] = mm(logits[k][b], head[...], 1, 1).astype(bf16)
     total = n * m * rows
-    size, chunk = min(TILE, w1.shape[1]), min(total, CHUNK)
+    size, chunk = weighed.shape[1], min(total, max(CHUNK, total // 4))
     half, part = keep.shape[0], keep2.shape[1]
     mix[...] = jnp.zeros_like(mix)
 
@@ -323,7 +329,16 @@
             gate = mm(gates[spot, :], picks)
             sig = sigmoid(linear)
             active = linear * sig
-            mix[spot, :] += mm((hidden * active).astype(bf16), picks, 1, 1)
+            product = hidden * active
+            if gate_rows % 128 == 0:
+                column = lax.broadcasted_iota(jnp.int32, (chunk, AUX), 1) - j * (size // gate_rows)
+                dots = jnp.zeros((chunk, AUX), f32)
+                for e in range(size // gate_rows):
+                    part_of = product[:, e * gate_rows : (e + 1) * gate_rows]
+                    dots = jnp.where(column == e, jnp.sum(part_of, axis=1, keepdims=True), dots)
+            else:
+                dots = mm(product.astype(bf16), picks, 1, 1)
+            mix[spot, :] += dots
             slope = sig + active * (1.0 - sig)
             linear_grad[spot, lanes] = (gate * hidden * slope).astype(bf16)
             weighed[spot, :] = (gate * active).astype(bf16)
@@ -339,7 +354,7 @@
             sent2[k] = jnp.where(core == 0, high, low).astype(bf16)
         return 0
 
-    lax.fori_loop(0, w1.shape[1] // size, tile, 0)
+    lax.fori_loop(0, w1.shape[1] // size, tile, 0, unroll=True)
     chunk = min(total, 1024)
     for at in range(0, total, chunk):
         spot = slice(at, at + chunk)
@@ -358,16 +373,14 @@
     xs[half:, :] = other[...]
     os[...] = mm(xs[:, width + 128 :], head[...], 1, 1).astype(bf16)
     mix[...] = jnp.zeros_like(mix)
-    size, chunk = min(TILE, total), min(2 * half, CHUNK)
+    size, chunk = min(TILE, total), min(2 * half, max(CHUNK, half // 2))
     for at in range(0, 2 * half, chunk):
         xt[:, at : at + chunk] = mm(eye(width), xs[at : at + chunk, :width], 1, 1).astype(bf16)
 
     def tile(j, _):
         lanes = hidden_lanes(j, size)
         column = (j * size) // hidden_units
-        picks = (
-            lax.broadcasted_iota(jnp.int32, (size, mix.shape[1]), 1) == column
-        ).astype(f32).astype(bf16)
+        lane = lax.broadcasted_iota(jnp.int32, (chunk, mix.shape[1]), 1)
         for at in range(0, 2 * half, chunk):
             spot = slice(at, at + chunk)
             x = xs[spot, :]
@@ -376,7 +389,8 @@
             hidden = mm(os[spot, :], narrow[lanes, :], 1, 1)
             sig = sigmoid(linear)
             active = linear * sig
-            mix[spot, :] += mm((hidden * active).astype(bf16), picks)
+            product = jnp.sum(hidden * active, axis=1, keepdims=True)
+            mix[spot, :] += jnp.where(lane == column, product, 0.0)
             slope = sig + active * (1.0 - sig)
             linear_grad[spot, lanes] = (gate * hidden * slope).astype(bf16)
             weighed[spot, :] = (gate * active).astype(bf16)
@@ -384,47 +398,61 @@
         dnarrow[lanes, :] = mm(weighed[...], os[...], 0, 0)
         return 0
 
-    lax.fori_loop(0, total // size, tile, 0)
+    lax.fori_loop(0, total // size, tile, 0, unroll=True)
     for at, out in ((0, out_own), (half, out_other)):
         out[:, :width] = mm(linear_grad[at : at + half, :], widen[...], 1, 1).astype(bf16)
         out[:, width:] = mix[at : at + half, :].astype(bf16)
 
 
-def scatter_kernel(n, gate_count, *refs):
+def scatter_kernel(n, split, gate_count, *refs):
     pieces = refs[:n]
-    dx, mix, from_own, from_other, home, away, gate_part = refs[n:]
+    dx, mix, from_own, from_other, home, *away, mix_out = refs[n:]
     m, packed, width = pieces[0].shape
     rows = packed - AUX // 2
     capacity = from_own.shape[0] // (n * m)
     places = own_place(pieces, gate_count)
-    live = lax.broadcasted_iota(jnp.int32, (rows, AUX), 1) < gate_count
-    total = jnp.zeros(gate_part.shape, f32)
+    picks = [gate_picks(first) for _, first in places]
     for k in range(n):
         for b in range(m):
             piece = k * m + b
-            out, to = (home, piece) if piece < home.shape[0] else (away, piece - home.shape[0])
             spot = slice(piece * capacity, (piece + 1) * capacity)
             full = slice(piece * rows, (piece + 1) * rows)
             side = side_of(pieces[k][b, rows:, :])
-            value, dots = dx[full, :].astype(f32), mix[full, :].astype(f32)
-            for (owner, first), source in zip(places, (from_own, from_other)):
-                extra = mm(selector(side, gate_count, owner, capacity), source[spot, :], 0, 0)
+            value = dx[full, :].astype(f32)
+            dots = mm(eye(AUX), mix[full, :].astype(bf16), 1, 1)
+            for (owner, _), pick, source in zip(places, picks, (from_own, from_other)):
+                sel = selector(side, gate_count, owner, capacity)
+                extra = mm(sel, source[spot, :], 0, 0)
                 value += extra[:, :width]
-                dots += mm(extra[:, width:].astype(bf16), gate_picks(first), 1, 1)
-            out[to, :rows, :] = value.astype(bf16)
-            turned = mm(eye(AUX), dots.astype(bf16), 1, 1).astype(bf16)
-            out[to, rows:, :rows] = turned[: AUX // 2]
-            out[to, rows:, rows:] = turned[AUX // 2 :]
-            share = mm(side, eye(AUX), 0, 0)
-            share = jnp.where(live, share, 0.0)
-            share = share / jnp.sum(share, axis=1, keepdims=True)
-            score = share * (dots - jnp.sum(share * dots, axis=1, keepdims=True))
-            score = mm(eye(AUX), score.astype(bf16), 1, 1)[:gate_count]
-            ids = side[gate_count : gate_count + 1, :].astype(f32)
-            wide = score[:, None, :] * by_scenario(ids.astype(jnp.int32), total.shape[0] // gate_count)
-            wide = wide.reshape(total.shape[0], rows).astype(bf16)
+                dots += mm(pick, extra[:, width:].astype(bf16), 1, 1)
+            turned = dots.astype(bf16)
+            mix_out[piece] = turned
+            outs, at, line = (away, k - 1, split) if k else ([home], 0, m)
+            put(outs, line, at, b, value.astype(bf16), slice(rows))
+            put(outs, line, at, b, turned[: AUX // 2], slice(rows, None), slice(rows))
+            put(outs, line, at, b, turned[AUX // 2 :], slice(rows, None), slice(rows, None))
+
+
+def gate_kernel(n, gate_count, *refs):
+    pieces, mix, out = refs[:n], refs[n], refs[n + 1]
+    m, packed, _ = pieces[0].shape
+    rows = packed - AUX // 2
+    live = lax.broadcasted_iota(jnp.int32, (AUX, rows), 0) < gate_count
+    count = out.shape[0] // 2
+    total = jnp.zeros((count, 2 * out.shape[1]), f32)
+    for k in range(n):
+        for b in range(m):
+            side = side_of(pieces[k][b, rows:, :]).astype(f32)
+            dots = mix[k * m + b].astype(f32)
+            share = jnp.where(live, side, 0.0)
+            share = share / jnp.sum(share, axis=0, keepdims=True)
+            score = share * (dots - jnp.sum(share * dots, axis=0, keepdims=True))
+            ids = side[gate_count : gate_count + 1, :].astype(jnp.int32)
+            wide = score[:gate_count, None, :] * by_scenario(ids, count // gate_count)
+            wide = wide.reshape(count, rows).astype(bf16)
             total = total + mm(wide, pieces[k][b, :rows, :])
-    gate_part[...] = total
+    out[:count, :] = total[:, : out.shape[1]]
+    out[count:, :] = total[:, out.shape[1] :]
 
 
 def final_kernel(count, gate_count, *refs):
@@ -497,10 +525,11 @@
         stacked = jnp.stack(column)
         return [stacked] + [send(stacked, 2 * a) for a in range(1, near)]
 
-    def total_of(value):
-        value = value + send(value, 1)
-        mask = 2
-        while mask < devices:
+    def total_of(value, mask, end):
+        if mask == 1:
+            value = value + send(value, 1)
+            mask = 2
+        while mask < end:
             half = value.astype(bf16)
             value = half.astype(f32) + send(half, mask).astype(f32)
             mask *= 2
@@ -523,16 +552,16 @@
         [pltpu.VMEM((AUX, rows), f32)],
         limit=FIRST,
     )
-    column = [pack] + [send(pack, 2 * near * b) for b in range(1, far)]
-    stacked = jnp.stack(column)
-    stacked, expand = lax.optimization_barrier((stacked, expand))
-    got = [stacked] + [send(stacked, 2 * a) for a in range(1, near)]
     (pieces,) = call(
         functools.partial(tile_kernel, tiled),
         [struct((chips, depth, hidden_chip), bf16)],
         [expand],
-        limit=8,
-    )
+        limit=SMALL,
+    )
+    column = [pack] + [send(pack, 2 * near * b) for b in range(1, far)]
+    stacked = jnp.stack(column)
+    stacked, pieces = lax.optimization_barrier((stacked, pieces))
+    got = [stacked] + [send(stacked, 2 * a) for a in range(1, near)]
     w2a = reduce
     w2b = send(reduce, 1)
     w1a = lax.all_to_all(
@@ -561,11 +590,13 @@
         pltpu.VMEM((hidden_chip, width), bf16),
     ]
 
-    def forward(pieces, start):
+    def forward(pieces, start, lines):
         count = len(pieces) * far
-        (out,) = call(
-            functools.partial(shared_forward_kernel, len(pieces), start, lanes, gates, depth),
-            [struct((count, rows, width), bf16)],
+        return call(
+            functools.partial(
+                shared_forward_kernel, len(pieces), start, lines[0], lanes, gates, depth
+            ),
+            [struct((len(pieces) * line, rows, width), bf16) for line in lines],
             [got[0], *pieces, *weights, out_own, out_other],
             scratch=[
                 pltpu.VMEM((count * rows, width), bf16),
@@ -575,15 +606,26 @@
             ],
             limit=BIG,
         )
-        return out
-
-    away = forward(got[1:], far)
-    home = forward(got[:1], 0)
-    total = home.astype(f32)
-    for a in range(1, near):
-        total = total + send(away[(a - 1) * far : a * far], 2 * a).astype(f32)
-    total = total.astype(bf16)
-    layer_parts = [total[0]] + [send(total[b], 2 * near * b) for b in range(1, far)]
+
+    split = far // 2
+    lines = (split, far - split)
+    away = forward(got[1:], far, lines)
+    (home,) = forward(got[:1], 0, (far,))
+
+    def along_near(home, away):
+        count = home.shape[0]
+        total = home.astype(f32)
+        for a in range(1, near):
+            total = total + send(away[(a - 1) * count : a * count], 2 * a).astype(f32)
+        return total.astype(bf16)
+
+    def along_far(low, high):
+        column = [low[b] for b in range(split)] + [high[b] for b in range(far - split)]
+        return [column[0]] + [send(column[b], 2 * near * b) for b in range(1, far)]
+
+    high = along_near(home[split:], away[1])
+    low = along_near(home[:split], away[0])
+    layer_parts = along_far(low, high)
     logit_grad, head_part = call(
         functools.partial(head_kernel, len(layer_parts)),
         [struct((rows, classes), bf16), struct((width, classes), f32)],
@@ -591,7 +633,8 @@
         limit=8,
     )
     logits = gather(logit_grad)
-    head_total = total_of(head_part)
+    head_part = total_of(head_part, 1, 2 * near)
+    logits[0], head_part = lax.optimization_barrier((logits[0], head_part))
 
     x_own, x_send = call(
         functools.partial(compact_kernel, n, gates, capacity),
@@ -599,6 +642,7 @@
         [*got, *logits],
         limit=SMALL,
     )
+    logits[0], x_send = lax.optimization_barrier((logits[0], x_send))
     x_other = send(x_send, 1)
     dx, mix, dw1_keep, dw1_send, dw2_keep, dw2_send = call(
         functools.partial(shared_backward_kernel, n, lanes, depth),
@@ -618,7 +662,7 @@
             *weight_scratch,
             pltpu.VMEM((all_rows, width), bf16),
             pltpu.VMEM((all_rows, hidden_chip), bf16),
-            pltpu.VMEM((all_rows, min(TILE, hidden_chip)), bf16),
+            pltpu.VMEM((all_rows, min(256, hidden_chip)), bf16),
         ],
         limit=BIG,
     )
@@ -646,23 +690,36 @@
     )
     dx_other = send(dx_send, 1)
     reduce_grad = dw2_keep + send(dw2_send, 1).astype(f32)
-    dw1, dx_own = lax.optimization_barrier((dw1, dx_own))
-    grad_home, grad_away, gate_part = call(
-        functools.partial(scatter_kernel, n, gates),
+    grad_home, low, high, mix = call(
+        functools.partial(scatter_kernel, n, split, gates),
         [
             struct((far, pack_rows, width), bf16),
-            struct((chips - far, pack_rows, width), bf16),
-            struct((gates * scenarios, width), f32),
+            *[struct(((near - 1) * line, pack_rows, width), bf16) for line in lines],
+            struct((chips, AUX, rows), bf16),
         ],
         [*got, dx, mix, dx_own, dx_other],
         limit=SMALL,
     )
-    total = grad_home.astype(f32)
-    for a in range(1, near):
-        total = total + send(grad_away[(a - 1) * far : a * far], 2 * a).astype(f32)
-    total = total.astype(bf16)
-    grad_parts = [total[0]] + [send(total[b], 2 * near * b) for b in range(1, far)]
-    gate_total = total_of(gate_part).reshape(gates, scenarios, width)
+    (gate_part,) = call(
+        functools.partial(gate_kernel, n, gates),
+        [struct((2 * gates * scenarios, width // 2), f32)],
+        [*got, mix],
+        limit=SMALL,
+    )
+    gate_part = total_of(gate_part, 1, 2 * near)
+    low, high, gate_part, dw1 = lax.optimization_barrier((low, high, gate_part, dw1))
+    high = along_near(grad_home[split:], high)
+    low = along_near(grad_home[:split], low)
+    grad_parts = along_far(low, high)
+    count = gate_part.shape[0]
+    if classes == width // 2:
+        sums = total_of(jnp.concatenate([gate_part, head_part]), 2 * near, devices)
+        gate_total, head_total = sums[:count], sums[count:]
+    else:
+        gate_total = total_of(gate_part, 2 * near, devices)
+        head_total = total_of(head_part, 2 * near, devices)
+    halves = [gate_total[: count // 2], gate_total[count // 2 :]]
+    gate_total = jnp.concatenate(halves, axis=1).reshape(gates, scenarios, width)
     gate_total = jnp.transpose(gate_total, (1, 2, 0))
     if tiled:
         (expand_grad,) = call(

time: 148 us -> 131 us (0.89)
  Pallas kernels: 42 us -> 31.7 us
  waiting for transfers between devices: 51.1 us -> 46.1 us
  local copies, waits for them, and re-layouts: 6.35 us -> 4.02 us
  starting transfers between devices: 41.8 us -> 43.5 us
    pallas_call x13 -> x14, Pallas kernels: 42 us -> 31.7 us  [call(): pl.pallas_call(kernel, out_shape=out_shapes, in_specs=specs, out_specs=[p...]
    ppermute x32, waiting for transfers between devices: 49.8 us -> 46.1 us  [send(): return lax.ppermute(value, AXIS, [(i, i ^ mask) for i in range(devices)])]
    unnamed x42 -> x40, local copies, waits for them, and re-layouts: 6.31 us -> 3.3 us
    ppermute x32, starting transfers between devices: 33.2 us -> 34.7 us  [send(): return lax.ppermute(value, AXIS, [(i, i ^ mask) for i in range(devices)])]
  transfers between devices with their start and end apart: 34 -> 34, of which waited for: 18 -> 22; matrix products, arithmetic and copies ran while one was open for 2% -> 2% of each run, Pallas kernels for 16% -> 13%
where the time goes in v4:
time: 131 us
  waiting for transfers between devices  46.1 us (35%)
  starting transfers between devices  43.5 us (33%)
  Pallas kernels  31.7 us (24%)
  other arithmetic  4.61 us (4%)
  local copies, waits for them, and re-layouts  4.02 us (3%)
    ppermute x32, waiting for transfers between devices, send(): return lax.ppermute(value, AXIS, [(i, i ^ mask) for i in range(devices)])  46.1 us
    ppermute x32, starting transfers between devices, send(): return lax.ppermute(value, AXIS, [(i, i ^ mask) for i in range(devices)])  34.7 us
    pallas_call x14, Pallas kernels, call(): pl.pallas_call(kernel, out_shape=out_shapes, in_specs=specs, out_specs=[p...  31.7 us
    all_to_all x1, starting transfers between devices, body(): lax.all_to_all(pieces, AXIS, split_axis=0, concat_axis=0, tiled=True, axi...  4.89 us
    all_to_all x1, starting transfers between devices, body(): lax.all_to_all(dw1.reshape(chips, depth, hidden_chip), AXIS, split_axis=0...  3.89 us
    unnamed x40, local copies, waits for them, and re-layouts  3.3 us
  transfers between devices with their start and end apart: 34, of which 22 were waited for; matrix products, arithmetic and copies ran while one was open for 2% of the time, Pallas kernels for 13%

profile of v4, /device:TPU:0, one launch (start us, length us, event | category | flops | bytes accessed | tf_op | source)
XLA Modules:
  0.0 131.0 jit_solution(13662428174366989454)
XLA Ops:
  0.7 1.9 %shard_map.162 = (bf16[144,256]{1,0:T(8,128)(2,1)}, f32[32,128]{1,0:T(8,128)}) custom-call(s32[8]{0:T(128)} %pads.1, s32[16]{0:T(128)} %slots.1, bf16[128,256]{1,0:T(8,128)(2,1)} %refs_4_.9, s32[1,128]{1,0:T(1,128)} %bitcast.49, bf16[160,256]{1,0:T(8,128)(2,1)} %bitcast.46), custom_call_target="tpu_custom_call" | custom-call | flops 100000 | bytes 100000 | tf_op jit(solution)/shard_map/pallas_call | solution.py:29
  2.6 5.0 %collective-permute-start.2 = (bf16[144,256]{1,0:T(8,128)(2,1)}, bf16[144,256]{1,0:T(8,128)(2,1)S(1)}, u32[]{:S(2)}, u32[]{:S(2)}) collective-permute-start(bf16[144,256]{1,0:T(8,128)(2,1)} %get-tuple-element.47), channel_id=1, source_target_pairs={{0,12},{1,13},{2,14},{3,15},{4,8},{5,9},{6,10},{7,11},{8,4},{9,5},... | collective-permute-start | bytes 221192 | tf_op jit(solution)/shard_map/ppermute | solution.py:521
  7.6 0.6 collective-permute-start
  8.2 1.0 copy-done.7
  9.2 0.9 shard_map.163
  10.2 0.5 collective-permute-done.2
  10.6 3.4 %collective-permute-done.1 = bf16[144,256]{1,0:T(8,128)(2,1)S(1)} collective-permute-done((bf16[144,256]{1,0:T(8,128)(2,1)}, bf16[144,256]{1,0:T(8,128)(2,1)S(1)}, u32[]{:S(2)}, u32[]{:S(2)}) %collective-permute-start.1) | collective-permute-done | bytes 73760 | tf_op jit(solution)/shard_map/ppermute | solution.py:521
  14.1 0.9 pad_maximum_fusion.refs_0_.refs_1_
  15.0 4.9 %all-to-all-start = ((bf16[8,16,2048]{2,1,0:T(8,128)(2,1)}), bf16[8,16,2048]{2,1,0:T(8,128)(2,1)S(1)}, u32[]{:S(2)}, u32[]{:S(2)}) async-start(bf16[8,16,2048]{2,1,0:T(8,128)(2,1)} %shard_map.163), calls=%async_computation | async-start | bytes 1048576 | tf_op jit(solution)/shard_map/all_to_all | solution.py:567
  19.9 2.0 %collective-permute-start.3 = (bf16[4,144,256]{2,1,0:T(8,128)(2,1)S(1)}, bf16[4,144,256]{2,1,0:T(8,128)(2,1)S(1)}, u32[]{:S(2)}, u32[]{:S(2)}) collective-permute-start(bf16[4,144,256]{2,1,0:T(8,128)(2,1)S(1)} %pad_maximum_fusion.refs_0_.refs_1_), channel_id=1, source_target_pairs={{0,2},{1,3},{2,0},{3,1},{4,6},{5,7},{6,4},{7,5},{8,10},{9,11},{10,... | collective-permute-start | bytes 884744 | tf_op jit(solution)/shard_map/ppermute | solution.py:521
  21.9 10.7 %collective-permute-done.3.refs_1_ = bf16[4,144,256]{2,1,0:T(8,128)(2,1)S(1)} collective-permute-done((bf16[4,144,256]{2,1,0:T(8,128)(2,1)S(1)}, bf16[4,144,256]{2,1,0:T(8,128)(2,1)S(1)}, u32[]{:S(2)}, u32[]{:S(2)}) %collective-permute-start.3) | collective-permute-done | bytes 294944 | tf_op jit(solution)/shard_map/ppermute | solution.py:521
  32.6 1.3 shard_map.164
  34.0 0.5 collective-permute-start.6
  34.5 0.9 collective-permute-done.4.other
  35.4 1.2 copy-done.2
  36.6 1.7 %shard_map.165 = (bf16[256,256]{1,0:T(8,128)(2,1)S(1)}, bf16[256,256]{1,0:T(8,128)(2,1)S(1)}) custom-call(bf16[256,384]{1,0:T(8,128)(2,1)S(1)} %get-tuple-element.50.own, bf16[256,384]{1,0:T(8,128)(2,1)S(1)} %collective-permute-done.4.other, bf16[256,2048]{1,0:T(8,128)(2,1)S(1)} %bitcast.42, bf16[2048,256]{1,0:T(8,128)(2,1)S(1)} %bitcast.44), custom_call_target="tpu_custom_call" | custom-call | flops 100000 | bytes 100000 | tf_op jit(solution)/shard_map/pallas_call | solution.py:29
  39.0 1.6 %collective-permute-done.7.refs_7_ = bf16[256,256]{1,0:T(8,128)(2,1)S(1)} collective-permute-done((bf16[256,256]{1,0:T(8,128)(2,1)S(1)}, bf16[256,256]{1,0:T(8,128)(2,1)S(1)}, u32[]{:S(2)}, u32[]{:S(2)}) %collective-permute-start.7) | collective-permute-done | bytes 131104 | tf_op jit(solution)/shard_map/ppermute | solution.py:521
  40.5 2.3 %shard_map.167 = (bf16[2,128,256]{2,1,0:T(8,128)(2,1)S(1)}, bf16[2,128,256]{2,1,0:T(8,128)(2,1)S(1)}) custom-call(bf16[4,144,256]{2,1,0:T(8,128)(2,1)S(1)} %pad_maximum_fusion.refs_0_.refs_1_, bf16[4,144,256]{2,1,0:T(8,128)(2,1)S(1)} %collective-permute-done.3.refs_1_, bf16[128,2048]{1,0:T(8,128)(2,1)S(1)} %bitcast.39, ...), custom_call_target="tpu_custom_call" | custom-call | flops 100000 | bytes 100000 | tf_op jit(solution)/shard_map/pallas_call | solution.py:29
  42.9 2.0 %collective-permute-start.10 = (bf16[2,128,256]{2,1,0:T(8,128)(2,1)S(1)}, bf16[2,128,256]{2,1,0:T(8,128)(2,1)S(1)}, u32[]{:S(2)}, u32[]{:S(2)}) collective-permute-start(bf16[2,128,256]{2,1,0:T(8,128)(2,1)S(1)} %get-tuple-element.57), channel_id=1, source_target_pairs={{0,2},{1,3},{2,0},{3,1},{4,6},{5,7},{6,4},{7,5},{8,10},{9,11},{10,... | collective-permute-start | bytes 393224 | tf_op jit(solution)/shard_map/ppermute | solution.py:521
  44.9 2.3 %shard_map.166 = bf16[4,128,256]{2,1,0:T(8,128)(2,1)S(1)} custom-call(bf16[4,144,256]{2,1,0:T(8,128)(2,1)S(1)} %pad_maximum_fusion.refs_0_.refs_1_, bf16[4,144,256]{2,1,0:T(8,128)(2,1)S(1)} %pad_maximum_fusion.refs_0_.refs_1_, bf16[128,2048]{1,0:T(8,128)(2,1)S(1)} %bitcast.40, bf16[128,2048]{1,0:T(8,128)(2,1)S(1)} %collective-permute-done.5.refs_3_.refs_6_, ...), custom_call_target="tpu_custom_call" | custom-call | flops 100000 | bytes 100000 | tf_op jit(solution)/shard_map/pallas_call | solution.py:29
  47.2 2.0 %collective-permute-done.8 = bf16[2,128,256]{2,1,0:T(8,128)(2,1)S(1)} collective-permute-done((bf16[2,128,256]{2,1,0:T(8,128)(2,1)S(1)}, bf16[2,128,256]{2,1,0:T(8,128)(2,1)S(1)}, u32[]{:S(2)}, u32[]{:S(2)}) %collective-permute-start.8) | collective-permute-done | bytes 131104 | tf_op jit(solution)/shard_map/ppermute | solution.py:521
  49.2 2.0 %collective-permute-done.10 = bf16[2,128,256]{2,1,0:T(8,128)(2,1)S(1)} collective-permute-done((bf16[2,128,256]{2,1,0:T(8,128)(2,1)S(1)}, bf16[2,128,256]{2,1,0:T(8,128)(2,1)S(1)}, u32[]{:S(2)}, u32[]{:S(2)}) %collective-permute-start.10) | collective-permute-done | bytes 131104 | tf_op jit(solution)/shard_map/ppermute | solution.py:521
  51.3 3.3 %collective-permute-start.12 = (bf16[128,256]{1,0:T(8,128)(2,1)S(1)}, bf16[128,256]{1,0:T(8,128)(2,1)S(1)}, u32[]{:S(2)}, u32[]{:S(2)}) collective-permute-start(bf16[128,256]{1,0:T(8,128)(2,1)S(1)} %get-tuple-element.97), channel_id=1, source_target_pairs={{0,12},{1,13},{2,14},{3,15},{4,8},{5,9},{6,10},{7,11},{8,4},{9,5},... | collective-permute-start | bytes 196616 | tf_op jit(solution)/shard_map/ppermute | solution.py:521
  54.7 1.2 collective-permute-start.9
  55.9 1.9 %collective-permute-done.12.refs_3_ = bf16[128,256]{1,0:T(8,128)(2,1)S(1)} collective-permute-done((bf16[128,256]{1,0:T(8,128)(2,1)S(1)}, bf16[128,256]{1,0:T(8,128)(2,1)S(1)}, u32[]{:S(2)}, u32[]{:S(2)}) %collective-permute-start.12) | collective-permute-done | bytes 65568 | tf_op jit(solution)/shard_map/ppermute | solution.py:521
  57.8 2.4 %collective-permute-done.11.refs_2_ = bf16[128,256]{1,0:T(8,128)(2,1)S(1)} collective-permute-done((bf16[128,256]{1,0:T(8,128)(2,1)S(1)}, bf16[128,256]{1,0:T(8,128)(2,1)S(1)}, u32[]{:S(2)}, u32[]{:S(2)}) %collective-permute-start.11) | collective-permute-done | bytes 65568 | tf_op jit(solution)/shard_map/ppermute | solution.py:521
  60.2 0.5 shard_map.168
  60.7 2.6 %collective-permute-start.15 = (bf16[128,128]{1,0:T(8,128)(2,1)S(1)}, bf16[128,128]{1,0:T(8,128)(2,1)S(1)}, u32[]{:S(2)}, u32[]{:S(2)}) collective-permute-start(bf16[128,128]{1,0:T(8,128)(2,1)S(1)} %get-tuple-element.58), channel_id=1, source_target_pairs={{0,12},{1,13},{2,14},{3,15},{4,8},{5,9},{6,10},{7,11},{8,4},{9,5},... | collective-permute-start | bytes 98312 | tf_op jit(solution)/shard_map/ppermute | solution.py:521
  63.3 1.9 %collective-permute-start.13 = (bf16[128,128]{1,0:T(8,128)(2,1)S(1)}, bf16[128,128]{1,0:T(8,128)(2,1)S(1)}, u32[]{:S(2)}, u32[]{:S(2)}) collective-permute-start(bf16[128,128]{1,0:T(8,128)(2,1)S(1)} %get-tuple-element.58), channel_id=1, source_target_pairs={{0,4},{1,5},{2,6},{3,7},{4,0},{5,1},{6,2},{7,3},{8,12},{9,13},{10,... | collective-permute-start | bytes 98312 | tf_op jit(solution)/shard_map/ppermute | solution.py:521
  65.2 0.5 collective-permute-start.17
  65.8 1.0 collective-permute-done.15
  66.8 1.3 %collective-permute-done.14 = bf16[128,128]{1,0:T(8,128)(2,1)S(1)} collective-permute-done((bf16[128,128]{1,0:T(8,128)(2,1)S(1)}, bf16[128,128]{1,0:T(8,128)(2,1)S(1)}, u32[]{:S(2)}, u32[]{:S(2)}) %collective-permute-start.14) | collective-permute-done | bytes 32800 | tf_op jit(solution)/shard_map/ppermute | solution.py:521
  68.2 0.6 collective-permute-start.18
  68.8 0.8 collective-permute-done.17
  69.5 0.6 convert_add_fusion.3
  70.2 3.0 %collective-permute-done.18.refs_3_ = bf16[4,128,128]{2,1,0:T(8,128)(2,1)S(1)} collective-permute-done((bf16[4,128,128]{2,1,0:T(8,128)(2,1)S(1)}, bf16[4,128,128]{2,1,0:T(8,128)(2,1)S(1)}, u32[]{:S(2)}, u32[]{:S(2)}) %collective-permute-start.18) | collective-permute-done | bytes 131104 | tf_op jit(solution)/shard_map/ppermute | solution.py:521
  73.2 1.5 %shard_map.169 = (bf16[256,512]{1,0:T(8,128)(2,1)S(1)}, bf16[256,512]{1,0:T(8,128)(2,1)}) custom-call(bf16[4,144,256]{2,1,0:T(8,128)(2,1)S(1)} %pad_maximum_fusion.refs_0_.refs_1_, bf16[4,144,256]{2,1,0:T(8,128)(2,1)S(1)} %collective-permute-done.3.refs_1_, bf16[4,128,128]{2,1,0:T(8,128)(2,1)S(1)} %pad_maximum_fusion.2.refs_2_, ...), custom_call_target="tpu_custom_call" | custom-call | flops 100000 | bytes 100000 | tf_op jit(solution)/shard_map/pallas_call | solution.py:29
  74.7 9.1 %shard_map.170 = (bf16[1024,256]{1,0:T(8,128)(2,1)S(1)}, f32[1024,32]{1,0:T(8,128)S(1)}, bf16[128,2048]{1,0:T(8,128)(2,1)S(1)}, bf16[128,2048]{1,0:T(8,128)(2,1)...) custom-call(bf16[4,144,256]{2,1,0:T(8,128)(2,1)S(1)} %pad_maximum_fusion.refs_0_.refs_1_, ...), custom_call_target="tpu_custom_call" | custom-call | flops 100000 | bytes 100000 | tf_op jit(solution)/shard_map/pallas_call | solution.py:29
  83.8 1.0 copy-done.4
  84.8 0.5 collective-permute-start.20
  85.3 1.4 %collective-permute-done.19 = bf16[128,2048]{1,0:T(8,128)(2,1)S(1)} collective-permute-done((bf16[128,2048]{1,0:T(8,128)(2,1)S(1)}, bf16[128,2048]{1,0:T(8,128)(2,1)S(1)}, u32[]{:S(2)}, u32[]{:S(2)}) %collective-permute-start.19) | collective-permute-done | bytes 524320 | tf_op jit(solution)/shard_map/ppermute | solution.py:521
  86.7 0.9 add_convert_fusion
  87.7 3.9 %all-to-all-start.1 = ((bf16[8,16,2048]{2,1,0:T(8,128)(2,1)}), bf16[8,16,2048]{2,1,0:T(8,128)(2,1)S(1)}, u32[]{:S(2)}, u32[]{:S(2)}) async-start(bf16[8,16,2048]{2,1,0:T(8,128)(2,1)} %bitcast.51), calls=%async_computation.1 | async-start | bytes 1048576 | tf_op jit(solution)/shard_map/all_to_all | solution.py:671
  91.6 6.5 %shard_map.171 = (bf16[256,384]{1,0:T(8,128)(2,1)S(1)}, bf16[256,384]{1,0:T(8,128)(2,1)S(1)}, f32[256,2048]{1,0:T(8,128)}, f32[2048,256]{1,0:T(8,128)}) custom-call(bf16[256,512]{1,0:T(8,128)(2,1)S(1)} %get-tuple-element.68.own, bf16[256,512]{1,0:T(8,128)(2,1)} %collective-permute-done.20.other, bf16[256,128]{1,0:T(8,128)(2,1)S(1)} %copy-done.6, ...), custom_call_target="tpu_custom_call" | custom-call | flops 100000 | bytes 100000 | tf_op jit(solution)/shard_map/pallas_call | solution.py:29
  98.1 1.4 %collective-permute-done.21.refs_5_ = bf16[256,384]{1,0:T(8,128)(2,1)S(1)} collective-permute-done((bf16[256,384]{1,0:T(8,128)(2,1)S(1)}, bf16[256,384]{1,0:T(8,128)(2,1)S(1)}, u32[]{:S(2)}, u32[]{:S(2)}) %collective-permute-start.21) | collective-permute-done | bytes 196640 | tf_op jit(solution)/shard_map/ppermute | solution.py:521
  99.5 1.6 %shard_map.172 = (bf16[4,144,256]{2,1,0:T(8,128)(2,1)S(1)}, bf16[2,144,256]{2,1,0:T(8,128)(2,1)S(1)}, bf16[2,144,256]{2,1,0:T(8,128)(2,1)S(1)}, bf16[8,32,128]{2,1,0:T(8,128)(2,1)S(1)}) custom-call(bf16[4,144,256]{2,1,0:T(8,128)(2,1)S(1)} %pad_maximum_fusion.refs_0_.refs_1_, bf16[4,144,256]{2,1,0:T(8,128)(2,1)S(1)} %collective-permute-done.3.refs_1_, ...), custom_call_target="tpu_custom_call" | custom-call | flops 100000 | bytes 100000 | tf_op jit(solution)/shard_map/pallas_call | solution.py:29
  101.7 1.3 collective-permute-done.22
  102.9 2.1 %collective-permute-start.23 = (bf16[320,128]{1,0:T(8,128)(2,1)S(1)}, bf16[320,128]{1,0:T(8,128)(2,1)S(1)}, u32[]{:S(2)}, u32[]{:S(2)}) collective-permute-start(bf16[320,128]{1,0:T(8,128)(2,1)S(1)} %add_convert_fusion.6), channel_id=1, source_target_pairs={{0,2},{1,3},{2,0},{3,1},{4,6},{5,7},{6,4},{7,5},{8,10},{9,11},{10,... | collective-permute-start | bytes 245768 | tf_op jit(solution)/shard_map/ppermute | solution.py:521
  105.0 2.8 %collective-permute-done.23 = bf16[320,128]{1,0:T(8,128)(2,1)S(1)} collective-permute-done((bf16[320,128]{1,0:T(8,128)(2,1)S(1)}, bf16[320,128]{1,0:T(8,128)(2,1)S(1)}, u32[]{:S(2)}, u32[]{:S(2)}) %collective-permute-start.23) | collective-permute-done | bytes 81952 | tf_op jit(solution)/shard_map/ppermute | solution.py:521
  107.8 1.8 %collective-permute-start.30 = (bf16[576,128]{1,0:T(8,128)(2,1)S(1)}, bf16[576,128]{1,0:T(8,128)(2,1)S(1)}, u32[]{:S(2)}, u32[]{:S(2)}) collective-permute-start(bf16[576,128]{1,0:T(8,128)(2,1)S(1)} %pad_maximum_fusion.1), channel_id=1, source_target_pairs={{0,4},{1,5},{2,6},{3,7},{4,0},{5,1},{6,2},{7,3},{8,12},{9,13},{10,... | collective-permute-start | bytes 442376 | tf_op jit(solution)/shard_map/ppermute | solution.py:521
  109.7 1.5 %collective-permute-start.24 = (bf16[2,144,256]{2,1,0:T(8,128)(2,1)S(1)}, bf16[2,144,256]{2,1,0:T(8,128)(2,1)S(1)}, u32[]{:S(2)}, u32[]{:S(2)}) collective-permute-start(bf16[2,144,256]{2,1,0:T(8,128)(2,1)S(1)} %get-tuple-element.77), channel_id=1, source_target_pairs={{0,2},{1,3},{2,0},{3,1},{4,6},{5,7},{6,4},{7,5},{8,10},{9,11},{10,... | collective-permute-start | bytes 442376 | tf_op jit(solution)/shard_map/ppermute | solution.py:521
  111.1 0.6 collective-permute-start.26
  111.7 1.6 %collective-permute-done.30 = bf16[576,128]{1,0:T(8,128)(2,1)S(1)} collective-permute-done((bf16[576,128]{1,0:T(8,128)(2,1)S(1)}, bf16[576,128]{1,0:T(8,128)(2,1)S(1)}, u32[]{:S(2)}, u32[]{:S(2)}) %collective-permute-start.30) | collective-permute-done | bytes 147488 | tf_op jit(solution)/shard_map/ppermute | solution.py:521
  113.3 2.5 %collective-permute-start.31 = (bf16[576,128]{1,0:T(8,128)(2,1)S(1)}, bf16[576,128]{1,0:T(8,128)(2,1)S(1)}, u32[]{:S(2)}, u32[]{:S(2)}) collective-permute-start(bf16[576,128]{1,0:T(8,128)(2,1)S(1)} %add_convert_fusion.1), channel_id=1, source_target_pairs={{0,8},{1,9},{2,10},{3,11},{4,12},{5,13},{6,14},{7,15},{8,0},{9,1},... | collective-permute-start | bytes 442376 | tf_op jit(solution)/shard_map/ppermute | solution.py:521
  115.8 0.5 collective-permute-done.24
  116.3 2.8 %collective-permute-done.26 = bf16[2,144,256]{2,1,0:T(8,128)(2,1)S(1)} collective-permute-done((bf16[2,144,256]{2,1,0:T(8,128)(2,1)S(1)}, bf16[2,144,256]{2,1,0:T(8,128)(2,1)S(1)}, u32[]{:S(2)}, u32[]{:S(2)}) %collective-permute-start.26) | collective-permute-done | bytes 147488 | tf_op jit(solution)/shard_map/ppermute | solution.py:521
  119.2 2.4 %collective-permute-start.28 = (bf16[144,256]{1,0:T(8,128)(2,1)S(1)}, bf16[144,256]{1,0:T(8,128)(2,1)S(1)}, u32[]{:S(2)}, u32[]{:S(2)}) collective-permute-start(bf16[144,256]{1,0:T(8,128)(2,1)S(1)} %get-tuple-element.93), channel_id=1, source_target_pairs={{0,12},{1,13},{2,14},{3,15},{4,8},{5,9},{6,10},{7,11},{8,4},{9,5},... | collective-permute-start | bytes 221192 | tf_op jit(solution)/shard_map/ppermute | solution.py:521
  121.7 2.0 %collective-permute-start.25 = (bf16[144,256]{1,0:T(8,128)(2,1)S(1)}, bf16[144,256]{1,0:T(8,128)(2,1)S(1)}, u32[]{:S(2)}, u32[]{:S(2)}) collective-permute-start(bf16[144,256]{1,0:T(8,128)(2,1)S(1)} %get-tuple-element.95), channel_id=1, source_target_pairs={{0,4},{1,5},{2,6},{3,7},{4,0},{5,1},{6,2},{7,3},{8,12},{9,13},{10,... | collective-permute-start | bytes 221192 | tf_op jit(solution)/shard_map/ppermute | solution.py:521
  123.7 1.1 convert_add_fusion
  124.9 1.0 shard_map.175
  126.2 2.5 %collective-permute-done.27.refs_2_ = bf16[144,256]{1,0:T(8,128)(2,1)S(1)} collective-permute-done((bf16[144,256]{1,0:T(8,128)(2,1)S(1)}, bf16[144,256]{1,0:T(8,128)(2,1)S(1)}, u32[]{:S(2)}, u32[]{:S(2)}) %collective-permute-start.27) | collective-permute-done | bytes 73760 | tf_op jit(solution)/shard_map/ppermute | solution.py:521
  128.7 0.9 shard_map.174
  129.6 0.7 slice.75
  130.3 0.7 maximum_bitcast_fusion
  (78 shorter events, 2.3 us)
Async XLA Ops:
  0.6 33.4 %copy-start = (bf16[16,64,256]{2,1,0:T(8,128)(2,1)S(1)}, bf16[16,64,256]{2,1,0:T(8,128)(2,1)}, u32[]{:S(2)}) copy-start(bf16[16,64,256]{2,1,0:T(8,128)(2,1)} %refs_7_.1) | copy-start | bytes 1572868
  0.6 34.8 %copy-start.1 = (bf16[1,256,2048]{2,1,0:T(8,128)(2,1)S(1)}, bf16[1,256,2048]{2,1,0:T(8,128)(2,1)}, u32[]{:S(2)}) copy-start(bf16[1,256,2048]{2,1,0:T(8,128)(2,1)} %param.19) | copy-start | bytes 3145732
  2.6 8.0 %collective-permute-start.2 = (bf16[144,256]{1,0:T(8,128)(2,1)}, bf16[144,256]{1,0:T(8,128)(2,1)S(1)}, u32[]{:S(2)}, u32[]{:S(2)}) collective-permute-start(bf16[144,256]{1,0:T(8,128)(2,1)} %get-tuple-element.47), channel_id=1, source_target_pairs={{0,12},{1,13},{2,14},{3,15},{4,8},{5,9},{6,10},{7,11},{8,4},{9,5},... | collective-permute-start | bytes 221192 | tf_op jit(solution)/shard_map/ppermute | solution.py:521
  7.6 6.4 %collective-permute-start.1 = (bf16[144,256]{1,0:T(8,128)(2,1)}, bf16[144,256]{1,0:T(8,128)(2,1)S(1)}, u32[]{:S(2)}, u32[]{:S(2)}) collective-permute-start(bf16[144,256]{1,0:T(8,128)(2,1)} %get-tuple-element.47), channel_id=1, source_target_pairs={{0,8},{1,9},{2,10},{3,11},{4,12},{5,13},{6,14},{7,15},{8,0},{9,1},... | collective-permute-start | bytes 221192 | tf_op jit(solution)/shard_map/ppermute | solution.py:521
  7.6 6.4 %collective-permute-start = (bf16[144,256]{1,0:T(8,128)(2,1)}, bf16[144,256]{1,0:T(8,128)(2,1)S(1)}, u32[]{:S(2)}, u32[]{:S(2)}) collective-permute-start(bf16[144,256]{1,0:T(8,128)(2,1)} %get-tuple-element.47), channel_id=1, source_target_pairs={{0,4},{1,5},{2,6},{3,7},{4,0},{5,1},{6,2},{7,3},{8,12},{9,13},{10,... | collective-permute-start | bytes 221192 | tf_op jit(solution)/shard_map/ppermute | solution.py:521
  8.2 1.0 copy-start.7
  15.0 23.4 %all-to-all-start = ((bf16[8,16,2048]{2,1,0:T(8,128)(2,1)}), bf16[8,16,2048]{2,1,0:T(8,128)(2,1)S(1)}, u32[]{:S(2)}, u32[]{:S(2)}) async-start(bf16[8,16,2048]{2,1,0:T(8,128)(2,1)} %shard_map.163), calls=%async_computation | async-start | bytes 1048576 | tf_op jit(solution)/shard_map/all_to_all | solution.py:567
  19.9 12.8 %collective-permute-start.3 = (bf16[4,144,256]{2,1,0:T(8,128)(2,1)S(1)}, bf16[4,144,256]{2,1,0:T(8,128)(2,1)S(1)}, u32[]{:S(2)}, u32[]{:S(2)}) collective-permute-start(bf16[4,144,256]{2,1,0:T(8,128)(2,1)S(1)} %pad_maximum_fusion.refs_0_.refs_1_), channel_id=1, source_target_pairs={{0,2},{1,3},{2,0},{3,1},{4,6},{5,7},{6,4},{7,5},{8,10},{9,11},{10,... | collective-permute-start | bytes 884744 | tf_op jit(solution)/shard_map/ppermute | solution.py:521
  33.9 1.5 %collective-permute-start.4 = (bf16[256,384]{1,0:T(8,128)(2,1)S(1)}, bf16[256,384]{1,0:T(8,128)(2,1)S(1)}, u32[]{:S(2)}, u32[]{:S(2)}) collective-permute-start(bf16[256,384]{1,0:T(8,128)(2,1)S(1)} %get-tuple-element.51), channel_id=1, source_target_pairs={{0,1},{1,0},{2,3},{3,2},{4,5},{5,4},{6,7},{7,6},{8,9},{9,8},{10,11... | collective-permute-start | bytes 589832 | tf_op jit(solution)/shard_map/ppermute | solution.py:521
  34.0 5.0 %collective-permute-start.6 = (bf16[16,64,256]{2,1,0:T(8,128)(2,1)S(1)}, bf16[16,64,256]{2,1,0:T(8,128)(2,1)S(1)}, u32[]{:S(2)}, u32[]{:S(2)}) collective-permute-start(bf16[16,64,256]{2,1,0:T(8,128)(2,1)S(1)} %copy-done), channel_id=1, source_target_pairs={{0,1},{1,0},{2,3},{3,2},{4,5},{5,4},{6,7},{7,6},{8,9},{9,8},{10,11... | collective-permute-start | bytes 1572872 | tf_op jit(solution)/shard_map/ppermute | solution.py:521
  35.4 1.2 copy-start.2
  38.4 2.2 %collective-permute-start.5 = (bf16[128,2048]{1,0:T(8,128)(2,1)S(1)}, bf16[128,2048]{1,0:T(8,128)(2,1)S(1)}, u32[]{:S(2)}, u32[]{:S(2)}) collective-permute-start(bf16[128,2048]{1,0:T(8,128)(2,1)S(1)} %bitcast.38), channel_id=1, source_target_pairs={{0,1},{1,0},{2,3},{3,2},{4,5},{5,4},{6,7},{7,6},{8,9},{9,8},{10,11... | collective-permute-start | bytes 1572872 | tf_op jit(solution)/shard_map/ppermute | solution.py:521
  38.6 2.0 %collective-permute-start.7 = (bf16[256,256]{1,0:T(8,128)(2,1)S(1)}, bf16[256,256]{1,0:T(8,128)(2,1)S(1)}, u32[]{:S(2)}, u32[]{:S(2)}) collective-permute-start(bf16[256,256]{1,0:T(8,128)(2,1)S(1)} %get-tuple-element.55), channel_id=1, source_target_pairs={{0,1},{1,0},{2,3},{3,2},{4,5},{5,4},{6,7},{7,6},{8,9},{9,8},{10,11... | collective-permute-start | bytes 393224 | tf_op jit(solution)/shard_map/ppermute | solution.py:521
  42.8 6.4 %collective-permute-start.8 = (bf16[2,128,256]{2,1,0:T(8,128)(2,1)S(1)}, bf16[2,128,256]{2,1,0:T(8,128)(2,1)S(1)}, u32[]{:S(2)}, u32[]{:S(2)}) collective-permute-start(bf16[2,128,256]{2,1,0:T(8,128)(2,1)S(1)} %get-tuple-element.56), channel_id=1, source_target_pairs={{0,2},{1,3},{2,0},{3,1},{4,6},{5,7},{6,4},{7,5},{8,10},{9,11},{10,... | collective-permute-start | bytes 393224 | tf_op jit(solution)/shard_map/ppermute | solution.py:521
  42.9 17.2 %copy-start.6 = (bf16[256,128]{1,0:T(8,128)(2,1)S(1)}, bf16[256,128]{1,0:T(8,128)(2,1)}, u32[]{:S(2)}) copy-start(bf16[256,128]{1,0:T(8,128)(2,1)} %head.1) | copy-start | bytes 196612
  42.9 17.2 %copy-start.14 = (f32[128,128]{1,0:T(8,128)S(1)}, f32[128,128]{1,0:T(8,128)}, u32[]{:S(2)}) copy-start(f32[128,128]{1,0:T(8,128)} %refs_5_.1) | copy-start | bytes 196612
  42.9 8.3 %collective-permute-start.10 = (bf16[2,128,256]{2,1,0:T(8,128)(2,1)S(1)}, bf16[2,128,256]{2,1,0:T(8,128)(2,1)S(1)}, u32[]{:S(2)}, u32[]{:S(2)}) collective-permute-start(bf16[2,128,256]{2,1,0:T(8,128)(2,1)S(1)} %get-tuple-element.57), channel_id=1, source_target_pairs={{0,2},{1,3},{2,0},{3,1},{4,6},{5,7},{6,4},{7,5},{8,10},{9,11},{10,... | collective-permute-start | bytes 393224 | tf_op jit(solution)/shard_map/ppermute | solution.py:521
  51.3 6.4 %collective-permute-start.12 = (bf16[128,256]{1,0:T(8,128)(2,1)S(1)}, bf16[128,256]{1,0:T(8,128)(2,1)S(1)}, u32[]{:S(2)}, u32[]{:S(2)}) collective-permute-start(bf16[128,256]{1,0:T(8,128)(2,1)S(1)} %get-tuple-element.97), channel_id=1, source_target_pairs={{0,12},{1,13},{2,14},{3,15},{4,8},{5,9},{6,10},{7,11},{8,4},{9,5},... | collective-permute-start | bytes 196616 | tf_op jit(solution)/shard_map/ppermute | solution.py:521
  54.6 5.5 %collective-permute-start.11 = (bf16[128,256]{1,0:T(8,128)(2,1)S(1)}, bf16[128,256]{1,0:T(8,128)(2,1)S(1)}, u32[]{:S(2)}, u32[]{:S(2)}) collective-permute-start(bf16[128,256]{1,0:T(8,128)(2,1)S(1)} %get-tuple-element.98), channel_id=1, source_target_pairs={{0,8},{1,9},{2,10},{3,11},{4,12},{5,13},{6,14},{7,15},{8,0},{9,1},... | collective-permute-start | bytes 196616 | tf_op jit(solution)/shard_map/ppermute | solution.py:521
  54.7 5.5 %collective-permute-start.9 = (bf16[128,256]{1,0:T(8,128)(2,1)S(1)}, bf16[128,256]{1,0:T(8,128)(2,1)S(1)}, u32[]{:S(2)}, u32[]{:S(2)}) collective-permute-start(bf16[128,256]{1,0:T(8,128)(2,1)S(1)} %get-tuple-element.99), channel_id=1, source_target_pairs={{0,4},{1,5},{2,6},{3,7},{4,0},{5,1},{6,2},{7,3},{8,12},{9,13},{10,... | collective-permute-start | bytes 196616 | tf_op jit(solution)/shard_map/ppermute | solution.py:521
  60.7 4.5 %collective-permute-start.16 = (f32[256,128]{1,0:T(8,128)S(1)}, f32[256,128]{1,0:T(8,128)S(1)}, u32[]{:S(2)}, u32[]{:S(2)}) collective-permute-start(f32[256,128]{1,0:T(8,128)S(1)} %get-tuple-element.59), channel_id=1, source_target_pairs={{0,1},{1,0},{2,3},{3,2},{4,5},{5,4},{6,7},{7,6},{8,9},{9,8},{10,11... | collective-permute-start | bytes 393224 | tf_op jit(solution)/shard_map/ppermute | solution.py:521
  60.7 6.1 %collective-permute-start.15 = (bf16[128,128]{1,0:T(8,128)(2,1)S(1)}, bf16[128,128]{1,0:T(8,128)(2,1)S(1)}, u32[]{:S(2)}, u32[]{:S(2)}) collective-permute-start(bf16[128,128]{1,0:T(8,128)(2,1)S(1)} %get-tuple-element.58), channel_id=1, source_target_pairs={{0,12},{1,13},{2,14},{3,15},{4,8},{5,9},{6,10},{7,11},{8,4},{9,5},... | collective-permute-start | bytes 98312 | tf_op jit(solution)/shard_map/ppermute | solution.py:521
  63.3 4.8 %collective-permute-start.14 = (bf16[128,128]{1,0:T(8,128)(2,1)S(1)}, bf16[128,128]{1,0:T(8,128)(2,1)S(1)}, u32[]{:S(2)}, u32[]{:S(2)}) collective-permute-start(bf16[128,128]{1,0:T(8,128)(2,1)S(1)} %get-tuple-element.58), channel_id=1, source_target_pairs={{0,8},{1,9},{2,10},{3,11},{4,12},{5,13},{6,14},{7,15},{8,0},{9,1},... | collective-permute-start | bytes 98312 | tf_op jit(solution)/shard_map/ppermute | solution.py:521
  63.3 4.8 %collective-permute-start.13 = (bf16[128,128]{1,0:T(8,128)(2,1)S(1)}, bf16[128,128]{1,0:T(8,128)(2,1)S(1)}, u32[]{:S(2)}, u32[]{:S(2)}) collective-permute-start(bf16[128,128]{1,0:T(8,128)(2,1)S(1)} %get-tuple-element.58), channel_id=1, source_target_pairs={{0,4},{1,5},{2,6},{3,7},{4,0},{5,1},{6,2},{7,3},{8,12},{9,13},{10,... | collective-permute-start | bytes 98312 | tf_op jit(solution)/shard_map/ppermute | solution.py:521
  65.2 4.3 %collective-permute-start.17 = (bf16[256,128]{1,0:T(8,128)(2,1)S(1)}, bf16[256,128]{1,0:T(8,128)(2,1)S(1)}, u32[]{:S(2)}, u32[]{:S(2)}) collective-permute-start(bf16[256,128]{1,0:T(8,128)(2,1)S(1)} %add_convert_fusion.7), channel_id=1, source_target_pairs={{0,2},{1,3},{2,0},{3,1},{4,6},{5,7},{6,4},{7,5},{8,10},{9,11},{10,... | collective-permute-start | bytes 196616 | tf_op jit(solution)/shard_map/ppermute | solution.py:521
  68.2 5.0 %collective-permute-start.18 = (bf16[4,128,128]{2,1,0:T(8,128)(2,1)S(1)}, bf16[4,128,128]{2,1,0:T(8,128)(2,1)S(1)}, u32[]{:S(2)}, u32[]{:S(2)}) collective-permute-start(bf16[4,128,128]{2,1,0:T(8,128)(2,1)S(1)} %pad_maximum_fusion.2.refs_2_), channel_id=1, source_target_pairs={{0,2},{1,3},{2,0},{3,1},{4,6},{5,7},{6,4},{7,5},{8,10},{9,11},{10,... | collective-permute-start | bytes 393224 | tf_op jit(solution)/shard_map/ppermute | solution.py:521
  83.8 1.0 copy-start.4
  84.7 2.9 %copy-start.8 = (bf16[1024,256]{1,0:T(8,128)(2,1)}, bf16[1024,256]{1,0:T(8,128)(2,1)S(1)}, u32[]{:S(2)}) copy-start(bf16[1024,256]{1,0:T(8,128)(2,1)S(1)} %get-tuple-element.63.refs_2_) | copy-start | bytes 1572868
  84.7 2.9 %copy-start.10 = (f32[1024,32]{1,0:T(8,128)}, f32[1024,32]{1,0:T(8,128)S(1)}, u32[]{:S(2)}) copy-start(f32[1024,32]{1,0:T(8,128)S(1)} %get-tuple-element.64.refs_3_) | copy-start | bytes 393220
  84.7 2.9 %copy-start.17 = (bf16[16,64,256]{2,1,0:T(8,128)(2,1)}, bf16[16,64,256]{2,1,0:T(8,128)(2,1)S(1)}, u32[]{:S(2)}) copy-start(bf16[16,64,256]{2,1,0:T(8,128)(2,1)S(1)} %get-tuple-element.82) | copy-start | bytes 1572868
  84.7 6.8 %copy-start.3 = (bf16[1,2048,256]{2,1,0:T(8,128)(2,1)S(1)}, bf16[1,2048,256]{2,1,0:T(8,128)(2,1)}, u32[]{:S(2)}) copy-start(bf16[1,2048,256]{2,1,0:T(8,128)(2,1)} %param.20) | copy-start | bytes 3145732
  84.7 2.0 %collective-permute-start.19 = (bf16[128,2048]{1,0:T(8,128)(2,1)S(1)}, bf16[128,2048]{1,0:T(8,128)(2,1)S(1)}, u32[]{:S(2)}, u32[]{:S(2)}) collective-permute-start(bf16[128,2048]{1,0:T(8,128)(2,1)S(1)} %get-tuple-element.66), channel_id=1, source_target_pairs={{0,1},{1,0},{2,3},{3,2},{4,5},{5,4},{6,7},{7,6},{8,9},{9,8},{10,11... | collective-permute-start | bytes 1572872 | tf_op jit(solution)/shard_map/ppermute | solution.py:521
  84.8 6.7 %collective-permute-start.20 = (bf16[256,512]{1,0:T(8,128)(2,1)}, bf16[256,512]{1,0:T(8,128)(2,1)}, u32[]{:S(2)}, u32[]{:S(2)}) collective-permute-start(bf16[256,512]{1,0:T(8,128)(2,1)} %get-tuple-element.69), channel_id=1, source_target_pairs={{0,1},{1,0},{2,3},{3,2},{4,5},{5,4},{6,7},{7,6},{8,9},{9,8},{10,11... | collective-permute-start | bytes 786440 | tf_op jit(solution)/shard_map/ppermute | solution.py:521
  87.7 20.1 %all-to-all-start.1 = ((bf16[8,16,2048]{2,1,0:T(8,128)(2,1)}), bf16[8,16,2048]{2,1,0:T(8,128)(2,1)S(1)}, u32[]{:S(2)}, u32[]{:S(2)}) async-start(bf16[8,16,2048]{2,1,0:T(8,128)(2,1)} %bitcast.51), calls=%async_computation.1 | async-start | bytes 1048576 | tf_op jit(solution)/shard_map/all_to_all | solution.py:671
  91.5 8.0 %copy-start.9 = (bf16[1024,256]{1,0:T(8,128)(2,1)S(1)}, bf16[1024,256]{1,0:T(8,128)(2,1)}, u32[]{:S(2)}) copy-start(bf16[1024,256]{1,0:T(8,128)(2,1)} %copy-done.8) | copy-start | bytes 1572868
  91.6 8.0 %copy-start.11 = (f32[1024,32]{1,0:T(8,128)S(1)}, f32[1024,32]{1,0:T(8,128)}, u32[]{:S(2)}) copy-start(f32[1024,32]{1,0:T(8,128)} %copy-done.10) | copy-start | bytes 393220
  98.1 9.8 %copy-start.19 = (bf16[256,128]{1,0:T(8,128)(2,1)S(1)}, bf16[256,128]{1,0:T(8,128)(2,1)}, u32[]{:S(2)}) copy-start(bf16[256,128]{1,0:T(8,128)(2,1)} %convert_add_fusion.3) | copy-start | bytes 196612
  98.1 11.6 %copy-start.18 = (bf16[16,64,256]{2,1,0:T(8,128)(2,1)S(1)}, bf16[16,64,256]{2,1,0:T(8,128)(2,1)}, u32[]{:S(2)}) copy-start(bf16[16,64,256]{2,1,0:T(8,128)(2,1)} %copy-done.17) | copy-start | bytes 1572868
  98.1 1.4 %collective-permute-start.21 = (bf16[256,384]{1,0:T(8,128)(2,1)S(1)}, bf16[256,384]{1,0:T(8,128)(2,1)S(1)}, u32[]{:S(2)}, u32[]{:S(2)}) collective-permute-start(bf16[256,384]{1,0:T(8,128)(2,1)S(1)} %get-tuple-element.71), channel_id=1, source_target_pairs={{0,1},{1,0},{2,3},{3,2},{4,5},{5,4},{6,7},{7,6},{8,9},{9,8},{10,11... | collective-permute-start | bytes 589832 | tf_op jit(solution)/shard_map/ppermute | solution.py:521
  101.1 22.6 %copy-start.5 = (f32[16,64,256]{2,1,0:T(8,128)S(1)}, f32[16,64,256]{2,1,0:T(8,128)}, u32[]{:S(2)}) copy-start(f32[16,64,256]{2,1,0:T(8,128)} %copy-done.4) | copy-start | bytes 3145732
  101.5 1.5 %collective-permute-start.22 = (f32[320,128]{1,0:T(8,128)S(1)}, f32[320,128]{1,0:T(8,128)S(1)}, u32[]{:S(2)}, u32[]{:S(2)}) collective-permute-start(f32[320,128]{1,0:T(8,128)S(1)} %shard_map.173), channel_id=1, source_target_pairs={{0,1},{1,0},{2,3},{3,2},{4,5},{5,4},{6,7},{7,6},{8,9},{9,8},{10,11... | collective-permute-start | bytes 491528 | tf_op jit(solution)/shard_map/ppermute | solution.py:521
  102.9 4.8 %collective-permute-start.23 = (bf16[320,128]{1,0:T(8,128)(2,1)S(1)}, bf16[320,128]{1,0:T(8,128)(2,1)S(1)}, u32[]{:S(2)}, u32[]{:S(2)}) collective-permute-start(bf16[320,128]{1,0:T(8,128)(2,1)S(1)} %add_convert_fusion.6), channel_id=1, source_target_pairs={{0,2},{1,3},{2,0},{3,1},{4,6},{5,7},{6,4},{7,5},{8,10},{9,11},{10,... | collective-permute-start | bytes 245768 | tf_op jit(solution)/shard_map/ppermute | solution.py:521
  107.8 5.4 %collective-permute-start.30 = (bf16[576,128]{1,0:T(8,128)(2,1)S(1)}, bf16[576,128]{1,0:T(8,128)(2,1)S(1)}, u32[]{:S(2)}, u32[]{:S(2)}) collective-permute-start(bf16[576,128]{1,0:T(8,128)(2,1)S(1)} %pad_maximum_fusion.1), channel_id=1, source_target_pairs={{0,4},{1,5},{2,6},{3,7},{4,0},{5,1},{6,2},{7,3},{8,12},{9,13},{10,... | collective-permute-start | bytes 442376 | tf_op jit(solution)/shard_map/ppermute | solution.py:521
  109.7 14.1 %collective-permute-start.29 = (bf16[16,64,256]{2,1,0:T(8,128)(2,1)S(1)}, bf16[16,64,256]{2,1,0:T(8,128)(2,1)S(1)}, u32[]{:S(2)}, u32[]{:S(2)}) collective-permute-start(bf16[16,64,256]{2,1,0:T(8,128)(2,1)S(1)} %copy-done.18), channel_id=1, source_target_pairs={{0,1},{1,0},{2,3},{3,2},{4,5},{5,4},{6,7},{7,6},{8,9},{9,8},{10,11... | collective-permute-start | bytes 1572872 | tf_op jit(solution)/shard_map/ppermute | solution.py:521
  109.7 6.6 %collective-permute-start.24 = (bf16[2,144,256]{2,1,0:T(8,128)(2,1)S(1)}, bf16[2,144,256]{2,1,0:T(8,128)(2,1)S(1)}, u32[]{:S(2)}, u32[]{:S(2)}) collective-permute-start(bf16[2,144,256]{2,1,0:T(8,128)(2,1)S(1)} %get-tuple-element.77), channel_id=1, source_target_pairs={{0,2},{1,3},{2,0},{3,1},{4,6},{5,7},{6,4},{7,5},{8,10},{9,11},{10,... | collective-permute-start | bytes 442376 | tf_op jit(solution)/shard_map/ppermute | solution.py:521
  111.1 8.0 %collective-permute-start.26 = (bf16[2,144,256]{2,1,0:T(8,128)(2,1)S(1)}, bf16[2,144,256]{2,1,0:T(8,128)(2,1)S(1)}, u32[]{:S(2)}, u32[]{:S(2)}) collective-permute-start(bf16[2,144,256]{2,1,0:T(8,128)(2,1)S(1)} %get-tuple-element.78), channel_id=1, source_target_pairs={{0,2},{1,3},{2,0},{3,1},{4,6},{5,7},{6,4},{7,5},{8,10},{9,11},{10,... | collective-permute-start | bytes 442376 | tf_op jit(solution)/shard_map/ppermute | solution.py:521
  113.3 16.2 %collective-permute-start.31 = (bf16[576,128]{1,0:T(8,128)(2,1)S(1)}, bf16[576,128]{1,0:T(8,128)(2,1)S(1)}, u32[]{:S(2)}, u32[]{:S(2)}) collective-permute-start(bf16[576,128]{1,0:T(8,128)(2,1)S(1)} %add_convert_fusion.1), channel_id=1, source_target_pairs={{0,8},{1,9},{2,10},{3,11},{4,12},{5,13},{6,14},{7,15},{8,0},{9,1},... | collective-permute-start | bytes 442376 | tf_op jit(solution)/shard_map/ppermute | solution.py:521
  119.2 7.0 %collective-permute-start.28 = (bf16[144,256]{1,0:T(8,128)(2,1)S(1)}, bf16[144,256]{1,0:T(8,128)(2,1)S(1)}, u32[]{:S(2)}, u32[]{:S(2)}) collective-permute-start(bf16[144,256]{1,0:T(8,128)(2,1)S(1)} %get-tuple-element.93), channel_id=1, source_target_pairs={{0,12},{1,13},{2,14},{3,15},{4,8},{5,9},{6,10},{7,11},{8,4},{9,5},... | collective-permute-start | bytes 221192 | tf_op jit(solution)/shard_map/ppermute | solution.py:521
  121.6 7.1 %collective-permute-start.27 = (bf16[144,256]{1,0:T(8,128)(2,1)S(1)}, bf16[144,256]{1,0:T(8,128)(2,1)S(1)}, u32[]{:S(2)}, u32[]{:S(2)}) collective-permute-start(bf16[144,256]{1,0:T(8,128)(2,1)S(1)} %get-tuple-element.94), channel_id=1, source_target_pairs={{0,8},{1,9},{2,10},{3,11},{4,12},{5,13},{6,14},{7,15},{8,0},{9,1},... | collective-permute-start | bytes 221192 | tf_op jit(solution)/shard_map/ppermute | solution.py:521
  121.7 7.0 %collective-permute-start.25 = (bf16[144,256]{1,0:T(8,128)(2,1)S(1)}, bf16[144,256]{1,0:T(8,128)(2,1)S(1)}, u32[]{:S(2)}, u32[]{:S(2)}) collective-permute-start(bf16[144,256]{1,0:T(8,128)(2,1)S(1)} %get-tuple-element.95), channel_id=1, source_target_pairs={{0,4},{1,5},{2,6},{3,7},{4,0},{5,1},{6,2},{7,3},{8,12},{9,13},{10,... | collective-permute-start | bytes 221192 | tf_op jit(solution)/shard_map/ppermute | solution.py:521
  123.7 5.0 %copy-start.12 = (bf16[8,256,20]{1,0,2:T(8,128)(2,1)S(1)}, bf16[8,256,20]{1,0,2:T(8,128)(2,1)}, u32[]{:S(2)}) copy-start(bf16[8,256,20]{1,0,2:T(8,128)(2,1)} %param.16) | copy-start | bytes 245764
  123.7 5.0 %copy-start.13 = (bf16[128,256]{1,0:T(8,128)(2,1)S(1)}, bf16[128,256]{1,0:T(8,128)(2,1)}, u32[]{:S(2)}) copy-start(bf16[128,256]{1,0:T(8,128)(2,1)} %refs_4_.9) | copy-start | bytes 196612
  123.7 5.0 %copy-start.15 = (f32[32,128]{1,0:T(8,128)S(1)}, f32[32,128]{1,0:T(8,128)}, u32[]{:S(2)}) copy-start(f32[32,128]{1,0:T(8,128)} %get-tuple-element.79.refs_6_) | copy-start | bytes 49156
  123.7 5.0 %copy-start.16 = (s32[128]{0:T(128)S(1)}, s32[128]{0:T(128)}, u32[]{:S(2)}) copy-start(s32[128]{0:T(128)} %param.12) | copy-start | bytes 1540

commit v5 on v4

--- a/solution.py
+++ b/solution.py
@@ -167,11 +167,11 @@
 
 
 def compact_kernel(n, gate_count, capacity, *refs):
-    pieces, logits, outs = refs[:n], refs[n:-2], refs[-2:]
+    own, pieces, logits, outs = refs[0], refs[1 : n + 1], refs[n + 1 : -2], refs[-2:]
     m = pieces[0].shape[0]
     rows = pieces[0].shape[1] - AUX // 2
     width = pieces[0].shape[2]
-    places = own_place(pieces, gate_count)
+    places = own_place([own], gate_count)
     for k in range(n):
         for b in range(m):
             x = pieces[k][b, :rows, :]
@@ -236,26 +236,29 @@
                 xt[:, spot] = mm(turn, x, 1, 1).astype(bf16)
 
 
-def join_weights(w1a, w1b, w2a, w2b, w1, w2):
-    half = w1a.shape[0]
-    w1[:half, :] = w1a[...]
-    w1[half:, :] = w1b[...]
-    experts, part, _ = w2a.shape
+def join_rows(top, bottom, out):
+    half = top.shape[0]
+    out[:half, :] = top[...]
+    out[half:, :] = bottom[...]
+
+
+def join_units_kernel(mine, theirs, out):
+    experts, part, _ = mine.shape
     core = own_core()
     for k in range(experts):
-        mine, theirs = w2a[k], w2b[k]
-        w2[2 * k * part : (2 * k + 1) * part, :] = jnp.where(core == 0, mine, theirs)
-        w2[(2 * k + 1) * part : 2 * (k + 1) * part, :] = jnp.where(core == 0, theirs, mine)
-
-
-def shared_forward_kernel(n, start, split, gate_rows, gate_count, depth, *refs):
+        own, other = mine[k], theirs[k]
+        out[2 * k * part : (2 * k + 1) * part, :] = jnp.where(core == 0, own, other)
+        out[(2 * k + 1) * part : 2 * (k + 1) * part, :] = jnp.where(core == 0, other, own)
+
+
+def shared_forward_kernel(n, split, gate_rows, gate_count, depth, *refs):
     own, pieces = refs[0], refs[1 : n + 1]
-    w1a, w1b, w2a, w2b, from_own, from_other, *outs, xs, gates, w1, w2, gated = refs[n + 1 :]
-    join_weights(w1a, w1b, w2a, w2b, w1, w2)
+    w1a, w1b, w2, from_own, from_other, *outs, xs, gates, w1, gated = refs[n + 1 :]
+    join_rows(w1a, w1b, w1)
     unpack(pieces, turn_matrix(w1.shape[0], depth, own_core()), xs, gates)
     m, packed, _ = pieces[0].shape
     count, rows = n * m, packed - AUX // 2
-    capacity = from_own.shape[0] // (w1.shape[0] // (2 * depth))
+    capacity = from_own.shape[0] // count
     places = own_place([own], gate_count)
     total = count * rows
     size, chunk = min(TILE, w1.shape[1]), min(total, max(CHUNK, total // 4))
@@ -275,7 +278,7 @@
         mixed = mm(gated[at : at + chunk, :], w2[...])
         for piece in range(at // rows, (at + chunk) // rows):
             side = side_of(pieces[piece // m][piece % m, rows:, :])
-            spot = slice((start + piece) * capacity, (start + piece + 1) * capacity)
+            spot = slice(piece * capacity, (piece + 1) * capacity)
             value = mixed[piece * rows - at : (piece + 1) * rows - at]
             for (owner, _), source in zip(places, (from_own, from_other)):
                 value += mm(selector(side, gate_count, owner, capacity), source[spot, :], 0, 0)
@@ -302,12 +305,12 @@
 
 def shared_backward_kernel(n, gate_rows, depth, *refs):
     pieces, logits = refs[:n], refs[n : 2 * n]
-    head, w1a, w1b, w2a, w2b = refs[2 * n : 2 * n + 5]
-    dx, mix, keep, sent, keep2, sent2 = refs[2 * n + 5 : 2 * n + 11]
-    xp, xpt, gates, w1, w2, os, linear_grad, weighed = refs[2 * n + 11 :]
+    head, w1a, w1b, w2 = refs[2 * n : 2 * n + 4]
+    dx, mix, keep, sent, keep2, sent2 = refs[2 * n + 4 : 2 * n + 10]
+    xp, xpt, gates, w1, os, linear_grad, weighed = refs[2 * n + 10 :]
     core = own_core()
     turn = turn_matrix(w1.shape[0], depth, core)
-    join_weights(w1a, w1b, w2a, w2b, w1, w2)
+    join_rows(w1a, w1b, w1)
     unpack(pieces, turn, xp, gates, xpt)
     m, rows, _ = logits[0].shape
     for k in range(n):
@@ -350,7 +353,7 @@
             low = second[e * gate_rows : e * gate_rows + part]
             high = second[e * gate_rows + part : (e + 1) * gate_rows]
             k = j * (size // gate_rows) + e
-            keep2[k] = jnp.where(core == 0, low, high)
+            keep2[k] = jnp.where(core == 0, low, high).astype(keep2.dtype)
             sent2[k] = jnp.where(core == 0, high, low).astype(bf16)
         return 0
 
@@ -525,14 +528,10 @@
         stacked = jnp.stack(column)
         return [stacked] + [send(stacked, 2 * a) for a in range(1, near)]
 
-    def total_of(value, mask, end):
-        if mask == 1:
-            value = value + send(value, 1)
-            mask = 2
-        while mask < end:
+    def total_of(value, masks):
+        for mask in masks:
             half = value.astype(bf16)
             value = half.astype(f32) + send(half, mask).astype(f32)
-            mask *= 2
         return value
 
     sid = scenario_id.reshape(1, rows)
@@ -559,45 +558,53 @@
         limit=SMALL,
     )
     column = [pack] + [send(pack, 2 * near * b) for b in range(1, far)]
+    column, pieces = lax.optimization_barrier((column, pieces))
     stacked = jnp.stack(column)
-    stacked, pieces = lax.optimization_barrier((stacked, pieces))
     got = [stacked] + [send(stacked, 2 * a) for a in range(1, near)]
-    w2a = reduce
-    w2b = send(reduce, 1)
+    (w2,) = call(
+        join_units_kernel,
+        [struct((hidden_chip, width), bf16)],
+        [reduce, send(reduce, 1)],
+        limit=SMALL,
+    )
     w1a = lax.all_to_all(
         pieces, AXIS, split_axis=0, concat_axis=0, tiled=True, axis_index_groups=groups
     ).reshape(width // 2, hidden_chip)
-    x_own, x_send = call(
-        functools.partial(compact_kernel, n, gates, capacity),
-        [struct((slots, width + 128), bf16)] * 2,
-        got,
-        limit=SMALL,
-    )
-    x_other = send(x_send, 1)
-    out_own, out_send = call(
-        functools.partial(scenario_forward_kernel, hidden),
-        [struct((slots, width), bf16)] * 2,
-        [x_own, x_other, widen, narrow],
-        scratch=[pltpu.VMEM((2 * slots, slot_width), bf16)],
-        limit=SMALL,
-    )
-    w1a, out_send = lax.optimization_barrier((w1a, out_send))
-    out_other = send(out_send, 1)
+    def compact(pieces, values):
+        count = len(pieces) * far * capacity
+        out_width = width + 128 + (classes if values else 0)
+        return call(
+            functools.partial(compact_kernel, len(pieces), gates, capacity),
+            [struct((count, out_width), bf16)] * 2,
+            [got[0], *pieces, *values],
+            limit=SMALL,
+        )
+
+    def scenario_forward(pieces):
+        count = len(pieces) * far * capacity
+        x_own, x_send = compact(pieces, [])
+        out_own, out_send = call(
+            functools.partial(scenario_forward_kernel, hidden),
+            [struct((count, width), bf16)] * 2,
+            [x_own, send(x_send, 1), widen, narrow],
+            scratch=[pltpu.VMEM((2 * count, slot_width), bf16)],
+            limit=SMALL,
+        )
+        return out_own, send(out_send, 1)
+
+    mixing_home = scenario_forward(got[:1])
+    got[1], mixing_home, w1a, w2 = lax.optimization_barrier((got[1], mixing_home, w1a, w2))
+    mixing_away = scenario_forward(got[1:])
     w1b = send(w1a, 1)
-    weights = [w1a, w1b, w2a, w2b]
-    weight_scratch = [
-        pltpu.VMEM((width, hidden_chip), bf16),
-        pltpu.VMEM((hidden_chip, width), bf16),
-    ]
-
-    def forward(pieces, start, lines):
+    weights = [w1a, w1b, w2]
+    weight_scratch = [pltpu.VMEM((width, hidden_chip), bf16)]
+
+    def forward(pieces, mixing, lines):
         count = len(pieces) * far
         return call(
-            functools.partial(
-                shared_forward_kernel, len(pieces), start, lines[0], lanes, gates, depth
-            ),
+            functools.partial(shared_forward_kernel, len(pieces), lines[0], lanes, gates, depth),
             [struct((len(pieces) * line, rows, width), bf16) for line in lines],
-            [got[0], *pieces, *weights, out_own, out_other],
+            [got[0], *pieces, *weights, *mixing],
             scratch=[
                 pltpu.VMEM((count * rows, width), bf16),
                 pltpu.VMEM((count * rows, AUX), bf16),
@@ -609,8 +616,8 @@
 
     split = far // 2
     lines = (split, far - split)
-    away = forward(got[1:], far, lines)
-    (home,) = forward(got[:1], 0, (far,))
+    away = forward(got[1:], mixing_away, lines)
+    (home,) = forward(got[:1], mixing_home, (far,))
 
     def along_near(home, away):
         count = home.shape[0]
@@ -633,15 +640,11 @@
         limit=8,
     )
     logits = gather(logit_grad)
-    head_part = total_of(head_part, 1, 2 * near)
+    masks = [2**i for i in range(devices.bit_length() - 2, 0, -1)]
+    head_part = total_of(head_part + send(head_part, 1), masks[:1])
     logits[0], head_part = lax.optimization_barrier((logits[0], head_part))
 
-    x_own, x_send = call(
-        functools.partial(compact_kernel, n, gates, capacity),
-        [struct((slots, width + 128 + classes), bf16)] * 2,
-        [*got, *logits],
-        limit=SMALL,
-    )
+    x_own, x_send = compact(got, logits)
     logits[0], x_send = lax.optimization_barrier((logits[0], x_send))
     x_other = send(x_send, 1)
     dx, mix, dw1_keep, dw1_send, dw2_keep, dw2_send = call(
@@ -651,7 +654,7 @@
             struct((all_rows, AUX), f32),
             struct((width // 2, hidden_chip), bf16),
             struct((width // 2, hidden_chip), bf16),
-            struct((shared, lanes // 2, width), f32),
+            struct((shared, lanes // 2, width), bf16),
             struct((shared, lanes // 2, width), bf16),
         ],
         [*got, *logits, head, *weights],
@@ -689,7 +692,7 @@
         limit=BIG,
     )
     dx_other = send(dx_send, 1)
-    reduce_grad = dw2_keep + send(dw2_send, 1).astype(f32)
+    dw2_came = send(dw2_send, 1)
     grad_home, low, high, mix = call(
         functools.partial(scatter_kernel, n, split, gates),
         [
@@ -706,18 +709,25 @@
         [*got, mix],
         limit=SMALL,
     )
-    gate_part = total_of(gate_part, 1, 2 * near)
+    gate_part = gate_part + send(gate_part, 1)
+    count = gate_part.shape[0]
+    joined = classes == width // 2
     low, high, gate_part, dw1 = lax.optimization_barrier((low, high, gate_part, dw1))
     high = along_near(grad_home[split:], high)
     low = along_near(grad_home[:split], low)
+    low, dw2_keep = lax.optimization_barrier((low, dw2_keep))
     grad_parts = along_far(low, high)
-    count = gate_part.shape[0]
-    if classes == width // 2:
-        sums = total_of(jnp.concatenate([gate_part, head_part]), 2 * near, devices)
-        gate_total, head_total = sums[:count], sums[count:]
+    reduce_grad = dw2_keep.astype(f32) + dw2_came.astype(f32)
+    gate_part = total_of(gate_part, masks[:1])
+    if joined:
+        value = total_of(jnp.concatenate([gate_part, head_part]), masks[1:-1])
+        kept = value.astype(bf16)
+        came = send(kept, masks[-1])
+        gate_total = kept[:count].astype(f32) + came[:count].astype(f32)
+        head_total = kept[count:].astype(f32) + came[count:].astype(f32)
     else:
-        gate_total = total_of(gate_part, 2 * near, devices)
-        head_total = total_of(head_part, 2 * near, devices)
+        gate_total = total_of(gate_part, masks[1:])
+        head_total = total_of(head_part, masks[1:])
     halves = [gate_total[: count // 2], gate_total[count // 2 :]]
     gate_total = jnp.concatenate(halves, axis=1).reshape(gates, scenarios, width)
     gate_total = jnp.transpose(gate_total, (1, 2, 0))
@@ -729,6 +739,9 @@
         expand_grad = dw1.reshape(chips, depth, shared, lanes).transpose(2, 1, 0, 3)
         expand_grad = expand_grad.reshape(shared, depth, hidden).astype(f32)
 
+    grad_parts, gate_total, head_total = lax.optimization_barrier(
+        (grad_parts, gate_total, head_total)
+    )
     (feature_grad,) = call(
         functools.partial(final_kernel, len(grad_parts), gates),
         [struct((rows, width), bf16)],

time: 131 us -> 127 us (0.969)
  starting transfers between devices: 43.5 us -> 39.6 us
  Pallas kernels: 31.7 us -> 29.6 us
  local copies, waits for them, and re-layouts: 4.02 us -> 5.75 us
    ppermute x32 -> x34, starting transfers between devices: 34.7 us -> 30.8 us  [send(): return lax.ppermute(value, AXIS, [(i, i ^ mask) for i in range(devices)])]
    ppermute x32 -> x34, waiting for transfers between devices: 46.1 us -> 43.4 us  [send(): return lax.ppermute(value, AXIS, [(i, i ^ mask) for i in range(devices)])]
    all_to_all x1, waiting for transfers between devices: 0.01 us -> 2.62 us  [body(): lax.all_to_all(dw1.reshape(chips, depth, hidden_chip), AXIS, split_axis=0...]
    unnamed x40 -> x48, local copies, waits for them, and re-layouts: 3.3 us -> 5.7 us
    pallas_call x14 -> x17, Pallas kernels: 31.7 us -> 29.6 us  [call(): pl.pallas_call(kernel, out_shape=out_shapes, in_specs=specs, out_specs=[p...]
  transfers between devices with their start and end apart: 34 -> 36, of which waited for: 22 -> 23; matrix products, arithmetic and copies ran while one was open for 2% -> 3% of each run, Pallas kernels for 13% -> 11%
where the time goes in v5:
time: 127 us; the launch traced here: 126 us
  waiting for transfers between devices  46 us (36%)
  starting transfers between devices  39.6 us (31%)
  Pallas kernels  29.6 us (23%)
  local copies, waits for them, and re-layouts  5.75 us (5%)
  other arithmetic  4.37 us (3%)
    ppermute x34, waiting for transfers between devices, send(): return lax.ppermute(value, AXIS, [(i, i ^ mask) for i in range(devices)])  43.4 us
    ppermute x34, starting transfers between devices, send(): return lax.ppermute(value, AXIS, [(i, i ^ mask) for i in range(devices)])  30.8 us
    pallas_call x17, Pallas kernels, call(): pl.pallas_call(kernel, out_shape=out_shapes, in_specs=specs, out_specs=[p...  29.6 us
    unnamed x48, local copies, waits for them, and re-layouts  5.7 us
    all_to_all x1, starting transfers between devices, body(): lax.all_to_all(pieces, AXIS, split_axis=0, concat_axis=0, tiled=True, axi...  4.88 us
    all_to_all x1, starting transfers between devices, body(): lax.all_to_all(dw1.reshape(chips, depth, hidden_chip), AXIS, split_axis=0...  3.92 us
    all_to_all x1, waiting for transfers between devices, body(): lax.all_to_all(dw1.reshape(chips, depth, hidden_chip), AXIS, split_axis=0...  2.62 us
  transfers between devices with their start and end apart: 36, of which 23 were waited for; matrix products, arithmetic and copies ran while one was open for 3% of the time, Pallas kernels for 11%

profile of v5, /device:TPU:0, one launch (start us, length us, event | category | flops | bytes accessed | tf_op | source)
XLA Modules:
  0.0 126.4 jit_solution(9156249727907177763)
XLA Ops:
  0.7 2.0 %shard_map.162 = (bf16[144,256]{1,0:T(8,128)(2,1)}, f32[32,128]{1,0:T(8,128)}) custom-call(s32[8]{0:T(128)} %pads.1, s32[16]{0:T(128)} %slots.1, bf16[128,256]{1,0:T(8,128)(2,1)} %refs_4_.5, s32[1,128]{1,0:T(1,128)} %bitcast.51, bf16[160,256]{1,0:T(8,128)(2,1)} %bitcast.48), custom_call_target="tpu_custom_call" | custom-call | flops 100000 | bytes 100000 | tf_op jit(solution)/shard_map/pallas_call | solution.py:29
  2.6 5.0 %collective-permute-start.2 = (bf16[144,256]{1,0:T(8,128)(2,1)}, bf16[144,256]{1,0:T(8,128)(2,1)S(1)}, u32[]{:S(2)}, u32[]{:S(2)}) collective-permute-start(bf16[144,256]{1,0:T(8,128)(2,1)} %get-tuple-element.66), channel_id=1, source_target_pairs={{0,12},{1,13},{2,14},{3,15},{4,8},{5,9},{6,10},{7,11},{8,4},{9,5},... | collective-permute-start | bytes 221192 | tf_op jit(solution)/shard_map/ppermute | solution.py:524
  7.7 0.6 collective-permute-start
  8.2 1.0 copy-done.6
  9.4 0.8 copy-done.4
  10.7 3.4 %collective-permute-done.1 = bf16[144,256]{1,0:T(8,128)(2,1)S(1)} collective-permute-done((bf16[144,256]{1,0:T(8,128)(2,1)}, bf16[144,256]{1,0:T(8,128)(2,1)S(1)}, u32[]{:S(2)}, u32[]{:S(2)}) %collective-permute-start.1) | collective-permute-done | bytes 73760 | tf_op jit(solution)/shard_map/ppermute | solution.py:524
  14.1 4.9 %all-to-all-start = ((bf16[8,16,2048]{2,1,0:T(8,128)(2,1)}), bf16[8,16,2048]{2,1,0:T(8,128)(2,1)S(1)}, u32[]{:S(2)}, u32[]{:S(2)}) async-start(bf16[8,16,2048]{2,1,0:T(8,128)(2,1)} %copy-done.4), calls=%async_computation | async-start | bytes 1048576 | tf_op jit(solution)/shard_map/all_to_all | solution.py:570
  19.0 2.1 %collective-permute-start.3 = (bf16[4,144,256]{2,1,0:T(8,128)(2,1)S(1)}, bf16[4,144,256]{2,1,0:T(8,128)(2,1)S(1)}, u32[]{:S(2)}, u32[]{:S(2)}) collective-permute-start(bf16[4,144,256]{2,1,0:T(8,128)(2,1)S(1)} %pad_maximum_fusion.refs_0_.refs_1_), channel_id=1, source_target_pairs={{0,2},{1,3},{2,0},{3,1},{4,6},{5,7},{6,4},{7,5},{8,10},{9,11},{10,... | collective-permute-start | bytes 884744 | tf_op jit(solution)/shard_map/ppermute | solution.py:524
  21.1 0.7 shard_map.164
  22.1 1.1 collective-permute-done.4.other
  23.2 1.0 shard_map.165
  24.4 1.0 copy-done.7
  25.5 7.1 %collective-permute-done.3.refs_1_.refs_2_ = bf16[4,144,256]{2,1,0:T(8,128)(2,1)S(1)} collective-permute-done((bf16[4,144,256]{2,1,0:T(8,128)(2,1)S(1)}, bf16[4,144,256]{2,1,0:T(8,128)(2,1)S(1)}, u32[]{:S(2)}, u32[]{:S(2)}) %collective-permute-start.3) | collective-permute-done | bytes 294944 | tf_op jit(solution)/shard_map/ppermute | solution.py:524
  32.6 0.7 shard_map.168
  33.3 0.6 collective-permute-start.8
  33.9 0.9 collective-permute-done.8.other
  34.9 1.2 copy-done.2
  36.1 0.9 shard_map.169
  37.5 0.9 collective-permute-done.9.refs_6_
  38.4 2.3 %shard_map.170 = (bf16[2,128,256]{2,1,0:T(8,128)(2,1)S(1)}, bf16[2,128,256]{2,1,0:T(8,128)(2,1)S(1)}) custom-call(bf16[4,144,256]{2,1,0:T(8,128)(2,1)S(1)} %pad_maximum_fusion.refs_0_.refs_1_, bf16[4,144,256]{2,1,0:T(8,128)(2,1)S(1)} %collective-permute-done.3.refs_1_.refs_2_, bf16[128,2048]{1,0:T(8,128)(2,1)S(1)} %bitcast.45, ...), custom_call_target="tpu_custom_call" | custom-call | flops 100000 | bytes 100000 | tf_op jit(solution)/shard_map/pallas_call | solution.py:29
  40.6 0.8 collective-permute-start.10
  41.5 1.3 collective-permute-start.12
  42.7 2.3 %shard_map.167 = bf16[4,128,256]{2,1,0:T(8,128)(2,1)S(1)} custom-call(bf16[4,144,256]{2,1,0:T(8,128)(2,1)S(1)} %pad_maximum_fusion.refs_0_.refs_1_, bf16[4,144,256]{2,1,0:T(8,128)(2,1)S(1)} %pad_maximum_fusion.refs_0_.refs_1_, bf16[128,2048]{1,0:T(8,128)(2,1)S(1)} %bitcast.46, bf16[128,2048]{1,0:T(8,128)(2,1)S(1)} %collective-permute-done.7.refs_3_.refs_6_, ...), custom_call_target="tpu_custom_call" | custom-call | flops 100000 | bytes 100000 | tf_op jit(solution)/shard_map/pallas_call | solution.py:29
  45.0 2.0 %collective-permute-done.10 = bf16[2,128,256]{2,1,0:T(8,128)(2,1)S(1)} collective-permute-done((bf16[2,128,256]{2,1,0:T(8,128)(2,1)S(1)}, bf16[2,128,256]{2,1,0:T(8,128)(2,1)S(1)}, u32[]{:S(2)}, u32[]{:S(2)}) %collective-permute-start.10) | collective-permute-done | bytes 131104 | tf_op jit(solution)/shard_map/ppermute | solution.py:524
  47.0 2.2 %collective-permute-done.12 = bf16[2,128,256]{2,1,0:T(8,128)(2,1)S(1)} collective-permute-done((bf16[2,128,256]{2,1,0:T(8,128)(2,1)S(1)}, bf16[2,128,256]{2,1,0:T(8,128)(2,1)S(1)}, u32[]{:S(2)}, u32[]{:S(2)}) %collective-permute-start.12) | collective-permute-done | bytes 131104 | tf_op jit(solution)/shard_map/ppermute | solution.py:524
  49.3 3.1 %collective-permute-start.14 = (bf16[128,256]{1,0:T(8,128)(2,1)S(1)}, bf16[128,256]{1,0:T(8,128)(2,1)S(1)}, u32[]{:S(2)}, u32[]{:S(2)}) collective-permute-start(bf16[128,256]{1,0:T(8,128)(2,1)S(1)} %get-tuple-element.133), channel_id=1, source_target_pairs={{0,12},{1,13},{2,14},{3,15},{4,8},{5,9},{6,10},{7,11},{8,4},{9,5},... | collective-permute-start | bytes 196616 | tf_op jit(solution)/shard_map/ppermute | solution.py:524
  52.8 1.0 collective-permute-start.11
  53.9 2.1 %collective-permute-done.14.refs_3_ = bf16[128,256]{1,0:T(8,128)(2,1)S(1)} collective-permute-done((bf16[128,256]{1,0:T(8,128)(2,1)S(1)}, bf16[128,256]{1,0:T(8,128)(2,1)S(1)}, u32[]{:S(2)}, u32[]{:S(2)}) %collective-permute-start.14) | collective-permute-done | bytes 65568 | tf_op jit(solution)/shard_map/ppermute | solution.py:524
  56.0 2.6 %collective-permute-done.13.refs_2_ = bf16[128,256]{1,0:T(8,128)(2,1)S(1)} collective-permute-done((bf16[128,256]{1,0:T(8,128)(2,1)S(1)}, bf16[128,256]{1,0:T(8,128)(2,1)S(1)}, u32[]{:S(2)}, u32[]{:S(2)}) %collective-permute-start.13) | collective-permute-done | bytes 65568 | tf_op jit(solution)/shard_map/ppermute | solution.py:524
  59.2 2.5 %collective-permute-start.17 = (bf16[128,128]{1,0:T(8,128)(2,1)S(1)}, bf16[128,128]{1,0:T(8,128)(2,1)S(1)}, u32[]{:S(2)}, u32[]{:S(2)}) collective-permute-start(bf16[128,128]{1,0:T(8,128)(2,1)S(1)} %get-tuple-element.86), channel_id=1, source_target_pairs={{0,12},{1,13},{2,14},{3,15},{4,8},{5,9},{6,10},{7,11},{8,4},{9,5},... | collective-permute-start | bytes 98312 | tf_op jit(solution)/shard_map/ppermute | solution.py:524
  61.7 1.9 %collective-permute-start.15 = (bf16[128,128]{1,0:T(8,128)(2,1)S(1)}, bf16[128,128]{1,0:T(8,128)(2,1)S(1)}, u32[]{:S(2)}, u32[]{:S(2)}) collective-permute-start(bf16[128,128]{1,0:T(8,128)(2,1)S(1)} %get-tuple-element.86), channel_id=1, source_target_pairs={{0,4},{1,5},{2,6},{3,7},{4,0},{5,1},{6,2},{7,3},{8,12},{9,13},{10,... | collective-permute-start | bytes 98312 | tf_op jit(solution)/shard_map/ppermute | solution.py:524
  63.7 1.1 collective-permute-start.19
  65.2 1.4 %collective-permute-done.16 = bf16[128,128]{1,0:T(8,128)(2,1)S(1)} collective-permute-done((bf16[128,128]{1,0:T(8,128)(2,1)S(1)}, bf16[128,128]{1,0:T(8,128)(2,1)S(1)}, u32[]{:S(2)}, u32[]{:S(2)}) %collective-permute-start.16) | collective-permute-done | bytes 32800 | tf_op jit(solution)/shard_map/ppermute | solution.py:524
  66.6 0.7 collective-permute-start.20
  67.2 2.4 %collective-permute-done.19 = bf16[256,128]{1,0:T(8,128)(2,1)S(1)} collective-permute-done((bf16[256,128]{1,0:T(8,128)(2,1)S(1)}, bf16[256,128]{1,0:T(8,128)(2,1)S(1)}, u32[]{:S(2)}, u32[]{:S(2)}) %collective-permute-start.19) | collective-permute-done | bytes 65568 | tf_op jit(solution)/shard_map/ppermute | solution.py:524
  69.6 0.6 convert_add_fusion.3
  70.3 1.3 %collective-permute-done.20.refs_4_.refs_3_ = bf16[4,128,128]{2,1,0:T(8,128)(2,1)S(1)} collective-permute-done((bf16[4,128,128]{2,1,0:T(8,128)(2,1)S(1)}, bf16[4,128,128]{2,1,0:T(8,128)(2,1)S(1)}, u32[]{:S(2)}, u32[]{:S(2)}) %collective-permute-start.20) | collective-permute-done | bytes 131104 | tf_op jit(solution)/shard_map/ppermute | solution.py:524
  71.6 0.8 shard_map.172
  72.4 0.7 copy-done.21
  73.1 9.1 %shard_map.173 = (bf16[1024,256]{1,0:T(8,128)(2,1)S(1)}, f32[1024,32]{1,0:T(8,128)S(1)}, bf16[128,2048]{1,0:T(8,128)(2,1)S(1)}, bf16[128,2048]{1,0:T(8,128)(2,1)...) custom-call(bf16[4,144,256]{2,1,0:T(8,128)(2,1)S(1)} %pad_maximum_fusion.refs_0_.refs_1_, ...), custom_call_target="tpu_custom_call" | custom-call | flops 100000 | bytes 100000 | tf_op jit(solution)/shard_map/pallas_call | solution.py:29
  82.2 0.8 copy-done.19
  83.1 1.9 %collective-permute-done.21 = bf16[128,2048]{1,0:T(8,128)(2,1)S(1)} collective-permute-done((bf16[128,2048]{1,0:T(8,128)(2,1)S(1)}, bf16[128,2048]{1,0:T(8,128)(2,1)S(1)}, u32[]{:S(2)}, u32[]{:S(2)}) %collective-permute-start.21) | collective-permute-done | bytes 524320 | tf_op jit(solution)/shard_map/ppermute | solution.py:524
  85.0 0.9 add_convert_fusion
  86.0 3.9 %all-to-all-start.1 = ((bf16[8,16,2048]{2,1,0:T(8,128)(2,1)}), bf16[8,16,2048]{2,1,0:T(8,128)(2,1)S(1)}, u32[]{:S(2)}, u32[]{:S(2)}) async-start(bf16[8,16,2048]{2,1,0:T(8,128)(2,1)} %bitcast.53), calls=%async_computation.1 | async-start | bytes 1048576 | tf_op jit(solution)/shard_map/all_to_all | solution.py:674
  90.0 1.7 %collective-permute-done.22.other = bf16[256,512]{1,0:T(8,128)(2,1)S(1)} collective-permute-done((bf16[256,512]{1,0:T(8,128)(2,1)}, bf16[256,512]{1,0:T(8,128)(2,1)S(1)}, u32[]{:S(2)}, u32[]{:S(2)}) %collective-permute-start.22) | collective-permute-done | bytes 262176 | tf_op jit(solution)/shard_map/ppermute | solution.py:524
  91.7 5.4 %shard_map.174 = (bf16[256,384]{1,0:T(8,128)(2,1)S(1)}, bf16[256,384]{1,0:T(8,128)(2,1)S(1)}, f32[256,2048]{1,0:T(8,128)}, f32[2048,256]{1,0:T(8,128)}) custom-call(bf16[256,512]{1,0:T(8,128)(2,1)S(1)} %get-tuple-element.96.own, bf16[256,512]{1,0:T(8,128)(2,1)S(1)} %collective-permute-done.22.other, bf16[256,128]{1,0:T(8,128)(2,1)S(1)} %copy-done.5, ...), custom_call_target="tpu_custom_call" | custom-call | flops 100000 | bytes 100000 | tf_op jit(solution)/shard_map/pallas_call | solution.py:29
  97.3 1.3 %collective-permute-done.23.refs_5_ = bf16[256,384]{1,0:T(8,128)(2,1)S(1)} collective-permute-done((bf16[256,384]{1,0:T(8,128)(2,1)S(1)}, bf16[256,384]{1,0:T(8,128)(2,1)S(1)}, u32[]{:S(2)}, u32[]{:S(2)}) %collective-permute-start.23) | collective-permute-done | bytes 196640 | tf_op jit(solution)/shard_map/ppermute | solution.py:524
  98.6 1.6 %shard_map.175 = (bf16[4,144,256]{2,1,0:T(8,128)(2,1)S(1)}, bf16[2,144,256]{2,1,0:T(8,128)(2,1)S(1)}, bf16[2,144,256]{2,1,0:T(8,128)(2,1)S(1)}, bf16[8,32,128]{2,1,0:T(8,128)(2,1)S(1)}) custom-call(bf16[4,144,256]{2,1,0:T(8,128)(2,1)S(1)} %pad_maximum_fusion.refs_0_.refs_1_, bf16[4,144,256]{2,1,0:T(8,128)(2,1)S(1)} %collective-permute-done.3.refs_1_.refs_2_, ...), custom_call_target="tpu_custom_call" | custom-call | flops 100000 | bytes 100000 | tf_op jit(solution)/shard_map/pallas_call | solution.py:29
  100.8 1.3 collective-permute-done.24
  102.1 2.6 %all-to-all-done.1.pieces = bf16[8,16,2048]{2,1,0:T(8,128)(2,1)S(1)} async-done(((bf16[8,16,2048]{2,1,0:T(8,128)(2,1)}), bf16[8,16,2048]{2,1,0:T(8,128)(2,1)S(1)}, u32[]{:S(2)}, u32[]{:S(2)}) %all-to-all-start.1) | async-done | bytes 524320 | tf_op jit(solution)/shard_map/all_to_all | solution.py:674
  105.0 1.5 %collective-permute-start.25 = (bf16[2,144,256]{2,1,0:T(8,128)(2,1)S(1)}, bf16[2,144,256]{2,1,0:T(8,128)(2,1)S(1)}, u32[]{:S(2)}, u32[]{:S(2)}) collective-permute-start(bf16[2,144,256]{2,1,0:T(8,128)(2,1)S(1)} %get-tuple-element.105), channel_id=1, source_target_pairs={{0,2},{1,3},{2,0},{3,1},{4,6},{5,7},{6,4},{7,5},{8,10},{9,11},{10,... | collective-permute-start | bytes 442376 | tf_op jit(solution)/shard_map/ppermute | solution.py:524
  106.5 0.6 collective-permute-start.27
  107.1 1.0 shard_map.178
  108.1 2.8 %collective-permute-done.30 = bf16[320,128]{1,0:T(8,128)(2,1)S(1)} collective-permute-done((bf16[320,128]{1,0:T(8,128)(2,1)S(1)}, bf16[320,128]{1,0:T(8,128)(2,1)S(1)}, u32[]{:S(2)}, u32[]{:S(2)}) %collective-permute-start.30) | collective-permute-done | bytes 81952 | tf_op jit(solution)/shard_map/ppermute | solution.py:524
  111.0 0.7 collective-permute-done.25
  111.7 2.8 %collective-permute-done.27 = bf16[2,144,256]{2,1,0:T(8,128)(2,1)S(1)} collective-permute-done((bf16[2,144,256]{2,1,0:T(8,128)(2,1)S(1)}, bf16[2,144,256]{2,1,0:T(8,128)(2,1)S(1)}, u32[]{:S(2)}, u32[]{:S(2)}) %collective-permute-start.27) | collective-permute-done | bytes 147488 | tf_op jit(solution)/shard_map/ppermute | solution.py:524
  114.6 1.5 %collective-permute-start.26 = (bf16[144,256]{1,0:T(8,128)(2,1)S(1)}, bf16[144,256]{1,0:T(8,128)(2,1)S(1)}, u32[]{:S(2)}, u32[]{:S(2)}) collective-permute-start(bf16[144,256]{1,0:T(8,128)(2,1)S(1)} %get-tuple-element.131), channel_id=1, source_target_pairs={{0,4},{1,5},{2,6},{3,7},{4,0},{5,1},{6,2},{7,3},{8,12},{9,13},{10,... | collective-permute-start | bytes 221192 | tf_op jit(solution)/shard_map/ppermute | solution.py:524
  116.2 2.6 %collective-permute-start.29 = (bf16[144,256]{1,0:T(8,128)(2,1)S(1)}, bf16[144,256]{1,0:T(8,128)(2,1)S(1)}, u32[]{:S(2)}, u32[]{:S(2)}) collective-permute-start(bf16[144,256]{1,0:T(8,128)(2,1)S(1)} %get-tuple-element.129), channel_id=1, source_target_pairs={{0,12},{1,13},{2,14},{3,15},{4,8},{5,9},{6,10},{7,11},{8,4},{9,5},... | collective-permute-start | bytes 221192 | tf_op jit(solution)/shard_map/ppermute | solution.py:524
  118.8 1.5 %collective-permute-start.32 = (bf16[576,128]{1,0:T(8,128)(2,1)S(1)}, bf16[576,128]{1,0:T(8,128)(2,1)S(1)}, u32[]{:S(2)}, u32[]{:S(2)}) collective-permute-start(bf16[576,128]{1,0:T(8,128)(2,1)S(1)} %add_convert_fusion.1), channel_id=1, source_target_pairs={{0,2},{1,3},{2,0},{3,1},{4,6},{5,7},{6,4},{7,5},{8,10},{9,11},{10,... | collective-permute-start | bytes 442376 | tf_op jit(solution)/shard_map/ppermute | solution.py:524
  120.4 1.1 convert_add_fusion
  121.5 2.6 %collective-permute-done.32 = bf16[576,128]{1,0:T(8,128)(2,1)S(1)} collective-permute-done((bf16[576,128]{1,0:T(8,128)(2,1)S(1)}, bf16[576,128]{1,0:T(8,128)(2,1)S(1)}, u32[]{:S(2)}, u32[]{:S(2)}) %collective-permute-start.32) | collective-permute-done | bytes 147488 | tf_op jit(solution)/shard_map/ppermute | solution.py:524
  124.1 0.7 convert_add_fusion.2
  124.8 0.7 maximum_bitcast_fusion
  125.5 0.9 shard_map.177
  (93 shorter events, 4.8 us)
Async XLA Ops:
  0.6 22.5 %copy-start.1 = (bf16[1,2048,256]{2,1,0:T(8,128)(2,1)S(1)}, bf16[1,2048,256]{2,1,0:T(8,128)(2,1)}, u32[]{:S(2)}) copy-start(bf16[1,2048,256]{2,1,0:T(8,128)(2,1)} %param.20) | copy-start | bytes 3145732
  0.6 22.5 %copy-start = (bf16[1,256,2048]{2,1,0:T(8,128)(2,1)S(1)}, bf16[1,256,2048]{2,1,0:T(8,128)(2,1)}, u32[]{:S(2)}) copy-start(bf16[1,256,2048]{2,1,0:T(8,128)(2,1)} %param.19) | copy-start | bytes 3145732
  2.6 8.0 %collective-permute-start.2 = (bf16[144,256]{1,0:T(8,128)(2,1)}, bf16[144,256]{1,0:T(8,128)(2,1)S(1)}, u32[]{:S(2)}, u32[]{:S(2)}) collective-permute-start(bf16[144,256]{1,0:T(8,128)(2,1)} %get-tuple-element.66), channel_id=1, source_target_pairs={{0,12},{1,13},{2,14},{3,15},{4,8},{5,9},{6,10},{7,11},{8,4},{9,5},... | collective-permute-start | bytes 221192 | tf_op jit(solution)/shard_map/ppermute | solution.py:524
  7.7 6.4 %collective-permute-start.1 = (bf16[144,256]{1,0:T(8,128)(2,1)}, bf16[144,256]{1,0:T(8,128)(2,1)S(1)}, u32[]{:S(2)}, u32[]{:S(2)}) collective-permute-start(bf16[144,256]{1,0:T(8,128)(2,1)} %get-tuple-element.66), channel_id=1, source_target_pairs={{0,8},{1,9},{2,10},{3,11},{4,12},{5,13},{6,14},{7,15},{8,0},{9,1},... | collective-permute-start | bytes 221192 | tf_op jit(solution)/shard_map/ppermute | solution.py:524
  7.7 6.4 %collective-permute-start = (bf16[144,256]{1,0:T(8,128)(2,1)}, bf16[144,256]{1,0:T(8,128)(2,1)S(1)}, u32[]{:S(2)}, u32[]{:S(2)}) collective-permute-start(bf16[144,256]{1,0:T(8,128)(2,1)} %get-tuple-element.66), channel_id=1, source_target_pairs={{0,4},{1,5},{2,6},{3,7},{4,0},{5,1},{6,2},{7,3},{8,12},{9,13},{10,... | collective-permute-start | bytes 221192 | tf_op jit(solution)/shard_map/ppermute | solution.py:524
  8.2 1.0 copy-start.6
  9.3 9.7 %copy-start.23 = (bf16[144,256]{1,0:T(8,128)(2,1)S(1)}, bf16[144,256]{1,0:T(8,128)(2,1)}, u32[]{:S(2)}) copy-start(bf16[144,256]{1,0:T(8,128)(2,1)} %get-tuple-element.66) | copy-start | bytes 221188
  9.4 0.8 copy-start.4
  14.1 18.6 %all-to-all-start = ((bf16[8,16,2048]{2,1,0:T(8,128)(2,1)}), bf16[8,16,2048]{2,1,0:T(8,128)(2,1)S(1)}, u32[]{:S(2)}, u32[]{:S(2)}) async-start(bf16[8,16,2048]{2,1,0:T(8,128)(2,1)} %copy-done.4), calls=%async_computation | async-start | bytes 1048576 | tf_op jit(solution)/shard_map/all_to_all | solution.py:570
  19.0 5.4 %collective-permute-start.6 = (bf16[16,64,256]{2,1,0:T(8,128)(2,1)}, bf16[16,64,256]{2,1,0:T(8,128)(2,1)S(1)}, u32[]{:S(2)}, u32[]{:S(2)}) collective-permute-start(bf16[16,64,256]{2,1,0:T(8,128)(2,1)} %mine.1), channel_id=1, source_target_pairs={{0,1},{1,0},{2,3},{3,2},{4,5},{5,4},{6,7},{7,6},{8,9},{9,8},{10,11... | collective-permute-start | bytes 1572872 | tf_op jit(solution)/shard_map/ppermute | solution.py:524
  19.0 13.6 %collective-permute-start.3 = (bf16[4,144,256]{2,1,0:T(8,128)(2,1)S(1)}, bf16[4,144,256]{2,1,0:T(8,128)(2,1)S(1)}, u32[]{:S(2)}, u32[]{:S(2)}) collective-permute-start(bf16[4,144,256]{2,1,0:T(8,128)(2,1)S(1)} %pad_maximum_fusion.refs_0_.refs_1_), channel_id=1, source_target_pairs={{0,2},{1,3},{2,0},{3,1},{4,6},{5,7},{6,4},{7,5},{8,10},{9,11},{10,... | collective-permute-start | bytes 884744 | tf_op jit(solution)/shard_map/ppermute | solution.py:524
  21.8 1.4 %collective-permute-start.4 = (bf16[128,384]{1,0:T(8,128)(2,1)S(1)}, bf16[128,384]{1,0:T(8,128)(2,1)S(1)}, u32[]{:S(2)}, u32[]{:S(2)}) collective-permute-start(bf16[128,384]{1,0:T(8,128)(2,1)S(1)} %get-tuple-element.71), channel_id=1, source_target_pairs={{0,1},{1,0},{2,3},{3,2},{4,5},{5,4},{6,7},{7,6},{8,9},{9,8},{10,11... | collective-permute-start | bytes 294920 | tf_op jit(solution)/shard_map/ppermute | solution.py:524
  24.1 1.4 %collective-permute-start.5 = (bf16[128,256]{1,0:T(8,128)(2,1)S(1)}, bf16[128,256]{1,0:T(8,128)(2,1)S(1)}, u32[]{:S(2)}, u32[]{:S(2)}) collective-permute-start(bf16[128,256]{1,0:T(8,128)(2,1)S(1)} %get-tuple-element.73), channel_id=1, source_target_pairs={{0,1},{1,0},{2,3},{3,2},{4,5},{5,4},{6,7},{7,6},{8,9},{9,8},{10,11... | collective-permute-start | bytes 196616 | tf_op jit(solution)/shard_map/ppermute | solution.py:524
  24.4 1.0 copy-start.7
  32.6 5.7 %collective-permute-start.7 = (bf16[128,2048]{1,0:T(8,128)(2,1)S(1)}, bf16[128,2048]{1,0:T(8,128)(2,1)S(1)}, u32[]{:S(2)}, u32[]{:S(2)}) collective-permute-start(bf16[128,2048]{1,0:T(8,128)(2,1)S(1)} %bitcast.44), channel_id=1, source_target_pairs={{0,1},{1,0},{2,3},{3,2},{4,5},{5,4},{6,7},{7,6},{8,9},{9,8},{10,11... | collective-permute-start | bytes 1572872 | tf_op jit(solution)/shard_map/ppermute | solution.py:524
  33.3 1.5 %collective-permute-start.8 = (bf16[128,384]{1,0:T(8,128)(2,1)S(1)}, bf16[128,384]{1,0:T(8,128)(2,1)S(1)}, u32[]{:S(2)}, u32[]{:S(2)}) collective-permute-start(bf16[128,384]{1,0:T(8,128)(2,1)S(1)} %get-tuple-element.81), channel_id=1, source_target_pairs={{0,1},{1,0},{2,3},{3,2},{4,5},{5,4},{6,7},{7,6},{8,9},{9,8},{10,11... | collective-permute-start | bytes 294920 | tf_op jit(solution)/shard_map/ppermute | solution.py:524
  34.9 1.2 copy-start.2
  37.0 1.3 %collective-permute-start.9 = (bf16[128,256]{1,0:T(8,128)(2,1)S(1)}, bf16[128,256]{1,0:T(8,128)(2,1)S(1)}, u32[]{:S(2)}, u32[]{:S(2)}) collective-permute-start(bf16[128,256]{1,0:T(8,128)(2,1)S(1)} %get-tuple-element.83), channel_id=1, source_target_pairs={{0,1},{1,0},{2,3},{3,2},{4,5},{5,4},{6,7},{7,6},{8,9},{9,8},{10,11... | collective-permute-start | bytes 196616 | tf_op jit(solution)/shard_map/ppermute | solution.py:524
  40.6 6.4 %collective-permute-start.10 = (bf16[2,128,256]{2,1,0:T(8,128)(2,1)S(1)}, bf16[2,128,256]{2,1,0:T(8,128)(2,1)S(1)}, u32[]{:S(2)}, u32[]{:S(2)}) collective-permute-start(bf16[2,128,256]{2,1,0:T(8,128)(2,1)S(1)} %get-tuple-element.84), channel_id=1, source_target_pairs={{0,2},{1,3},{2,0},{3,1},{4,6},{5,7},{6,4},{7,5},{8,10},{9,11},{10,... | collective-permute-start | bytes 393224 | tf_op jit(solution)/shard_map/ppermute | solution.py:524
  41.5 17.1 %copy-start.5 = (bf16[256,128]{1,0:T(8,128)(2,1)S(1)}, bf16[256,128]{1,0:T(8,128)(2,1)}, u32[]{:S(2)}) copy-start(bf16[256,128]{1,0:T(8,128)(2,1)} %head.1) | copy-start | bytes 196612
  41.5 17.1 %copy-start.16 = (f32[128,128]{1,0:T(8,128)S(1)}, f32[128,128]{1,0:T(8,128)}, u32[]{:S(2)}) copy-start(f32[128,128]{1,0:T(8,128)} %refs_5_.1) | copy-start | bytes 196612
  41.5 7.8 %collective-permute-start.12 = (bf16[2,128,256]{2,1,0:T(8,128)(2,1)S(1)}, bf16[2,128,256]{2,1,0:T(8,128)(2,1)S(1)}, u32[]{:S(2)}, u32[]{:S(2)}) collective-permute-start(bf16[2,128,256]{2,1,0:T(8,128)(2,1)S(1)} %get-tuple-element.85), channel_id=1, source_target_pairs={{0,2},{1,3},{2,0},{3,1},{4,6},{5,7},{6,4},{7,5},{8,10},{9,11},{10,... | collective-permute-start | bytes 393224 | tf_op jit(solution)/shard_map/ppermute | solution.py:524
  49.3 6.6 %collective-permute-start.14 = (bf16[128,256]{1,0:T(8,128)(2,1)S(1)}, bf16[128,256]{1,0:T(8,128)(2,1)S(1)}, u32[]{:S(2)}, u32[]{:S(2)}) collective-permute-start(bf16[128,256]{1,0:T(8,128)(2,1)S(1)} %get-tuple-element.133), channel_id=1, source_target_pairs={{0,12},{1,13},{2,14},{3,15},{4,8},{5,9},{6,10},{7,11},{8,4},{9,5},... | collective-permute-start | bytes 196616 | tf_op jit(solution)/shard_map/ppermute | solution.py:524
  52.5 6.1 %collective-permute-start.13 = (bf16[128,256]{1,0:T(8,128)(2,1)S(1)}, bf16[128,256]{1,0:T(8,128)(2,1)S(1)}, u32[]{:S(2)}, u32[]{:S(2)}) collective-permute-start(bf16[128,256]{1,0:T(8,128)(2,1)S(1)} %get-tuple-element.134), channel_id=1, source_target_pairs={{0,8},{1,9},{2,10},{3,11},{4,12},{5,13},{6,14},{7,15},{8,0},{9,1},... | collective-permute-start | bytes 196616 | tf_op jit(solution)/shard_map/ppermute | solution.py:524
  52.8 5.7 %collective-permute-start.11 = (bf16[128,256]{1,0:T(8,128)(2,1)S(1)}, bf16[128,256]{1,0:T(8,128)(2,1)S(1)}, u32[]{:S(2)}, u32[]{:S(2)}) collective-permute-start(bf16[128,256]{1,0:T(8,128)(2,1)S(1)} %get-tuple-element.135), channel_id=1, source_target_pairs={{0,4},{1,5},{2,6},{3,7},{4,0},{5,1},{6,2},{7,3},{8,12},{9,13},{10,... | collective-permute-start | bytes 196616 | tf_op jit(solution)/shard_map/ppermute | solution.py:524
  59.1 4.5 %collective-permute-start.18 = (f32[256,128]{1,0:T(8,128)S(1)}, f32[256,128]{1,0:T(8,128)S(1)}, u32[]{:S(2)}, u32[]{:S(2)}) collective-permute-start(f32[256,128]{1,0:T(8,128)S(1)} %get-tuple-element.87), channel_id=1, source_target_pairs={{0,1},{1,0},{2,3},{3,2},{4,5},{5,4},{6,7},{7,6},{8,9},{9,8},{10,11... | collective-permute-start | bytes 393224 | tf_op jit(solution)/shard_map/ppermute | solution.py:524
  59.2 6.0 %collective-permute-start.17 = (bf16[128,128]{1,0:T(8,128)(2,1)S(1)}, bf16[128,128]{1,0:T(8,128)(2,1)S(1)}, u32[]{:S(2)}, u32[]{:S(2)}) collective-permute-start(bf16[128,128]{1,0:T(8,128)(2,1)S(1)} %get-tuple-element.86), channel_id=1, source_target_pairs={{0,12},{1,13},{2,14},{3,15},{4,8},{5,9},{6,10},{7,11},{8,4},{9,5},... | collective-permute-start | bytes 98312 | tf_op jit(solution)/shard_map/ppermute | solution.py:524
  61.7 4.8 %collective-permute-start.16 = (bf16[128,128]{1,0:T(8,128)(2,1)S(1)}, bf16[128,128]{1,0:T(8,128)(2,1)S(1)}, u32[]{:S(2)}, u32[]{:S(2)}) collective-permute-start(bf16[128,128]{1,0:T(8,128)(2,1)S(1)} %get-tuple-element.86), channel_id=1, source_target_pairs={{0,8},{1,9},{2,10},{3,11},{4,12},{5,13},{6,14},{7,15},{8,0},{9,1},... | collective-permute-start | bytes 98312 | tf_op jit(solution)/shard_map/ppermute | solution.py:524
  61.7 4.8 %collective-permute-start.15 = (bf16[128,128]{1,0:T(8,128)(2,1)S(1)}, bf16[128,128]{1,0:T(8,128)(2,1)S(1)}, u32[]{:S(2)}, u32[]{:S(2)}) collective-permute-start(bf16[128,128]{1,0:T(8,128)(2,1)S(1)} %get-tuple-element.86), channel_id=1, source_target_pairs={{0,4},{1,5},{2,6},{3,7},{4,0},{5,1},{6,2},{7,3},{8,12},{9,13},{10,... | collective-permute-start | bytes 98312 | tf_op jit(solution)/shard_map/ppermute | solution.py:524
  63.7 6.0 %collective-permute-start.19 = (bf16[256,128]{1,0:T(8,128)(2,1)S(1)}, bf16[256,128]{1,0:T(8,128)(2,1)S(1)}, u32[]{:S(2)}, u32[]{:S(2)}) collective-permute-start(bf16[256,128]{1,0:T(8,128)(2,1)S(1)} %add_convert_fusion.7), channel_id=1, source_target_pairs={{0,8},{1,9},{2,10},{3,11},{4,12},{5,13},{6,14},{7,15},{8,0},{9,1},... | collective-permute-start | bytes 196616 | tf_op jit(solution)/shard_map/ppermute | solution.py:524
  66.6 5.0 %collective-permute-start.20 = (bf16[4,128,128]{2,1,0:T(8,128)(2,1)S(1)}, bf16[4,128,128]{2,1,0:T(8,128)(2,1)S(1)}, u32[]{:S(2)}, u32[]{:S(2)}) collective-permute-start(bf16[4,128,128]{2,1,0:T(8,128)(2,1)S(1)} %pad_maximum_fusion.2.refs_3_.refs_2_), channel_id=1, source_target_pairs={{0,2},{1,3},{2,0},{3,1},{4,6},{5,7},{6,4},{7,5},{8,10},{9,11},{10,... | collective-permute-start | bytes 393224 | tf_op jit(solution)/shard_map/ppermute | solution.py:524
  72.4 0.7 copy-start.21
  82.2 0.8 copy-start.19
  83.0 2.9 %copy-start.8 = (bf16[16,64,256]{2,1,0:T(8,128)(2,1)}, bf16[16,64,256]{2,1,0:T(8,128)(2,1)S(1)}, u32[]{:S(2)}) copy-start(bf16[16,64,256]{2,1,0:T(8,128)(2,1)S(1)} %get-tuple-element.117) | copy-start | bytes 1572868
  83.0 2.9 %copy-start.10 = (bf16[1024,256]{1,0:T(8,128)(2,1)}, bf16[1024,256]{1,0:T(8,128)(2,1)S(1)}, u32[]{:S(2)}) copy-start(bf16[1024,256]{1,0:T(8,128)(2,1)S(1)} %get-tuple-element.91.refs_2_) | copy-start | bytes 1572868
  83.0 2.9 %copy-start.12 = (f32[1024,32]{1,0:T(8,128)}, f32[1024,32]{1,0:T(8,128)S(1)}, u32[]{:S(2)}) copy-start(f32[1024,32]{1,0:T(8,128)S(1)} %get-tuple-element.92.refs_3_) | copy-start | bytes 393220
  83.0 8.7 %copy-start.3 = (bf16[1,2048,256]{2,1,0:T(8,128)(2,1)S(1)}, bf16[1,2048,256]{2,1,0:T(8,128)(2,1)}, u32[]{:S(2)}) copy-start(bf16[1,2048,256]{2,1,0:T(8,128)(2,1)} %param.20) | copy-start | bytes 3145732
  83.0 2.0 %collective-permute-start.21 = (bf16[128,2048]{1,0:T(8,128)(2,1)S(1)}, bf16[128,2048]{1,0:T(8,128)(2,1)S(1)}, u32[]{:S(2)}, u32[]{:S(2)}) collective-permute-start(bf16[128,2048]{1,0:T(8,128)(2,1)S(1)} %get-tuple-element.94), channel_id=1, source_target_pairs={{0,1},{1,0},{2,3},{3,2},{4,5},{5,4},{6,7},{7,6},{8,9},{9,8},{10,11... | collective-permute-start | bytes 1572872 | tf_op jit(solution)/shard_map/ppermute | solution.py:524
  86.0 18.7 %all-to-all-start.1 = ((bf16[8,16,2048]{2,1,0:T(8,128)(2,1)}), bf16[8,16,2048]{2,1,0:T(8,128)(2,1)S(1)}, u32[]{:S(2)}, u32[]{:S(2)}) async-start(bf16[8,16,2048]{2,1,0:T(8,128)(2,1)} %bitcast.53), calls=%async_computation.1 | async-start | bytes 1048576 | tf_op jit(solution)/shard_map/all_to_all | solution.py:674
  89.9 8.7 %copy-start.11 = (bf16[1024,256]{1,0:T(8,128)(2,1)S(1)}, bf16[1024,256]{1,0:T(8,128)(2,1)}, u32[]{:S(2)}) copy-start(bf16[1024,256]{1,0:T(8,128)(2,1)} %copy-done.10) | copy-start | bytes 1572868
  89.9 8.7 %copy-start.13 = (f32[1024,32]{1,0:T(8,128)S(1)}, f32[1024,32]{1,0:T(8,128)}, u32[]{:S(2)}) copy-start(f32[1024,32]{1,0:T(8,128)} %copy-done.12) | copy-start | bytes 393220
  89.9 1.8 %collective-permute-start.22 = (bf16[256,512]{1,0:T(8,128)(2,1)}, bf16[256,512]{1,0:T(8,128)(2,1)S(1)}, u32[]{:S(2)}, u32[]{:S(2)}) collective-permute-start(bf16[256,512]{1,0:T(8,128)(2,1)} %copy-done.21), channel_id=1, source_target_pairs={{0,1},{1,0},{2,3},{3,2},{4,5},{5,4},{6,7},{7,6},{8,9},{9,8},{10,11... | collective-permute-start | bytes 786440 | tf_op jit(solution)/shard_map/ppermute | solution.py:524
  97.2 7.9 %copy-start.20 = (bf16[16,64,256]{2,1,0:T(8,128)(2,1)S(1)}, bf16[16,64,256]{2,1,0:T(8,128)(2,1)}, u32[]{:S(2)}) copy-start(bf16[16,64,256]{2,1,0:T(8,128)(2,1)} %copy-done.19) | copy-start | bytes 1572868
  97.2 1.4 %collective-permute-start.23 = (bf16[256,384]{1,0:T(8,128)(2,1)S(1)}, bf16[256,384]{1,0:T(8,128)(2,1)S(1)}, u32[]{:S(2)}, u32[]{:S(2)}) collective-permute-start(bf16[256,384]{1,0:T(8,128)(2,1)S(1)} %get-tuple-element.99), channel_id=1, source_target_pairs={{0,1},{1,0},{2,3},{3,2},{4,5},{5,4},{6,7},{7,6},{8,9},{9,8},{10,11... | collective-permute-start | bytes 589832 | tf_op jit(solution)/shard_map/ppermute | solution.py:524
  98.6 12.3 %copy-start.22 = (bf16[256,128]{1,0:T(8,128)(2,1)S(1)}, bf16[256,128]{1,0:T(8,128)(2,1)}, u32[]{:S(2)}) copy-start(bf16[256,128]{1,0:T(8,128)(2,1)} %convert_add_fusion.3) | copy-start | bytes 196612
  100.6 1.5 %collective-permute-start.24 = (f32[320,128]{1,0:T(8,128)S(1)}, f32[320,128]{1,0:T(8,128)S(1)}, u32[]{:S(2)}, u32[]{:S(2)}) collective-permute-start(f32[320,128]{1,0:T(8,128)S(1)} %shard_map.176), channel_id=1, source_target_pairs={{0,1},{1,0},{2,3},{3,2},{4,5},{5,4},{6,7},{7,6},{8,9},{9,8},{10,11... | collective-permute-start | bytes 491528 | tf_op jit(solution)/shard_map/ppermute | solution.py:524
  102.0 18.3 %copy-start.9 = (bf16[16,64,256]{2,1,0:T(8,128)(2,1)S(1)}, bf16[16,64,256]{2,1,0:T(8,128)(2,1)}, u32[]{:S(2)}) copy-start(bf16[16,64,256]{2,1,0:T(8,128)(2,1)} %copy-done.8) | copy-start | bytes 1572868
  104.7 6.2 %collective-permute-start.30 = (bf16[320,128]{1,0:T(8,128)(2,1)S(1)}, bf16[320,128]{1,0:T(8,128)(2,1)S(1)}, u32[]{:S(2)}, u32[]{:S(2)}) collective-permute-start(bf16[320,128]{1,0:T(8,128)(2,1)S(1)} %add.44), channel_id=1, source_target_pairs={{0,8},{1,9},{2,10},{3,11},{4,12},{5,13},{6,14},{7,15},{8,0},{9,1},... | collective-permute-start | bytes 245768 | tf_op jit(solution)/shard_map/ppermute | solution.py:524
  105.0 15.3 %collective-permute-start.33 = (bf16[16,64,256]{2,1,0:T(8,128)(2,1)S(1)}, bf16[16,64,256]{2,1,0:T(8,128)(2,1)S(1)}, u32[]{:S(2)}, u32[]{:S(2)}) collective-permute-start(bf16[16,64,256]{2,1,0:T(8,128)(2,1)S(1)} %copy-done.20), channel_id=1, source_target_pairs={{0,1},{1,0},{2,3},{3,2},{4,5},{5,4},{6,7},{7,6},{8,9},{9,8},{10,11... | collective-permute-start | bytes 1572872 | tf_op jit(solution)/shard_map/ppermute | solution.py:524
  105.0 6.6 %collective-permute-start.25 = (bf16[2,144,256]{2,1,0:T(8,128)(2,1)S(1)}, bf16[2,144,256]{2,1,0:T(8,128)(2,1)S(1)}, u32[]{:S(2)}, u32[]{:S(2)}) collective-permute-start(bf16[2,144,256]{2,1,0:T(8,128)(2,1)S(1)} %get-tuple-element.105), channel_id=1, source_target_pairs={{0,2},{1,3},{2,0},{3,1},{4,6},{5,7},{6,4},{7,5},{8,10},{9,11},{10,... | collective-permute-start | bytes 442376 | tf_op jit(solution)/shard_map/ppermute | solution.py:524
  106.5 8.0 %collective-permute-start.27 = (bf16[2,144,256]{2,1,0:T(8,128)(2,1)S(1)}, bf16[2,144,256]{2,1,0:T(8,128)(2,1)S(1)}, u32[]{:S(2)}, u32[]{:S(2)}) collective-permute-start(bf16[2,144,256]{2,1,0:T(8,128)(2,1)S(1)} %get-tuple-element.108), channel_id=1, source_target_pairs={{0,2},{1,3},{2,0},{3,1},{4,6},{5,7},{6,4},{7,5},{8,10},{9,11},{10,... | collective-permute-start | bytes 442376 | tf_op jit(solution)/shard_map/ppermute | solution.py:524
  111.0 7.8 %collective-permute-start.31 = (bf16[576,128]{1,0:T(8,128)(2,1)S(1)}, bf16[576,128]{1,0:T(8,128)(2,1)S(1)}, u32[]{:S(2)}, u32[]{:S(2)}) collective-permute-start(bf16[576,128]{1,0:T(8,128)(2,1)S(1)} %pad_maximum_fusion.1), channel_id=1, source_target_pairs={{0,4},{1,5},{2,6},{3,7},{4,0},{5,1},{6,2},{7,3},{8,12},{9,13},{10,... | collective-permute-start | bytes 442376 | tf_op jit(solution)/shard_map/ppermute | solution.py:524
  114.6 10.9 %copy-start.14 = (bf16[8,256,20]{1,0,2:T(8,128)(2,1)S(1)}, bf16[8,256,20]{1,0,2:T(8,128)(2,1)}, u32[]{:S(2)}) copy-start(bf16[8,256,20]{1,0,2:T(8,128)(2,1)} %param.16) | copy-start | bytes 245764
  114.6 10.9 %copy-start.15 = (bf16[128,256]{1,0:T(8,128)(2,1)S(1)}, bf16[128,256]{1,0:T(8,128)(2,1)}, u32[]{:S(2)}) copy-start(bf16[128,256]{1,0:T(8,128)(2,1)} %refs_4_.5) | copy-start | bytes 196612
  114.6 10.9 %copy-start.17 = (f32[32,128]{1,0:T(8,128)S(1)}, f32[32,128]{1,0:T(8,128)}, u32[]{:S(2)}) copy-start(f32[32,128]{1,0:T(8,128)} %get-tuple-element.115.refs_6_) | copy-start | bytes 49156
  114.6 10.9 %copy-start.18 = (s32[128]{0:T(128)S(1)}, s32[128]{0:T(128)}, u32[]{:S(2)}) copy-start(s32[128]{0:T(128)} %param.12) | copy-start | bytes 1540
  114.6 10.8 %collective-permute-start.26 = (bf16[144,256]{1,0:T(8,128)(2,1)S(1)}, bf16[144,256]{1,0:T(8,128)(2,1)S(1)}, u32[]{:S(2)}, u32[]{:S(2)}) collective-permute-start(bf16[144,256]{1,0:T(8,128)(2,1)S(1)} %get-tuple-element.131), channel_id=1, source_target_pairs={{0,4},{1,5},{2,6},{3,7},{4,0},{5,1},{6,2},{7,3},{8,12},{9,13},{10,... | collective-permute-start | bytes 221192 | tf_op jit(solution)/shard_map/ppermute | solution.py:524
  116.2 9.3 %collective-permute-start.29 = (bf16[144,256]{1,0:T(8,128)(2,1)S(1)}, bf16[144,256]{1,0:T(8,128)(2,1)S(1)}, u32[]{:S(2)}, u32[]{:S(2)}) collective-permute-start(bf16[144,256]{1,0:T(8,128)(2,1)S(1)} %get-tuple-element.129), channel_id=1, source_target_pairs={{0,12},{1,13},{2,14},{3,15},{4,8},{5,9},{6,10},{7,11},{8,4},{9,5},... | collective-permute-start | bytes 221192 | tf_op jit(solution)/shard_map/ppermute | solution.py:524
  118.8 6.7 %collective-permute-start.28 = (bf16[144,256]{1,0:T(8,128)(2,1)S(1)}, bf16[144,256]{1,0:T(8,128)(2,1)S(1)}, u32[]{:S(2)}, u32[]{:S(2)}) collective-permute-start(bf16[144,256]{1,0:T(8,128)(2,1)S(1)} %get-tuple-element.130), channel_id=1, source_target_pairs={{0,8},{1,9},{2,10},{3,11},{4,12},{5,13},{6,14},{7,15},{8,0},{9,1},... | collective-permute-start | bytes 221192 | tf_op jit(solution)/shard_map/ppermute | solution.py:524
  118.8 5.2 %collective-permute-start.32 = (bf16[576,128]{1,0:T(8,128)(2,1)S(1)}, bf16[576,128]{1,0:T(8,128)(2,1)S(1)}, u32[]{:S(2)}, u32[]{:S(2)}) collective-permute-start(bf16[576,128]{1,0:T(8,128)(2,1)S(1)} %add_convert_fusion.1), channel_id=1, source_target_pairs={{0,2},{1,3},{2,0},{3,1},{4,6},{5,7},{6,4},{7,5},{8,10},{9,11},{10,... | collective-permute-start | bytes 442376 | tf_op jit(solution)/shard_map/ppermute | solution.py:524

commit v6 on v5

--- a/solution.py
+++ b/solution.py
@@ -561,12 +561,7 @@
     column, pieces = lax.optimization_barrier((column, pieces))
     stacked = jnp.stack(column)
     got = [stacked] + [send(stacked, 2 * a) for a in range(1, near)]
-    (w2,) = call(
-        join_units_kernel,
-        [struct((hidden_chip, width), bf16)],
-        [reduce, send(reduce, 1)],
-        limit=SMALL,
-    )
+    reduce_other = send(reduce, 1)
     w1a = lax.all_to_all(
         pieces, AXIS, split_axis=0, concat_axis=0, tiled=True, axis_index_groups=groups
     ).reshape(width // 2, hidden_chip)
@@ -593,8 +588,16 @@
         return out_own, send(out_send, 1)
 
     mixing_home = scenario_forward(got[:1])
-    got[1], mixing_home, w1a, w2 = lax.optimization_barrier((got[1], mixing_home, w1a, w2))
+    got[1], mixing_home, w1a = lax.optimization_barrier((got[1], mixing_home, w1a))
     mixing_away = scenario_forward(got[1:])
+    out_own, reduce_other = lax.optimization_barrier((mixing_away[0], reduce_other))
+    mixing_away = (out_own, mixing_away[1])
+    (w2,) = call(
+        join_units_kernel,
+        [struct((hidden_chip, width), bf16)],
+        [reduce, reduce_other],
+        limit=SMALL,
+    )
     w1b = send(w1a, 1)
     weights = [w1a, w1b, w2]
     weight_scratch = [pltpu.VMEM((width, hidden_chip), bf16)]

time: 127 us -> 125 us (0.984)
  local copies, waits for them, and re-layouts: 5.75 us -> 2.68 us
  Pallas kernels: 29.6 us -> 31.5 us
  waiting for transfers between devices: 46 us -> 44.7 us
    unnamed x48 -> x42, local copies, waits for them, and re-layouts: 5.7 us -> 2.62 us
    pallas_call x17, Pallas kernels: 29.6 us -> 31.5 us  [call(): pl.pallas_call(kernel, out_shape=out_shapes, in_specs=specs, out_specs=[p...]
    ppermute x34, waiting for transfers between devices: 43.4 us -> 41.8 us  [send(): return lax.ppermute(value, AXIS, [(i, i ^ mask) for i in range(devices)])]
  transfers between devices with their start and end apart: 36 -> 36, of which waited for: 23 -> 24; matrix products, arithmetic and copies ran while one was open for 3% -> 3% of each run, Pallas kernels for 11% -> 13%
where the time goes in v6:
time: 125 us; the launch traced here: 124 us
  waiting for transfers between devices  44.7 us (36%)
  starting transfers between devices  39.9 us (32%)
  Pallas kernels  31.5 us (25%)
  other arithmetic  4.39 us (4%)
  local copies, waits for them, and re-layouts  2.68 us (2%)
    ppermute x34, waiting for transfers between devices, send(): return lax.ppermute(value, AXIS, [(i, i ^ mask) for i in range(devices)])  41.8 us
    pallas_call x17, Pallas kernels, call(): pl.pallas_call(kernel, out_shape=out_shapes, in_specs=specs, out_specs=[p...  31.5 us
    ppermute x34, starting transfers between devices, send(): return lax.ppermute(value, AXIS, [(i, i ^ mask) for i in range(devices)])  31 us
    all_to_all x1, starting transfers between devices, body(): lax.all_to_all(pieces, AXIS, split_axis=0, concat_axis=0, tiled=True, axi...  4.88 us
    all_to_all x1, starting transfers between devices, body(): lax.all_to_all(dw1.reshape(chips, depth, hidden_chip), AXIS, split_axis=0...  4.01 us
    unnamed x42, local copies, waits for them, and re-layouts  2.62 us
    all_to_all x1, waiting for transfers between devices, body(): lax.all_to_all(dw1.reshape(chips, depth, hidden_chip), AXIS, split_axis=0...  2.62 us
  transfers between devices with their start and end apart: 36, of which 24 were waited for; matrix products, arithmetic and copies ran while one was open for 3% of the time, Pallas kernels for 13%

profile of v6, /device:TPU:0, one launch (start us, length us, event | category | flops | bytes accessed | tf_op | source)
XLA Modules:
  0.0 124.1 jit_solution(16375138892705447776)
XLA Ops:
  0.7 2.0 %shard_map.162 = (bf16[144,256]{1,0:T(8,128)(2,1)}, f32[32,128]{1,0:T(8,128)}) custom-call(s32[8]{0:T(128)} %pads.1, s32[16]{0:T(128)} %slots.1, bf16[128,256]{1,0:T(8,128)(2,1)} %refs_4_.5, s32[1,128]{1,0:T(1,128)} %bitcast.51, bf16[160,256]{1,0:T(8,128)(2,1)} %bitcast.48), custom_call_target="tpu_custom_call" | custom-call | flops 100000 | bytes 100000 | tf_op jit(solution)/shard_map/pallas_call | solution.py:29
  2.6 5.0 %collective-permute-start.2 = (bf16[144,256]{1,0:T(8,128)(2,1)}, bf16[144,256]{1,0:T(8,128)(2,1)S(1)}, u32[]{:S(2)}, u32[]{:S(2)}) collective-permute-start(bf16[144,256]{1,0:T(8,128)(2,1)} %get-tuple-element.67), channel_id=1, source_target_pairs={{0,12},{1,13},{2,14},{3,15},{4,8},{5,9},{6,10},{7,11},{8,4},{9,5},... | collective-permute-start | bytes 221192 | tf_op jit(solution)/shard_map/ppermute | solution.py:524
  7.7 0.6 collective-permute-start
  8.2 1.0 copy-done.3
  9.3 0.9 shard_map.163
  10.7 3.4 %collective-permute-done.1 = bf16[144,256]{1,0:T(8,128)(2,1)S(1)} collective-permute-done((bf16[144,256]{1,0:T(8,128)(2,1)}, bf16[144,256]{1,0:T(8,128)(2,1)S(1)}, u32[]{:S(2)}, u32[]{:S(2)}) %collective-permute-start.1) | collective-permute-done | bytes 73760 | tf_op jit(solution)/shard_map/ppermute | solution.py:524
  14.1 4.9 %all-to-all-start = ((bf16[8,16,2048]{2,1,0:T(8,128)(2,1)}), bf16[8,16,2048]{2,1,0:T(8,128)(2,1)S(1)}, u32[]{:S(2)}, u32[]{:S(2)}) async-start(bf16[8,16,2048]{2,1,0:T(8,128)(2,1)} %shard_map.163), calls=%async_computation | async-start | bytes 1048576 | tf_op jit(solution)/shard_map/all_to_all | solution.py:565
  19.0 2.1 %collective-permute-start.3 = (bf16[4,144,256]{2,1,0:T(8,128)(2,1)S(1)}, bf16[4,144,256]{2,1,0:T(8,128)(2,1)S(1)}, u32[]{:S(2)}, u32[]{:S(2)}) collective-permute-start(bf16[4,144,256]{2,1,0:T(8,128)(2,1)S(1)} %pad_maximum_fusion.refs_0_.refs_1_), channel_id=1, source_target_pairs={{0,2},{1,3},{2,0},{3,1},{4,6},{5,7},{6,4},{7,5},{8,10},{9,11},{10,... | collective-permute-start | bytes 884744 | tf_op jit(solution)/shard_map/ppermute | solution.py:524
  21.1 0.7 shard_map.164
  21.9 1.3 %collective-permute-done.4.other = bf16[128,384]{1,0:T(8,128)(2,1)S(1)} collective-permute-done((bf16[128,384]{1,0:T(8,128)(2,1)S(1)}, bf16[128,384]{1,0:T(8,128)(2,1)S(1)}, u32[]{:S(2)}, u32[]{:S(2)}) %collective-permute-start.4) | collective-permute-done | bytes 98336 | tf_op jit(solution)/shard_map/ppermute | solution.py:524
  23.2 0.9 shard_map.165
  24.7 0.7 collective-permute-done.5.refs_6_
  25.4 6.3 %collective-permute-done.3.refs_1_.refs_2_ = bf16[4,144,256]{2,1,0:T(8,128)(2,1)S(1)} collective-permute-done((bf16[4,144,256]{2,1,0:T(8,128)(2,1)S(1)}, bf16[4,144,256]{2,1,0:T(8,128)(2,1)S(1)}, u32[]{:S(2)}, u32[]{:S(2)}) %collective-permute-start.3) | collective-permute-done | bytes 294944 | tf_op jit(solution)/shard_map/ppermute | solution.py:524
  32.0 0.7 shard_map.166
  32.6 0.6 collective-permute-start.7
  33.2 0.9 collective-permute-done.7.other
  34.2 0.9 shard_map.167
  35.5 1.1 shard_map.168.refs_4_.refs_7_
  36.7 2.3 %shard_map.170 = (bf16[2,128,256]{2,1,0:T(8,128)(2,1)S(1)}, bf16[2,128,256]{2,1,0:T(8,128)(2,1)S(1)}) custom-call(bf16[4,144,256]{2,1,0:T(8,128)(2,1)S(1)} %pad_maximum_fusion.refs_0_.refs_1_, bf16[4,144,256]{2,1,0:T(8,128)(2,1)S(1)} %collective-permute-done.3.refs_1_.refs_2_, bf16[128,2048]{1,0:T(8,128)(2,1)S(1)} %bitcast.45, ...), custom_call_target="tpu_custom_call" | custom-call | flops 100000 | bytes 100000 | tf_op jit(solution)/shard_map/pallas_call | solution.py:29
  39.0 1.5 %collective-permute-start.10 = (bf16[2,128,256]{2,1,0:T(8,128)(2,1)S(1)}, bf16[2,128,256]{2,1,0:T(8,128)(2,1)S(1)}, u32[]{:S(2)}, u32[]{:S(2)}) collective-permute-start(bf16[2,128,256]{2,1,0:T(8,128)(2,1)S(1)} %get-tuple-element.86), channel_id=1, source_target_pairs={{0,2},{1,3},{2,0},{3,1},{4,6},{5,7},{6,4},{7,5},{8,10},{9,11},{10,... | collective-permute-start | bytes 393224 | tf_op jit(solution)/shard_map/ppermute | solution.py:524
  40.5 0.6 collective-permute-start.12
  41.1 2.3 %shard_map.169 = bf16[4,128,256]{2,1,0:T(8,128)(2,1)S(1)} custom-call(bf16[4,144,256]{2,1,0:T(8,128)(2,1)S(1)} %pad_maximum_fusion.refs_0_.refs_1_, bf16[4,144,256]{2,1,0:T(8,128)(2,1)S(1)} %pad_maximum_fusion.refs_0_.refs_1_, bf16[128,2048]{1,0:T(8,128)(2,1)S(1)} %bitcast.46, bf16[128,2048]{1,0:T(8,128)(2,1)S(1)} %collective-permute-done.6.refs_3_.refs_6_, ...), custom_call_target="tpu_custom_call" | custom-call | flops 100000 | bytes 100000 | tf_op jit(solution)/shard_map/pallas_call | solution.py:29
  43.3 2.0 %collective-permute-done.10 = bf16[2,128,256]{2,1,0:T(8,128)(2,1)S(1)} collective-permute-done((bf16[2,128,256]{2,1,0:T(8,128)(2,1)S(1)}, bf16[2,128,256]{2,1,0:T(8,128)(2,1)S(1)}, u32[]{:S(2)}, u32[]{:S(2)}) %collective-permute-start.10) | collective-permute-done | bytes 131104 | tf_op jit(solution)/shard_map/ppermute | solution.py:524
  45.4 2.0 %collective-permute-done.12 = bf16[2,128,256]{2,1,0:T(8,128)(2,1)S(1)} collective-permute-done((bf16[2,128,256]{2,1,0:T(8,128)(2,1)S(1)}, bf16[2,128,256]{2,1,0:T(8,128)(2,1)S(1)}, u32[]{:S(2)}, u32[]{:S(2)}) %collective-permute-start.12) | collective-permute-done | bytes 131104 | tf_op jit(solution)/shard_map/ppermute | solution.py:524
  47.5 3.1 %collective-permute-start.14 = (bf16[128,256]{1,0:T(8,128)(2,1)S(1)}, bf16[128,256]{1,0:T(8,128)(2,1)S(1)}, u32[]{:S(2)}, u32[]{:S(2)}) collective-permute-start(bf16[128,256]{1,0:T(8,128)(2,1)S(1)} %get-tuple-element.135), channel_id=1, source_target_pairs={{0,12},{1,13},{2,14},{3,15},{4,8},{5,9},{6,10},{7,11},{8,4},{9,5},... | collective-permute-start | bytes 196616 | tf_op jit(solution)/shard_map/ppermute | solution.py:524
  50.6 1.4 %collective-permute-start.11 = (bf16[128,256]{1,0:T(8,128)(2,1)S(1)}, bf16[128,256]{1,0:T(8,128)(2,1)S(1)}, u32[]{:S(2)}, u32[]{:S(2)}) collective-permute-start(bf16[128,256]{1,0:T(8,128)(2,1)S(1)} %get-tuple-element.137), channel_id=1, source_target_pairs={{0,4},{1,5},{2,6},{3,7},{4,0},{5,1},{6,2},{7,3},{8,12},{9,13},{10,... | collective-permute-start | bytes 196616 | tf_op jit(solution)/shard_map/ppermute | solution.py:524
  52.0 1.7 %collective-permute-done.14.refs_3_ = bf16[128,256]{1,0:T(8,128)(2,1)S(1)} collective-permute-done((bf16[128,256]{1,0:T(8,128)(2,1)S(1)}, bf16[128,256]{1,0:T(8,128)(2,1)S(1)}, u32[]{:S(2)}, u32[]{:S(2)}) %collective-permute-start.14) | collective-permute-done | bytes 65568 | tf_op jit(solution)/shard_map/ppermute | solution.py:524
  53.7 2.5 %collective-permute-done.13.refs_2_ = bf16[128,256]{1,0:T(8,128)(2,1)S(1)} collective-permute-done((bf16[128,256]{1,0:T(8,128)(2,1)S(1)}, bf16[128,256]{1,0:T(8,128)(2,1)S(1)}, u32[]{:S(2)}, u32[]{:S(2)}) %collective-permute-start.13) | collective-permute-done | bytes 65568 | tf_op jit(solution)/shard_map/ppermute | solution.py:524
  56.2 0.5 shard_map.171
  56.8 2.7 %collective-permute-start.17 = (bf16[128,128]{1,0:T(8,128)(2,1)S(1)}, bf16[128,128]{1,0:T(8,128)(2,1)S(1)}, u32[]{:S(2)}, u32[]{:S(2)}) collective-permute-start(bf16[128,128]{1,0:T(8,128)(2,1)S(1)} %get-tuple-element.88), channel_id=1, source_target_pairs={{0,12},{1,13},{2,14},{3,15},{4,8},{5,9},{6,10},{7,11},{8,4},{9,5},... | collective-permute-start | bytes 98312 | tf_op jit(solution)/shard_map/ppermute | solution.py:524
  59.5 1.7 %collective-permute-start.15 = (bf16[128,128]{1,0:T(8,128)(2,1)S(1)}, bf16[128,128]{1,0:T(8,128)(2,1)S(1)}, u32[]{:S(2)}, u32[]{:S(2)}) collective-permute-start(bf16[128,128]{1,0:T(8,128)(2,1)S(1)} %get-tuple-element.88), channel_id=1, source_target_pairs={{0,4},{1,5},{2,6},{3,7},{4,0},{5,1},{6,2},{7,3},{8,12},{9,13},{10,... | collective-permute-start | bytes 98312 | tf_op jit(solution)/shard_map/ppermute | solution.py:524
  61.3 1.3 %collective-permute-start.19 = (bf16[256,128]{1,0:T(8,128)(2,1)S(1)}, bf16[256,128]{1,0:T(8,128)(2,1)S(1)}, u32[]{:S(2)}, u32[]{:S(2)}) collective-permute-start(bf16[256,128]{1,0:T(8,128)(2,1)S(1)} %add_convert_fusion.7), channel_id=1, source_target_pairs={{0,8},{1,9},{2,10},{3,11},{4,12},{5,13},{6,14},{7,15},{8,0},{9,1},... | collective-permute-start | bytes 196616 | tf_op jit(solution)/shard_map/ppermute | solution.py:524
  62.9 1.4 %collective-permute-done.16 = bf16[128,128]{1,0:T(8,128)(2,1)S(1)} collective-permute-done((bf16[128,128]{1,0:T(8,128)(2,1)S(1)}, bf16[128,128]{1,0:T(8,128)(2,1)S(1)}, u32[]{:S(2)}, u32[]{:S(2)}) %collective-permute-start.16) | collective-permute-done | bytes 32800 | tf_op jit(solution)/shard_map/ppermute | solution.py:524
  64.3 0.8 collective-permute-start.20
  65.1 2.1 %collective-permute-done.19 = bf16[256,128]{1,0:T(8,128)(2,1)S(1)} collective-permute-done((bf16[256,128]{1,0:T(8,128)(2,1)S(1)}, bf16[256,128]{1,0:T(8,128)(2,1)S(1)}, u32[]{:S(2)}, u32[]{:S(2)}) %collective-permute-start.19) | collective-permute-done | bytes 65568 | tf_op jit(solution)/shard_map/ppermute | solution.py:524
  67.2 0.6 convert_add_fusion.3
  67.9 1.5 %collective-permute-done.20.refs_4_.refs_3_ = bf16[4,128,128]{2,1,0:T(8,128)(2,1)S(1)} collective-permute-done((bf16[4,128,128]{2,1,0:T(8,128)(2,1)S(1)}, bf16[4,128,128]{2,1,0:T(8,128)(2,1)S(1)}, u32[]{:S(2)}, u32[]{:S(2)}) %collective-permute-start.20) | collective-permute-done | bytes 131104 | tf_op jit(solution)/shard_map/ppermute | solution.py:524
  69.4 0.8 shard_map.172
  70.1 0.7 copy-done.18
  70.8 9.1 %shard_map.173 = (bf16[1024,256]{1,0:T(8,128)(2,1)S(1)}, f32[1024,32]{1,0:T(8,128)S(1)}, bf16[128,2048]{1,0:T(8,128)(2,1)S(1)}, bf16[128,2048]{1,0:T(8,128)(2,1)...) custom-call(bf16[4,144,256]{2,1,0:T(8,128)(2,1)S(1)} %pad_maximum_fusion.refs_0_.refs_1_, ...), custom_call_target="tpu_custom_call" | custom-call | flops 100000 | bytes 100000 | tf_op jit(solution)/shard_map/pallas_call | solution.py:29
  80.0 0.8 copy-done.16
  80.8 1.9 %collective-permute-done.21 = bf16[128,2048]{1,0:T(8,128)(2,1)S(1)} collective-permute-done((bf16[128,2048]{1,0:T(8,128)(2,1)S(1)}, bf16[128,2048]{1,0:T(8,128)(2,1)S(1)}, u32[]{:S(2)}, u32[]{:S(2)}) %collective-permute-start.21) | collective-permute-done | bytes 524320 | tf_op jit(solution)/shard_map/ppermute | solution.py:524
  82.7 0.9 add_convert_fusion
  83.7 4.0 %all-to-all-start.1 = ((bf16[8,16,2048]{2,1,0:T(8,128)(2,1)}), bf16[8,16,2048]{2,1,0:T(8,128)(2,1)S(1)}, u32[]{:S(2)}, u32[]{:S(2)}) async-start(bf16[8,16,2048]{2,1,0:T(8,128)(2,1)} %bitcast.53), calls=%async_computation.1 | async-start | bytes 1048576 | tf_op jit(solution)/shard_map/all_to_all | solution.py:677
  87.8 1.7 %collective-permute-done.22.other = bf16[256,512]{1,0:T(8,128)(2,1)S(1)} collective-permute-done((bf16[256,512]{1,0:T(8,128)(2,1)}, bf16[256,512]{1,0:T(8,128)(2,1)S(1)}, u32[]{:S(2)}, u32[]{:S(2)}) %collective-permute-start.22) | collective-permute-done | bytes 262176 | tf_op jit(solution)/shard_map/ppermute | solution.py:524
  89.5 5.4 %shard_map.174 = (bf16[256,384]{1,0:T(8,128)(2,1)S(1)}, bf16[256,384]{1,0:T(8,128)(2,1)S(1)}, f32[256,2048]{1,0:T(8,128)}, f32[2048,256]{1,0:T(8,128)}) custom-call(bf16[256,512]{1,0:T(8,128)(2,1)S(1)} %get-tuple-element.98.own, bf16[256,512]{1,0:T(8,128)(2,1)S(1)} %collective-permute-done.22.other, bf16[256,128]{1,0:T(8,128)(2,1)S(1)} %copy-done.2, ...), custom_call_target="tpu_custom_call" | custom-call | flops 100000 | bytes 100000 | tf_op jit(solution)/shard_map/pallas_call | solution.py:29
  95.1 1.3 %collective-permute-done.23.refs_5_ = bf16[256,384]{1,0:T(8,128)(2,1)S(1)} collective-permute-done((bf16[256,384]{1,0:T(8,128)(2,1)S(1)}, bf16[256,384]{1,0:T(8,128)(2,1)S(1)}, u32[]{:S(2)}, u32[]{:S(2)}) %collective-permute-start.23) | collective-permute-done | bytes 196640 | tf_op jit(solution)/shard_map/ppermute | solution.py:524
  96.4 1.6 %shard_map.175 = (bf16[4,144,256]{2,1,0:T(8,128)(2,1)S(1)}, bf16[2,144,256]{2,1,0:T(8,128)(2,1)S(1)}, bf16[2,144,256]{2,1,0:T(8,128)(2,1)S(1)}, bf16[8,32,128]{2,1,0:T(8,128)(2,1)S(1)}) custom-call(bf16[4,144,256]{2,1,0:T(8,128)(2,1)S(1)} %pad_maximum_fusion.refs_0_.refs_1_, bf16[4,144,256]{2,1,0:T(8,128)(2,1)S(1)} %collective-permute-done.3.refs_1_.refs_2_, ...), custom_call_target="tpu_custom_call" | custom-call | flops 100000 | bytes 100000 | tf_op jit(solution)/shard_map/pallas_call | solution.py:29
  98.5 1.3 %collective-permute-done.24 = f32[320,128]{1,0:T(8,128)S(1)} collective-permute-done((f32[320,128]{1,0:T(8,128)S(1)}, f32[320,128]{1,0:T(8,128)S(1)}, u32[]{:S(2)}, u32[]{:S(2)}) %collective-permute-start.24) | collective-permute-done | bytes 163872 | tf_op jit(solution)/shard_map/ppermute | solution.py:524
  99.8 2.6 %all-to-all-done.1.pieces = bf16[8,16,2048]{2,1,0:T(8,128)(2,1)S(1)} async-done(((bf16[8,16,2048]{2,1,0:T(8,128)(2,1)}), bf16[8,16,2048]{2,1,0:T(8,128)(2,1)S(1)}, u32[]{:S(2)}, u32[]{:S(2)}) %all-to-all-start.1) | async-done | bytes 524320 | tf_op jit(solution)/shard_map/all_to_all | solution.py:677
  102.8 1.5 %collective-permute-start.25 = (bf16[2,144,256]{2,1,0:T(8,128)(2,1)S(1)}, bf16[2,144,256]{2,1,0:T(8,128)(2,1)S(1)}, u32[]{:S(2)}, u32[]{:S(2)}) collective-permute-start(bf16[2,144,256]{2,1,0:T(8,128)(2,1)S(1)} %get-tuple-element.107), channel_id=1, source_target_pairs={{0,2},{1,3},{2,0},{3,1},{4,6},{5,7},{6,4},{7,5},{8,10},{9,11},{10,... | collective-permute-start | bytes 442376 | tf_op jit(solution)/shard_map/ppermute | solution.py:524
  104.3 0.6 collective-permute-start.27
  104.8 1.0 shard_map.178
  105.9 2.8 %collective-permute-done.30 = bf16[320,128]{1,0:T(8,128)(2,1)S(1)} collective-permute-done((bf16[320,128]{1,0:T(8,128)(2,1)S(1)}, bf16[320,128]{1,0:T(8,128)(2,1)S(1)}, u32[]{:S(2)}, u32[]{:S(2)}) %collective-permute-start.30) | collective-permute-done | bytes 81952 | tf_op jit(solution)/shard_map/ppermute | solution.py:524
  108.8 0.6 collective-permute-done.25
  109.5 2.8 %collective-permute-done.27 = bf16[2,144,256]{2,1,0:T(8,128)(2,1)S(1)} collective-permute-done((bf16[2,144,256]{2,1,0:T(8,128)(2,1)S(1)}, bf16[2,144,256]{2,1,0:T(8,128)(2,1)S(1)}, u32[]{:S(2)}, u32[]{:S(2)}) %collective-permute-start.27) | collective-permute-done | bytes 147488 | tf_op jit(solution)/shard_map/ppermute | solution.py:524
  112.4 1.5 %collective-permute-start.26 = (bf16[144,256]{1,0:T(8,128)(2,1)S(1)}, bf16[144,256]{1,0:T(8,128)(2,1)S(1)}, u32[]{:S(2)}, u32[]{:S(2)}) collective-permute-start(bf16[144,256]{1,0:T(8,128)(2,1)S(1)} %get-tuple-element.133), channel_id=1, source_target_pairs={{0,4},{1,5},{2,6},{3,7},{4,0},{5,1},{6,2},{7,3},{8,12},{9,13},{10,... | collective-permute-start | bytes 221192 | tf_op jit(solution)/shard_map/ppermute | solution.py:524
  113.9 2.6 %collective-permute-start.29 = (bf16[144,256]{1,0:T(8,128)(2,1)S(1)}, bf16[144,256]{1,0:T(8,128)(2,1)S(1)}, u32[]{:S(2)}, u32[]{:S(2)}) collective-permute-start(bf16[144,256]{1,0:T(8,128)(2,1)S(1)} %get-tuple-element.131), channel_id=1, source_target_pairs={{0,12},{1,13},{2,14},{3,15},{4,8},{5,9},{6,10},{7,11},{8,4},{9,5},... | collective-permute-start | bytes 221192 | tf_op jit(solution)/shard_map/ppermute | solution.py:524
  116.6 1.5 %collective-permute-start.32 = (bf16[576,128]{1,0:T(8,128)(2,1)S(1)}, bf16[576,128]{1,0:T(8,128)(2,1)S(1)}, u32[]{:S(2)}, u32[]{:S(2)}) collective-permute-start(bf16[576,128]{1,0:T(8,128)(2,1)S(1)} %add_convert_fusion.1), channel_id=1, source_target_pairs={{0,2},{1,3},{2,0},{3,1},{4,6},{5,7},{6,4},{7,5},{8,10},{9,11},{10,... | collective-permute-start | bytes 442376 | tf_op jit(solution)/shard_map/ppermute | solution.py:524
  118.1 1.1 convert_add_fusion
  119.3 2.6 %collective-permute-done.32 = bf16[576,128]{1,0:T(8,128)(2,1)S(1)} collective-permute-done((bf16[576,128]{1,0:T(8,128)(2,1)S(1)}, bf16[576,128]{1,0:T(8,128)(2,1)S(1)}, u32[]{:S(2)}, u32[]{:S(2)}) %collective-permute-start.32) | collective-permute-done | bytes 147488 | tf_op jit(solution)/shard_map/ppermute | solution.py:524
  121.9 0.7 convert_add_fusion.2
  122.5 0.7 maximum_bitcast_fusion
  123.3 0.9 shard_map.177
  (87 shorter events, 4.0 us)
Async XLA Ops:
  0.6 22.5 %copy-start.1 = (bf16[1,2048,256]{2,1,0:T(8,128)(2,1)S(1)}, bf16[1,2048,256]{2,1,0:T(8,128)(2,1)}, u32[]{:S(2)}) copy-start(bf16[1,2048,256]{2,1,0:T(8,128)(2,1)} %param.20) | copy-start | bytes 3145732
  0.6 22.5 %copy-start = (bf16[1,256,2048]{2,1,0:T(8,128)(2,1)S(1)}, bf16[1,256,2048]{2,1,0:T(8,128)(2,1)}, u32[]{:S(2)}) copy-start(bf16[1,256,2048]{2,1,0:T(8,128)(2,1)} %param.19) | copy-start | bytes 3145732
  2.6 8.0 %collective-permute-start.2 = (bf16[144,256]{1,0:T(8,128)(2,1)}, bf16[144,256]{1,0:T(8,128)(2,1)S(1)}, u32[]{:S(2)}, u32[]{:S(2)}) collective-permute-start(bf16[144,256]{1,0:T(8,128)(2,1)} %get-tuple-element.67), channel_id=1, source_target_pairs={{0,12},{1,13},{2,14},{3,15},{4,8},{5,9},{6,10},{7,11},{8,4},{9,5},... | collective-permute-start | bytes 221192 | tf_op jit(solution)/shard_map/ppermute | solution.py:524
  7.7 6.4 %collective-permute-start.1 = (bf16[144,256]{1,0:T(8,128)(2,1)}, bf16[144,256]{1,0:T(8,128)(2,1)S(1)}, u32[]{:S(2)}, u32[]{:S(2)}) collective-permute-start(bf16[144,256]{1,0:T(8,128)(2,1)} %get-tuple-element.67), channel_id=1, source_target_pairs={{0,8},{1,9},{2,10},{3,11},{4,12},{5,13},{6,14},{7,15},{8,0},{9,1},... | collective-permute-start | bytes 221192 | tf_op jit(solution)/shard_map/ppermute | solution.py:524
  7.7 6.4 %collective-permute-start = (bf16[144,256]{1,0:T(8,128)(2,1)}, bf16[144,256]{1,0:T(8,128)(2,1)S(1)}, u32[]{:S(2)}, u32[]{:S(2)}) collective-permute-start(bf16[144,256]{1,0:T(8,128)(2,1)} %get-tuple-element.67), channel_id=1, source_target_pairs={{0,4},{1,5},{2,6},{3,7},{4,0},{5,1},{6,2},{7,3},{8,12},{9,13},{10,... | collective-permute-start | bytes 221192 | tf_op jit(solution)/shard_map/ppermute | solution.py:524
  8.2 1.0 copy-start.3
  9.3 9.7 %copy-start.20 = (bf16[144,256]{1,0:T(8,128)(2,1)S(1)}, bf16[144,256]{1,0:T(8,128)(2,1)}, u32[]{:S(2)}) copy-start(bf16[144,256]{1,0:T(8,128)(2,1)} %get-tuple-element.67) | copy-start | bytes 221188
  14.1 17.9 %all-to-all-start = ((bf16[8,16,2048]{2,1,0:T(8,128)(2,1)}), bf16[8,16,2048]{2,1,0:T(8,128)(2,1)S(1)}, u32[]{:S(2)}, u32[]{:S(2)}) async-start(bf16[8,16,2048]{2,1,0:T(8,128)(2,1)} %shard_map.163), calls=%async_computation | async-start | bytes 1048576 | tf_op jit(solution)/shard_map/all_to_all | solution.py:565
  19.0 12.7 %collective-permute-start.3 = (bf16[4,144,256]{2,1,0:T(8,128)(2,1)S(1)}, bf16[4,144,256]{2,1,0:T(8,128)(2,1)S(1)}, u32[]{:S(2)}, u32[]{:S(2)}) collective-permute-start(bf16[4,144,256]{2,1,0:T(8,128)(2,1)S(1)} %pad_maximum_fusion.refs_0_.refs_1_), channel_id=1, source_target_pairs={{0,2},{1,3},{2,0},{3,1},{4,6},{5,7},{6,4},{7,5},{8,10},{9,11},{10,... | collective-permute-start | bytes 884744 | tf_op jit(solution)/shard_map/ppermute | solution.py:524
  21.8 1.4 %collective-permute-start.4 = (bf16[128,384]{1,0:T(8,128)(2,1)S(1)}, bf16[128,384]{1,0:T(8,128)(2,1)S(1)}, u32[]{:S(2)}, u32[]{:S(2)}) collective-permute-start(bf16[128,384]{1,0:T(8,128)(2,1)S(1)} %get-tuple-element.72), channel_id=1, source_target_pairs={{0,1},{1,0},{2,3},{3,2},{4,5},{5,4},{6,7},{7,6},{8,9},{9,8},{10,11... | collective-permute-start | bytes 294920 | tf_op jit(solution)/shard_map/ppermute | solution.py:524
  24.1 1.3 %collective-permute-start.5 = (bf16[128,256]{1,0:T(8,128)(2,1)S(1)}, bf16[128,256]{1,0:T(8,128)(2,1)S(1)}, u32[]{:S(2)}, u32[]{:S(2)}) collective-permute-start(bf16[128,256]{1,0:T(8,128)(2,1)S(1)} %get-tuple-element.74), channel_id=1, source_target_pairs={{0,1},{1,0},{2,3},{3,2},{4,5},{5,4},{6,7},{7,6},{8,9},{9,8},{10,11... | collective-permute-start | bytes 196616 | tf_op jit(solution)/shard_map/ppermute | solution.py:524
  24.3 11.2 %collective-permute-start.8 = (bf16[16,64,256]{2,1,0:T(8,128)(2,1)}, bf16[16,64,256]{2,1,0:T(8,128)(2,1)}, u32[]{:S(2)}, u32[]{:S(2)}) collective-permute-start(bf16[16,64,256]{2,1,0:T(8,128)(2,1)} %mine.1), channel_id=1, source_target_pairs={{0,1},{1,0},{2,3},{3,2},{4,5},{5,4},{6,7},{7,6},{8,9},{9,8},{10,11... | collective-permute-start | bytes 1572872 | tf_op jit(solution)/shard_map/ppermute | solution.py:524
  32.0 3.6 %copy-start.4 = (bf16[16,64,256]{2,1,0:T(8,128)(2,1)S(1)}, bf16[16,64,256]{2,1,0:T(8,128)(2,1)}, u32[]{:S(2)}) copy-start(bf16[16,64,256]{2,1,0:T(8,128)(2,1)} %mine.1) | copy-start | bytes 1572868
  32.0 4.7 %collective-permute-start.6 = (bf16[128,2048]{1,0:T(8,128)(2,1)S(1)}, bf16[128,2048]{1,0:T(8,128)(2,1)S(1)}, u32[]{:S(2)}, u32[]{:S(2)}) collective-permute-start(bf16[128,2048]{1,0:T(8,128)(2,1)S(1)} %bitcast.44), channel_id=1, source_target_pairs={{0,1},{1,0},{2,3},{3,2},{4,5},{5,4},{6,7},{7,6},{8,9},{9,8},{10,11... | collective-permute-start | bytes 1572872 | tf_op jit(solution)/shard_map/ppermute | solution.py:524
  32.6 1.5 %collective-permute-start.7 = (bf16[128,384]{1,0:T(8,128)(2,1)S(1)}, bf16[128,384]{1,0:T(8,128)(2,1)S(1)}, u32[]{:S(2)}, u32[]{:S(2)}) collective-permute-start(bf16[128,384]{1,0:T(8,128)(2,1)S(1)} %get-tuple-element.79), channel_id=1, source_target_pairs={{0,1},{1,0},{2,3},{3,2},{4,5},{5,4},{6,7},{7,6},{8,9},{9,8},{10,11... | collective-permute-start | bytes 294920 | tf_op jit(solution)/shard_map/ppermute | solution.py:524
  35.1 1.6 %collective-permute-start.9 = (bf16[128,256]{1,0:T(8,128)(2,1)S(1)}, bf16[128,256]{1,0:T(8,128)(2,1)S(1)}, u32[]{:S(2)}, u32[]{:S(2)}) collective-permute-start(bf16[128,256]{1,0:T(8,128)(2,1)S(1)} %get-tuple-element.85), channel_id=1, source_target_pairs={{0,1},{1,0},{2,3},{3,2},{4,5},{5,4},{6,7},{7,6},{8,9},{9,8},{10,11... | collective-permute-start | bytes 196616 | tf_op jit(solution)/shard_map/ppermute | solution.py:524
  39.0 6.4 %collective-permute-start.10 = (bf16[2,128,256]{2,1,0:T(8,128)(2,1)S(1)}, bf16[2,128,256]{2,1,0:T(8,128)(2,1)S(1)}, u32[]{:S(2)}, u32[]{:S(2)}) collective-permute-start(bf16[2,128,256]{2,1,0:T(8,128)(2,1)S(1)} %get-tuple-element.86), channel_id=1, source_target_pairs={{0,2},{1,3},{2,0},{3,1},{4,6},{5,7},{6,4},{7,5},{8,10},{9,11},{10,... | collective-permute-start | bytes 393224 | tf_op jit(solution)/shard_map/ppermute | solution.py:524
  40.5 15.7 %copy-start.2 = (bf16[256,128]{1,0:T(8,128)(2,1)S(1)}, bf16[256,128]{1,0:T(8,128)(2,1)}, u32[]{:S(2)}) copy-start(bf16[256,128]{1,0:T(8,128)(2,1)} %head.1) | copy-start | bytes 196612
  40.5 15.7 %copy-start.13 = (f32[128,128]{1,0:T(8,128)S(1)}, f32[128,128]{1,0:T(8,128)}, u32[]{:S(2)}) copy-start(f32[128,128]{1,0:T(8,128)} %refs_5_.1) | copy-start | bytes 196612
  40.5 6.9 %collective-permute-start.12 = (bf16[2,128,256]{2,1,0:T(8,128)(2,1)S(1)}, bf16[2,128,256]{2,1,0:T(8,128)(2,1)S(1)}, u32[]{:S(2)}, u32[]{:S(2)}) collective-permute-start(bf16[2,128,256]{2,1,0:T(8,128)(2,1)S(1)} %get-tuple-element.87), channel_id=1, source_target_pairs={{0,2},{1,3},{2,0},{3,1},{4,6},{5,7},{6,4},{7,5},{8,10},{9,11},{10,... | collective-permute-start | bytes 393224 | tf_op jit(solution)/shard_map/ppermute | solution.py:524
  47.5 6.2 %collective-permute-start.14 = (bf16[128,256]{1,0:T(8,128)(2,1)S(1)}, bf16[128,256]{1,0:T(8,128)(2,1)S(1)}, u32[]{:S(2)}, u32[]{:S(2)}) collective-permute-start(bf16[128,256]{1,0:T(8,128)(2,1)S(1)} %get-tuple-element.135), channel_id=1, source_target_pairs={{0,12},{1,13},{2,14},{3,15},{4,8},{5,9},{6,10},{7,11},{8,4},{9,5},... | collective-permute-start | bytes 196616 | tf_op jit(solution)/shard_map/ppermute | solution.py:524
  50.6 5.6 %collective-permute-start.13 = (bf16[128,256]{1,0:T(8,128)(2,1)S(1)}, bf16[128,256]{1,0:T(8,128)(2,1)S(1)}, u32[]{:S(2)}, u32[]{:S(2)}) collective-permute-start(bf16[128,256]{1,0:T(8,128)(2,1)S(1)} %get-tuple-element.136), channel_id=1, source_target_pairs={{0,8},{1,9},{2,10},{3,11},{4,12},{5,13},{6,14},{7,15},{8,0},{9,1},... | collective-permute-start | bytes 196616 | tf_op jit(solution)/shard_map/ppermute | solution.py:524
  50.6 5.6 %collective-permute-start.11 = (bf16[128,256]{1,0:T(8,128)(2,1)S(1)}, bf16[128,256]{1,0:T(8,128)(2,1)S(1)}, u32[]{:S(2)}, u32[]{:S(2)}) collective-permute-start(bf16[128,256]{1,0:T(8,128)(2,1)S(1)} %get-tuple-element.137), channel_id=1, source_target_pairs={{0,4},{1,5},{2,6},{3,7},{4,0},{5,1},{6,2},{7,3},{8,12},{9,13},{10,... | collective-permute-start | bytes 196616 | tf_op jit(solution)/shard_map/ppermute | solution.py:524
  56.7 4.5 %collective-permute-start.18 = (f32[256,128]{1,0:T(8,128)S(1)}, f32[256,128]{1,0:T(8,128)S(1)}, u32[]{:S(2)}, u32[]{:S(2)}) collective-permute-start(f32[256,128]{1,0:T(8,128)S(1)} %get-tuple-element.89), channel_id=1, source_target_pairs={{0,1},{1,0},{2,3},{3,2},{4,5},{5,4},{6,7},{7,6},{8,9},{9,8},{10,11... | collective-permute-start | bytes 393224 | tf_op jit(solution)/shard_map/ppermute | solution.py:524
  56.8 6.2 %collective-permute-start.17 = (bf16[128,128]{1,0:T(8,128)(2,1)S(1)}, bf16[128,128]{1,0:T(8,128)(2,1)S(1)}, u32[]{:S(2)}, u32[]{:S(2)}) collective-permute-start(bf16[128,128]{1,0:T(8,128)(2,1)S(1)} %get-tuple-element.88), channel_id=1, source_target_pairs={{0,12},{1,13},{2,14},{3,15},{4,8},{5,9},{6,10},{7,11},{8,4},{9,5},... | collective-permute-start | bytes 98312 | tf_op jit(solution)/shard_map/ppermute | solution.py:524
  59.5 4.8 %collective-permute-start.16 = (bf16[128,128]{1,0:T(8,128)(2,1)S(1)}, bf16[128,128]{1,0:T(8,128)(2,1)S(1)}, u32[]{:S(2)}, u32[]{:S(2)}) collective-permute-start(bf16[128,128]{1,0:T(8,128)(2,1)S(1)} %get-tuple-element.88), channel_id=1, source_target_pairs={{0,8},{1,9},{2,10},{3,11},{4,12},{5,13},{6,14},{7,15},{8,0},{9,1},... | collective-permute-start | bytes 98312 | tf_op jit(solution)/shard_map/ppermute | solution.py:524
  59.5 4.8 %collective-permute-start.15 = (bf16[128,128]{1,0:T(8,128)(2,1)S(1)}, bf16[128,128]{1,0:T(8,128)(2,1)S(1)}, u32[]{:S(2)}, u32[]{:S(2)}) collective-permute-start(bf16[128,128]{1,0:T(8,128)(2,1)S(1)} %get-tuple-element.88), channel_id=1, source_target_pairs={{0,4},{1,5},{2,6},{3,7},{4,0},{5,1},{6,2},{7,3},{8,12},{9,13},{10,... | collective-permute-start | bytes 98312 | tf_op jit(solution)/shard_map/ppermute | solution.py:524
  61.3 6.0 %collective-permute-start.19 = (bf16[256,128]{1,0:T(8,128)(2,1)S(1)}, bf16[256,128]{1,0:T(8,128)(2,1)S(1)}, u32[]{:S(2)}, u32[]{:S(2)}) collective-permute-start(bf16[256,128]{1,0:T(8,128)(2,1)S(1)} %add_convert_fusion.7), channel_id=1, source_target_pairs={{0,8},{1,9},{2,10},{3,11},{4,12},{5,13},{6,14},{7,15},{8,0},{9,1},... | collective-permute-start | bytes 196616 | tf_op jit(solution)/shard_map/ppermute | solution.py:524
  64.3 5.0 %collective-permute-start.20 = (bf16[4,128,128]{2,1,0:T(8,128)(2,1)S(1)}, bf16[4,128,128]{2,1,0:T(8,128)(2,1)S(1)}, u32[]{:S(2)}, u32[]{:S(2)}) collective-permute-start(bf16[4,128,128]{2,1,0:T(8,128)(2,1)S(1)} %pad_maximum_fusion.2.refs_3_.refs_2_), channel_id=1, source_target_pairs={{0,2},{1,3},{2,0},{3,1},{4,6},{5,7},{6,4},{7,5},{8,10},{9,11},{10,... | collective-permute-start | bytes 393224 | tf_op jit(solution)/shard_map/ppermute | solution.py:524
  70.1 0.7 copy-start.18
  80.0 0.8 copy-start.16
  80.8 2.9 %copy-start.5 = (bf16[16,64,256]{2,1,0:T(8,128)(2,1)}, bf16[16,64,256]{2,1,0:T(8,128)(2,1)S(1)}, u32[]{:S(2)}) copy-start(bf16[16,64,256]{2,1,0:T(8,128)(2,1)S(1)} %get-tuple-element.119) | copy-start | bytes 1572868
  80.8 2.9 %copy-start.7 = (bf16[1024,256]{1,0:T(8,128)(2,1)}, bf16[1024,256]{1,0:T(8,128)(2,1)S(1)}, u32[]{:S(2)}) copy-start(bf16[1024,256]{1,0:T(8,128)(2,1)S(1)} %get-tuple-element.93.refs_2_) | copy-start | bytes 1572868
  80.8 2.9 %copy-start.9 = (f32[1024,32]{1,0:T(8,128)}, f32[1024,32]{1,0:T(8,128)S(1)}, u32[]{:S(2)}) copy-start(f32[1024,32]{1,0:T(8,128)S(1)} %get-tuple-element.94.refs_3_) | copy-start | bytes 393220
  80.8 1.9 %collective-permute-start.21 = (bf16[128,2048]{1,0:T(8,128)(2,1)S(1)}, bf16[128,2048]{1,0:T(8,128)(2,1)S(1)}, u32[]{:S(2)}, u32[]{:S(2)}) collective-permute-start(bf16[128,2048]{1,0:T(8,128)(2,1)S(1)} %get-tuple-element.96), channel_id=1, source_target_pairs={{0,1},{1,0},{2,3},{3,2},{4,5},{5,4},{6,7},{7,6},{8,9},{9,8},{10,11... | collective-permute-start | bytes 1572872 | tf_op jit(solution)/shard_map/ppermute | solution.py:524
  83.7 18.8 %all-to-all-start.1 = ((bf16[8,16,2048]{2,1,0:T(8,128)(2,1)}), bf16[8,16,2048]{2,1,0:T(8,128)(2,1)S(1)}, u32[]{:S(2)}, u32[]{:S(2)}) async-start(bf16[8,16,2048]{2,1,0:T(8,128)(2,1)} %bitcast.53), calls=%async_computation.1 | async-start | bytes 1048576 | tf_op jit(solution)/shard_map/all_to_all | solution.py:677
  87.7 8.7 %copy-start.8 = (bf16[1024,256]{1,0:T(8,128)(2,1)S(1)}, bf16[1024,256]{1,0:T(8,128)(2,1)}, u32[]{:S(2)}) copy-start(bf16[1024,256]{1,0:T(8,128)(2,1)} %copy-done.7) | copy-start | bytes 1572868
  87.7 8.7 %copy-start.10 = (f32[1024,32]{1,0:T(8,128)S(1)}, f32[1024,32]{1,0:T(8,128)}, u32[]{:S(2)}) copy-start(f32[1024,32]{1,0:T(8,128)} %copy-done.9) | copy-start | bytes 393220
  87.7 1.8 %collective-permute-start.22 = (bf16[256,512]{1,0:T(8,128)(2,1)}, bf16[256,512]{1,0:T(8,128)(2,1)S(1)}, u32[]{:S(2)}, u32[]{:S(2)}) collective-permute-start(bf16[256,512]{1,0:T(8,128)(2,1)} %copy-done.18), channel_id=1, source_target_pairs={{0,1},{1,0},{2,3},{3,2},{4,5},{5,4},{6,7},{7,6},{8,9},{9,8},{10,11... | collective-permute-start | bytes 786440 | tf_op jit(solution)/shard_map/ppermute | solution.py:524
  94.9 7.9 %copy-start.17 = (bf16[16,64,256]{2,1,0:T(8,128)(2,1)S(1)}, bf16[16,64,256]{2,1,0:T(8,128)(2,1)}, u32[]{:S(2)}) copy-start(bf16[16,64,256]{2,1,0:T(8,128)(2,1)} %copy-done.16) | copy-start | bytes 1572868
  94.9 1.4 %collective-permute-start.23 = (bf16[256,384]{1,0:T(8,128)(2,1)S(1)}, bf16[256,384]{1,0:T(8,128)(2,1)S(1)}, u32[]{:S(2)}, u32[]{:S(2)}) collective-permute-start(bf16[256,384]{1,0:T(8,128)(2,1)S(1)} %get-tuple-element.101), channel_id=1, source_target_pairs={{0,1},{1,0},{2,3},{3,2},{4,5},{5,4},{6,7},{7,6},{8,9},{9,8},{10,11... | collective-permute-start | bytes 589832 | tf_op jit(solution)/shard_map/ppermute | solution.py:524
  96.4 12.3 %copy-start.19 = (bf16[256,128]{1,0:T(8,128)(2,1)S(1)}, bf16[256,128]{1,0:T(8,128)(2,1)}, u32[]{:S(2)}) copy-start(bf16[256,128]{1,0:T(8,128)(2,1)} %convert_add_fusion.3) | copy-start | bytes 196612
  98.3 1.5 %collective-permute-start.24 = (f32[320,128]{1,0:T(8,128)S(1)}, f32[320,128]{1,0:T(8,128)S(1)}, u32[]{:S(2)}, u32[]{:S(2)}) collective-permute-start(f32[320,128]{1,0:T(8,128)S(1)} %shard_map.176), channel_id=1, source_target_pairs={{0,1},{1,0},{2,3},{3,2},{4,5},{5,4},{6,7},{7,6},{8,9},{9,8},{10,11... | collective-permute-start | bytes 491528 | tf_op jit(solution)/shard_map/ppermute | solution.py:524
  99.8 18.3 %copy-start.6 = (bf16[16,64,256]{2,1,0:T(8,128)(2,1)S(1)}, bf16[16,64,256]{2,1,0:T(8,128)(2,1)}, u32[]{:S(2)}) copy-start(bf16[16,64,256]{2,1,0:T(8,128)(2,1)} %copy-done.5) | copy-start | bytes 1572868
  102.5 6.2 %collective-permute-start.30 = (bf16[320,128]{1,0:T(8,128)(2,1)S(1)}, bf16[320,128]{1,0:T(8,128)(2,1)S(1)}, u32[]{:S(2)}, u32[]{:S(2)}) collective-permute-start(bf16[320,128]{1,0:T(8,128)(2,1)S(1)} %add.44), channel_id=1, source_target_pairs={{0,8},{1,9},{2,10},{3,11},{4,12},{5,13},{6,14},{7,15},{8,0},{9,1},... | collective-permute-start | bytes 245768 | tf_op jit(solution)/shard_map/ppermute | solution.py:524
  102.8 15.3 %collective-permute-start.33 = (bf16[16,64,256]{2,1,0:T(8,128)(2,1)S(1)}, bf16[16,64,256]{2,1,0:T(8,128)(2,1)S(1)}, u32[]{:S(2)}, u32[]{:S(2)}) collective-permute-start(bf16[16,64,256]{2,1,0:T(8,128)(2,1)S(1)} %copy-done.17), channel_id=1, source_target_pairs={{0,1},{1,0},{2,3},{3,2},{4,5},{5,4},{6,7},{7,6},{8,9},{9,8},{10,11... | collective-permute-start | bytes 1572872 | tf_op jit(solution)/shard_map/ppermute | solution.py:524
  102.8 6.6 %collective-permute-start.25 = (bf16[2,144,256]{2,1,0:T(8,128)(2,1)S(1)}, bf16[2,144,256]{2,1,0:T(8,128)(2,1)S(1)}, u32[]{:S(2)}, u32[]{:S(2)}) collective-permute-start(bf16[2,144,256]{2,1,0:T(8,128)(2,1)S(1)} %get-tuple-element.107), channel_id=1, source_target_pairs={{0,2},{1,3},{2,0},{3,1},{4,6},{5,7},{6,4},{7,5},{8,10},{9,11},{10,... | collective-permute-start | bytes 442376 | tf_op jit(solution)/shard_map/ppermute | solution.py:524
  104.3 8.0 %collective-permute-start.27 = (bf16[2,144,256]{2,1,0:T(8,128)(2,1)S(1)}, bf16[2,144,256]{2,1,0:T(8,128)(2,1)S(1)}, u32[]{:S(2)}, u32[]{:S(2)}) collective-permute-start(bf16[2,144,256]{2,1,0:T(8,128)(2,1)S(1)} %get-tuple-element.110), channel_id=1, source_target_pairs={{0,2},{1,3},{2,0},{3,1},{4,6},{5,7},{6,4},{7,5},{8,10},{9,11},{10,... | collective-permute-start | bytes 442376 | tf_op jit(solution)/shard_map/ppermute | solution.py:524
  108.7 7.8 %collective-permute-start.31 = (bf16[576,128]{1,0:T(8,128)(2,1)S(1)}, bf16[576,128]{1,0:T(8,128)(2,1)S(1)}, u32[]{:S(2)}, u32[]{:S(2)}) collective-permute-start(bf16[576,128]{1,0:T(8,128)(2,1)S(1)} %pad_maximum_fusion.1), channel_id=1, source_target_pairs={{0,4},{1,5},{2,6},{3,7},{4,0},{5,1},{6,2},{7,3},{8,12},{9,13},{10,... | collective-permute-start | bytes 442376 | tf_op jit(solution)/shard_map/ppermute | solution.py:524
  112.3 10.9 %copy-start.11 = (bf16[8,256,20]{1,0,2:T(8,128)(2,1)S(1)}, bf16[8,256,20]{1,0,2:T(8,128)(2,1)}, u32[]{:S(2)}) copy-start(bf16[8,256,20]{1,0,2:T(8,128)(2,1)} %param.16) | copy-start | bytes 245764
  112.3 10.9 %copy-start.12 = (bf16[128,256]{1,0:T(8,128)(2,1)S(1)}, bf16[128,256]{1,0:T(8,128)(2,1)}, u32[]{:S(2)}) copy-start(bf16[128,256]{1,0:T(8,128)(2,1)} %refs_4_.5) | copy-start | bytes 196612
  112.4 10.9 %copy-start.14 = (f32[32,128]{1,0:T(8,128)S(1)}, f32[32,128]{1,0:T(8,128)}, u32[]{:S(2)}) copy-start(f32[32,128]{1,0:T(8,128)} %get-tuple-element.117.refs_6_) | copy-start | bytes 49156
  112.4 10.9 %copy-start.15 = (s32[128]{0:T(128)S(1)}, s32[128]{0:T(128)}, u32[]{:S(2)}) copy-start(s32[128]{0:T(128)} %param.12) | copy-start | bytes 1540
  112.4 10.8 %collective-permute-start.26 = (bf16[144,256]{1,0:T(8,128)(2,1)S(1)}, bf16[144,256]{1,0:T(8,128)(2,1)S(1)}, u32[]{:S(2)}, u32[]{:S(2)}) collective-permute-start(bf16[144,256]{1,0:T(8,128)(2,1)S(1)} %get-tuple-element.133), channel_id=1, source_target_pairs={{0,4},{1,5},{2,6},{3,7},{4,0},{5,1},{6,2},{7,3},{8,12},{9,13},{10,... | collective-permute-start | bytes 221192 | tf_op jit(solution)/shard_map/ppermute | solution.py:524
  113.9 9.3 %collective-permute-start.29 = (bf16[144,256]{1,0:T(8,128)(2,1)S(1)}, bf16[144,256]{1,0:T(8,128)(2,1)S(1)}, u32[]{:S(2)}, u32[]{:S(2)}) collective-permute-start(bf16[144,256]{1,0:T(8,128)(2,1)S(1)} %get-tuple-element.131), channel_id=1, source_target_pairs={{0,12},{1,13},{2,14},{3,15},{4,8},{5,9},{6,10},{7,11},{8,4},{9,5},... | collective-permute-start | bytes 221192 | tf_op jit(solution)/shard_map/ppermute | solution.py:524
  116.6 6.7 %collective-permute-start.28 = (bf16[144,256]{1,0:T(8,128)(2,1)S(1)}, bf16[144,256]{1,0:T(8,128)(2,1)S(1)}, u32[]{:S(2)}, u32[]{:S(2)}) collective-permute-start(bf16[144,256]{1,0:T(8,128)(2,1)S(1)} %get-tuple-element.132), channel_id=1, source_target_pairs={{0,8},{1,9},{2,10},{3,11},{4,12},{5,13},{6,14},{7,15},{8,0},{9,1},... | collective-permute-start | bytes 221192 | tf_op jit(solution)/shard_map/ppermute | solution.py:524
  116.6 5.2 %collective-permute-start.32 = (bf16[576,128]{1,0:T(8,128)(2,1)S(1)}, bf16[576,128]{1,0:T(8,128)(2,1)S(1)}, u32[]{:S(2)}, u32[]{:S(2)}) collective-permute-start(bf16[576,128]{1,0:T(8,128)(2,1)S(1)} %add_convert_fusion.1), channel_id=1, source_target_pairs={{0,2},{1,3},{2,0},{3,1},{4,6},{5,7},{6,4},{7,5},{8,10},{9,11},{10,... | collective-permute-start | bytes 442376 | tf_op jit(solution)/shard_map/ppermute | solution.py:524
